TPU v7x, 32 devices: a whole 2x2x4 slice. The times are simulated.
32 devices in a mesh: dom: 8 (over y, x, core), plane: 4 (over z).
Axes of the slice: x: 2, y: 2, z: 4, core: 2. Of those that a mesh axis runs over, the one named last changes fastest.
Arguments:
- adjoint: float32 [3, 64, 9, 9, 256], P(None, 'plane', None, None, 'dom'), may hold values from -6 to 6
- metric: float32 [4, 256], P(None, 'dom'), may hold values from 0.5 to 2
- base_flow: float32 [2, 12, 1327104], P(None, None, ('dom', 'plane')), may hold values from -6 to 6
- edge_list: int32 [8, 5, 24], P('dom'), may hold values from -1 to 127, as said below
- flips: int32 [8, 5, 24], P('dom'), may hold values from 0 to 1, as said below
Outputs:
- adjoint_next: float32 [3, 64, 9, 9, 256], P(None, 'plane', None, None, 'dom')
Inputs may be any that keep to these rules, and one draw needn't show every extreme that they name: `edge_list`: entries are -1 or a local edge id j * 32 + l; no edge appears twice in one partition; filled slots come first in each block; a slot is filled exactly where its pair (as the steps define it) is filled, so block 2 has an even count; some block of some partition has all 24 slots filled, and every partition has an empty slot. `flips`: paired slots carry the same flag.
All inputs are finite; a program needn't handle non-finite values.
Results may differ from a plain program's by a relative error of at most 0.0003.
Values sent between devices are 32-bit elements; how exact they have to be, the bound alone decides.
No kernel may reach another device: no remote copies, remote signals or barrier semaphores. Data moves between devices by JAX's collectives and lax.ppermute only.
A program may use at most 128 MiB of HBM per device.

v0:
```python
import functools

import jax
import jax.numpy as jnp
import numpy as np
from jax import lax
from jax.experimental import pallas as pl
from jax.experimental.pallas import tpu as pltpu
from jax.sharding import PartitionSpec as P

MODES = 64
STEPS = 2


step_size = 0.01
viscosity = 0.02


def passed_along(shard, axis, by):
    size = lax.axis_size(axis)
    return lax.ppermute(shard, axis, [(i, (i + by) % size) for i in range(size)])


def cheb_table(node_count):
    order = node_count - 1
    node_ids = jnp.arange(node_count, dtype=jnp.int32)
    node_coords = -jnp.cos(jnp.pi * node_ids.astype(jnp.float32) / order)
    weight = jnp.where((node_ids == 0) | (node_ids == order), 2.0, 1.0).astype(jnp.float32)
    parity = jnp.where((node_ids[:, None] + node_ids[None, :]) % 2 == 0, 1.0, -1.0).astype(
        jnp.float32
    )
    on_diag = node_ids[:, None] == node_ids[None, :]
    differ = jnp.where(on_diag, 1.0, node_coords[:, None] - node_coords[None, :])
    off_diag = jnp.where(on_diag, 0.0, weight[:, None] / weight[None, :] * parity / differ)
    return off_diag - jnp.diag(jnp.sum(off_diag, axis=1))


def span_tables(modes):
    mode_ids = jnp.arange(modes, dtype=jnp.int32)
    wavenumber = (mode_ids + 1) // 2
    is_cosine = (mode_ids % 2 == 1) | (mode_ids == 0)
    span_ids = jnp.arange(modes, dtype=jnp.int32)
    phase_num = span_ids[:, None] * wavenumber[None, :] % modes
    angles = 2.0 * jnp.pi * phase_num.astype(jnp.float32) / modes
    cosines = jnp.cos(angles)
    sines = jnp.sin(angles)
    wave_f = wavenumber.astype(jnp.float32)
    span_basis = jnp.where(is_cosine[None, :], cosines, sines)
    span_slope = jnp.where(is_cosine[None, :], -wave_f[None, :] * sines, wave_f[None, :] * cosines)
    scaling = jnp.where((mode_ids == 0) | (mode_ids == modes - 1), 1.0 / modes, 2.0 / modes).astype(
        jnp.float32
    )
    forward = span_basis.T * scaling[:, None]
    return (span_basis, span_slope, forward, wave_f * wave_f)


def directional(field_data, metric, deriv_table, xi_row, eta_row):
    along_xi = jnp.einsum(
        "ai,cmije->cmaje", deriv_table, field_data, precision=lax.Precision.HIGHEST
    )
    along_eta = jnp.einsum(
        "bj,cmije->cmibe", deriv_table, field_data, precision=lax.Precision.HIGHEST
    )
    return metric[xi_row] * along_xi + metric[eta_row] * along_eta


def advect(coeffs, base_now, span_basis, span_slope, forward):
    values = jnp.einsum("nm,fmq->fnq", span_basis, coeffs, precision=lax.Precision.HIGHEST)
    along_z = jnp.einsum("nm,cmq->cnq", span_slope, coeffs[0:3], precision=lax.Precision.HIGHEST)
    products = []
    for comp in range(3):
        term = (
            base_now[0] * values[3 + comp]
            + base_now[1] * values[6 + comp]
            + base_now[2] * along_z[comp]
        )
        term = term - (
            values[0] * base_now[3 + comp]
            + values[1] * base_now[6 + comp]
            + values[2] * base_now[9 + comp]
        )
        products.append(term)
    return jnp.einsum("mn,cnq->cmq", forward, jnp.stack(products), precision=lax.Precision.HIGHEST)


def accumulate(field_data, edge_sums, counts):
    node_count = field_data.shape[2]
    last = node_count - 1
    total = field_data
    total = total.at[:, :, :, 0, :].add(edge_sums[:, :, :, 0, :])
    total = total.at[:, :, last, :, :].add(edge_sums[:, :, :, 1, :])
    total = total.at[:, :, :, last, :].add(edge_sums[:, :, :, 2, :])
    total = total.at[:, :, 0, :, :].add(edge_sums[:, :, :, 3, :])
    weight = jnp.ones((node_count, node_count, field_data.shape[4]), jnp.float32)
    weight = weight.at[:, 0, :].add(counts[0][None, :])
    weight = weight.at[last, :, :].add(counts[1][None, :])
    weight = weight.at[:, last, :].add(counts[2][None, :])
    weight = weight.at[0, :, :].add(counts[3][None, :])
    return total / weight


def assemble(field_data, edge_slots, flip_flags):
    components, local_modes, node_count, _, elements = field_data.shape
    last = node_count - 1
    row_count = components * local_modes * node_count
    traces = jnp.stack(
        [
            field_data[:, :, :, 0, :],
            field_data[:, :, last, :, :],
            field_data[:, :, :, last, :],
            field_data[:, :, 0, :, :],
        ],
        axis=3,
    )
    edge_table = traces.reshape(row_count, 4 * elements)
    blocks, capacity = edge_slots.shape
    half_span = (blocks - 1) // 2
    slot_edges = edge_slots.reshape(-1)
    occupied = (slot_edges >= 0).astype(jnp.float32)
    outgoing = jnp.take(edge_table, jnp.maximum(slot_edges, 0), axis=1) * occupied[None, :]

    def block_of(block_id):
        return outgoing[:, block_id * capacity : (block_id + 1) * capacity]

    own_pairs = (
        block_of(half_span)
        .reshape(row_count, capacity // 2, 2)[:, :, ::-1]
        .reshape(row_count, capacity)
    )
    received = {half_span: own_pairs}
    for block_id in range(blocks):
        if block_id != half_span:
            received[block_id] = passed_along(
                block_of(blocks - 1 - block_id), "dom", half_span - block_id
            )
    partners = jnp.concatenate([received[block_id] for block_id in range(blocks)], axis=1)
    shaped = partners.reshape(components * local_modes, node_count, blocks * capacity)
    shaped = (
        jnp.where(flip_flags.reshape(-1)[None, None, :] == 1, shaped[:, ::-1, :], shaped)
        * occupied[None, None, :]
    )
    onehot = (slot_edges[:, None] == jnp.arange(4 * elements, dtype=jnp.int32)[None, :]).astype(
        jnp.float32
    )
    edge_sums = jnp.dot(
        shaped.reshape(row_count, blocks * capacity), onehot, precision=lax.Precision.HIGHEST
    )
    edge_sums = edge_sums.reshape(components, local_modes, node_count, 4, elements)
    counts = jnp.sum(onehot, axis=0).reshape(4, elements)
    return accumulate(field_data, edge_sums, counts)


def advance(
    adjoint_state,
    metric,
    base_now,
    edge_slots,
    flip_flags,
    deriv_table,
    span_basis,
    span_slope,
    forward,
    wave_local,
):
    components, local_modes, node_count, _, elements = adjoint_state.shape
    points = node_count * node_count * elements
    grad_x = directional(adjoint_state, metric, deriv_table, 0, 2)
    grad_y = directional(adjoint_state, metric, deriv_table, 1, 3)
    stacked = jnp.concatenate([adjoint_state, grad_x, grad_y], axis=0).reshape(
        9, local_modes, points
    )
    gathered = lax.all_to_all(stacked, "plane", split_axis=2, concat_axis=1, tiled=True)
    advective = advect(gathered, base_now, span_basis, span_slope, forward)
    returned = lax.all_to_all(advective, "plane", split_axis=1, concat_axis=2, tiled=True).reshape(
        adjoint_state.shape
    )
    laplacian = directional(grad_x, metric, deriv_table, 0, 2) + directional(
        grad_y, metric, deriv_table, 1, 3
    )
    updated = adjoint_state + step_size * (
        returned + viscosity * (laplacian - wave_local[None, :, None, None, None] * adjoint_state)
    )
    return assemble(updated, edge_slots, flip_flags)


NODES = 9
LANES = 128
SLAB_TILES = 3
STATE_TILES = 7
SEND_TILES = 12
CHUNK_TILES = 6
BODY_TILES = 5
BACK_TILES = 31
GROUP = 8
PARTNERS = (0, 2, 3, 1)
STEP_VISC = step_size * viscosity


def cheb_numbers():
    order = NODES - 1
    coords = -np.cos(np.pi * np.arange(NODES) / order)
    weight = np.ones(NODES)
    weight[0] = weight[-1] = 2.0
    table = np.zeros((NODES, NODES))
    for a in range(NODES):
        for i in range(NODES):
            if a != i:
                table[a, i] = weight[a] / weight[i] * (-1.0) ** (a + i) / (coords[a] - coords[i])
    return table - np.diag(table.sum(axis=1))


DERIV = cheb_numbers()


def span_numbers():
    modes = np.arange(MODES)
    wave = (modes + 1) // 2
    is_cosine = (modes % 2 == 1) | (modes == 0)
    angles = 2.0 * np.pi * (np.arange(MODES)[:, None] * wave[None, :] % MODES) / MODES
    cosines, sines = np.cos(angles), np.sin(angles)
    basis = np.where(is_cosine, cosines, sines)
    slope = np.where(is_cosine, -wave * sines, wave * cosines)
    scaling = np.where((modes == 0) | (modes == MODES - 1), 1.0 / MODES, 2.0 / MODES)
    return basis, slope, basis.T * scaling[:, None]


def in_two(table):
    table = table.astype(np.float32)
    high = table.astype(jnp.bfloat16)
    low = (table - high.astype(np.float32)).astype(jnp.bfloat16)
    return high, low


def span_weights(planes):
    basis, slope, forward = span_numbers()
    local = MODES // planes
    to_span, to_modes = [], []
    for me in range(planes):
        came = np.concatenate([(me ^ step) * local + np.arange(local) for step in PARTNERS])
        high, low = in_two(np.concatenate([basis, slope])[:, came])
        to_span.append(np.concatenate([high, high, low], axis=1))
        high, low = in_two(forward[came])
        to_modes.append(np.concatenate([high, high, low], axis=1))
    return np.stack(to_span), np.stack(to_modes)


def eta_bands(first_lane, lanes, count):
    bands = np.zeros((24, lanes), np.float32)
    for lane in range(count):
        j = (first_lane + lane) % 288 // 32
        for d in range(-8, 9):
            if 0 <= j + d < NODES:
                bands[d + 8, lane] = DERIV[j, j + d]
    return bands


def tile_plan(segments, tiles):
    plan = [[] for _ in range(tiles)]
    for source, src, dst, length in segments:
        done = 0
        while done < length:
            s, d = src + done, dst + done
            size = min(length - done, LANES - s % LANES, LANES - d % LANES)
            plan[d // LANES].append((source, s // LANES, (d - s) % LANES, d % LANES, size))
            done += size
    return plan


def send_segments(chunk, points):
    ring, slab = STATE_TILES * LANES, NODES * 32
    turned = (points - 2 * slab) * chunk
    segments = []
    for r in range(3):
        start = (r * slab - turned) % ring
        first = min(slab, ring - start)
        segments.append((("state", 2 * chunk + r), 0, start, first))
        if first < slab:
            segments.append((("state", 2 * chunk + r), first, 0, slab - first))
    gap = (3 * slab - turned) % ring
    body = (points // LANES) * LANES
    lane = points * chunk
    for lane in range(points * chunk, points * (chunk + 1), 8):
        at = lane - points * chunk
        target = ring + at if at < body else gap + at - body
        source = ("xi", lane // slab)
        if segments[-1][0] == source and segments[-1][1] + segments[-1][3] == lane % slab and (
            segments[-1][2] + segments[-1][3] == target
        ):
            segments[-1] = (source, segments[-1][1], segments[-1][2], segments[-1][3] + 8)
        else:
            segments.append((source, lane % slab, target, 8))
    return segments, gap


def return_segments(points):
    slab = NODES * 32
    body = points // LANES * LANES
    plans = []
    for i in range(NODES):
        segments = []
        for chunk in range(4):
            for name, start, stop in (("body", 0, body), ("tail", body, points)):
                low = max(i * slab, chunk * points + start)
                high = min((i + 1) * slab, chunk * points + stop)
                if low < high:
                    segments.append(((name, chunk), low - chunk * points - start, low - i * slab, high - low))
        plans.append(tile_plan(segments, SLAB_TILES))
    return plans


def lane_ids(rows):
    return lax.broadcasted_iota(jnp.int32, (rows, LANES), 1)


def turn(value, shift):
    return value if shift % LANES == 0 else pltpu.roll(value, shift % LANES, 1)


def pieced(pieces, load, lanes):
    total = None
    for source, tile, shift, low, size in pieces:
        value = turn(load(source, tile), shift)
        if total is None:
            total = value
        else:
            total = jnp.where((lanes >= low) & (lanes < low + size), value, total)
    return total


def tile_at(ref, lead, rows, tile):
    return ref[(*lead, rows, pl.ds(tile * LANES, LANES))]


def along_i(tiles):
    return [
        sum(tiles[i] * float(DERIV[a, i]) for i in range(1, NODES)) + tiles[0] * float(DERIV[a, 0])
        for a in range(NODES)
    ]


def turned_tiles(tiles, lanes):
    out = [tiles]
    for s in range(1, 4):
        spun = [pltpu.roll(t, LANES - 32 * s, 1) for t in tiles]
        out.append(
            [
                jnp.where(lanes < LANES - 32 * s, spun[t], spun[(t + 1) % len(tiles)])
                for t in range(len(tiles))
            ]
        )
    return out


def along_j(turned, ring, tile, band, used):
    total = None
    for d in used:
        term = turned[d % 4][(tile + d // 4) % ring] * band(d)
        total = term if total is None else total + term
    return total


def make_sends(me, plans, rows_total, state, xi, staged, outs):
    rows_step = 8
    lanes = lane_ids(rows_step)

    def some_rows(g, _):
        rows = pl.ds(pl.multiple_of(g * rows_step, rows_step), rows_step)
        for t in range(SLAB_TILES):
            for a, value in enumerate(along_i([tile_at(state, (i,), rows, t) for i in range(NODES)])):
                xi[a, rows, pl.ds(t * LANES, LANES)] = value

        def load(source, tile):
            return tile_at(state if source[0] == "state" else xi, (source[1],), rows, tile)

        for chunk, plan in enumerate(plans):
            for t, pieces in enumerate(plan):
                staged[chunk, rows, pl.ds(t * LANES, LANES)] = pieced(pieces, load, lanes)
        return 0

    lax.fori_loop(0, rows_total // rows_step, some_rows, 0)
    for k, out in enumerate(outs):
        out[...] = staged[me ^ PARTNERS[k]]


def first_kernel(plans, adjoint, state, out0, out1, out2, out3, xi, staged, taken, sems):
    me = lax.axis_index("plane")
    comps, local = taken.shape[0], taken.shape[3]
    copies = [pltpu.make_async_copy(adjoint.at[:, i], taken.at[:, i], sems.at[i]) for i in range(NODES)]
    for copy in copies:
        copy.start()
    for i in range(NODES):
        copies[i].wait()
        for c in range(comps):
            rows = pl.ds(c * local, local)
            for t in range(SLAB_TILES):
                parts = [taken[c, i, j] for j in range(4 * t, min(4 * t + 4, NODES))]
                parts += [jnp.zeros_like(parts[0])] * (4 - len(parts))
                state[i, rows, pl.ds(t * LANES, LANES)] = jnp.concatenate(parts, axis=1)
    make_sends(me, plans, comps * local, state, xi, staged, (out0, out1, out2, out3))


def flow_kernel(points, flow, metric, out0, out1):
    me = lax.axis_index("plane")
    per_field = MODES * points // LANES
    lanes, subs = lane_ids(8), lax.broadcasted_iota(jnp.int32, (8, LANES), 0)
    shift = lax.rem(LANES - lax.rem(me * points, LANES), LANES)
    turned = pltpu.roll(metric[...], shift, 1)
    xi_x, xi_y, eta_x, eta_y = (turned[r : r + 1, :] for r in range(4))
    last = CHUNK_TILES - 1

    for s, out in enumerate((out0, out1)):
        for half in range(2):

            moved = (lanes + 64 * half + 8 * subs) & (LANES - 1)
            kept = lanes < LANES - 64 * half - 8 * subs

            def some_rows(h, _, s=s, half=half, out=out, moved=moved, kept=kept):
                rows = pl.ds(pl.multiple_of(16 * h + 8 * half, 8), 8)

                def field(f):
                    spun = []
                    for k in range(CHUNK_TILES):
                        start = 2 * (f * per_field + 40 * half + k) + s + h * (16 * points // LANES * 2)
                        block = flow[pl.ds(start, 8, stride=10), :]
                        spun.append(pick(block, moved))
                    tiles = [jnp.where(kept, spun[k], spun[k + 1]) for k in range(last)]
                    return tiles + [spun[last]]

                def put(f, t, value):
                    out[f, rows, pl.ds(t * LANES, LANES)] = value

                first, second = field(0), field(1)
                for t in range(CHUNK_TILES):
                    put(0, t, first[t] * xi_x + second[t] * xi_y)
                    put(1, t, first[t] * eta_x + second[t] * eta_y)
                for f in range(2, 12):
                    for t, value in enumerate(field(f)):
                        put(f, t, value)
                return 0

            lax.fori_loop(0, MODES // 16, some_rows, 0)


def tables_kernel(edges, flags, table):
    capacity, blocks = edges.shape
    lanes = lane_ids(capacity)
    slots = lax.broadcasted_iota(jnp.int32, (capacity, LANES), 0)
    here = slots == lax.rem(lanes, capacity)
    flag = jnp.zeros((1, LANES), jnp.int32)
    count = jnp.zeros((1, LANES), jnp.int32)
    table[...] = jnp.zeros(table.shape, jnp.int32)
    for o in range(blocks):
        column = jnp.broadcast_to(edges[:, o : o + 1], (capacity, LANES))
        held = column == lanes

        def summed(mask, value):
            return jnp.sum(jnp.where(mask, value, 0), axis=0, keepdims=True)

        table[o : o + 1, :] = summed(here, jnp.maximum(column, 0))
        table[5 + o : 6 + o, :] = summed(held, slots)
        present = summed(held, jnp.ones_like(slots))
        table[10 + o : 11 + o, :] = present
        flag += summed(held, jnp.broadcast_to(flags[:, o : o + 1], (capacity, LANES)))
        count += present
        if o == blocks // 2:
            partner = slots + 1 - 2 * lax.rem(slots, 2)
            slot_of = jnp.broadcast_to(summed(held, partner), (capacity, LANES))
            partner_edge = summed(slots == slot_of, jnp.maximum(column, 0))
            table[16:17, :] = jnp.where(present > 0, partner_edge, 0)
    table[15:16, :] = flag
    table[17:18, :] = count


def diffuse_kernel(state, metric, bands, local_sum, first, second):
    me = lax.axis_index("plane")
    rows_total = state.shape[1]
    lanes = lane_ids(8)
    local = rows_total // 3
    xi_x, xi_y, eta_x, eta_y = (metric[r : r + 1, :] for r in range(4))
    g_ii = xi_x * xi_x + xi_y * xi_y
    g_ij = xi_x * eta_x + xi_y * eta_y
    g_jj = eta_x * eta_x + eta_y * eta_y
    used = [[d for d in range(-8, 9) if any(0 <= j + d < NODES for j in range(4 * t, min(4 * t + 4, NODES)))]
            for t in range(SLAB_TILES)]

    def eta_of(tiles):
        turned = turned_tiles(tiles, lanes)
        return [
            along_j(turned, SLAB_TILES, t, lambda d, t=t: tile_at(bands, (), pl.ds(d + 8, 1), t), used[t])
            for t in range(SLAB_TILES)
        ]

    def some_rows(g, _):
        rows = pl.ds(pl.multiple_of(g * 8, 8), 8)
        first_mode = me * local + lax.rem(g * 8, local)
        wave = ((first_mode + lax.broadcasted_iota(jnp.int32, (8, LANES), 0) + 1) // 2).astype(jnp.float32)
        wave_sq = wave * wave
        for t in range(SLAB_TILES):
            for a, value in enumerate(along_i([tile_at(state, (i,), rows, t) for i in range(NODES)])):
                first[a, :, pl.ds(t * LANES, LANES)] = value
        for i in range(NODES):
            eta = eta_of([tile_at(state, (i,), rows, t) for t in range(SLAB_TILES)])
            mixed = []
            for t in range(SLAB_TILES):
                xi = first[i, :, pl.ds(t * LANES, LANES)]
                first[i, :, pl.ds(t * LANES, LANES)] = g_ii * xi + g_ij * eta[t]
                mixed.append(g_ij * xi + g_jj * eta[t])
            for t, value in enumerate(eta_of(mixed)):
                second[i, :, pl.ds(t * LANES, LANES)] = value
        for t in range(SLAB_TILES):
            tiles = [first[i, :, pl.ds(t * LANES, LANES)] for i in range(NODES)]
            for a, value in enumerate(along_i(tiles)):
                now = tile_at(state, (a,), rows, t)
                laplacian = value + second[a, :, pl.ds(t * LANES, LANES)]
                local_sum[a, rows, pl.ds(t * LANES, LANES)] = now + STEP_VISC * (laplacian - wave_sq * now)
        return 0

    lax.fori_loop(0, rows_total // 8, some_rows, 0)


def halves(value):
    high = value.astype(jnp.bfloat16)
    return high, (value - high.astype(jnp.float32)).astype(jnp.bfloat16)


def fields_kernel(gaps, source, bands, fields):
    me = lax.axis_index("plane")
    rows_total = source.shape[0]
    local = fields.shape[2]
    lanes = lane_ids(GROUP)
    gap = sum(jnp.where(me == b, g, 0) for b, g in enumerate(gaps))
    gap_tile, gap_lane = gap // LANES, lax.rem(gap, LANES)

    def some_rows(g, _):
        rows = pl.ds(pl.multiple_of(g * GROUP, GROUP), GROUP)
        c = g * GROUP // local
        target = pl.ds(pl.multiple_of(lax.rem(g * GROUP, local), GROUP), GROUP)

        def put(kind, t, value):
            fields[kind, c, target, pl.ds(t * LANES, LANES)] = value

        tiles = [tile_at(source, (), rows, t) for t in range(STATE_TILES)]
        turned = turned_tiles(tiles, lanes)
        for t in range(CHUNK_TILES):
            put(0, t, tiles[t])
            put(2, t, along_j(turned, STATE_TILES, t,
                              lambda d, t=t: bands[me, pl.ds(d + 8, 1), pl.ds(t * LANES, LANES)],
                              range(-8, 9)))
        for t in range(BODY_TILES):
            put(1, t, tile_at(source, (), rows, STATE_TILES + t))
        tail = source[rows, pl.ds(pl.multiple_of(gap_tile * LANES, LANES), LANES)]
        put(1, BODY_TILES, pltpu.roll(tail, lax.rem(LANES - gap_lane, LANES), 1))
        return 0

    lax.fori_loop(0, rows_total // GROUP, some_rows, 0)


def advect_kernel(fields0, fields1, fields2, fields3, flow, to_span, to_modes, *outs):
    me = lax.axis_index("plane")
    comps = fields0.shape[1]
    both = to_span[me]
    basis = both[:MODES]
    back = to_modes[me]
    width = 2 * LANES
    chunks = CHUNK_TILES * LANES // width
    lanes = lane_ids(GROUP)

    def dot(a, value):
        high, low = halves(value)
        stacked = jnp.concatenate([high, low, high], axis=0)
        return jnp.dot(a, stacked, preferred_element_type=jnp.float32)

    def results(part):
        def field(kind, c):
            return jnp.concatenate(
                [fields[kind, c, :, part] for fields in (fields0, fields1, fields2, fields3)], axis=0
            )

        values, sums = [], []
        for c in range(comps):
            out = dot(both, field(0, c))
            values.append(out[:MODES])
            along_x = flow[0, :, part] * dot(basis, field(1, c))
            along_y = flow[1, :, part] * dot(basis, field(2, c))
            sums.append(along_x + along_y + flow[2, :, part] * out[MODES:])
        for c in range(comps):
            taken = values[0] * flow[3 + c, :, part]
            taken += values[1] * flow[6 + c, :, part]
            taken += values[2] * flow[9 + c, :, part]
            yield c, dot(back, sums[c] - taken)

    def split(c, result):
        for k, out in enumerate(outs):
            for half in range(MODES // len(outs) // GROUP):
                first = k * (MODES // len(outs)) + half * GROUP
                yield k, out, c * (MODES // len(outs) // GROUP) + half, result[first : first + GROUP]

    def some_lanes(p, _):
        first = pl.multiple_of(p * width, width)
        for c, result in results(pl.ds(first, width)):
            for _, out, g, piece in split(c, result):
                out[:, pl.ds(pl.multiple_of(BODY_TILES * g * LANES + first, LANES), width)] = piece
        return 0

    lax.fori_loop(0, chunks - 1, some_lanes, 0)
    tails = [None] * len(outs)
    for c, result in results(pl.ds((chunks - 1) * width, width)):
        for k, out, g, piece in split(c, result):
            out[:, pl.ds((BODY_TILES * (g + 1) - 1) * LANES, LANES)] = piece[:, :LANES]
            tail = turn(piece[:, LANES:], 8 * g)
            tails[k] = tail if g == 0 else jnp.where(lanes >= 8 * g, tail, tails[k])
    for out, tail in zip(outs, tails):
        out[:, pl.ds((BACK_TILES - 1) * LANES, LANES)] = tail


def trace_blocks(me):
    odd, late = lax.rem(me, 2), lax.rem(me, 4) // 2
    return 3 - 2 * odd, 1 + 2 * odd, 4 - 4 * late, 4 * late


def trace_partner(me, matching, size):
    step, start = ((1, 0), (1, 1), (2, 0), (2, 2))[matching]
    return (((me + start) ^ step) - start) % size


def update_kernel(plans, in0, in1, in2, in3, local_sum, table, updated, own, out0, out1, out2, out3, chunks):
    me = lax.axis_index("plane")
    rows_total = local_sum.shape[1]
    last = NODES - 1
    lanes = lane_ids(8)
    for k, source in enumerate((in0, in1, in2, in3)):
        chunks[me ^ PARTNERS[k]] = source[...]

    trace_plans = [
        tile_plan([(k, 0, 0, 32), (last, 32 * k, 32, 32), (k, 256, 64, 32), (0, 32 * k, 96, 32)], 1)[0]
        for k in range(NODES)
    ]

    blocks = trace_blocks(lax.axis_index("dom"))

    def wide(row):
        return jnp.broadcast_to(table[pl.ds(row, 1), :], (8, LANES))

    def some_rows(g, _):
        rows = pl.ds(pl.multiple_of(g * 8, 8), 8)
        tails = [
            pltpu.roll(tile_at(chunks, (b,), slice(None), BACK_TILES - 1), lax.rem(LANES - 8 * g, LANES), 1)
            for b in range(4)
        ]

        def load(source, tile):
            if source[0] == "tail":
                return tails[source[1]]
            at = pl.multiple_of((BODY_TILES * g + tile) * LANES, LANES)
            return chunks[source[1], :, pl.ds(at, LANES)]

        for i in range(NODES):
            for t in range(SLAB_TILES):
                value = pieced(plans[i][t], load, lanes)
                updated[i, rows, pl.ds(t * LANES, LANES)] = (
                    tile_at(local_sum, (i,), rows, t) + step_size * value
                )
        raw = [
            pieced(plan, lambda i, tile: tile_at(updated, (i,), rows, tile), lanes) for plan in trace_plans
        ]
        turned_round = wide(15) == 1
        seen = [jnp.where(turned_round, raw[last - k], raw[k]) for k in range(NODES)]
        partner = wide(16)
        for k in range(NODES):
            own[k, rows, :] = pick(seen[k], partner)
        for o, out in zip(blocks, (out0, out1, out2, out3)):
            slot_edge = wide(o)
            for t in range(2):
                total = None
                for k in range(5 * t, min(5 * t + 5, NODES)):
                    value = pick(seen[k], slot_edge)
                    total = value if total is None else jnp.where(lanes >= 24 * (k - 5 * t), value, total)
                out[rows, pl.ds(t * LANES, LANES)] = total
        return 0

    lax.fori_loop(0, rows_total // 8, some_rows, 0)


def pick(value, index):
    return jnp.take_along_axis(value, index, axis=1, mode="promise_in_bounds")


def join_edges(table, updated, own, came, state):
    rows_total = updated.shape[1]
    last = NODES - 1
    lanes = lane_ids(8)
    blocks = trace_blocks(lax.axis_index("dom"))

    def wide(row):
        return jnp.broadcast_to(table[pl.ds(row, 1), :], (8, LANES))

    share = wide(17).astype(jnp.float32)
    quarter = lanes // 32

    def group(value, at):
        return turn(value, -32 * at)

    def some_rows(g, _):
        rows = pl.ds(pl.multiple_of(g * 8, 8), 8)
        sums = []
        for k in range(NODES):
            total = jnp.where(wide(12) > 0, own[k, rows, :], 0.0)
            for o, source in zip(blocks, came):
                value = pick(tile_at(source, (), rows, k // 5), wide(5 + o) + 24 * (k % 5))
                total = jnp.where(wide(10 + o) > 0, value, total)
            sums.append(total)

        def spread(at, t):
            nodes = range(4 * t, min(4 * t + 4, NODES))
            value, number = None, None
            for k in nodes:
                q = k - 4 * t
                moved = turn(sums[k], 32 * (q - at))
                many = turn(share, 32 * (q - at))
                value = jnp.where(quarter == q, moved, 0.0 if value is None else value)
                number = jnp.where(quarter == q, many, 0.0 if number is None else number)
            return value, number

        for i in range(NODES):
            for t in range(SLAB_TILES):
                total = tile_at(updated, (i,), rows, t)
                weight = None
                if t == 0:
                    total += jnp.where(quarter == 0, sums[i], 0.0)
                    weight = 1.0 + jnp.where(quarter == 0, share, 0.0)
                if i == last:
                    value, number = spread(1, t)
                    total += value
                    weight = (1.0 if weight is None else weight) + number
                if t == 2:
                    total += jnp.where(quarter == 0, group(sums[i], 2), 0.0)
                    weight = (1.0 if weight is None else weight) + jnp.where(quarter == 0, group(share, 2), 0.0)
                if i == 0:
                    value, number = spread(3, t)
                    total += value
                    weight = (1.0 if weight is None else weight) + number
                if weight is not None:
                    total = total / weight
                state[i, rows, pl.ds(t * LANES, LANES)] = total
        return 0

    lax.fori_loop(0, rows_total // 8, some_rows, 0)


def next_kernel(plans, table, updated, own, r0, r1, r2, r3, state, out0, out1, out2, out3, xi, staged):
    me = lax.axis_index("plane")
    join_edges(table, updated, own, (r0, r1, r2, r3), state)
    make_sends(me, plans, updated.shape[1], state, xi, staged, (out0, out1, out2, out3))


def last_kernel(table, updated, own, r0, r1, r2, r3, out, state, given, sems):
    join_edges(table, updated, own, (r0, r1, r2, r3), state)
    comps, local, elements = given.shape[0], given.shape[3], given.shape[4]
    copies = []
    for i in range(NODES):
        for c in range(comps):
            rows = pl.ds(c * local, local)
            for t in range(SLAB_TILES):
                tile = tile_at(state, (i,), rows, t)
                for q in range(min(4, NODES - 4 * t)):
                    given[c, i, 4 * t + q] = turn(tile, -32 * q)[:, :elements]
        copies.append(pltpu.make_async_copy(given.at[:, i], out.at[:, i], sems.at[i]))
        copies[-1].start()
    for copy in copies:
        copy.wait()


def f32(*shape):
    return jax.ShapeDtypeStruct(shape, jnp.float32)


def kernel_call(body, outs, scratch, flops, moved, **more):
    return pl.pallas_call(
        body,
        out_shape=outs,
        scratch_shapes=scratch,
        compiler_params=pltpu.CompilerParams(vmem_limit_bytes=16 * 1024 * 1024),
        cost_estimate=pl.CostEstimate(flops=flops, bytes_accessed=moved, transcendentals=0),
        **more,
    )


def swapped(buffers):
    planes = range(len(buffers))
    return [buffers[0]] + [
        lax.ppermute(buffer, "plane", [(i, i ^ step) for i in planes])
        for buffer, step in zip(buffers[1:], PARTNERS[1:])
    ]


def packed_shards(adjoint, metric, base_flow, edge_list, flips):
    comps, local, nodes, _, elements = adjoint.shape
    planes = MODES // local
    points = nodes * nodes * elements // planes
    rows_total = comps * local
    partitions = lax.axis_size("dom")
    state_shape = (nodes, rows_total, SLAB_TILES * LANES)

    layouts = [send_segments(chunk, points) for chunk in range(planes)]
    plans = [tile_plan(segments, SEND_TILES) for segments, _ in layouts]
    gaps = [gap for _, gap in layouts]
    back_plans = return_segments(points)
    to_span, to_modes = span_weights(planes)
    slab_bands = eta_bands(0, SLAB_TILES * LANES, nodes * elements)
    chunk_bands = np.stack(
        [eta_bands((points - 2 * nodes * elements) * b, CHUNK_TILES * LANES, points) for b in range(planes)]
    )

    metric_tile = jnp.pad(jnp.tile(metric, (1, LANES // elements)), ((0, 4), (0, 0)))
    flow_rows = (
        base_flow.reshape(STEPS, 12, -1, LANES).transpose(1, 2, 0, 3).reshape(-1, LANES)
    )

    in_hbm = pl.BlockSpec(memory_space=pltpu.HBM)
    sends = [f32(rows_total, SEND_TILES * LANES)] * planes
    send_scratch = [
        pltpu.VMEM(state_shape, jnp.float32),
        pltpu.VMEM((planes, rows_total, SEND_TILES * LANES), jnp.float32),
    ]
    row_copies = [
        pltpu.VMEM((comps, nodes, nodes, local, elements), jnp.float32),
        pltpu.SemaphoreType.DMA((nodes,)),
    ]
    in_rows = pltpu.with_memory_space_constraint(adjoint.transpose(0, 2, 3, 1, 4), pltpu.HBM)
    state, *outgoing = kernel_call(
        functools.partial(first_kernel, plans),
        [f32(*state_shape), *sends],
        send_scratch + row_copies,
        4 * 10**6,
        4 * 10**6,
        in_specs=[in_hbm],
    )(in_rows)
    flows = kernel_call(
        functools.partial(flow_kernel, points),
        [f32(12, MODES, CHUNK_TILES * LANES)] * STEPS,
        [],
        4 * 10**6,
        9 * 10**6,
    )(flow_rows, metric_tile)
    table = kernel_call(
        tables_kernel, jax.ShapeDtypeStruct((24, LANES), jnp.int32), [], 10**5, 10**5
    )(edge_list[0].T, flips[0].T)

    for step_index in range(STEPS):
        fields = [
            kernel_call(
                functools.partial(fields_kernel, gaps),
                f32(3, comps, local, CHUNK_TILES * LANES),
                [],
                2 * 10**6,
                10**6,
            )(came, chunk_bands)
            for came in swapped(outgoing)
        ]
        returning = kernel_call(
            advect_kernel,
            [f32(GROUP, BACK_TILES * LANES)] * planes,
            [],
            80 * 10**6,
            5 * 10**6,
        )(*fields, flows[step_index], to_span, to_modes)
        local_sum = kernel_call(
            diffuse_kernel,
            f32(*state_shape),
            [pltpu.VMEM((nodes, GROUP, SLAB_TILES * LANES), jnp.float32)] * 2,
            12 * 10**6,
            2 * 10**6,
        )(state, metric_tile, slab_bands)
        updated, own, *leaving = kernel_call(
            functools.partial(update_kernel, back_plans),
            [f32(*state_shape), f32(nodes, rows_total, LANES)] + [f32(rows_total, 2 * LANES)] * 4,
            [pltpu.VMEM((planes, GROUP, BACK_TILES * LANES), jnp.float32)],
            2 * 10**6,
            3 * 10**6,
        )(*swapped(returning), local_sum, table)
        traces = [
            lax.ppermute(
                buffer, "dom", [(i, trace_partner(i, matching, partitions)) for i in range(partitions)]
            )
            for matching, buffer in enumerate(leaving)
        ]
        if step_index + 1 < STEPS:
            state, *outgoing = kernel_call(
                functools.partial(next_kernel, plans),
                [f32(*state_shape), *sends],
                send_scratch,
                6 * 10**6,
                4 * 10**6,
            )(table, updated, own, *traces)
        else:
            result = kernel_call(
                last_kernel,
                f32(comps, nodes, nodes, local, elements),
                [pltpu.VMEM(state_shape, jnp.float32), *row_copies],
                2 * 10**6,
                3 * 10**6,
                out_specs=in_hbm,
            )(table, updated, own, *traces)
    return result.transpose(0, 3, 1, 2, 4)


def plain_shards(adjoint, metric, base_flow, edge_list, flips):
    local_modes = adjoint.shape[1]
    deriv_table = cheb_table(adjoint.shape[2])
    span_basis, span_slope, forward, wave_sq = span_tables(MODES)
    wave_local = lax.dynamic_slice_in_dim(
        wave_sq, lax.axis_index("plane") * local_modes, local_modes, 0
    )
    adjoint_state = adjoint
    for step_index in range(STEPS):
        base_now = base_flow[step_index].reshape(12, MODES, -1)
        adjoint_state = advance(
            adjoint_state,
            metric,
            base_now,
            edge_list[0],
            flips[0],
            deriv_table,
            span_basis,
            span_slope,
            forward,
            wave_local,
        )
    return adjoint_state


def shards(adjoint, metric, base_flow, edge_list, flips):
    if adjoint.shape[1:] == (MODES // 4, NODES, NODES, 32) and (
        edge_list.shape[1:] == (5, 24) and lax.axis_size("dom") % 4 == 0
    ):
        return packed_shards(adjoint, metric, base_flow, edge_list, flips)
    return plain_shards(adjoint, metric, base_flow, edge_list, flips)


def solution(mesh):
    placed = (
        P(None, "plane", None, None, "dom"),
        P(None, "dom"),
        P(None, None, ("dom", "plane")),
        P("dom", None, None),
        P("dom", None, None),
    )
    return jax.shard_map(
        shards,
        mesh=mesh,
        in_specs=placed,
        out_specs=P(None, "plane", None, None, "dom"),
        check_vma=False,
    )
```

profile of v0, /device:TPU:0, one launch (start us, length us, event | category | flops | bytes accessed | tf_op | source)
XLA Modules:
  0.0 121.1 jit_solution(15592883031506885)
XLA Ops:
  0.0 4.0 %shard_map.92 = (f32[9,48,384]{2,1,0:T(8,128)S(1)}, f32[48,1536]{1,0:T(8,128)S(1)}, f32[48,1536]{1,0:T(8,128)}, f32[48,1536]{1,0:T(8,128)}, f32[48,1536]{1,0:T(8,128)}) custom-call(f32[3,9,9,16,32]{4,3,2,1,0:T(8,128)} %bitcast.16), custom_call_target="tpu_custom_call" | custom-call | flops 4000000 | bytes 4000000 | tf_op jit(solution)/shard_map/pallas_call | solution.py:830
  4.9 4.0 %collective-permute-start = (f32[48,1536]{1,0:T(8,128)}, f32[48,1536]{1,0:T(8,128)}, u32[]{:S(2)}, u32[]{:S(2)}) collective-permute-start(f32[48,1536]{1,0:T(8,128)} %get-tuple-element.38), channel_id=1, source_target_pairs={{0,2},{1,3},{2,0},{3,1},{4,6},{5,7},{6,4},{7,5},{8,10},{9,11},{10,... | collective-permute-start | bytes 884744 | tf_op jit(solution)/shard_map/ppermute | solution.py:791
  8.9 1.3 %collective-permute-start.1 = (f32[48,1536]{1,0:T(8,128)}, f32[48,1536]{1,0:T(8,128)}, u32[]{:S(2)}, u32[]{:S(2)}) collective-permute-start(f32[48,1536]{1,0:T(8,128)} %get-tuple-element.39), channel_id=1, source_target_pairs={{0,3},{1,2},{2,1},{3,0},{4,7},{5,6},{6,5},{7,4},{8,11},{9,10},{10,... | collective-permute-start | bytes 884744 | tf_op jit(solution)/shard_map/ppermute | solution.py:791
  11.2 6.2 %reshape.10 = f32[2,12,324,128]{3,2,0,1:T(8,128)} reshape(f32[2,12,41472]{2,0,1:T(2,128)} %param.11) | data formatting | bytes 7962624 | tf_op jit(solution)/shard_map/reshape | solution.py:816
  17.5 4.2 %copy.15 = f32[12,324,2,128]{3,2,1,0:T(2,128)S(1)} copy(f32[12,324,2,128]{3,1,2,0:T(8,128)} %bitcast.15) | data formatting | bytes 7962624 | tf_op jit(solution)/shard_map/transpose | solution.py:816
  22.4 2.4 %shard_map.97 = (f32[12,64,768]{2,1,0:T(8,128)S(1)}, f32[12,64,768]{2,1,0:T(8,128)S(1)}) custom-call(f32[7776,128]{1,0:T(8,128)S(1)} %bitcast.12, f32[8,128]{1,0:T(8,128)S(1)} %pad.4.metric), custom_call_target="tpu_custom_call" | custom-call | flops 4000000 | bytes 9000000 | tf_op jit(solution)/shard_map/pallas_call | solution.py:838
  24.8 4.9 %collective-permute-done.source = f32[48,1536]{1,0:T(8,128)} collective-permute-done((f32[48,1536]{1,0:T(8,128)}, f32[48,1536]{1,0:T(8,128)}, u32[]{:S(2)}, u32[]{:S(2)}) %collective-permute-start) | collective-permute-done | bytes 294944 | tf_op jit(solution)/shard_map/ppermute | solution.py:791
  29.7 1.6 %shard_map.94.fields1 = f32[3,3,16,768]{3,2,1,0:T(8,128)S(1)} custom-call(f32[48,1536]{1,0:T(8,128)} %collective-permute-done.source, f32[4,24,768]{2,1,0:T(8,128)S(1)} %copy-done), custom_call_target="tpu_custom_call" | custom-call | flops 2000000 | bytes 1000000 | tf_op jit(solution)/shard_map/pallas_call | solution.py:851
  31.3 1.6 %shard_map.95.fields2 = f32[3,3,16,768]{3,2,1,0:T(8,128)S(1)} custom-call(f32[48,1536]{1,0:T(8,128)} %collective-permute-done.1.source, f32[4,24,768]{2,1,0:T(8,128)S(1)} %copy-done), custom_call_target="tpu_custom_call" | custom-call | flops 2000000 | bytes 1000000 | tf_op jit(solution)/shard_map/pallas_call | solution.py:851
  33.7 2.2 %shard_map.98 = (f32[8,3968]{1,0:T(8,128)S(1)}, f32[8,3968]{1,0:T(8,128)}, f32[8,3968]{1,0:T(8,128)}, f32[8,3968]{1,0:T(8,128)}) custom-call(f32[3,3,16,768]{3,2,1,0:T(8,128)S(1)} %shard_map.93.fields0, f32[3,3,16,768]{3,2,1,0:T(8,128)S(1)} %shard_map.94.fields1, f32[3,3,16,768]{3,2,1,0:T(8,128)S(1)} %shard_map.95.fields2, ...), custom_call_target="tpu_custom_call" | custom-call | flops 80000000 | bytes 5000000 | tf_op jit(solution)/shard_map/pallas_call | solution.py:860
  35.9 6.5 %collective-permute-start.3 = (f32[8,3968]{1,0:T(8,128)}, f32[8,3968]{1,0:T(8,128)S(1)}, u32[]{:S(2)}, u32[]{:S(2)}) collective-permute-start(f32[8,3968]{1,0:T(8,128)} %get-tuple-element.43), channel_id=1, source_target_pairs={{0,2},{1,3},{2,0},{3,1},{4,6},{5,7},{6,4},{7,5},{8,10},{9,11},{10,... | collective-permute-start | bytes 380936 | tf_op jit(solution)/shard_map/ppermute | solution.py:791
  43.3 1.1 copy-done.3
  44.4 2.7 %shard_map.99.local_sum = f32[9,48,384]{2,1,0:T(8,128)S(1)} custom-call(f32[9,48,384]{2,1,0:T(8,128)S(1)} %copy-done.3, f32[8,128]{1,0:T(8,128)S(1)} %pad.4.metric, f32[24,384]{1,0:T(8,128)S(1)} %copy-done.5), custom_call_target="tpu_custom_call" | custom-call | flops 12000000 | bytes 2000000 | tf_op jit(solution)/shard_map/pallas_call | solution.py:867
  47.1 4.9 %collective-permute-done.3.in1 = f32[8,3968]{1,0:T(8,128)S(1)} collective-permute-done((f32[8,3968]{1,0:T(8,128)}, f32[8,3968]{1,0:T(8,128)S(1)}, u32[]{:S(2)}, u32[]{:S(2)}) %collective-permute-start.3) | collective-permute-done | bytes 127008 | tf_op jit(solution)/shard_map/ppermute | solution.py:791
  52.0 1.1 collective-permute-done.5.in3
  53.1 3.1 %shard_map.100 = (f32[9,48,384]{2,1,0:T(8,128)S(1)}, f32[9,48,128]{2,1,0:T(8,128)S(1)}, f32[48,256]{1,0:T(8,128)S(1)}, f32[48,256]{1,0:T(8,128)S(1)}, f32[48,256]{1,0:T(8,128)S(1)}, /*index=5*/f32[48,256]{1,0:T(8,128)S(1)}) custom-call(f32[8,3968]{1,0:T(8,128)S(1)} %get-tuple-element.42.in0, f32[8,3968]{1,0:T(8,128)S(1)} %collective-permute-done.3.in1, ...), custom_call_target="tpu_custom_call" | custom-call | flops 2000000 | bytes 3000000 | tf_op jit(solution)/shard_map/pallas_call | solution.py:874
  56.3 2.5 %collective-permute-start.7 = (f32[48,256]{1,0:T(8,128)S(1)}, f32[48,256]{1,0:T(8,128)S(1)}, u32[]{:S(2)}, u32[]{:S(2)}) collective-permute-start(f32[48,256]{1,0:T(8,128)S(1)} %get-tuple-element.50), channel_id=1, source_target_pairs={{0,28},{4,8},{8,4},{12,16},{16,12},{20,24},{24,20},{28,0},{1,29},{... | collective-permute-start | bytes 147464 | tf_op jit(solution)/shard_map/ppermute | solution.py:882
  58.8 2.0 %collective-permute-start.9 = (f32[48,256]{1,0:T(8,128)S(1)}, f32[48,256]{1,0:T(8,128)S(1)}, u32[]{:S(2)}, u32[]{:S(2)}) collective-permute-start(f32[48,256]{1,0:T(8,128)S(1)} %get-tuple-element.52), channel_id=1, source_target_pairs={{0,24},{4,28},{8,16},{12,20},{16,8},{20,12},{24,0},{28,4},{1,25},{... | collective-permute-start | bytes 147464 | tf_op jit(solution)/shard_map/ppermute | solution.py:882
  60.8 2.1 %collective-permute-done.8.r2 = f32[48,256]{1,0:T(8,128)S(1)} collective-permute-done((f32[48,256]{1,0:T(8,128)S(1)}, f32[48,256]{1,0:T(8,128)S(1)}, u32[]{:S(2)}, u32[]{:S(2)}) %collective-permute-start.8) | collective-permute-done | bytes 49184 | tf_op jit(solution)/shard_map/ppermute | solution.py:882
  63.9 2.6 %shard_map.101 = (f32[9,48,384]{2,1,0:T(8,128)S(1)}, f32[48,1536]{1,0:T(8,128)S(1)}, f32[48,1536]{1,0:T(8,128)S(1)}, f32[48,1536]{1,0:T(8,128)S(1)}, f32[48,1536]{1,0:T(8,128)S(1)}) custom-call(s32[24,128]{1,0:T(8,128)S(1)} %shard_map.91.table, f32[9,48,384]{2,1,0:T(8,128)S(1)} %get-tuple-element.47.updated, f32[9,48,128]{2,1,0:T(8,128)S(1)} %get-tuple-element.48.own, ...), custom_call_target="tpu_custom_call" | custom-call | flops 6000000 | bytes 4000000 | tf_op jit(solution)/shard_map/pallas_call | solution.py:888
  67.5 3.3 %collective-permute-start.11 = (f32[48,1536]{1,0:T(8,128)S(1)}, f32[48,1536]{1,0:T(8,128)S(1)}, u32[]{:S(2)}, u32[]{:S(2)}) collective-permute-start(f32[48,1536]{1,0:T(8,128)S(1)} %get-tuple-element.55), channel_id=1, source_target_pairs={{0,3},{1,2},{2,1},{3,0},{4,7},{5,6},{6,5},{7,4},{8,11},{9,10},{10,... | collective-permute-start | bytes 884744 | tf_op jit(solution)/shard_map/ppermute | solution.py:791
  71.4 18.6 %collective-permute-done.10.source = f32[48,1536]{1,0:T(8,128)S(1)} collective-permute-done((f32[48,1536]{1,0:T(8,128)S(1)}, f32[48,1536]{1,0:T(8,128)S(1)}, u32[]{:S(2)}, u32[]{:S(2)}) %collective-permute-start.10) | collective-permute-done | bytes 294944 | tf_op jit(solution)/shard_map/ppermute | solution.py:791
  92.1 1.5 %shard_map.106 = (f32[8,3968]{1,0:T(8,128)S(1)}, f32[8,3968]{1,0:T(8,128)S(1)}, f32[8,3968]{1,0:T(8,128)S(1)}, f32[8,3968]{1,0:T(8,128)S(1)}) custom-call(f32[3,3,16,768]{3,2,1,0:T(8,128)S(1)} %shard_map.102.fields0, f32[3,3,16,768]{3,2,1,0:T(8,128)S(1)} %shard_map.103.fields1, f32[3,3,16,768]{3,2,1,0:T(8,128)S(1)} %shard_map.104.fields2, ...), custom_call_target="tpu_custom_call" | custom-call | flops 80000000 | bytes 5000000 | tf_op jit(solution)/shard_map/pallas_call | solution.py:860
  93.5 5.1 %collective-permute-start.13 = (f32[8,3968]{1,0:T(8,128)S(1)}, f32[8,3968]{1,0:T(8,128)S(1)}, u32[]{:S(2)}, u32[]{:S(2)}) collective-permute-start(f32[8,3968]{1,0:T(8,128)S(1)} %get-tuple-element.59), channel_id=1, source_target_pairs={{0,2},{1,3},{2,0},{3,1},{4,6},{5,7},{6,4},{7,5},{8,10},{9,11},{10,... | collective-permute-start | bytes 380936 | tf_op jit(solution)/shard_map/ppermute | solution.py:791
  98.7 2.3 %collective-permute-start.14 = (f32[8,3968]{1,0:T(8,128)S(1)}, f32[8,3968]{1,0:T(8,128)S(1)}, u32[]{:S(2)}, u32[]{:S(2)}) collective-permute-start(f32[8,3968]{1,0:T(8,128)S(1)} %get-tuple-element.60), channel_id=1, source_target_pairs={{0,3},{1,2},{2,1},{3,0},{4,7},{5,6},{6,5},{7,4},{8,11},{9,10},{10,... | collective-permute-start | bytes 380936 | tf_op jit(solution)/shard_map/ppermute | solution.py:791
  100.9 2.7 %shard_map.107.local_sum = f32[9,48,384]{2,1,0:T(8,128)S(1)} custom-call(f32[9,48,384]{2,1,0:T(8,128)S(1)} %get-tuple-element.62.state, f32[8,128]{1,0:T(8,128)S(1)} %pad.4.metric, f32[24,384]{1,0:T(8,128)S(1)} %copy-done.5), custom_call_target="tpu_custom_call" | custom-call | flops 12000000 | bytes 2000000 | tf_op jit(solution)/shard_map/pallas_call | solution.py:867
  103.6 4.7 %collective-permute-done.13.in1 = f32[8,3968]{1,0:T(8,128)S(1)} collective-permute-done((f32[8,3968]{1,0:T(8,128)S(1)}, f32[8,3968]{1,0:T(8,128)S(1)}, u32[]{:S(2)}, u32[]{:S(2)}) %collective-permute-start.13) | collective-permute-done | bytes 127008 | tf_op jit(solution)/shard_map/ppermute | solution.py:791
  108.8 2.2 %shard_map.108 = (f32[9,48,384]{2,1,0:T(8,128)S(1)}, f32[9,48,128]{2,1,0:T(8,128)S(1)}, f32[48,256]{1,0:T(8,128)S(1)}, f32[48,256]{1,0:T(8,128)S(1)}, f32[48,256]{1,0:T(8,128)S(1)}, /*index=5*/f32[48,256]{1,0:T(8,128)S(1)}) custom-call(f32[8,3968]{1,0:T(8,128)S(1)} %get-tuple-element.58.in0, f32[8,3968]{1,0:T(8,128)S(1)} %collective-permute-done.13.in1, ...), custom_call_target="tpu_custom_call" | custom-call | flops 2000000 | bytes 3000000 | tf_op jit(solution)/shard_map/pallas_call | solution.py:874
  111.1 1.2 %collective-permute-start.17 = (f32[48,256]{1,0:T(8,128)S(1)}, f32[48,256]{1,0:T(8,128)S(1)}, u32[]{:S(2)}, u32[]{:S(2)}) collective-permute-start(f32[48,256]{1,0:T(8,128)S(1)} %get-tuple-element.66), channel_id=1, source_target_pairs={{0,28},{4,8},{8,4},{12,16},{16,12},{20,24},{24,20},{28,0},{1,29},{... | collective-permute-start | bytes 147464 | tf_op jit(solution)/shard_map/ppermute | solution.py:882
  113.2 1.4 %collective-permute-start.19 = (f32[48,256]{1,0:T(8,128)S(1)}, f32[48,256]{1,0:T(8,128)S(1)}, u32[]{:S(2)}, u32[]{:S(2)}) collective-permute-start(f32[48,256]{1,0:T(8,128)S(1)} %get-tuple-element.68), channel_id=1, source_target_pairs={{0,24},{4,28},{8,16},{12,20},{16,8},{20,12},{24,0},{28,4},{1,25},{... | collective-permute-start | bytes 147464 | tf_op jit(solution)/shard_map/ppermute | solution.py:882
  116.4 1.8 %collective-permute-done.19.r3 = f32[48,256]{1,0:T(8,128)S(1)} collective-permute-done((f32[48,256]{1,0:T(8,128)S(1)}, f32[48,256]{1,0:T(8,128)S(1)}, u32[]{:S(2)}, u32[]{:S(2)}) %collective-permute-start.19) | collective-permute-done | bytes 49184 | tf_op jit(solution)/shard_map/ppermute | solution.py:882
  118.2 2.9 %shard_map.109 = f32[3,9,9,16,32]{4,3,2,1,0:T(8,128)} custom-call(s32[24,128]{1,0:T(8,128)S(1)} %shard_map.91.table, f32[9,48,384]{2,1,0:T(8,128)S(1)} %get-tuple-element.63.updated, f32[9,48,128]{2,1,0:T(8,128)S(1)} %get-tuple-element.64.own, f32[48,256]{1,0:T(8,128)S(1)} %collective-permute-done.16.r0, f32[48,256]{1,0:T(8,128)S(1)} %collective-permute-done.17.r1, ...), custom_call_target="tpu_custom_call" | custom-call | flops 2000000 | bytes 3000000 | tf_op jit(solution)/shard_map/pallas_call | solution.py:896
  (50 shorter events, 11.9 us)
Async XLA Ops:
  4.0 0.8 copy-start.2
  4.9 24.9 %collective-permute-start = (f32[48,1536]{1,0:T(8,128)}, f32[48,1536]{1,0:T(8,128)}, u32[]{:S(2)}, u32[]{:S(2)}) collective-permute-start(f32[48,1536]{1,0:T(8,128)} %get-tuple-element.38), channel_id=1, source_target_pairs={{0,2},{1,3},{2,0},{3,1},{4,6},{5,7},{6,4},{7,5},{8,10},{9,11},{10,... | collective-permute-start | bytes 884744 | tf_op jit(solution)/shard_map/ppermute | solution.py:791
  8.9 22.4 %collective-permute-start.1 = (f32[48,1536]{1,0:T(8,128)}, f32[48,1536]{1,0:T(8,128)}, u32[]{:S(2)}, u32[]{:S(2)}) collective-permute-start(f32[48,1536]{1,0:T(8,128)} %get-tuple-element.39), channel_id=1, source_target_pairs={{0,3},{1,2},{2,1},{3,0},{4,7},{5,6},{6,5},{7,4},{8,11},{9,10},{10,... | collective-permute-start | bytes 884744 | tf_op jit(solution)/shard_map/ppermute | solution.py:791
  10.2 22.7 %collective-permute-start.2 = (f32[48,1536]{1,0:T(8,128)}, f32[48,1536]{1,0:T(8,128)S(1)}, u32[]{:S(2)}, u32[]{:S(2)}) collective-permute-start(f32[48,1536]{1,0:T(8,128)} %get-tuple-element.40), channel_id=1, source_target_pairs={{0,1},{1,0},{2,3},{3,2},{4,5},{5,4},{6,7},{7,6},{8,9},{9,8},{10,11... | collective-permute-start | bytes 884744 | tf_op jit(solution)/shard_map/ppermute | solution.py:791
  17.5 4.3 %copy-start = (f32[4,24,768]{2,1,0:T(8,128)S(1)}, f32[4,24,768]{2,1,0:T(8,128)}, u32[]{:S(2)}) copy-start(f32[4,24,768]{2,1,0:T(8,128)} %constant.11.clone.bands) | copy-start | bytes 884740
  24.8 8.9 %copy-start.1 = (bf16[4,128,192]{2,1,0:T(8,128)(2,1)S(1)}, bf16[4,128,192]{2,1,0:T(8,128)(2,1)}, u32[]{:S(2)}) copy-start(bf16[4,128,192]{2,1,0:T(8,128)(2,1)} %constant.12.clone.to_span) | copy-start | bytes 589828
  24.8 8.9 %copy-start.4 = (bf16[4,64,192]{2,1,0:T(8,128)(2,1)S(1)}, bf16[4,64,192]{2,1,0:T(8,128)(2,1)}, u32[]{:S(2)}) copy-start(bf16[4,64,192]{2,1,0:T(8,128)(2,1)} %constant.13.clone.to_modes) | copy-start | bytes 294916
  33.6 9.4 %copy-start.6 = (s32[1,5,24]{2,0,1:T(1,128)S(1)}, s32[1,5,24]{2,0,1:T(1,128)}, u32[]{:S(2)}) copy-start(s32[1,5,24]{2,0,1:T(1,128)} %param.12) | copy-start | bytes 1444
  33.6 9.4 %copy-start.7 = (s32[1,5,24]{2,0,1:T(1,128)S(1)}, s32[1,5,24]{2,0,1:T(1,128)}, u32[]{:S(2)}) copy-start(s32[1,5,24]{2,0,1:T(1,128)} %param.13) | copy-start | bytes 1444
  33.7 9.6 %copy-start.5 = (f32[24,384]{1,0:T(8,128)S(1)}, f32[24,384]{1,0:T(8,128)}, u32[]{:S(2)}) copy-start(f32[24,384]{1,0:T(8,128)} %constant.14.clone.bands) | copy-start | bytes 110596
  35.9 16.1 %collective-permute-start.3 = (f32[8,3968]{1,0:T(8,128)}, f32[8,3968]{1,0:T(8,128)S(1)}, u32[]{:S(2)}, u32[]{:S(2)}) collective-permute-start(f32[8,3968]{1,0:T(8,128)} %get-tuple-element.43), channel_id=1, source_target_pairs={{0,2},{1,3},{2,0},{3,1},{4,6},{5,7},{6,4},{7,5},{8,10},{9,11},{10,... | collective-permute-start | bytes 380936 | tf_op jit(solution)/shard_map/ppermute | solution.py:791
  42.4 9.6 %collective-permute-start.4 = (f32[8,3968]{1,0:T(8,128)}, f32[8,3968]{1,0:T(8,128)S(1)}, u32[]{:S(2)}, u32[]{:S(2)}) collective-permute-start(f32[8,3968]{1,0:T(8,128)} %get-tuple-element.44), channel_id=1, source_target_pairs={{0,3},{1,2},{2,1},{3,0},{4,7},{5,6},{6,5},{7,4},{8,11},{9,10},{10,... | collective-permute-start | bytes 380936 | tf_op jit(solution)/shard_map/ppermute | solution.py:791
  42.9 10.2 %collective-permute-start.5 = (f32[8,3968]{1,0:T(8,128)}, f32[8,3968]{1,0:T(8,128)}, u32[]{:S(2)}, u32[]{:S(2)}) collective-permute-start(f32[8,3968]{1,0:T(8,128)} %get-tuple-element.45), channel_id=1, source_target_pairs={{0,1},{1,0},{2,3},{3,2},{4,5},{5,4},{6,7},{7,6},{8,9},{9,8},{10,11... | collective-permute-start | bytes 380936 | tf_op jit(solution)/shard_map/ppermute | solution.py:791
  43.3 1.1 copy-start.3
  56.2 4.6 %collective-permute-start.6 = (f32[48,256]{1,0:T(8,128)S(1)}, f32[48,256]{1,0:T(8,128)S(1)}, u32[]{:S(2)}, u32[]{:S(2)}) collective-permute-start(f32[48,256]{1,0:T(8,128)S(1)} %get-tuple-element.49), channel_id=1, source_target_pairs={{0,4},{4,0},{8,12},{12,8},{16,20},{20,16},{24,28},{28,24},{1,5},{5... | collective-permute-start | bytes 147464 | tf_op jit(solution)/shard_map/ppermute | solution.py:882
  56.3 4.5 %collective-permute-start.7 = (f32[48,256]{1,0:T(8,128)S(1)}, f32[48,256]{1,0:T(8,128)S(1)}, u32[]{:S(2)}, u32[]{:S(2)}) collective-permute-start(f32[48,256]{1,0:T(8,128)S(1)} %get-tuple-element.50), channel_id=1, source_target_pairs={{0,28},{4,8},{8,4},{12,16},{16,12},{20,24},{24,20},{28,0},{1,29},{... | collective-permute-start | bytes 147464 | tf_op jit(solution)/shard_map/ppermute | solution.py:882
  58.8 4.1 %collective-permute-start.8 = (f32[48,256]{1,0:T(8,128)S(1)}, f32[48,256]{1,0:T(8,128)S(1)}, u32[]{:S(2)}, u32[]{:S(2)}) collective-permute-start(f32[48,256]{1,0:T(8,128)S(1)} %get-tuple-element.51), channel_id=1, source_target_pairs={{0,8},{4,12},{8,0},{12,4},{16,24},{20,28},{24,16},{28,20},{1,9},{5... | collective-permute-start | bytes 147464 | tf_op jit(solution)/shard_map/ppermute | solution.py:882
  58.8 5.1 %collective-permute-start.9 = (f32[48,256]{1,0:T(8,128)S(1)}, f32[48,256]{1,0:T(8,128)S(1)}, u32[]{:S(2)}, u32[]{:S(2)}) collective-permute-start(f32[48,256]{1,0:T(8,128)S(1)} %get-tuple-element.52), channel_id=1, source_target_pairs={{0,24},{4,28},{8,16},{12,20},{16,8},{20,12},{24,0},{28,4},{1,25},{... | collective-permute-start | bytes 147464 | tf_op jit(solution)/shard_map/ppermute | solution.py:882
  66.5 23.6 %collective-permute-start.10 = (f32[48,1536]{1,0:T(8,128)S(1)}, f32[48,1536]{1,0:T(8,128)S(1)}, u32[]{:S(2)}, u32[]{:S(2)}) collective-permute-start(f32[48,1536]{1,0:T(8,128)S(1)} %get-tuple-element.54), channel_id=1, source_target_pairs={{0,2},{1,3},{2,0},{3,1},{4,6},{5,7},{6,4},{7,5},{8,10},{9,11},{10,... | collective-permute-start | bytes 884744 | tf_op jit(solution)/shard_map/ppermute | solution.py:791
  67.5 23.2 %collective-permute-start.11 = (f32[48,1536]{1,0:T(8,128)S(1)}, f32[48,1536]{1,0:T(8,128)S(1)}, u32[]{:S(2)}, u32[]{:S(2)}) collective-permute-start(f32[48,1536]{1,0:T(8,128)S(1)} %get-tuple-element.55), channel_id=1, source_target_pairs={{0,3},{1,2},{2,1},{3,0},{4,7},{5,6},{6,5},{7,4},{8,11},{9,10},{10,... | collective-permute-start | bytes 884744 | tf_op jit(solution)/shard_map/ppermute | solution.py:791
  70.8 20.6 %collective-permute-start.12 = (f32[48,1536]{1,0:T(8,128)S(1)}, f32[48,1536]{1,0:T(8,128)S(1)}, u32[]{:S(2)}, u32[]{:S(2)}) collective-permute-start(f32[48,1536]{1,0:T(8,128)S(1)} %get-tuple-element.56), channel_id=1, source_target_pairs={{0,1},{1,0},{2,3},{3,2},{4,5},{5,4},{6,7},{7,6},{8,9},{9,8},{10,11... | collective-permute-start | bytes 884744 | tf_op jit(solution)/shard_map/ppermute | solution.py:791
  93.5 14.8 %collective-permute-start.13 = (f32[8,3968]{1,0:T(8,128)S(1)}, f32[8,3968]{1,0:T(8,128)S(1)}, u32[]{:S(2)}, u32[]{:S(2)}) collective-permute-start(f32[8,3968]{1,0:T(8,128)S(1)} %get-tuple-element.59), channel_id=1, source_target_pairs={{0,2},{1,3},{2,0},{3,1},{4,6},{5,7},{6,4},{7,5},{8,10},{9,11},{10,... | collective-permute-start | bytes 380936 | tf_op jit(solution)/shard_map/ppermute | solution.py:791
  98.7 9.7 %collective-permute-start.14 = (f32[8,3968]{1,0:T(8,128)S(1)}, f32[8,3968]{1,0:T(8,128)S(1)}, u32[]{:S(2)}, u32[]{:S(2)}) collective-permute-start(f32[8,3968]{1,0:T(8,128)S(1)} %get-tuple-element.60), channel_id=1, source_target_pairs={{0,3},{1,2},{2,1},{3,0},{4,7},{5,6},{6,5},{7,4},{8,11},{9,10},{10,... | collective-permute-start | bytes 380936 | tf_op jit(solution)/shard_map/ppermute | solution.py:791
  100.9 7.9 %collective-permute-start.15 = (f32[8,3968]{1,0:T(8,128)S(1)}, f32[8,3968]{1,0:T(8,128)S(1)}, u32[]{:S(2)}, u32[]{:S(2)}) collective-permute-start(f32[8,3968]{1,0:T(8,128)S(1)} %get-tuple-element.61), channel_id=1, source_target_pairs={{0,1},{1,0},{2,3},{3,2},{4,5},{5,4},{6,7},{7,6},{8,9},{9,8},{10,11... | collective-permute-start | bytes 380936 | tf_op jit(solution)/shard_map/ppermute | solution.py:791
  111.0 3.6 %collective-permute-start.16 = (f32[48,256]{1,0:T(8,128)S(1)}, f32[48,256]{1,0:T(8,128)S(1)}, u32[]{:S(2)}, u32[]{:S(2)}) collective-permute-start(f32[48,256]{1,0:T(8,128)S(1)} %get-tuple-element.65), channel_id=1, source_target_pairs={{0,4},{4,0},{8,12},{12,8},{16,20},{20,16},{24,28},{28,24},{1,5},{5... | collective-permute-start | bytes 147464 | tf_op jit(solution)/shard_map/ppermute | solution.py:882
  111.1 4.5 %collective-permute-start.17 = (f32[48,256]{1,0:T(8,128)S(1)}, f32[48,256]{1,0:T(8,128)S(1)}, u32[]{:S(2)}, u32[]{:S(2)}) collective-permute-start(f32[48,256]{1,0:T(8,128)S(1)} %get-tuple-element.66), channel_id=1, source_target_pairs={{0,28},{4,8},{8,4},{12,16},{16,12},{20,24},{24,20},{28,0},{1,29},{... | collective-permute-start | bytes 147464 | tf_op jit(solution)/shard_map/ppermute | solution.py:882
  112.3 4.1 %collective-permute-start.18 = (f32[48,256]{1,0:T(8,128)S(1)}, f32[48,256]{1,0:T(8,128)S(1)}, u32[]{:S(2)}, u32[]{:S(2)}) collective-permute-start(f32[48,256]{1,0:T(8,128)S(1)} %get-tuple-element.67), channel_id=1, source_target_pairs={{0,8},{4,12},{8,0},{12,4},{16,24},{20,28},{24,16},{28,20},{1,9},{5... | collective-permute-start | bytes 147464 | tf_op jit(solution)/shard_map/ppermute | solution.py:882
  113.2 5.0 %collective-permute-start.19 = (f32[48,256]{1,0:T(8,128)S(1)}, f32[48,256]{1,0:T(8,128)S(1)}, u32[]{:S(2)}, u32[]{:S(2)}) collective-permute-start(f32[48,256]{1,0:T(8,128)S(1)} %get-tuple-element.68), channel_id=1, source_target_pairs={{0,24},{4,28},{8,16},{12,20},{16,8},{20,12},{24,0},{28,4},{1,25},{... | collective-permute-start | bytes 147464 | tf_op jit(solution)/shard_map/ppermute | solution.py:882
where the time goes:
time: 121 us
  waiting for transfers between devices  41.5 us (34%)
  Pallas kernels  33.4 us (28%)
  starting transfers between devices  32.6 us (27%)
  local copies, waits for them, and re-layouts  13.3 us (11%)
    ppermute x12, waiting for transfers between devices, swapped(): lax.ppermute(buffer, 'plane', [(i, i ^ step) for i in planes])  34.8 us
    ppermute x12, starting transfers between devices, swapped(): lax.ppermute(buffer, 'plane', [(i, i ^ step) for i in planes])  24.4 us
    ppermute x8, starting transfers between devices, packed_shards(): lax.ppermute(buffer, 'dom', [(i, trace_partner(i, matching, partitions))...  8.19 us
    pallas_call x8, Pallas kernels, packed_shards(): kernel_call(functools.partial(fields_kernel, gaps), f32(3, comps, local,...  7.08 us
    ppermute x8, waiting for transfers between devices, packed_shards(): lax.ppermute(buffer, 'dom', [(i, trace_partner(i, matching, partitions))...  6.7 us
    reshape x1, local copies, waits for them, and re-layouts, packed_shards(): base_flow.reshape(STEPS, 12, -1, LANES).transpose(1, 2, 0, 3)  6.22 us
    pallas_call x2, Pallas kernels, packed_shards(): kernel_call(diffuse_kernel, f32(*state_shape), [pltpu.VMEM((nodes, GROUP,...  5.34 us
    pallas_call x2, Pallas kernels, packed_shards(): kernel_call(functools.partial(update_kernel, back_plans), [f32(*state_sha...  5.24 us
  transfers between devices with their start and end apart: 20, of which 11 were waited for; matrix products, arithmetic and copies ran while one was open for 9% of the time, Pallas kernels for 11%

commit v1 on v0

--- a/solution.py
+++ b/solution.py
@@ -192,7 +192,7 @@
 BODY_TILES = 5
 BACK_TILES = 31
 GROUP = 8
-PARTNERS = (0, 2, 3, 1)
+PARTNERS = (0, 2, 1, 3)
 STEP_VISC = step_size * viscosity
 
 
@@ -316,15 +316,37 @@
     return value if shift % LANES == 0 else pltpu.roll(value, shift % LANES, 1)
 
 
-def pieced(pieces, load, lanes):
+def turner(load):
+    made = {}
+
+    def turned(source, tile, shift):
+        key = source, tile, shift
+        if key not in made:
+            made[key] = turn(load(source, tile), shift)
+        return made[key]
+
+    return turned
+
+
+def pieced(pieces, turned, lanes):
     total = None
     for source, tile, shift, low, size in pieces:
-        value = turn(load(source, tile), shift)
+        value = turned(source, tile, shift)
         if total is None:
             total = value
+        elif low + size == LANES:
+            total = jnp.where(lanes >= low, value, total)
         else:
             total = jnp.where((lanes >= low) & (lanes < low + size), value, total)
     return total
+
+
+def aligned(index, unit):
+    return index if isinstance(index, int) else pl.multiple_of(index, unit)
+
+
+def group_rows(g):
+    return pl.ds(aligned(g * GROUP, GROUP), GROUP)
 
 
 def tile_at(ref, lead, rows, tile):
@@ -359,58 +381,76 @@
     return total
 
 
-def make_sends(me, plans, rows_total, state, xi, staged, outs):
-    rows_step = 8
-    lanes = lane_ids(rows_step)
-
-    def some_rows(g, _):
-        rows = pl.ds(pl.multiple_of(g * rows_step, rows_step), rows_step)
+def make_sends(plans, groups, state, xi, staged):
+    lanes = lane_ids(GROUP)
+    for g in groups:
+        rows = group_rows(g)
         for t in range(SLAB_TILES):
             for a, value in enumerate(along_i([tile_at(state, (i,), rows, t) for i in range(NODES)])):
                 xi[a, rows, pl.ds(t * LANES, LANES)] = value
-
-        def load(source, tile):
+    for g in groups:
+        rows = group_rows(g)
+
+        def load(source, tile, rows=rows):
             return tile_at(state if source[0] == "state" else xi, (source[1],), rows, tile)
 
+        turned = turner(load)
         for chunk, plan in enumerate(plans):
             for t, pieces in enumerate(plan):
-                staged[chunk, rows, pl.ds(t * LANES, LANES)] = pieced(pieces, load, lanes)
-        return 0
-
-    lax.fori_loop(0, rows_total // rows_step, some_rows, 0)
-    for k, out in enumerate(outs):
-        out[...] = staged[me ^ PARTNERS[k]]
+                staged[chunk, rows, pl.ds(t * LANES, LANES)] = pieced(pieces, turned, lanes)
+
+
+def hand_out(me, staged, outs):
+    for step, out in zip(PARTNERS, outs):
+        out[...] = staged[me ^ step]
 
 
 def first_kernel(plans, adjoint, state, out0, out1, out2, out3, xi, staged, taken, sems):
     me = lax.axis_index("plane")
     comps, local = taken.shape[0], taken.shape[3]
-    copies = [pltpu.make_async_copy(adjoint.at[:, i], taken.at[:, i], sems.at[i]) for i in range(NODES)]
-    for copy in copies:
-        copy.start()
-    for i in range(NODES):
-        copies[i].wait()
-        for c in range(comps):
-            rows = pl.ds(c * local, local)
+
+    def copy(c):
+        return pltpu.make_async_copy(adjoint.at[c], taken.at[c], sems.at[c])
+
+    for c in range(comps):
+        copy(c).start()
+
+    for c in range(comps):
+        copy(c).wait()
+        rows = pl.ds(c * local, local)
+        for i in range(NODES):
             for t in range(SLAB_TILES):
                 parts = [taken[c, i, j] for j in range(4 * t, min(4 * t + 4, NODES))]
                 parts += [jnp.zeros_like(parts[0])] * (4 - len(parts))
                 state[i, rows, pl.ds(t * LANES, LANES)] = jnp.concatenate(parts, axis=1)
-    make_sends(me, plans, comps * local, state, xi, staged, (out0, out1, out2, out3))
-
-
-def flow_kernel(points, flow, metric, out0, out1):
+        make_sends(plans, range(c * local // GROUP, (c + 1) * local // GROUP), state, xi, staged)
+    hand_out(me, staged, (out0, out1, out2, out3))
+
+
+def metric_rows(metric):
+    wide = jnp.concatenate([metric[...]] * (LANES // metric.shape[1]), axis=1)
+    return jnp.concatenate([wide, wide], axis=0)
+
+
+def flow_kernel(points, flow, metric, out0, out1, flat):
     me = lax.axis_index("plane")
-    per_field = MODES * points // LANES
     lanes, subs = lane_ids(8), lax.broadcasted_iota(jnp.int32, (8, LANES), 0)
     shift = lax.rem(LANES - lax.rem(me * points, LANES), LANES)
-    turned = pltpu.roll(metric[...], shift, 1)
-    xi_x, xi_y, eta_x, eta_y = (turned[r : r + 1, :] for r in range(4))
+    turned = pltpu.roll(metric_rows(metric), shift, 1)
+    ahead = pl.program_id(0) == 0
+    first_first = jnp.where(ahead, turned[0:1], 1.0)
+    first_second = jnp.where(ahead, turned[1:2], 0.0)
+    second_first = jnp.where(ahead, turned[2:3], 0.0)
+    second_second = jnp.where(ahead, turned[3:4], 1.0)
+    per_sixteen = 16 * points // LANES
     last = CHUNK_TILES - 1
+
+    for f in range(2):
+        for s in range(STEPS):
+            flat[f, s] = flow[f, s].reshape(flat.shape[2:])
 
     for s, out in enumerate((out0, out1)):
         for half in range(2):
-
             moved = (lanes + 64 * half + 8 * subs) & (LANES - 1)
             kept = lanes < LANES - 64 * half - 8 * subs
 
@@ -420,37 +460,33 @@
                 def field(f):
                     spun = []
                     for k in range(CHUNK_TILES):
-                        start = 2 * (f * per_field + 40 * half + k) + s + h * (16 * points // LANES * 2)
-                        block = flow[pl.ds(start, 8, stride=10), :]
-                        spun.append(pick(block, moved))
-                    tiles = [jnp.where(kept, spun[k], spun[k + 1]) for k in range(last)]
-                    return tiles + [spun[last]]
-
-                def put(f, t, value):
-                    out[f, rows, pl.ds(t * LANES, LANES)] = value
-
-                first, second = field(0), field(1)
-                for t in range(CHUNK_TILES):
-                    put(0, t, first[t] * xi_x + second[t] * xi_y)
-                    put(1, t, first[t] * eta_x + second[t] * eta_y)
-                for f in range(2, 12):
-                    for t, value in enumerate(field(f)):
-                        put(f, t, value)
+                        start = per_sixteen * h + 40 * half + k
+                        spun.append(pick(flat[f, s, pl.ds(start, 8, stride=5), :], moved))
+                    return [jnp.where(kept, spun[k], spun[k + 1]) for k in range(last)] + [spun[last]]
+
+                for t, (one, two) in enumerate(zip(field(0), field(1))):
+                    out[0, rows, pl.ds(t * LANES, LANES)] = one * first_first + two * first_second
+                    out[1, rows, pl.ds(t * LANES, LANES)] = one * second_first + two * second_second
                 return 0
 
             lax.fori_loop(0, MODES // 16, some_rows, 0)
 
 
-def tables_kernel(edges, flags, table):
-    capacity, blocks = edges.shape
+def tables_kernel(edges, flags, table, square):
+    blocks, _, capacity = edges.shape
     lanes = lane_ids(capacity)
     slots = lax.broadcasted_iota(jnp.int32, (capacity, LANES), 0)
     here = slots == lax.rem(lanes, capacity)
     flag = jnp.zeros((1, LANES), jnp.int32)
     count = jnp.zeros((1, LANES), jnp.int32)
     table[...] = jnp.zeros(table.shape, jnp.int32)
+    square[...] = jnp.zeros(square.shape, jnp.float32)
     for o in range(blocks):
-        column = jnp.broadcast_to(edges[:, o : o + 1], (capacity, LANES))
+        square[o : o + 1, 0:capacity] = edges[o].astype(jnp.float32)
+        square[blocks + o : blocks + o + 1, 0:capacity] = flags[o].astype(jnp.float32)
+    columns = square[...].T[0:capacity].astype(jnp.int32)
+    for o in range(blocks):
+        column = jnp.broadcast_to(columns[:, o : o + 1], (capacity, LANES))
         held = column == lanes
 
         def summed(mask, value):
@@ -460,7 +496,7 @@
         table[5 + o : 6 + o, :] = summed(held, slots)
         present = summed(held, jnp.ones_like(slots))
         table[10 + o : 11 + o, :] = present
-        flag += summed(held, jnp.broadcast_to(flags[:, o : o + 1], (capacity, LANES)))
+        flag += summed(held, jnp.broadcast_to(columns[:, blocks + o : blocks + o + 1], (capacity, LANES)))
         count += present
         if o == blocks // 2:
             partner = slots + 1 - 2 * lax.rem(slots, 2)
@@ -476,7 +512,8 @@
     rows_total = state.shape[1]
     lanes = lane_ids(8)
     local = rows_total // 3
-    xi_x, xi_y, eta_x, eta_y = (metric[r : r + 1, :] for r in range(4))
+    wide = metric_rows(metric)
+    xi_x, xi_y, eta_x, eta_y = (wide[r : r + 1] for r in range(4))
     g_ii = xi_x * xi_x + xi_y * xi_y
     g_ij = xi_x * eta_x + xi_y * eta_y
     g_jj = eta_x * eta_x + eta_y * eta_y
@@ -531,28 +568,24 @@
     gap = sum(jnp.where(me == b, g, 0) for b, g in enumerate(gaps))
     gap_tile, gap_lane = gap // LANES, lax.rem(gap, LANES)
 
-    def some_rows(g, _):
-        rows = pl.ds(pl.multiple_of(g * GROUP, GROUP), GROUP)
+    for g in range(rows_total // GROUP):
+        rows = group_rows(g)
         c = g * GROUP // local
-        target = pl.ds(pl.multiple_of(lax.rem(g * GROUP, local), GROUP), GROUP)
-
-        def put(kind, t, value):
-            fields[kind, c, target, pl.ds(t * LANES, LANES)] = value
-
+        target = pl.ds(g * GROUP % local, GROUP)
         tiles = [tile_at(source, (), rows, t) for t in range(STATE_TILES)]
         turned = turned_tiles(tiles, lanes)
         for t in range(CHUNK_TILES):
-            put(0, t, tiles[t])
-            put(2, t, along_j(turned, STATE_TILES, t,
-                              lambda d, t=t: bands[me, pl.ds(d + 8, 1), pl.ds(t * LANES, LANES)],
-                              range(-8, 9)))
+            at = pl.ds(t * LANES, LANES)
+            fields[0, c, target, at] = tiles[t]
+            fields[2, c, target, at] = along_j(
+                turned, STATE_TILES, t, lambda d, at=at: bands[me, pl.ds(d + 8, 1), at], range(-8, 9)
+            )
         for t in range(BODY_TILES):
-            put(1, t, tile_at(source, (), rows, STATE_TILES + t))
+            fields[1, c, target, pl.ds(t * LANES, LANES)] = tile_at(source, (), rows, STATE_TILES + t)
         tail = source[rows, pl.ds(pl.multiple_of(gap_tile * LANES, LANES), LANES)]
-        put(1, BODY_TILES, pltpu.roll(tail, lax.rem(LANES - gap_lane, LANES), 1))
-        return 0
-
-    lax.fori_loop(0, rows_total // GROUP, some_rows, 0)
+        fields[1, c, target, pl.ds(BODY_TILES * LANES, LANES)] = pltpu.roll(
+            tail, lax.rem(LANES - gap_lane, LANES), 1
+        )
 
 
 def advect_kernel(fields0, fields1, fields2, fields3, flow, to_span, to_modes, *outs):
@@ -595,14 +628,10 @@
                 first = k * (MODES // len(outs)) + half * GROUP
                 yield k, out, c * (MODES // len(outs) // GROUP) + half, result[first : first + GROUP]
 
-    def some_lanes(p, _):
-        first = pl.multiple_of(p * width, width)
+    for first in range(0, (chunks - 1) * width, width):
         for c, result in results(pl.ds(first, width)):
             for _, out, g, piece in split(c, result):
-                out[:, pl.ds(pl.multiple_of(BODY_TILES * g * LANES + first, LANES), width)] = piece
-        return 0
-
-    lax.fori_loop(0, chunks - 1, some_lanes, 0)
+                out[:, pl.ds(BODY_TILES * g * LANES + first, width)] = piece
     tails = [None] * len(outs)
     for c, result in results(pl.ds((chunks - 1) * width, width)):
         for k, out, g, piece in split(c, result):
@@ -615,11 +644,11 @@
 
 def trace_blocks(me):
     odd, late = lax.rem(me, 2), lax.rem(me, 4) // 2
-    return 3 - 2 * odd, 1 + 2 * odd, 4 - 4 * late, 4 * late
+    return 4 * late, 1 + 2 * odd, 4 - 4 * late, 3 - 2 * odd
 
 
 def trace_partner(me, matching, size):
-    step, start = ((1, 0), (1, 1), (2, 0), (2, 2))[matching]
+    step, start = ((2, 2), (1, 1), (2, 0), (1, 0))[matching]
     return (((me + start) ^ step) - start) % size
 
 
@@ -628,8 +657,8 @@
     rows_total = local_sum.shape[1]
     last = NODES - 1
     lanes = lane_ids(8)
-    for k, source in enumerate((in0, in1, in2, in3)):
-        chunks[me ^ PARTNERS[k]] = source[...]
+    for step, source in zip(PARTNERS, (in0, in1, in2, in3)):
+        chunks[me ^ step] = source[...]
 
     trace_plans = [
         tile_plan([(k, 0, 0, 32), (last, 32 * k, 32, 32), (k, 256, 64, 32), (0, 32 * k, 96, 32)], 1)[0]
@@ -641,44 +670,35 @@
     def wide(row):
         return jnp.broadcast_to(table[pl.ds(row, 1), :], (8, LANES))
 
-    def some_rows(g, _):
-        rows = pl.ds(pl.multiple_of(g * 8, 8), 8)
-        tails = [
-            pltpu.roll(tile_at(chunks, (b,), slice(None), BACK_TILES - 1), lax.rem(LANES - 8 * g, LANES), 1)
-            for b in range(4)
-        ]
-
-        def load(source, tile):
+    turned_round, partner = wide(15) == 1, wide(16)
+    slot_edges = [wide(o) for o in blocks]
+    for g in range(rows_total // GROUP):
+        rows = group_rows(g)
+
+        def load(source, tile, g=g):
             if source[0] == "tail":
-                return tails[source[1]]
-            at = pl.multiple_of((BODY_TILES * g + tile) * LANES, LANES)
-            return chunks[source[1], :, pl.ds(at, LANES)]
-
+                return turn(tile_at(chunks, (source[1],), slice(None), BACK_TILES - 1), -8 * g)
+            return tile_at(chunks, (source[1],), slice(None), BODY_TILES * g + tile)
+
+        turned = turner(load)
+        new = {}
         for i in range(NODES):
             for t in range(SLAB_TILES):
-                value = pieced(plans[i][t], load, lanes)
-                updated[i, rows, pl.ds(t * LANES, LANES)] = (
-                    tile_at(local_sum, (i,), rows, t) + step_size * value
-                )
-        raw = [
-            pieced(plan, lambda i, tile: tile_at(updated, (i,), rows, tile), lanes) for plan in trace_plans
-        ]
-        turned_round = wide(15) == 1
+                value = pieced(plans[i][t], turned, lanes)
+                new[i, t] = tile_at(local_sum, (i,), rows, t) + step_size * value
+                updated[i, rows, pl.ds(t * LANES, LANES)] = new[i, t]
+        edges = turner(lambda i, tile, new=new: new[i, tile])
+        raw = [pieced(plan, edges, lanes) for plan in trace_plans]
         seen = [jnp.where(turned_round, raw[last - k], raw[k]) for k in range(NODES)]
-        partner = wide(16)
-        for k in range(NODES):
-            own[k, rows, :] = pick(seen[k], partner)
-        for o, out in zip(blocks, (out0, out1, out2, out3)):
-            slot_edge = wide(o)
+        for slot_edge, out in zip(slot_edges, (out0, out1, out2, out3)):
             for t in range(2):
                 total = None
                 for k in range(5 * t, min(5 * t + 5, NODES)):
                     value = pick(seen[k], slot_edge)
                     total = value if total is None else jnp.where(lanes >= 24 * (k - 5 * t), value, total)
                 out[rows, pl.ds(t * LANES, LANES)] = total
-        return 0
-
-    lax.fori_loop(0, rows_total // 8, some_rows, 0)
+        for k in range(NODES):
+            own[k, rows, :] = pick(seen[k], partner)
 
 
 def pick(value, index):
@@ -696,61 +716,61 @@
 
     share = wide(17).astype(jnp.float32)
     quarter = lanes // 32
-
-    def group(value, at):
-        return turn(value, -32 * at)
-
-    def some_rows(g, _):
-        rows = pl.ds(pl.multiple_of(g * 8, 8), 8)
+    own_has = wide(12) > 0
+    has = [wide(10 + o) > 0 for o in blocks]
+    slots = [wide(5 + o) for o in blocks]
+
+    def spread(values, at, t):
+        value = None
+        for k in range(4 * t, min(4 * t + 4, NODES)):
+            moved = turn(values[k], 32 * (k - 4 * t - at))
+            value = jnp.where(quarter == k - 4 * t, moved, 0.0 if value is None else value)
+        return value
+
+    def edge_parts(values, i, t):
+        parts = []
+        if t == 0:
+            parts.append(jnp.where(quarter == 0, values[i], 0.0))
+        if i == last:
+            parts.append(spread(values, 1, t))
+        if t == 2:
+            parts.append(jnp.where(quarter == 0, turn(values[i], -64), 0.0))
+        if i == 0:
+            parts.append(spread(values, 3, t))
+        return parts
+
+    shares, scale = [share] * NODES, {}
+    for i in (0, 1, last):
+        for t in range(SLAB_TILES):
+            parts = edge_parts(shares, i, t)
+            if parts:
+                scale[i, t] = 1.0 / (1.0 + sum(parts[1:], parts[0]))
+
+    for g in range(rows_total // GROUP):
+        rows = group_rows(g)
         sums = []
         for k in range(NODES):
-            total = jnp.where(wide(12) > 0, own[k, rows, :], 0.0)
-            for o, source in zip(blocks, came):
-                value = pick(tile_at(source, (), rows, k // 5), wide(5 + o) + 24 * (k % 5))
-                total = jnp.where(wide(10 + o) > 0, value, total)
+            total = jnp.where(own_has, own[k, rows, :], 0.0)
+            for slot, there, source in zip(slots, has, came):
+                value = pick(tile_at(source, (), rows, k // 5), slot + 24 * (k % 5))
+                total = jnp.where(there, value, total)
             sums.append(total)
-
-        def spread(at, t):
-            nodes = range(4 * t, min(4 * t + 4, NODES))
-            value, number = None, None
-            for k in nodes:
-                q = k - 4 * t
-                moved = turn(sums[k], 32 * (q - at))
-                many = turn(share, 32 * (q - at))
-                value = jnp.where(quarter == q, moved, 0.0 if value is None else value)
-                number = jnp.where(quarter == q, many, 0.0 if number is None else number)
-            return value, number
-
         for i in range(NODES):
             for t in range(SLAB_TILES):
                 total = tile_at(updated, (i,), rows, t)
-                weight = None
-                if t == 0:
-                    total += jnp.where(quarter == 0, sums[i], 0.0)
-                    weight = 1.0 + jnp.where(quarter == 0, share, 0.0)
-                if i == last:
-                    value, number = spread(1, t)
-                    total += value
-                    weight = (1.0 if weight is None else weight) + number
-                if t == 2:
-                    total += jnp.where(quarter == 0, group(sums[i], 2), 0.0)
-                    weight = (1.0 if weight is None else weight) + jnp.where(quarter == 0, group(share, 2), 0.0)
-                if i == 0:
-                    value, number = spread(3, t)
-                    total += value
-                    weight = (1.0 if weight is None else weight) + number
-                if weight is not None:
-                    total = total / weight
+                parts = edge_parts(sums, i, t)
+                for part in parts:
+                    total += part
+                if parts:
+                    total *= scale[i if i in (0, last) else 1, t]
                 state[i, rows, pl.ds(t * LANES, LANES)] = total
-        return 0
-
-    lax.fori_loop(0, rows_total // 8, some_rows, 0)
 
 
 def next_kernel(plans, table, updated, own, r0, r1, r2, r3, state, out0, out1, out2, out3, xi, staged):
     me = lax.axis_index("plane")
     join_edges(table, updated, own, (r0, r1, r2, r3), state)
-    make_sends(me, plans, updated.shape[1], state, xi, staged, (out0, out1, out2, out3))
+    make_sends(plans, range(updated.shape[1] // GROUP), state, xi, staged)
+    hand_out(me, staged, (out0, out1, out2, out3))
 
 
 def last_kernel(table, updated, own, r0, r1, r2, r3, out, state, given, sems):
@@ -809,11 +829,6 @@
     slab_bands = eta_bands(0, SLAB_TILES * LANES, nodes * elements)
     chunk_bands = np.stack(
         [eta_bands((points - 2 * nodes * elements) * b, CHUNK_TILES * LANES, points) for b in range(planes)]
-    )
-
-    metric_tile = jnp.pad(jnp.tile(metric, (1, LANES // elements)), ((0, 4), (0, 0)))
-    flow_rows = (
-        base_flow.reshape(STEPS, 12, -1, LANES).transpose(1, 2, 0, 3).reshape(-1, LANES)
     )
 
     in_hbm = pl.BlockSpec(memory_space=pltpu.HBM)
@@ -835,16 +850,28 @@
         4 * 10**6,
         in_specs=[in_hbm],
     )(in_rows)
+    whole, two_fields = (12, MODES, CHUNK_TILES * LANES), (2, MODES, CHUNK_TILES * LANES)
+    lay = base_flow.transpose(1, 0, 2)
     flows = kernel_call(
         functools.partial(flow_kernel, points),
-        [f32(12, MODES, CHUNK_TILES * LANES)] * STEPS,
-        [],
+        [f32(*whole)] * STEPS,
+        [pltpu.VMEM((2, STEPS, lay.shape[2] // LANES, LANES), jnp.float32)],
         4 * 10**6,
         9 * 10**6,
-    )(flow_rows, metric_tile)
+        grid=(6,),
+        in_specs=[
+            pl.BlockSpec((2, *lay.shape[1:]), lambda pair: (pair, 0, 0)),
+            pl.BlockSpec(metric.shape, lambda pair: (0, 0)),
+        ],
+        out_specs=[pl.BlockSpec(two_fields, lambda pair: (pair, 0, 0))] * STEPS,
+    )(lay, metric)
     table = kernel_call(
-        tables_kernel, jax.ShapeDtypeStruct((24, LANES), jnp.int32), [], 10**5, 10**5
-    )(edge_list[0].T, flips[0].T)
+        tables_kernel,
+        jax.ShapeDtypeStruct((24, LANES), jnp.int32),
+        [pltpu.VMEM((LANES, LANES), jnp.float32)],
+        10**5,
+        10**5,
+    )(edge_list.transpose(1, 0, 2), flips.transpose(1, 0, 2))
 
     for step_index in range(STEPS):
         fields = [
@@ -870,7 +897,7 @@
             [pltpu.VMEM((nodes, GROUP, SLAB_TILES * LANES), jnp.float32)] * 2,
             12 * 10**6,
             2 * 10**6,
-        )(state, metric_tile, slab_bands)
+        )(state, metric, slab_bands)
         updated, own, *leaving = kernel_call(
             functools.partial(update_kernel, back_plans),
             [f32(*state_shape), f32(nodes, rows_total, LANES)] + [f32(rows_total, 2 * LANES)] * 4,

time: 121 us -> 112 us (0.926)
  local copies, waits for them, and re-layouts: 13.3 us -> 3.12 us
  starting transfers between devices: 32.6 us -> 35.7 us
  waiting for transfers between devices: 41.5 us -> 39.3 us
    pallas_call x1, Pallas kernels: 2.4 us -> 11.3 us  [packed_shards(): kernel_call(functools.partial(flow_kernel, points), [f32(*whole)] * STEPS...]
    reshape x1 -> x0, local copies, waits for them, and re-layouts: 6.22 us -> none  [packed_shards(): base_flow.reshape(STEPS, 12, -1, LANES).transpose(1, 2, 0, 3)]
    pallas_call x8, Pallas kernels: 7.08 us -> 2.31 us  [packed_shards(): kernel_call(functools.partial(fields_kernel, gaps), f32(3, comps, local,...]
    transpose x1 -> x0, local copies, waits for them, and re-layouts: 4.23 us -> none  [packed_shards(): base_flow.reshape(STEPS, 12, -1, LANES).transpose(1, 2, 0, 3)]
    ppermute x12, starting transfers between devices: 24.4 us -> 27.2 us  [swapped(): lax.ppermute(buffer, 'plane', [(i, i ^ step) for i in planes])]
    pallas_call x1, Pallas kernels: 4.01 us -> 2.39 us  [packed_shards(): kernel_call(functools.partial(first_kernel, plans), [f32(*state_shape), *...]
    pallas_call x2, Pallas kernels: 3.68 us -> 2.39 us  [packed_shards(): kernel_call(advect_kernel, [f32(GROUP, BACK_TILES * LANES)] * planes, [],...]
    unnamed x16 -> x18, local copies, waits for them, and re-layouts: 1.96 us -> 3.12 us
  transfers between devices with their start and end apart: 20 -> 20, of which waited for: 11 -> 12; matrix products, arithmetic and copies ran while one was open for 9% -> 0% of each run, Pallas kernels for 11% -> 17%
where the time goes in v1:
time: 112 us; the launch traced here: 111 us
  waiting for transfers between devices  39.3 us (35%)
  starting transfers between devices  35.7 us (32%)
  Pallas kernels  33 us (29%)
  local copies, waits for them, and re-layouts  3.12 us (3%)
    ppermute x12, waiting for transfers between devices, swapped(): lax.ppermute(buffer, 'plane', [(i, i ^ step) for i in planes])  33.8 us
    ppermute x12, starting transfers between devices, swapped(): lax.ppermute(buffer, 'plane', [(i, i ^ step) for i in planes])  27.2 us
    pallas_call x1, Pallas kernels, packed_shards(): kernel_call(functools.partial(flow_kernel, points), [f32(*whole)] * STEPS...  11.3 us
    ppermute x8, starting transfers between devices, packed_shards(): lax.ppermute(buffer, 'dom', [(i, trace_partner(i, matching, partitions))...  8.53 us
    pallas_call x2, Pallas kernels, packed_shards(): kernel_call(diffuse_kernel, f32(*state_shape), [pltpu.VMEM((nodes, GROUP,...  5.62 us
    ppermute x8, waiting for transfers between devices, packed_shards(): lax.ppermute(buffer, 'dom', [(i, trace_partner(i, matching, partitions))...  5.54 us
    pallas_call x2, Pallas kernels, packed_shards(): kernel_call(functools.partial(update_kernel, back_plans), [f32(*state_sha...  4.71 us
    unnamed x18, local copies, waits for them, and re-layouts  3.12 us
  transfers between devices with their start and end apart: 20, of which 12 were waited for; matrix products, arithmetic and copies ran while one was open for 0% of the time, Pallas kernels for 17%

profile of v1, /device:TPU:0, one launch (start us, length us, event | category | flops | bytes accessed | tf_op | source)
XLA Modules:
  0.0 111.4 jit_solution(14683099908090536277)
XLA Ops:
  0.0 2.4 %shard_map.92 = (f32[9,48,384]{2,1,0:T(8,128)S(1)}, f32[48,1536]{1,0:T(8,128)S(1)}, f32[48,1536]{1,0:T(8,128)S(1)}, f32[48,1536]{1,0:T(8,128)S(1)}, f32[48,1536]{1,0:T(8,128)S(1)}) custom-call(f32[3,9,9,16,32]{4,3,2,1,0:T(8,128)} %bitcast.8), custom_call_target="tpu_custom_call" | custom-call | flops 4000000 | bytes 4000000 | tf_op jit(solution)/shard_map/pallas_call | solution.py:845
  2.4 4.1 %collective-permute-start = (f32[48,1536]{1,0:T(8,128)S(1)}, f32[48,1536]{1,0:T(8,128)S(1)}, u32[]{:S(2)}, u32[]{:S(2)}) collective-permute-start(f32[48,1536]{1,0:T(8,128)S(1)} %get-tuple-element.38), channel_id=1, source_target_pairs={{0,2},{1,3},{2,0},{3,1},{4,6},{5,7},{6,4},{7,5},{8,10},{9,11},{10,... | collective-permute-start | bytes 884744 | tf_op jit(solution)/shard_map/ppermute | solution.py:811
  6.5 1.6 %collective-permute-start.1 = (f32[48,1536]{1,0:T(8,128)S(1)}, f32[48,1536]{1,0:T(8,128)S(1)}, u32[]{:S(2)}, u32[]{:S(2)}) collective-permute-start(f32[48,1536]{1,0:T(8,128)S(1)} %get-tuple-element.39), channel_id=1, source_target_pairs={{0,1},{1,0},{2,3},{3,2},{4,5},{5,4},{6,7},{7,6},{8,9},{9,8},{10,11... | collective-permute-start | bytes 884744 | tf_op jit(solution)/shard_map/ppermute | solution.py:811
  9.4 2.1 %copy-done.2 = f32[2,12,41472]{2,0,1:T(2,128)S(1)} copy-done((f32[2,12,41472]{2,0,1:T(2,128)S(1)}, f32[2,12,41472]{2,0,1:T(2,128)}, u32[]{:S(2)}) %copy-start.2) | copy-done | bytes 3981336
  11.5 11.3 %shard_map.97 = (f32[12,64,768]{2,1,0:T(8,128)S(1)}, f32[12,64,768]{2,1,0:T(8,128)S(1)}) custom-call(f32[12,2,41472]{2,1,0:T(2,128)S(1)} %bitcast.5, f32[4,32]{1,0:T(4,128)S(1)} %copy-done.6), custom_call_target="tpu_custom_call" | custom-call | flops 4000000 | bytes 9000000 | tf_op jit(solution)/shard_map/pallas_call | solution.py:855
  23.4 4.0 %collective-permute-done.2.source = f32[48,1536]{1,0:T(8,128)S(1)} collective-permute-done((f32[48,1536]{1,0:T(8,128)S(1)}, f32[48,1536]{1,0:T(8,128)S(1)}, u32[]{:S(2)}, u32[]{:S(2)}) %collective-permute-start.2) | collective-permute-done | bytes 294944 | tf_op jit(solution)/shard_map/ppermute | solution.py:811
  27.7 1.2 %shard_map.98 = (f32[8,3968]{1,0:T(8,128)S(1)}, f32[8,3968]{1,0:T(8,128)S(1)}, f32[8,3968]{1,0:T(8,128)S(1)}, f32[8,3968]{1,0:T(8,128)S(1)}) custom-call(f32[3,3,16,768]{3,2,1,0:T(8,128)S(1)} %shard_map.93.fields0, f32[3,3,16,768]{3,2,1,0:T(8,128)S(1)} %shard_map.94.fields1, f32[3,3,16,768]{3,2,1,0:T(8,128)S(1)} %shard_map.95.fields2, ...), custom_call_target="tpu_custom_call" | custom-call | flops 80000000 | bytes 5000000 | tf_op jit(solution)/shard_map/pallas_call | solution.py:887
  28.9 7.8 %collective-permute-start.3 = (f32[8,3968]{1,0:T(8,128)S(1)}, f32[8,3968]{1,0:T(8,128)S(1)}, u32[]{:S(2)}, u32[]{:S(2)}) collective-permute-start(f32[8,3968]{1,0:T(8,128)S(1)} %get-tuple-element.43), channel_id=1, source_target_pairs={{0,2},{1,3},{2,0},{3,1},{4,6},{5,7},{6,4},{7,5},{8,10},{9,11},{10,... | collective-permute-start | bytes 380936 | tf_op jit(solution)/shard_map/ppermute | solution.py:811
  36.7 1.5 %collective-permute-start.5 = (f32[8,3968]{1,0:T(8,128)S(1)}, f32[8,3968]{1,0:T(8,128)S(1)}, u32[]{:S(2)}, u32[]{:S(2)}) collective-permute-start(f32[8,3968]{1,0:T(8,128)S(1)} %get-tuple-element.45), channel_id=1, source_target_pairs={{0,3},{1,2},{2,1},{3,0},{4,7},{5,6},{6,5},{7,4},{8,11},{9,10},{10,... | collective-permute-start | bytes 380936 | tf_op jit(solution)/shard_map/ppermute | solution.py:811
  38.5 2.8 %shard_map.99.local_sum = f32[9,48,384]{2,1,0:T(8,128)S(1)} custom-call(f32[9,48,384]{2,1,0:T(8,128)S(1)} %get-tuple-element.46.state, f32[4,32]{1,0:T(4,128)S(1)} %copy-done.6, f32[24,384]{1,0:T(8,128)S(1)} %copy-done.5), custom_call_target="tpu_custom_call" | custom-call | flops 12000000 | bytes 2000000 | tf_op jit(solution)/shard_map/pallas_call | solution.py:894
  41.3 4.7 %collective-permute-done.3.in1 = f32[8,3968]{1,0:T(8,128)S(1)} collective-permute-done((f32[8,3968]{1,0:T(8,128)S(1)}, f32[8,3968]{1,0:T(8,128)S(1)}, u32[]{:S(2)}, u32[]{:S(2)}) %collective-permute-start.3) | collective-permute-done | bytes 127008 | tf_op jit(solution)/shard_map/ppermute | solution.py:811
  47.0 2.4 %shard_map.100 = (f32[9,48,384]{2,1,0:T(8,128)S(1)}, f32[9,48,128]{2,1,0:T(8,128)S(1)}, f32[48,256]{1,0:T(8,128)S(1)}, f32[48,256]{1,0:T(8,128)S(1)}, f32[48,256]{1,0:T(8,128)S(1)}, /*index=5*/f32[48,256]{1,0:T(8,128)S(1)}) custom-call(f32[8,3968]{1,0:T(8,128)S(1)} %get-tuple-element.42.in0, f32[8,3968]{1,0:T(8,128)S(1)} %collective-permute-done.3.in1, ...), custom_call_target="tpu_custom_call" | custom-call | flops 2000000 | bytes 3000000 | tf_op jit(solution)/shard_map/pallas_call | solution.py:901
  49.3 2.5 %collective-permute-start.6 = (f32[48,256]{1,0:T(8,128)S(1)}, f32[48,256]{1,0:T(8,128)S(1)}, u32[]{:S(2)}, u32[]{:S(2)}) collective-permute-start(f32[48,256]{1,0:T(8,128)S(1)} %get-tuple-element.49), channel_id=1, source_target_pairs={{0,24},{4,28},{8,16},{12,20},{16,8},{20,12},{24,0},{28,4},{1,25},{... | collective-permute-start | bytes 147464 | tf_op jit(solution)/shard_map/ppermute | solution.py:909
  52.4 1.2 %collective-permute-start.9 = (f32[48,256]{1,0:T(8,128)S(1)}, f32[48,256]{1,0:T(8,128)S(1)}, u32[]{:S(2)}, u32[]{:S(2)}) collective-permute-start(f32[48,256]{1,0:T(8,128)S(1)} %get-tuple-element.52), channel_id=1, source_target_pairs={{0,4},{4,0},{8,12},{12,8},{16,20},{20,16},{24,28},{28,24},{1,5},{5... | collective-permute-start | bytes 147464 | tf_op jit(solution)/shard_map/ppermute | solution.py:909
  54.4 2.0 %collective-permute-done.7.r1 = f32[48,256]{1,0:T(8,128)S(1)} collective-permute-done((f32[48,256]{1,0:T(8,128)S(1)}, f32[48,256]{1,0:T(8,128)S(1)}, u32[]{:S(2)}, u32[]{:S(2)}) %collective-permute-start.7) | collective-permute-done | bytes 49184 | tf_op jit(solution)/shard_map/ppermute | solution.py:909
  56.4 1.6 %shard_map.101 = (f32[9,48,384]{2,1,0:T(8,128)S(1)}, f32[48,1536]{1,0:T(8,128)S(1)}, f32[48,1536]{1,0:T(8,128)S(1)}, f32[48,1536]{1,0:T(8,128)S(1)}, f32[48,1536]{1,0:T(8,128)S(1)}) custom-call(s32[24,128]{1,0:T(8,128)S(1)} %shard_map.91.table, f32[9,48,384]{2,1,0:T(8,128)S(1)} %get-tuple-element.47.updated, f32[9,48,128]{2,1,0:T(8,128)S(1)} %get-tuple-element.48.own, ...), custom_call_target="tpu_custom_call" | custom-call | flops 6000000 | bytes 4000000 | tf_op jit(solution)/shard_map/pallas_call | solution.py:915
  58.0 1.3 %collective-permute-start.10 = (f32[48,1536]{1,0:T(8,128)S(1)}, f32[48,1536]{1,0:T(8,128)S(1)}, u32[]{:S(2)}, u32[]{:S(2)}) collective-permute-start(f32[48,1536]{1,0:T(8,128)S(1)} %get-tuple-element.54), channel_id=1, source_target_pairs={{0,2},{1,3},{2,0},{3,1},{4,6},{5,7},{6,4},{7,5},{8,10},{9,11},{10,... | collective-permute-start | bytes 884744 | tf_op jit(solution)/shard_map/ppermute | solution.py:811
  59.3 1.7 %collective-permute-start.11 = (f32[48,1536]{1,0:T(8,128)S(1)}, f32[48,1536]{1,0:T(8,128)S(1)}, u32[]{:S(2)}, u32[]{:S(2)}) collective-permute-start(f32[48,1536]{1,0:T(8,128)S(1)} %get-tuple-element.55), channel_id=1, source_target_pairs={{0,1},{1,0},{2,3},{3,2},{4,5},{5,4},{6,7},{7,6},{8,9},{9,8},{10,11... | collective-permute-start | bytes 884744 | tf_op jit(solution)/shard_map/ppermute | solution.py:811
  61.0 1.7 %collective-permute-start.12 = (f32[48,1536]{1,0:T(8,128)S(1)}, f32[48,1536]{1,0:T(8,128)S(1)}, u32[]{:S(2)}, u32[]{:S(2)}) collective-permute-start(f32[48,1536]{1,0:T(8,128)S(1)} %get-tuple-element.56), channel_id=1, source_target_pairs={{0,3},{1,2},{2,1},{3,0},{4,7},{5,6},{6,5},{7,4},{8,11},{9,10},{10,... | collective-permute-start | bytes 884744 | tf_op jit(solution)/shard_map/ppermute | solution.py:811
  63.0 12.2 %collective-permute-done.10.source = f32[48,1536]{1,0:T(8,128)S(1)} collective-permute-done((f32[48,1536]{1,0:T(8,128)S(1)}, f32[48,1536]{1,0:T(8,128)S(1)}, u32[]{:S(2)}, u32[]{:S(2)}) %collective-permute-start.10) | collective-permute-done | bytes 294944 | tf_op jit(solution)/shard_map/ppermute | solution.py:811
  75.8 6.7 %collective-permute-done.12.source = f32[48,1536]{1,0:T(8,128)S(1)} collective-permute-done((f32[48,1536]{1,0:T(8,128)S(1)}, f32[48,1536]{1,0:T(8,128)S(1)}, u32[]{:S(2)}, u32[]{:S(2)}) %collective-permute-start.12) | collective-permute-done | bytes 294944 | tf_op jit(solution)/shard_map/ppermute | solution.py:811
  82.8 1.2 %shard_map.106 = (f32[8,3968]{1,0:T(8,128)S(1)}, f32[8,3968]{1,0:T(8,128)S(1)}, f32[8,3968]{1,0:T(8,128)S(1)}, f32[8,3968]{1,0:T(8,128)S(1)}) custom-call(f32[3,3,16,768]{3,2,1,0:T(8,128)S(1)} %shard_map.102.fields0, f32[3,3,16,768]{3,2,1,0:T(8,128)S(1)} %shard_map.103.fields1, f32[3,3,16,768]{3,2,1,0:T(8,128)S(1)} %shard_map.104.fields2, ...), custom_call_target="tpu_custom_call" | custom-call | flops 80000000 | bytes 5000000 | tf_op jit(solution)/shard_map/pallas_call | solution.py:887
  84.0 5.8 %collective-permute-start.13 = (f32[8,3968]{1,0:T(8,128)S(1)}, f32[8,3968]{1,0:T(8,128)S(1)}, u32[]{:S(2)}, u32[]{:S(2)}) collective-permute-start(f32[8,3968]{1,0:T(8,128)S(1)} %get-tuple-element.59), channel_id=1, source_target_pairs={{0,2},{1,3},{2,0},{3,1},{4,6},{5,7},{6,4},{7,5},{8,10},{9,11},{10,... | collective-permute-start | bytes 380936 | tf_op jit(solution)/shard_map/ppermute | solution.py:811
  89.8 1.7 %collective-permute-start.15 = (f32[8,3968]{1,0:T(8,128)S(1)}, f32[8,3968]{1,0:T(8,128)S(1)}, u32[]{:S(2)}, u32[]{:S(2)}) collective-permute-start(f32[8,3968]{1,0:T(8,128)S(1)} %get-tuple-element.61), channel_id=1, source_target_pairs={{0,3},{1,2},{2,1},{3,0},{4,7},{5,6},{6,5},{7,4},{8,11},{9,10},{10,... | collective-permute-start | bytes 380936 | tf_op jit(solution)/shard_map/ppermute | solution.py:811
  91.5 2.8 %shard_map.107.local_sum = f32[9,48,384]{2,1,0:T(8,128)S(1)} custom-call(f32[9,48,384]{2,1,0:T(8,128)S(1)} %get-tuple-element.62.state, f32[4,32]{1,0:T(4,128)S(1)} %copy-done.6, f32[24,384]{1,0:T(8,128)S(1)} %copy-done.5), custom_call_target="tpu_custom_call" | custom-call | flops 12000000 | bytes 2000000 | tf_op jit(solution)/shard_map/pallas_call | solution.py:894
  94.3 3.8 %collective-permute-done.13.in1 = f32[8,3968]{1,0:T(8,128)S(1)} collective-permute-done((f32[8,3968]{1,0:T(8,128)S(1)}, f32[8,3968]{1,0:T(8,128)S(1)}, u32[]{:S(2)}, u32[]{:S(2)}) %collective-permute-start.13) | collective-permute-done | bytes 127008 | tf_op jit(solution)/shard_map/ppermute | solution.py:811
  98.3 1.3 %collective-permute-done.15.in3 = f32[8,3968]{1,0:T(8,128)S(1)} collective-permute-done((f32[8,3968]{1,0:T(8,128)S(1)}, f32[8,3968]{1,0:T(8,128)S(1)}, u32[]{:S(2)}, u32[]{:S(2)}) %collective-permute-start.15) | collective-permute-done | bytes 127008 | tf_op jit(solution)/shard_map/ppermute | solution.py:811
  99.6 2.4 %shard_map.108 = (f32[9,48,384]{2,1,0:T(8,128)S(1)}, f32[9,48,128]{2,1,0:T(8,128)S(1)}, f32[48,256]{1,0:T(8,128)S(1)}, f32[48,256]{1,0:T(8,128)S(1)}, f32[48,256]{1,0:T(8,128)S(1)}, /*index=5*/f32[48,256]{1,0:T(8,128)S(1)}) custom-call(f32[8,3968]{1,0:T(8,128)S(1)} %get-tuple-element.58.in0, f32[8,3968]{1,0:T(8,128)S(1)} %collective-permute-done.13.in1, ...), custom_call_target="tpu_custom_call" | custom-call | flops 2000000 | bytes 3000000 | tf_op jit(solution)/shard_map/pallas_call | solution.py:901
  102.0 2.3 %collective-permute-start.16 = (f32[48,256]{1,0:T(8,128)S(1)}, f32[48,256]{1,0:T(8,128)S(1)}, u32[]{:S(2)}, u32[]{:S(2)}) collective-permute-start(f32[48,256]{1,0:T(8,128)S(1)} %get-tuple-element.65), channel_id=1, source_target_pairs={{0,24},{4,28},{8,16},{12,20},{16,8},{20,12},{24,0},{28,4},{1,25},{... | collective-permute-start | bytes 147464 | tf_op jit(solution)/shard_map/ppermute | solution.py:909
  104.5 1.7 %collective-permute-start.19 = (f32[48,256]{1,0:T(8,128)S(1)}, f32[48,256]{1,0:T(8,128)S(1)}, u32[]{:S(2)}, u32[]{:S(2)}) collective-permute-start(f32[48,256]{1,0:T(8,128)S(1)} %get-tuple-element.68), channel_id=1, source_target_pairs={{0,4},{4,0},{8,12},{12,8},{16,20},{20,16},{24,28},{28,24},{1,5},{5... | collective-permute-start | bytes 147464 | tf_op jit(solution)/shard_map/ppermute | solution.py:909
  107.0 1.9 %collective-permute-done.17.r1 = f32[48,256]{1,0:T(8,128)S(1)} collective-permute-done((f32[48,256]{1,0:T(8,128)S(1)}, f32[48,256]{1,0:T(8,128)S(1)}, u32[]{:S(2)}, u32[]{:S(2)}) %collective-permute-start.17) | collective-permute-done | bytes 49184 | tf_op jit(solution)/shard_map/ppermute | solution.py:909
  108.9 2.5 %shard_map.109 = f32[3,9,9,16,32]{4,3,2,1,0:T(8,128)} custom-call(s32[24,128]{1,0:T(8,128)S(1)} %shard_map.91.table, f32[9,48,384]{2,1,0:T(8,128)S(1)} %get-tuple-element.63.updated, f32[9,48,128]{2,1,0:T(8,128)S(1)} %get-tuple-element.64.own, f32[48,256]{1,0:T(8,128)S(1)} %collective-permute-done.16.r0, f32[48,256]{1,0:T(8,128)S(1)} %collective-permute-done.17.r1, ...), custom_call_target="tpu_custom_call" | custom-call | flops 2000000 | bytes 3000000 | tf_op jit(solution)/shard_map/pallas_call | solution.py:923
  (45 shorter events, 7.1 us)
Async XLA Ops:
  0.0 9.3 %copy-start.6 = (f32[4,32]{1,0:T(4,128)S(1)}, f32[4,32]{1,0:T(4,128)}, u32[]{:S(2)}) copy-start(f32[4,32]{1,0:T(4,128)} %metric.5) | copy-start | bytes 1540
  2.4 20.4 %collective-permute-start = (f32[48,1536]{1,0:T(8,128)S(1)}, f32[48,1536]{1,0:T(8,128)S(1)}, u32[]{:S(2)}, u32[]{:S(2)}) collective-permute-start(f32[48,1536]{1,0:T(8,128)S(1)} %get-tuple-element.38), channel_id=1, source_target_pairs={{0,2},{1,3},{2,0},{3,1},{4,6},{5,7},{6,4},{7,5},{8,10},{9,11},{10,... | collective-permute-start | bytes 884744 | tf_op jit(solution)/shard_map/ppermute | solution.py:811
  6.5 16.6 %collective-permute-start.1 = (f32[48,1536]{1,0:T(8,128)S(1)}, f32[48,1536]{1,0:T(8,128)S(1)}, u32[]{:S(2)}, u32[]{:S(2)}) collective-permute-start(f32[48,1536]{1,0:T(8,128)S(1)} %get-tuple-element.39), channel_id=1, source_target_pairs={{0,1},{1,0},{2,3},{3,2},{4,5},{5,4},{6,7},{7,6},{8,9},{9,8},{10,11... | collective-permute-start | bytes 884744 | tf_op jit(solution)/shard_map/ppermute | solution.py:811
  8.1 19.3 %collective-permute-start.2 = (f32[48,1536]{1,0:T(8,128)S(1)}, f32[48,1536]{1,0:T(8,128)S(1)}, u32[]{:S(2)}, u32[]{:S(2)}) collective-permute-start(f32[48,1536]{1,0:T(8,128)S(1)} %get-tuple-element.40), channel_id=1, source_target_pairs={{0,3},{1,2},{2,1},{3,0},{4,7},{5,6},{6,5},{7,4},{8,11},{9,10},{10,... | collective-permute-start | bytes 884744 | tf_op jit(solution)/shard_map/ppermute | solution.py:811
  8.1 1.0 copy-start
  9.1 13.7 %copy-start.1 = (f32[4,24,768]{2,1,0:T(8,128)S(1)}, f32[4,24,768]{2,1,0:T(8,128)}, u32[]{:S(2)}) copy-start(f32[4,24,768]{2,1,0:T(8,128)} %constant.8.clone.bands) | copy-start | bytes 884740
  9.3 2.1 %copy-start.2 = (f32[2,12,41472]{2,0,1:T(2,128)S(1)}, f32[2,12,41472]{2,0,1:T(2,128)}, u32[]{:S(2)}) copy-start(f32[2,12,41472]{2,0,1:T(2,128)} %param.11) | copy-start | bytes 11943940
  22.7 5.0 %copy-start.3 = (bf16[4,128,192]{2,1,0:T(8,128)(2,1)S(1)}, bf16[4,128,192]{2,1,0:T(8,128)(2,1)}, u32[]{:S(2)}) copy-start(bf16[4,128,192]{2,1,0:T(8,128)(2,1)} %constant.9.clone.to_span) | copy-start | bytes 589828
  22.8 5.0 %copy-start.4 = (bf16[4,64,192]{2,1,0:T(8,128)(2,1)S(1)}, bf16[4,64,192]{2,1,0:T(8,128)(2,1)}, u32[]{:S(2)}) copy-start(bf16[4,64,192]{2,1,0:T(8,128)(2,1)} %constant.10.clone.to_modes) | copy-start | bytes 294916
  27.7 10.6 %copy-start.7 = (s32[1,5,24]{2,0,1:T(1,128)S(1)}, s32[1,5,24]{2,0,1:T(1,128)}, u32[]{:S(2)}) copy-start(s32[1,5,24]{2,0,1:T(1,128)} %param.12) | copy-start | bytes 1444
  27.7 10.6 %copy-start.8 = (s32[1,5,24]{2,0,1:T(1,128)S(1)}, s32[1,5,24]{2,0,1:T(1,128)}, u32[]{:S(2)}) copy-start(s32[1,5,24]{2,0,1:T(1,128)} %param.13) | copy-start | bytes 1444
  27.7 10.8 %copy-start.5 = (f32[24,384]{1,0:T(8,128)S(1)}, f32[24,384]{1,0:T(8,128)}, u32[]{:S(2)}) copy-start(f32[24,384]{1,0:T(8,128)} %constant.11.clone.bands) | copy-start | bytes 110596
  28.9 17.2 %collective-permute-start.3 = (f32[8,3968]{1,0:T(8,128)S(1)}, f32[8,3968]{1,0:T(8,128)S(1)}, u32[]{:S(2)}, u32[]{:S(2)}) collective-permute-start(f32[8,3968]{1,0:T(8,128)S(1)} %get-tuple-element.43), channel_id=1, source_target_pairs={{0,2},{1,3},{2,0},{3,1},{4,6},{5,7},{6,4},{7,5},{8,10},{9,11},{10,... | collective-permute-start | bytes 380936 | tf_op jit(solution)/shard_map/ppermute | solution.py:811
  36.7 10.2 %collective-permute-start.4 = (f32[8,3968]{1,0:T(8,128)S(1)}, f32[8,3968]{1,0:T(8,128)S(1)}, u32[]{:S(2)}, u32[]{:S(2)}) collective-permute-start(f32[8,3968]{1,0:T(8,128)S(1)} %get-tuple-element.44), channel_id=1, source_target_pairs={{0,1},{1,0},{2,3},{3,2},{4,5},{5,4},{6,7},{7,6},{8,9},{9,8},{10,11... | collective-permute-start | bytes 380936 | tf_op jit(solution)/shard_map/ppermute | solution.py:811
  36.7 10.2 %collective-permute-start.5 = (f32[8,3968]{1,0:T(8,128)S(1)}, f32[8,3968]{1,0:T(8,128)S(1)}, u32[]{:S(2)}, u32[]{:S(2)}) collective-permute-start(f32[8,3968]{1,0:T(8,128)S(1)} %get-tuple-element.45), channel_id=1, source_target_pairs={{0,3},{1,2},{2,1},{3,0},{4,7},{5,6},{6,5},{7,4},{8,11},{9,10},{10,... | collective-permute-start | bytes 380936 | tf_op jit(solution)/shard_map/ppermute | solution.py:811
  49.3 5.1 %collective-permute-start.6 = (f32[48,256]{1,0:T(8,128)S(1)}, f32[48,256]{1,0:T(8,128)S(1)}, u32[]{:S(2)}, u32[]{:S(2)}) collective-permute-start(f32[48,256]{1,0:T(8,128)S(1)} %get-tuple-element.49), channel_id=1, source_target_pairs={{0,24},{4,28},{8,16},{12,20},{16,8},{20,12},{24,0},{28,4},{1,25},{... | collective-permute-start | bytes 147464 | tf_op jit(solution)/shard_map/ppermute | solution.py:909
  51.8 4.6 %collective-permute-start.7 = (f32[48,256]{1,0:T(8,128)S(1)}, f32[48,256]{1,0:T(8,128)S(1)}, u32[]{:S(2)}, u32[]{:S(2)}) collective-permute-start(f32[48,256]{1,0:T(8,128)S(1)} %get-tuple-element.50), channel_id=1, source_target_pairs={{0,28},{4,8},{8,4},{12,16},{16,12},{20,24},{24,20},{28,0},{1,29},{... | collective-permute-start | bytes 147464 | tf_op jit(solution)/shard_map/ppermute | solution.py:909
  51.8 4.6 %collective-permute-start.8 = (f32[48,256]{1,0:T(8,128)S(1)}, f32[48,256]{1,0:T(8,128)S(1)}, u32[]{:S(2)}, u32[]{:S(2)}) collective-permute-start(f32[48,256]{1,0:T(8,128)S(1)} %get-tuple-element.51), channel_id=1, source_target_pairs={{0,8},{4,12},{8,0},{12,4},{16,24},{20,28},{24,16},{28,20},{1,9},{5... | collective-permute-start | bytes 147464 | tf_op jit(solution)/shard_map/ppermute | solution.py:909
  52.4 4.0 %collective-permute-start.9 = (f32[48,256]{1,0:T(8,128)S(1)}, f32[48,256]{1,0:T(8,128)S(1)}, u32[]{:S(2)}, u32[]{:S(2)}) collective-permute-start(f32[48,256]{1,0:T(8,128)S(1)} %get-tuple-element.52), channel_id=1, source_target_pairs={{0,4},{4,0},{8,12},{12,8},{16,20},{20,16},{24,28},{28,24},{1,5},{5... | collective-permute-start | bytes 147464 | tf_op jit(solution)/shard_map/ppermute | solution.py:909
  58.0 17.2 %collective-permute-start.10 = (f32[48,1536]{1,0:T(8,128)S(1)}, f32[48,1536]{1,0:T(8,128)S(1)}, u32[]{:S(2)}, u32[]{:S(2)}) collective-permute-start(f32[48,1536]{1,0:T(8,128)S(1)} %get-tuple-element.54), channel_id=1, source_target_pairs={{0,2},{1,3},{2,0},{3,1},{4,6},{5,7},{6,4},{7,5},{8,10},{9,11},{10,... | collective-permute-start | bytes 884744 | tf_op jit(solution)/shard_map/ppermute | solution.py:811
  59.3 16.2 %collective-permute-start.11 = (f32[48,1536]{1,0:T(8,128)S(1)}, f32[48,1536]{1,0:T(8,128)S(1)}, u32[]{:S(2)}, u32[]{:S(2)}) collective-permute-start(f32[48,1536]{1,0:T(8,128)S(1)} %get-tuple-element.55), channel_id=1, source_target_pairs={{0,1},{1,0},{2,3},{3,2},{4,5},{5,4},{6,7},{7,6},{8,9},{9,8},{10,11... | collective-permute-start | bytes 884744 | tf_op jit(solution)/shard_map/ppermute | solution.py:811
  61.0 21.4 %collective-permute-start.12 = (f32[48,1536]{1,0:T(8,128)S(1)}, f32[48,1536]{1,0:T(8,128)S(1)}, u32[]{:S(2)}, u32[]{:S(2)}) collective-permute-start(f32[48,1536]{1,0:T(8,128)S(1)} %get-tuple-element.56), channel_id=1, source_target_pairs={{0,3},{1,2},{2,1},{3,0},{4,7},{5,6},{6,5},{7,4},{8,11},{9,10},{10,... | collective-permute-start | bytes 884744 | tf_op jit(solution)/shard_map/ppermute | solution.py:811
  84.0 14.1 %collective-permute-start.13 = (f32[8,3968]{1,0:T(8,128)S(1)}, f32[8,3968]{1,0:T(8,128)S(1)}, u32[]{:S(2)}, u32[]{:S(2)}) collective-permute-start(f32[8,3968]{1,0:T(8,128)S(1)} %get-tuple-element.59), channel_id=1, source_target_pairs={{0,2},{1,3},{2,0},{3,1},{4,6},{5,7},{6,4},{7,5},{8,10},{9,11},{10,... | collective-permute-start | bytes 380936 | tf_op jit(solution)/shard_map/ppermute | solution.py:811
  89.8 8.5 %collective-permute-start.14 = (f32[8,3968]{1,0:T(8,128)S(1)}, f32[8,3968]{1,0:T(8,128)S(1)}, u32[]{:S(2)}, u32[]{:S(2)}) collective-permute-start(f32[8,3968]{1,0:T(8,128)S(1)} %get-tuple-element.60), channel_id=1, source_target_pairs={{0,1},{1,0},{2,3},{3,2},{4,5},{5,4},{6,7},{7,6},{8,9},{9,8},{10,11... | collective-permute-start | bytes 380936 | tf_op jit(solution)/shard_map/ppermute | solution.py:811
  89.8 9.8 %collective-permute-start.15 = (f32[8,3968]{1,0:T(8,128)S(1)}, f32[8,3968]{1,0:T(8,128)S(1)}, u32[]{:S(2)}, u32[]{:S(2)}) collective-permute-start(f32[8,3968]{1,0:T(8,128)S(1)} %get-tuple-element.61), channel_id=1, source_target_pairs={{0,3},{1,2},{2,1},{3,0},{4,7},{5,6},{6,5},{7,4},{8,11},{9,10},{10,... | collective-permute-start | bytes 380936 | tf_op jit(solution)/shard_map/ppermute | solution.py:811
  102.0 5.1 %collective-permute-start.16 = (f32[48,256]{1,0:T(8,128)S(1)}, f32[48,256]{1,0:T(8,128)S(1)}, u32[]{:S(2)}, u32[]{:S(2)}) collective-permute-start(f32[48,256]{1,0:T(8,128)S(1)} %get-tuple-element.65), channel_id=1, source_target_pairs={{0,24},{4,28},{8,16},{12,20},{16,8},{20,12},{24,0},{28,4},{1,25},{... | collective-permute-start | bytes 147464 | tf_op jit(solution)/shard_map/ppermute | solution.py:909
  104.2 4.7 %collective-permute-start.17 = (f32[48,256]{1,0:T(8,128)S(1)}, f32[48,256]{1,0:T(8,128)S(1)}, u32[]{:S(2)}, u32[]{:S(2)}) collective-permute-start(f32[48,256]{1,0:T(8,128)S(1)} %get-tuple-element.66), channel_id=1, source_target_pairs={{0,28},{4,8},{8,4},{12,16},{16,12},{20,24},{24,20},{28,0},{1,29},{... | collective-permute-start | bytes 147464 | tf_op jit(solution)/shard_map/ppermute | solution.py:909
  104.2 4.7 %collective-permute-start.18 = (f32[48,256]{1,0:T(8,128)S(1)}, f32[48,256]{1,0:T(8,128)S(1)}, u32[]{:S(2)}, u32[]{:S(2)}) collective-permute-start(f32[48,256]{1,0:T(8,128)S(1)} %get-tuple-element.67), channel_id=1, source_target_pairs={{0,8},{4,12},{8,0},{12,4},{16,24},{20,28},{24,16},{28,20},{1,9},{5... | collective-permute-start | bytes 147464 | tf_op jit(solution)/shard_map/ppermute | solution.py:909
  104.5 4.4 %collective-permute-start.19 = (f32[48,256]{1,0:T(8,128)S(1)}, f32[48,256]{1,0:T(8,128)S(1)}, u32[]{:S(2)}, u32[]{:S(2)}) collective-permute-start(f32[48,256]{1,0:T(8,128)S(1)} %get-tuple-element.68), channel_id=1, source_target_pairs={{0,4},{4,0},{8,12},{12,8},{16,20},{20,16},{24,28},{28,24},{1,5},{5... | collective-permute-start | bytes 147464 | tf_op jit(solution)/shard_map/ppermute | solution.py:909

commit v2 on v1

--- a/solution.py
+++ b/solution.py
@@ -381,13 +381,16 @@
     return total
 
 
-def make_sends(plans, groups, state, xi, staged):
-    lanes = lane_ids(GROUP)
+def make_xi(groups, state, xi):
     for g in groups:
         rows = group_rows(g)
         for t in range(SLAB_TILES):
             for a, value in enumerate(along_i([tile_at(state, (i,), rows, t) for i in range(NODES)])):
                 xi[a, rows, pl.ds(t * LANES, LANES)] = value
+
+
+def make_buffer(plan, groups, state, xi, put):
+    lanes = lane_ids(GROUP)
     for g in groups:
         rows = group_rows(g)
 
@@ -395,18 +398,35 @@
             return tile_at(state if source[0] == "state" else xi, (source[1],), rows, tile)
 
         turned = turner(load)
-        for chunk, plan in enumerate(plans):
-            for t, pieces in enumerate(plan):
-                staged[chunk, rows, pl.ds(t * LANES, LANES)] = pieced(pieces, turned, lanes)
-
-
-def hand_out(me, staged, outs):
-    for step, out in zip(PARTNERS, outs):
-        out[...] = staged[me ^ step]
-
-
-def first_kernel(plans, adjoint, state, out0, out1, out2, out3, xi, staged, taken, sems):
+        for t, pieces in enumerate(plan):
+            put(rows, pl.ds(t * LANES, LANES), pieced(pieces, turned, lanes))
+
+
+def make_first(plans, state, xi, out):
+    target = lax.axis_index("plane") ^ PARTNERS[1]
+
+    def put(rows, at, value):
+        out[rows, at] = value
+
+    for chunk, plan in enumerate(plans):
+        pl.when(target == chunk)(
+            functools.partial(make_buffer, plan, range(state.shape[1] // GROUP), state, xi, put)
+        )
+
+
+def rest_kernel(plans, state, xi, out0, out2, out3, staged):
     me = lax.axis_index("plane")
+    for chunk, plan in enumerate(plans):
+
+        def put(rows, at, value, chunk=chunk):
+            staged[chunk, rows, at] = value
+
+        make_buffer(plan, range(state.shape[1] // GROUP), state, xi, put)
+    for k, out in ((0, out0), (2, out2), (3, out3)):
+        out[...] = staged[me ^ PARTNERS[k]]
+
+
+def first_kernel(plans, adjoint, state, xi, out, taken, sems):
     comps, local = taken.shape[0], taken.shape[3]
 
     def copy(c):
@@ -423,8 +443,8 @@
                 parts = [taken[c, i, j] for j in range(4 * t, min(4 * t + 4, NODES))]
                 parts += [jnp.zeros_like(parts[0])] * (4 - len(parts))
                 state[i, rows, pl.ds(t * LANES, LANES)] = jnp.concatenate(parts, axis=1)
-        make_sends(plans, range(c * local // GROUP, (c + 1) * local // GROUP), state, xi, staged)
-    hand_out(me, staged, (out0, out1, out2, out3))
+        make_xi(range(c * local // GROUP, (c + 1) * local // GROUP), state, xi)
+    make_first(plans, state, xi, out)
 
 
 def metric_rows(metric):
@@ -560,7 +580,8 @@
     return high, (value - high.astype(jnp.float32)).astype(jnp.bfloat16)
 
 
-def fields_kernel(gaps, source, bands, fields):
+def fields_kernel(gaps, source, bands, *refs):
+    fields = refs[-1]
     me = lax.axis_index("plane")
     rows_total = source.shape[0]
     local = fields.shape[2]
@@ -652,7 +673,7 @@
     return (((me + start) ^ step) - start) % size
 
 
-def update_kernel(plans, in0, in1, in2, in3, local_sum, table, updated, own, out0, out1, out2, out3, chunks):
+def update_kernel(plans, in0, in1, in2, in3, local_sum, table, updated, own, out0, out1, out2, out3, chunks, traces):
     me = lax.axis_index("plane")
     rows_total = local_sum.shape[1]
     last = NODES - 1
@@ -672,7 +693,8 @@
 
     turned_round, partner = wide(15) == 1, wide(16)
     slot_edges = [wide(o) for o in blocks]
-    for g in range(rows_total // GROUP):
+    groups = range(rows_total // GROUP)
+    for g in groups:
         rows = group_rows(g)
 
         def load(source, tile, g=g):
@@ -681,31 +703,36 @@
             return tile_at(chunks, (source[1],), slice(None), BODY_TILES * g + tile)
 
         turned = turner(load)
-        new = {}
         for i in range(NODES):
             for t in range(SLAB_TILES):
                 value = pieced(plans[i][t], turned, lanes)
-                new[i, t] = tile_at(local_sum, (i,), rows, t) + step_size * value
-                updated[i, rows, pl.ds(t * LANES, LANES)] = new[i, t]
-        edges = turner(lambda i, tile, new=new: new[i, tile])
+                updated[i, rows, pl.ds(t * LANES, LANES)] = (
+                    tile_at(local_sum, (i,), rows, t) + step_size * value
+                )
+    for g in groups:
+        rows = group_rows(g)
+        edges = turner(lambda i, tile, rows=rows: tile_at(updated, (i,), rows, tile))
         raw = [pieced(plan, edges, lanes) for plan in trace_plans]
-        seen = [jnp.where(turned_round, raw[last - k], raw[k]) for k in range(NODES)]
+        for k in range(NODES):
+            traces[k, rows, :] = jnp.where(turned_round, raw[last - k], raw[k])
+    for g in groups:
+        rows = group_rows(g)
         for slot_edge, out in zip(slot_edges, (out0, out1, out2, out3)):
             for t in range(2):
                 total = None
                 for k in range(5 * t, min(5 * t + 5, NODES)):
-                    value = pick(seen[k], slot_edge)
+                    value = pick(traces[k, rows, :], slot_edge)
                     total = value if total is None else jnp.where(lanes >= 24 * (k - 5 * t), value, total)
                 out[rows, pl.ds(t * LANES, LANES)] = total
         for k in range(NODES):
-            own[k, rows, :] = pick(seen[k], partner)
+            own[k, rows, :] = pick(traces[k, rows, :], partner)
 
 
 def pick(value, index):
     return jnp.take_along_axis(value, index, axis=1, mode="promise_in_bounds")
 
 
-def join_edges(table, updated, own, came, state):
+def join_edges(table, updated, own, came, sums, put):
     rows_total = updated.shape[1]
     last = NODES - 1
     lanes = lane_ids(8)
@@ -746,46 +773,73 @@
             if parts:
                 scale[i, t] = 1.0 / (1.0 + sum(parts[1:], parts[0]))
 
-    for g in range(rows_total // GROUP):
+    groups = range(rows_total // GROUP)
+    for g in groups:
         rows = group_rows(g)
-        sums = []
         for k in range(NODES):
             total = jnp.where(own_has, own[k, rows, :], 0.0)
             for slot, there, source in zip(slots, has, came):
                 value = pick(tile_at(source, (), rows, k // 5), slot + 24 * (k % 5))
                 total = jnp.where(there, value, total)
-            sums.append(total)
+            sums[k, rows, :] = total
+    for g in groups:
+        rows = group_rows(g)
+        values = [sums[k, rows, :] for k in range(NODES)]
         for i in range(NODES):
             for t in range(SLAB_TILES):
-                total = tile_at(updated, (i,), rows, t)
-                parts = edge_parts(sums, i, t)
-                for part in parts:
-                    total += part
+                parts = edge_parts(values, i, t)
                 if parts:
-                    total *= scale[i if i in (0, last) else 1, t]
-                state[i, rows, pl.ds(t * LANES, LANES)] = total
-
-
-def next_kernel(plans, table, updated, own, r0, r1, r2, r3, state, out0, out1, out2, out3, xi, staged):
-    me = lax.axis_index("plane")
-    join_edges(table, updated, own, (r0, r1, r2, r3), state)
-    make_sends(plans, range(updated.shape[1] // GROUP), state, xi, staged)
-    hand_out(me, staged, (out0, out1, out2, out3))
-
-
-def last_kernel(table, updated, own, r0, r1, r2, r3, out, state, given, sems):
-    join_edges(table, updated, own, (r0, r1, r2, r3), state)
+                    total = tile_at(updated, (i,), rows, t)
+                    for part in parts:
+                        total += part
+                    put(g, i, t, total * scale[i if i in (0, last) else 1, t])
+
+
+def next_kernel(plans, table, updated, own, r0, r1, r2, r3, state, xi, out, sums):
+    def put(g, i, t, value):
+        state[i, group_rows(g), pl.ds(t * LANES, LANES)] = value
+
+    for i in range(1, NODES - 1):
+        state[i, :, pl.ds(LANES, LANES)] = updated[i, :, pl.ds(LANES, LANES)]
+    join_edges(table, updated, own, (r0, r1, r2, r3), sums, put)
+    make_xi(range(updated.shape[1] // GROUP), state, xi)
+    make_first(plans, state, xi, out)
+
+
+def inner_kernel(updated, out, given, sems):
     comps, local, elements = given.shape[0], given.shape[3], given.shape[4]
+    inner = pl.ds(1, NODES - 2)
     copies = []
-    for i in range(NODES):
+    for i in range(1, NODES - 1):
         for c in range(comps):
             rows = pl.ds(c * local, local)
-            for t in range(SLAB_TILES):
-                tile = tile_at(state, (i,), rows, t)
-                for q in range(min(4, NODES - 4 * t)):
-                    given[c, i, 4 * t + q] = turn(tile, -32 * q)[:, :elements]
-        copies.append(pltpu.make_async_copy(given.at[:, i], out.at[:, i], sems.at[i]))
+            for j in range(1, NODES - 1):
+                tile = tile_at(updated, (i,), rows, j // 4)
+                given[c, i, j] = turn(tile, -32 * (j % 4))[:, :elements]
+        copies.append(pltpu.make_async_copy(given.at[:, i, inner], out.at[:, i, inner], sems.at[i]))
         copies[-1].start()
+    for copy in copies:
+        copy.wait()
+
+
+def last_kernel(table, updated, own, r0, r1, r2, r3, _, out, given, sums, sems):
+    local, elements = given.shape[3], given.shape[4]
+    last = NODES - 1
+
+    def put(g, i, t, value):
+        c, rows = g * GROUP // local, pl.ds(g * GROUP % local, GROUP)
+        for j in range(4 * t, min(4 * t + 4, NODES)):
+            if i in (0, last) or j in (0, last):
+                given[c, i, j, rows, :] = turn(value, -32 * (j % 4))[:, :elements]
+
+    join_edges(table, updated, own, (r0, r1, r2, r3), sums, put)
+    inner = pl.ds(1, NODES - 2)
+    places = [(slice(None), 0), (slice(None), last), (slice(None), inner, 0), (slice(None), inner, last)]
+    copies = [
+        pltpu.make_async_copy(given.at[place], out.at[place], sems.at[n]) for n, place in enumerate(places)
+    ]
+    for copy in copies:
+        copy.start()
     for copy in copies:
         copy.wait()
 
@@ -831,25 +885,34 @@
         [eta_bands((points - 2 * nodes * elements) * b, CHUNK_TILES * LANES, points) for b in range(planes)]
     )
 
-    in_hbm = pl.BlockSpec(memory_space=pltpu.HBM)
-    sends = [f32(rows_total, SEND_TILES * LANES)] * planes
-    send_scratch = [
-        pltpu.VMEM(state_shape, jnp.float32),
-        pltpu.VMEM((planes, rows_total, SEND_TILES * LANES), jnp.float32),
-    ]
+    in_hbm, vmem = (pl.BlockSpec(memory_space=space) for space in (pltpu.HBM, pltpu.VMEM))
+    buffer = f32(rows_total, SEND_TILES * LANES)
     row_copies = [
         pltpu.VMEM((comps, nodes, nodes, local, elements), jnp.float32),
         pltpu.SemaphoreType.DMA((nodes,)),
     ]
+    edge_scratch = pltpu.VMEM((nodes, rows_total, LANES), jnp.float32)
+
+    def with_rest(state, xi, first):
+        own, *others = kernel_call(
+            functools.partial(rest_kernel, plans),
+            [buffer] * (planes - 1),
+            [pltpu.VMEM((planes, *buffer.shape), jnp.float32)],
+            10**6,
+            2 * 10**6,
+        )(state, xi)
+        return [own, first, *others]
+
     in_rows = pltpu.with_memory_space_constraint(adjoint.transpose(0, 2, 3, 1, 4), pltpu.HBM)
-    state, *outgoing = kernel_call(
+    state, xi, first = kernel_call(
         functools.partial(first_kernel, plans),
-        [f32(*state_shape), *sends],
-        send_scratch + row_copies,
+        [f32(*state_shape), f32(*state_shape), buffer],
+        row_copies,
         4 * 10**6,
         4 * 10**6,
         in_specs=[in_hbm],
     )(in_rows)
+    outgoing = with_rest(state, xi, first)
     whole, two_fields = (12, MODES, CHUNK_TILES * LANES), (2, MODES, CHUNK_TILES * LANES)
     lay = base_flow.transpose(1, 0, 2)
     flows = kernel_call(
@@ -874,16 +937,19 @@
     )(edge_list.transpose(1, 0, 2), flips.transpose(1, 0, 2))
 
     for step_index in range(STEPS):
-        fields = [
-            kernel_call(
-                functools.partial(fields_kernel, gaps),
-                f32(3, comps, local, CHUNK_TILES * LANES),
-                [],
-                2 * 10**6,
-                10**6,
-            )(came, chunk_bands)
-            for came in swapped(outgoing)
-        ]
+        fields = []
+        for came in swapped(outgoing):
+            before = fields[1:][-1:]
+            fields.append(
+                kernel_call(
+                    functools.partial(fields_kernel, gaps),
+                    f32(3, comps, local, CHUNK_TILES * LANES),
+                    [],
+                    2 * 10**6,
+                    10**6,
+                    in_specs=[vmem, vmem] + [pl.BlockSpec(memory_space=pl.ANY)] * len(before),
+                )(came, chunk_bands, *before)
+            )
         returning = kernel_call(
             advect_kernel,
             [f32(GROUP, BACK_TILES * LANES)] * planes,
@@ -901,7 +967,7 @@
         updated, own, *leaving = kernel_call(
             functools.partial(update_kernel, back_plans),
             [f32(*state_shape), f32(nodes, rows_total, LANES)] + [f32(rows_total, 2 * LANES)] * 4,
-            [pltpu.VMEM((planes, GROUP, BACK_TILES * LANES), jnp.float32)],
+            [pltpu.VMEM((planes, GROUP, BACK_TILES * LANES), jnp.float32), edge_scratch],
             2 * 10**6,
             3 * 10**6,
         )(*swapped(returning), local_sum, table)
@@ -912,22 +978,33 @@
             for matching, buffer in enumerate(leaving)
         ]
         if step_index + 1 < STEPS:
-            state, *outgoing = kernel_call(
+            state, xi, first = kernel_call(
                 functools.partial(next_kernel, plans),
-                [f32(*state_shape), *sends],
-                send_scratch,
+                [f32(*state_shape), f32(*state_shape), buffer],
+                [edge_scratch],
                 6 * 10**6,
                 4 * 10**6,
             )(table, updated, own, *traces)
+            outgoing = with_rest(state, xi, first)
         else:
+            inner = kernel_call(
+                inner_kernel,
+                f32(comps, nodes, nodes, local, elements),
+                row_copies,
+                10**6,
+                2 * 10**6,
+                out_specs=in_hbm,
+            )(updated)
             result = kernel_call(
                 last_kernel,
                 f32(comps, nodes, nodes, local, elements),
-                [pltpu.VMEM(state_shape, jnp.float32), *row_copies],
+                [row_copies[0], edge_scratch, row_copies[1]],
                 2 * 10**6,
                 3 * 10**6,
+                in_specs=[vmem] * 7 + [in_hbm],
                 out_specs=in_hbm,
-            )(table, updated, own, *traces)
+                input_output_aliases={7: 0},
+            )(table, updated, own, *traces, inner)
     return result.transpose(0, 3, 1, 2, 4)
 
 

time: 112 us -> 110 us (0.982)
  local copies, waits for them, and re-layouts: 3.12 us -> 0.04 us
    unnamed x18 -> x16, local copies, waits for them, and re-layouts: 3.12 us -> 0.04 us
    pallas_call x3 -> x6, Pallas kernels: 6.48 us -> 8.67 us  [the longest x1 2.93 us: packed_shards(): kernel_call(last_kernel, f32(comps, nodes, nodes, local, elements), [row_...]
    ppermute x12, waiting for transfers between devices: 33.8 us -> 35.6 us  [swapped(): lax.ppermute(buffer, 'plane', [(i, i ^ step) for i in planes])]
    pallas_call x2, Pallas kernels: 4.71 us -> 3.25 us  [packed_shards(): kernel_call(functools.partial(update_kernel, back_plans), [f32(*state_sha...]
    ppermute x8, waiting for transfers between devices: 5.54 us -> 4.32 us  [packed_shards(): lax.ppermute(buffer, 'dom', [(i, trace_partner(i, matching, partitions))...]
  transfers between devices with their start and end apart: 20 -> 20, of which waited for: 12 -> 12; matrix products, arithmetic and copies ran while one was open for 0% -> 0% of each run, Pallas kernels for 17% -> 19%
where the time goes in v2:
time: 110 us
  waiting for transfers between devices  39.9 us (36%)
  starting transfers between devices  35.9 us (33%)
  Pallas kernels  33.8 us (31%)
    ppermute x12, waiting for transfers between devices, swapped(): lax.ppermute(buffer, 'plane', [(i, i ^ step) for i in planes])  35.6 us
    ppermute x12, starting transfers between devices, swapped(): lax.ppermute(buffer, 'plane', [(i, i ^ step) for i in planes])  27.4 us
    pallas_call x1, Pallas kernels, packed_shards(): kernel_call(functools.partial(flow_kernel, points), [f32(*whole)] * STEPS...  11.3 us
    ppermute x8, starting transfers between devices, packed_shards(): lax.ppermute(buffer, 'dom', [(i, trace_partner(i, matching, partitions))...  8.51 us
    pallas_call x2, Pallas kernels, packed_shards(): kernel_call(diffuse_kernel, f32(*state_shape), [pltpu.VMEM((nodes, GROUP,...  5.62 us
    ppermute x8, waiting for transfers between devices, packed_shards(): lax.ppermute(buffer, 'dom', [(i, trace_partner(i, matching, partitions))...  4.32 us
    pallas_call x2, Pallas kernels, packed_shards(): kernel_call(functools.partial(update_kernel, back_plans), [f32(*state_sha...  3.25 us
    pallas_call x1, Pallas kernels, packed_shards(): kernel_call(last_kernel, f32(comps, nodes, nodes, local, elements), [row_...  2.93 us
  transfers between devices with their start and end apart: 20, of which 12 were waited for; matrix products, arithmetic and copies ran while one was open for 0% of the time, Pallas kernels for 19%

profile of v2, /device:TPU:0, one launch (start us, length us, event | category | flops | bytes accessed | tf_op | source)
XLA Modules:
  0.0 110.0 jit_solution(12387608867639144918)
XLA Ops:
  0.0 2.1 %shard_map.92 = (f32[9,48,384]{2,1,0:T(8,128)S(1)}, f32[9,48,384]{2,1,0:T(8,128)S(1)}, f32[48,1536]{1,0:T(8,128)S(1)}) custom-call(f32[3,9,9,16,32]{4,3,2,1,0:T(8,128)} %bitcast.8), custom_call_target="tpu_custom_call" | custom-call | flops 4000000 | bytes 4000000 | tf_op jit(solution)/shard_map/pallas_call | solution.py:907
  2.1 4.1 %collective-permute-start = (f32[48,1536]{1,0:T(8,128)S(1)}, f32[48,1536]{1,0:T(8,128)S(1)}, u32[]{:S(2)}, u32[]{:S(2)}) collective-permute-start(f32[48,1536]{1,0:T(8,128)S(1)} %get-tuple-element.42), channel_id=1, source_target_pairs={{0,2},{1,3},{2,0},{3,1},{4,6},{5,7},{6,4},{7,5},{8,10},{9,11},{10,... | collective-permute-start | bytes 884744 | tf_op jit(solution)/shard_map/ppermute | solution.py:865
  6.7 1.7 %collective-permute-start.1 = (f32[48,1536]{1,0:T(8,128)S(1)}, f32[48,1536]{1,0:T(8,128)S(1)}, u32[]{:S(2)}, u32[]{:S(2)}) collective-permute-start(f32[48,1536]{1,0:T(8,128)S(1)} %get-tuple-element.43), channel_id=1, source_target_pairs={{0,1},{1,0},{2,3},{3,2},{4,5},{5,4},{6,7},{7,6},{8,9},{9,8},{10,11... | collective-permute-start | bytes 884744 | tf_op jit(solution)/shard_map/ppermute | solution.py:865
  8.8 11.3 %shard_map.98 = (f32[12,64,768]{2,1,0:T(8,128)S(1)}, f32[12,64,768]{2,1,0:T(8,128)S(1)}) custom-call(f32[12,2,41472]{2,1,0:T(2,128)S(1)} %bitcast.5, f32[4,32]{1,0:T(4,128)S(1)} %copy-done.5), custom_call_target="tpu_custom_call" | custom-call | flops 4000000 | bytes 9000000 | tf_op jit(solution)/shard_map/pallas_call | solution.py:918
  21.8 5.3 %collective-permute-done.2.source = f32[48,1536]{1,0:T(8,128)S(1)} collective-permute-done((f32[48,1536]{1,0:T(8,128)S(1)}, f32[48,1536]{1,0:T(8,128)S(1)}, u32[]{:S(2)}, u32[]{:S(2)}) %collective-permute-start.2) | collective-permute-done | bytes 294944 | tf_op jit(solution)/shard_map/ppermute | solution.py:865
  27.5 1.2 %shard_map.99 = (f32[8,3968]{1,0:T(8,128)S(1)}, f32[8,3968]{1,0:T(8,128)S(1)}, f32[8,3968]{1,0:T(8,128)S(1)}, f32[8,3968]{1,0:T(8,128)S(1)}) custom-call(f32[3,3,16,768]{3,2,1,0:T(8,128)S(1)} %shard_map.94.fields0, f32[3,3,16,768]{3,2,1,0:T(8,128)S(1)} %shard_map.95.refs_0_.fields1, f32[3,3,16,768]{3,2,1,0:T(8,128)S(1)} %shard_map.96.refs_0_.fields2, ...), custom_call_target="tpu_custom_call" | custom-call | flops 80000000 | bytes 5000000 | tf_op jit(solution)/shard_map/pallas_call | solution.py:953
  28.7 7.8 %collective-permute-start.3 = (f32[8,3968]{1,0:T(8,128)S(1)}, f32[8,3968]{1,0:T(8,128)S(1)}, u32[]{:S(2)}, u32[]{:S(2)}) collective-permute-start(f32[8,3968]{1,0:T(8,128)S(1)} %get-tuple-element.47), channel_id=1, source_target_pairs={{0,2},{1,3},{2,0},{3,1},{4,6},{5,7},{6,4},{7,5},{8,10},{9,11},{10,... | collective-permute-start | bytes 380936 | tf_op jit(solution)/shard_map/ppermute | solution.py:865
  36.4 1.5 %collective-permute-start.5 = (f32[8,3968]{1,0:T(8,128)S(1)}, f32[8,3968]{1,0:T(8,128)S(1)}, u32[]{:S(2)}, u32[]{:S(2)}) collective-permute-start(f32[8,3968]{1,0:T(8,128)S(1)} %get-tuple-element.49), channel_id=1, source_target_pairs={{0,3},{1,2},{2,1},{3,0},{4,7},{5,6},{6,5},{7,4},{8,11},{9,10},{10,... | collective-permute-start | bytes 380936 | tf_op jit(solution)/shard_map/ppermute | solution.py:865
  38.2 2.8 %shard_map.100.local_sum = f32[9,48,384]{2,1,0:T(8,128)S(1)} custom-call(f32[9,48,384]{2,1,0:T(8,128)S(1)} %get-tuple-element.39.state, f32[4,32]{1,0:T(4,128)S(1)} %copy-done.5, f32[24,384]{1,0:T(8,128)S(1)} %copy-done.4), custom_call_target="tpu_custom_call" | custom-call | flops 12000000 | bytes 2000000 | tf_op jit(solution)/shard_map/pallas_call | solution.py:960
  41.0 4.7 %collective-permute-done.3.in1 = f32[8,3968]{1,0:T(8,128)S(1)} collective-permute-done((f32[8,3968]{1,0:T(8,128)S(1)}, f32[8,3968]{1,0:T(8,128)S(1)}, u32[]{:S(2)}, u32[]{:S(2)}) %collective-permute-start.3) | collective-permute-done | bytes 127008 | tf_op jit(solution)/shard_map/ppermute | solution.py:865
  46.7 1.6 %shard_map.101 = (f32[9,48,384]{2,1,0:T(8,128)S(1)}, f32[9,48,128]{2,1,0:T(8,128)S(1)}, f32[48,256]{1,0:T(8,128)S(1)}, f32[48,256]{1,0:T(8,128)S(1)}, f32[48,256]{1,0:T(8,128)S(1)}, /*index=5*/f32[48,256]{1,0:T(8,128)S(1)}) custom-call(f32[8,3968]{1,0:T(8,128)S(1)} %get-tuple-element.46.in0, f32[8,3968]{1,0:T(8,128)S(1)} %collective-permute-done.3.in1, ...), custom_call_target="tpu_custom_call" | custom-call | flops 2000000 | bytes 3000000 | tf_op jit(solution)/shard_map/pallas_call | solution.py:967
  48.3 2.5 %collective-permute-start.6 = (f32[48,256]{1,0:T(8,128)S(1)}, f32[48,256]{1,0:T(8,128)S(1)}, u32[]{:S(2)}, u32[]{:S(2)}) collective-permute-start(f32[48,256]{1,0:T(8,128)S(1)} %get-tuple-element.52), channel_id=1, source_target_pairs={{0,24},{4,28},{8,16},{12,20},{16,8},{20,12},{24,0},{28,4},{1,25},{... | collective-permute-start | bytes 147464 | tf_op jit(solution)/shard_map/ppermute | solution.py:975
  51.4 1.2 %collective-permute-start.9 = (f32[48,256]{1,0:T(8,128)S(1)}, f32[48,256]{1,0:T(8,128)S(1)}, u32[]{:S(2)}, u32[]{:S(2)}) collective-permute-start(f32[48,256]{1,0:T(8,128)S(1)} %get-tuple-element.55), channel_id=1, source_target_pairs={{0,4},{4,0},{8,12},{12,8},{16,20},{20,16},{24,28},{28,24},{1,5},{5... | collective-permute-start | bytes 147464 | tf_op jit(solution)/shard_map/ppermute | solution.py:975
  53.4 2.0 %collective-permute-done.7.r1 = f32[48,256]{1,0:T(8,128)S(1)} collective-permute-done((f32[48,256]{1,0:T(8,128)S(1)}, f32[48,256]{1,0:T(8,128)S(1)}, u32[]{:S(2)}, u32[]{:S(2)}) %collective-permute-start.7) | collective-permute-done | bytes 49184 | tf_op jit(solution)/shard_map/ppermute | solution.py:975
  55.4 1.4 %shard_map.102 = (f32[9,48,384]{2,1,0:T(8,128)S(1)}, f32[9,48,384]{2,1,0:T(8,128)S(1)}, f32[48,1536]{1,0:T(8,128)S(1)}) custom-call(s32[24,128]{1,0:T(8,128)S(1)} %shard_map.91.table, f32[9,48,384]{2,1,0:T(8,128)S(1)} %get-tuple-element.50.updated, f32[9,48,128]{2,1,0:T(8,128)S(1)} %get-tuple-element.51.own, f32[48,256]{1,0:T(8,128)S(1)} %collective-permute-done.6.r0, ...), custom_call_target="tpu_custom_call" | custom-call | flops 6000000 | bytes 4000000 | tf_op jit(solution)/shard_map/pallas_call | solution.py:981
  56.8 1.2 %collective-permute-start.10 = (f32[48,1536]{1,0:T(8,128)S(1)}, f32[48,1536]{1,0:T(8,128)S(1)}, u32[]{:S(2)}, u32[]{:S(2)}) collective-permute-start(f32[48,1536]{1,0:T(8,128)S(1)} %get-tuple-element.59), channel_id=1, source_target_pairs={{0,2},{1,3},{2,0},{3,1},{4,6},{5,7},{6,4},{7,5},{8,10},{9,11},{10,... | collective-permute-start | bytes 884744 | tf_op jit(solution)/shard_map/ppermute | solution.py:865
  58.6 1.8 %collective-permute-start.11 = (f32[48,1536]{1,0:T(8,128)S(1)}, f32[48,1536]{1,0:T(8,128)S(1)}, u32[]{:S(2)}, u32[]{:S(2)}) collective-permute-start(f32[48,1536]{1,0:T(8,128)S(1)} %get-tuple-element.60), channel_id=1, source_target_pairs={{0,1},{1,0},{2,3},{3,2},{4,5},{5,4},{6,7},{7,6},{8,9},{9,8},{10,11... | collective-permute-start | bytes 884744 | tf_op jit(solution)/shard_map/ppermute | solution.py:865
  60.4 1.8 %collective-permute-start.12 = (f32[48,1536]{1,0:T(8,128)S(1)}, f32[48,1536]{1,0:T(8,128)S(1)}, u32[]{:S(2)}, u32[]{:S(2)}) collective-permute-start(f32[48,1536]{1,0:T(8,128)S(1)} %get-tuple-element.61), channel_id=1, source_target_pairs={{0,3},{1,2},{2,1},{3,0},{4,7},{5,6},{6,5},{7,4},{8,11},{9,10},{10,... | collective-permute-start | bytes 884744 | tf_op jit(solution)/shard_map/ppermute | solution.py:865
  62.5 11.5 %collective-permute-done.10.source = f32[48,1536]{1,0:T(8,128)S(1)} collective-permute-done((f32[48,1536]{1,0:T(8,128)S(1)}, f32[48,1536]{1,0:T(8,128)S(1)}, u32[]{:S(2)}, u32[]{:S(2)}) %collective-permute-start.10) | collective-permute-done | bytes 294944 | tf_op jit(solution)/shard_map/ppermute | solution.py:865
  74.5 6.7 %collective-permute-done.12.source = f32[48,1536]{1,0:T(8,128)S(1)} collective-permute-done((f32[48,1536]{1,0:T(8,128)S(1)}, f32[48,1536]{1,0:T(8,128)S(1)}, u32[]{:S(2)}, u32[]{:S(2)}) %collective-permute-start.12) | collective-permute-done | bytes 294944 | tf_op jit(solution)/shard_map/ppermute | solution.py:865
  81.5 1.2 %shard_map.108 = (f32[8,3968]{1,0:T(8,128)S(1)}, f32[8,3968]{1,0:T(8,128)S(1)}, f32[8,3968]{1,0:T(8,128)S(1)}, f32[8,3968]{1,0:T(8,128)S(1)}) custom-call(f32[3,3,16,768]{3,2,1,0:T(8,128)S(1)} %shard_map.104.fields0, f32[3,3,16,768]{3,2,1,0:T(8,128)S(1)} %shard_map.105.refs_0_.fields1, f32[3,3,16,768]{3,2,1,0:T(8,128)S(1)} %shard_map.106.refs_0_.fields2, ...), custom_call_target="tpu_custom_call" | custom-call | flops 80000000 | bytes 5000000 | tf_op jit(solution)/shard_map/pallas_call | solution.py:953
  82.7 5.8 %collective-permute-start.13 = (f32[8,3968]{1,0:T(8,128)S(1)}, f32[8,3968]{1,0:T(8,128)S(1)}, u32[]{:S(2)}, u32[]{:S(2)}) collective-permute-start(f32[8,3968]{1,0:T(8,128)S(1)} %get-tuple-element.64), channel_id=1, source_target_pairs={{0,2},{1,3},{2,0},{3,1},{4,6},{5,7},{6,4},{7,5},{8,10},{9,11},{10,... | collective-permute-start | bytes 380936 | tf_op jit(solution)/shard_map/ppermute | solution.py:865
  88.5 1.7 %collective-permute-start.15 = (f32[8,3968]{1,0:T(8,128)S(1)}, f32[8,3968]{1,0:T(8,128)S(1)}, u32[]{:S(2)}, u32[]{:S(2)}) collective-permute-start(f32[8,3968]{1,0:T(8,128)S(1)} %get-tuple-element.66), channel_id=1, source_target_pairs={{0,3},{1,2},{2,1},{3,0},{4,7},{5,6},{6,5},{7,4},{8,11},{9,10},{10,... | collective-permute-start | bytes 380936 | tf_op jit(solution)/shard_map/ppermute | solution.py:865
  90.2 2.8 %shard_map.109.local_sum = f32[9,48,384]{2,1,0:T(8,128)S(1)} custom-call(f32[9,48,384]{2,1,0:T(8,128)S(1)} %get-tuple-element.56.state, f32[4,32]{1,0:T(4,128)S(1)} %copy-done.5, f32[24,384]{1,0:T(8,128)S(1)} %copy-done.4), custom_call_target="tpu_custom_call" | custom-call | flops 12000000 | bytes 2000000 | tf_op jit(solution)/shard_map/pallas_call | solution.py:960
  93.0 3.8 %collective-permute-done.13.in1 = f32[8,3968]{1,0:T(8,128)S(1)} collective-permute-done((f32[8,3968]{1,0:T(8,128)S(1)}, f32[8,3968]{1,0:T(8,128)S(1)}, u32[]{:S(2)}, u32[]{:S(2)}) %collective-permute-start.13) | collective-permute-done | bytes 127008 | tf_op jit(solution)/shard_map/ppermute | solution.py:865
  97.1 1.2 %collective-permute-done.15.in3 = f32[8,3968]{1,0:T(8,128)S(1)} collective-permute-done((f32[8,3968]{1,0:T(8,128)S(1)}, f32[8,3968]{1,0:T(8,128)S(1)}, u32[]{:S(2)}, u32[]{:S(2)}) %collective-permute-start.15) | collective-permute-done | bytes 127008 | tf_op jit(solution)/shard_map/ppermute | solution.py:865
  98.3 1.6 %shard_map.110 = (f32[9,48,384]{2,1,0:T(8,128)S(1)}, f32[9,48,128]{2,1,0:T(8,128)S(1)}, f32[48,256]{1,0:T(8,128)S(1)}, f32[48,256]{1,0:T(8,128)S(1)}, f32[48,256]{1,0:T(8,128)S(1)}, /*index=5*/f32[48,256]{1,0:T(8,128)S(1)}) custom-call(f32[8,3968]{1,0:T(8,128)S(1)} %get-tuple-element.63.in0, f32[8,3968]{1,0:T(8,128)S(1)} %collective-permute-done.13.in1, ...), custom_call_target="tpu_custom_call" | custom-call | flops 2000000 | bytes 3000000 | tf_op jit(solution)/shard_map/pallas_call | solution.py:967
  99.9 2.1 %collective-permute-start.16 = (f32[48,256]{1,0:T(8,128)S(1)}, f32[48,256]{1,0:T(8,128)S(1)}, u32[]{:S(2)}, u32[]{:S(2)}) collective-permute-start(f32[48,256]{1,0:T(8,128)S(1)} %get-tuple-element.69), channel_id=1, source_target_pairs={{0,24},{4,28},{8,16},{12,20},{16,8},{20,12},{24,0},{28,4},{1,25},{... | collective-permute-start | bytes 147464 | tf_op jit(solution)/shard_map/ppermute | solution.py:975
  102.6 1.5 %collective-permute-start.19 = (f32[48,256]{1,0:T(8,128)S(1)}, f32[48,256]{1,0:T(8,128)S(1)}, u32[]{:S(2)}, u32[]{:S(2)}) collective-permute-start(f32[48,256]{1,0:T(8,128)S(1)} %get-tuple-element.72), channel_id=1, source_target_pairs={{0,4},{4,0},{8,12},{12,8},{16,20},{20,16},{24,28},{28,24},{1,5},{5... | collective-permute-start | bytes 147464 | tf_op jit(solution)/shard_map/ppermute | solution.py:975
  104.2 1.2 %shard_map.111._ = f32[3,9,9,16,32]{4,3,2,1,0:T(8,128)} custom-call(f32[9,48,384]{2,1,0:T(8,128)S(1)} %get-tuple-element.67.updated), custom_call_target="tpu_custom_call" | custom-call | flops 1000000 | bytes 2000000 | tf_op jit(solution)/shard_map/pallas_call | solution.py:990
  105.4 1.5 %collective-permute-done.17.r1 = f32[48,256]{1,0:T(8,128)S(1)} collective-permute-done((f32[48,256]{1,0:T(8,128)S(1)}, f32[48,256]{1,0:T(8,128)S(1)}, u32[]{:S(2)}, u32[]{:S(2)}) %collective-permute-start.17) | collective-permute-done | bytes 49184 | tf_op jit(solution)/shard_map/ppermute | solution.py:975
  106.9 2.9 %shard_map.112 = f32[3,9,9,16,32]{4,3,2,1,0:T(8,128)} custom-call(s32[24,128]{1,0:T(8,128)S(1)} %shard_map.91.table, f32[9,48,384]{2,1,0:T(8,128)S(1)} %get-tuple-element.67.updated, f32[9,48,128]{2,1,0:T(8,128)S(1)} %get-tuple-element.68.own, f32[48,256]{1,0:T(8,128)S(1)} %collective-permute-done.16.r0, ...), custom_call_target="tpu_custom_call", output_to_operand_aliasing={{}: (7, {})} | custom-call | flops 2000000 | bytes 3000000 | tf_op jit(solution)/shard_map/pallas_call | solution.py:998
  (46 shorter events, 7.9 us)
Async XLA Ops:
  0.0 8.4 %copy-start = (f32[4,24,768]{2,1,0:T(8,128)S(1)}, f32[4,24,768]{2,1,0:T(8,128)}, u32[]{:S(2)}) copy-start(f32[4,24,768]{2,1,0:T(8,128)} %constant.8.clone.bands) | copy-start | bytes 884740
  0.0 8.7 %copy-start.1 = (f32[2,12,41472]{2,0,1:T(2,128)S(1)}, f32[2,12,41472]{2,0,1:T(2,128)}, u32[]{:S(2)}) copy-start(f32[2,12,41472]{2,0,1:T(2,128)} %param.11) | copy-start | bytes 11943940
  0.0 8.7 %copy-start.5 = (f32[4,32]{1,0:T(4,128)S(1)}, f32[4,32]{1,0:T(4,128)}, u32[]{:S(2)}) copy-start(f32[4,32]{1,0:T(4,128)} %metric.5) | copy-start | bytes 1540
  2.1 19.1 %collective-permute-start = (f32[48,1536]{1,0:T(8,128)S(1)}, f32[48,1536]{1,0:T(8,128)S(1)}, u32[]{:S(2)}, u32[]{:S(2)}) collective-permute-start(f32[48,1536]{1,0:T(8,128)S(1)} %get-tuple-element.42), channel_id=1, source_target_pairs={{0,2},{1,3},{2,0},{3,1},{4,6},{5,7},{6,4},{7,5},{8,10},{9,11},{10,... | collective-permute-start | bytes 884744 | tf_op jit(solution)/shard_map/ppermute | solution.py:865
  6.7 14.8 %collective-permute-start.1 = (f32[48,1536]{1,0:T(8,128)S(1)}, f32[48,1536]{1,0:T(8,128)S(1)}, u32[]{:S(2)}, u32[]{:S(2)}) collective-permute-start(f32[48,1536]{1,0:T(8,128)S(1)} %get-tuple-element.43), channel_id=1, source_target_pairs={{0,1},{1,0},{2,3},{3,2},{4,5},{5,4},{6,7},{7,6},{8,9},{9,8},{10,11... | collective-permute-start | bytes 884744 | tf_op jit(solution)/shard_map/ppermute | solution.py:865
  8.4 18.7 %collective-permute-start.2 = (f32[48,1536]{1,0:T(8,128)S(1)}, f32[48,1536]{1,0:T(8,128)S(1)}, u32[]{:S(2)}, u32[]{:S(2)}) collective-permute-start(f32[48,1536]{1,0:T(8,128)S(1)} %get-tuple-element.44), channel_id=1, source_target_pairs={{0,3},{1,2},{2,1},{3,0},{4,7},{5,6},{6,5},{7,4},{8,11},{9,10},{10,... | collective-permute-start | bytes 884744 | tf_op jit(solution)/shard_map/ppermute | solution.py:865
  20.0 7.4 %copy-start.2 = (bf16[4,128,192]{2,1,0:T(8,128)(2,1)S(1)}, bf16[4,128,192]{2,1,0:T(8,128)(2,1)}, u32[]{:S(2)}) copy-start(bf16[4,128,192]{2,1,0:T(8,128)(2,1)} %constant.9.clone.to_span) | copy-start | bytes 589828
  20.1 7.4 %copy-start.3 = (bf16[4,64,192]{2,1,0:T(8,128)(2,1)S(1)}, bf16[4,64,192]{2,1,0:T(8,128)(2,1)}, u32[]{:S(2)}) copy-start(bf16[4,64,192]{2,1,0:T(8,128)(2,1)} %constant.10.clone.to_modes) | copy-start | bytes 294916
  27.4 10.6 %copy-start.6 = (s32[1,5,24]{2,0,1:T(1,128)S(1)}, s32[1,5,24]{2,0,1:T(1,128)}, u32[]{:S(2)}) copy-start(s32[1,5,24]{2,0,1:T(1,128)} %param.12) | copy-start | bytes 1444
  27.4 10.6 %copy-start.7 = (s32[1,5,24]{2,0,1:T(1,128)S(1)}, s32[1,5,24]{2,0,1:T(1,128)}, u32[]{:S(2)}) copy-start(s32[1,5,24]{2,0,1:T(1,128)} %param.13) | copy-start | bytes 1444
  27.4 10.8 %copy-start.4 = (f32[24,384]{1,0:T(8,128)S(1)}, f32[24,384]{1,0:T(8,128)}, u32[]{:S(2)}) copy-start(f32[24,384]{1,0:T(8,128)} %constant.11.clone.bands) | copy-start | bytes 110596
  28.7 17.1 %collective-permute-start.3 = (f32[8,3968]{1,0:T(8,128)S(1)}, f32[8,3968]{1,0:T(8,128)S(1)}, u32[]{:S(2)}, u32[]{:S(2)}) collective-permute-start(f32[8,3968]{1,0:T(8,128)S(1)} %get-tuple-element.47), channel_id=1, source_target_pairs={{0,2},{1,3},{2,0},{3,1},{4,6},{5,7},{6,4},{7,5},{8,10},{9,11},{10,... | collective-permute-start | bytes 380936 | tf_op jit(solution)/shard_map/ppermute | solution.py:865
  36.4 10.2 %collective-permute-start.4 = (f32[8,3968]{1,0:T(8,128)S(1)}, f32[8,3968]{1,0:T(8,128)S(1)}, u32[]{:S(2)}, u32[]{:S(2)}) collective-permute-start(f32[8,3968]{1,0:T(8,128)S(1)} %get-tuple-element.48), channel_id=1, source_target_pairs={{0,1},{1,0},{2,3},{3,2},{4,5},{5,4},{6,7},{7,6},{8,9},{9,8},{10,11... | collective-permute-start | bytes 380936 | tf_op jit(solution)/shard_map/ppermute | solution.py:865
  36.4 10.2 %collective-permute-start.5 = (f32[8,3968]{1,0:T(8,128)S(1)}, f32[8,3968]{1,0:T(8,128)S(1)}, u32[]{:S(2)}, u32[]{:S(2)}) collective-permute-start(f32[8,3968]{1,0:T(8,128)S(1)} %get-tuple-element.49), channel_id=1, source_target_pairs={{0,3},{1,2},{2,1},{3,0},{4,7},{5,6},{6,5},{7,4},{8,11},{9,10},{10,... | collective-permute-start | bytes 380936 | tf_op jit(solution)/shard_map/ppermute | solution.py:865
  48.3 5.1 %collective-permute-start.6 = (f32[48,256]{1,0:T(8,128)S(1)}, f32[48,256]{1,0:T(8,128)S(1)}, u32[]{:S(2)}, u32[]{:S(2)}) collective-permute-start(f32[48,256]{1,0:T(8,128)S(1)} %get-tuple-element.52), channel_id=1, source_target_pairs={{0,24},{4,28},{8,16},{12,20},{16,8},{20,12},{24,0},{28,4},{1,25},{... | collective-permute-start | bytes 147464 | tf_op jit(solution)/shard_map/ppermute | solution.py:975
  50.8 4.6 %collective-permute-start.7 = (f32[48,256]{1,0:T(8,128)S(1)}, f32[48,256]{1,0:T(8,128)S(1)}, u32[]{:S(2)}, u32[]{:S(2)}) collective-permute-start(f32[48,256]{1,0:T(8,128)S(1)} %get-tuple-element.53), channel_id=1, source_target_pairs={{0,28},{4,8},{8,4},{12,16},{16,12},{20,24},{24,20},{28,0},{1,29},{... | collective-permute-start | bytes 147464 | tf_op jit(solution)/shard_map/ppermute | solution.py:975
  50.8 4.6 %collective-permute-start.8 = (f32[48,256]{1,0:T(8,128)S(1)}, f32[48,256]{1,0:T(8,128)S(1)}, u32[]{:S(2)}, u32[]{:S(2)}) collective-permute-start(f32[48,256]{1,0:T(8,128)S(1)} %get-tuple-element.54), channel_id=1, source_target_pairs={{0,8},{4,12},{8,0},{12,4},{16,24},{20,28},{24,16},{28,20},{1,9},{5... | collective-permute-start | bytes 147464 | tf_op jit(solution)/shard_map/ppermute | solution.py:975
  51.4 4.0 %collective-permute-start.9 = (f32[48,256]{1,0:T(8,128)S(1)}, f32[48,256]{1,0:T(8,128)S(1)}, u32[]{:S(2)}, u32[]{:S(2)}) collective-permute-start(f32[48,256]{1,0:T(8,128)S(1)} %get-tuple-element.55), channel_id=1, source_target_pairs={{0,4},{4,0},{8,12},{12,8},{16,20},{20,16},{24,28},{28,24},{1,5},{5... | collective-permute-start | bytes 147464 | tf_op jit(solution)/shard_map/ppermute | solution.py:975
  56.8 17.1 %collective-permute-start.10 = (f32[48,1536]{1,0:T(8,128)S(1)}, f32[48,1536]{1,0:T(8,128)S(1)}, u32[]{:S(2)}, u32[]{:S(2)}) collective-permute-start(f32[48,1536]{1,0:T(8,128)S(1)} %get-tuple-element.59), channel_id=1, source_target_pairs={{0,2},{1,3},{2,0},{3,1},{4,6},{5,7},{6,4},{7,5},{8,10},{9,11},{10,... | collective-permute-start | bytes 884744 | tf_op jit(solution)/shard_map/ppermute | solution.py:865
  58.6 15.7 %collective-permute-start.11 = (f32[48,1536]{1,0:T(8,128)S(1)}, f32[48,1536]{1,0:T(8,128)S(1)}, u32[]{:S(2)}, u32[]{:S(2)}) collective-permute-start(f32[48,1536]{1,0:T(8,128)S(1)} %get-tuple-element.60), channel_id=1, source_target_pairs={{0,1},{1,0},{2,3},{3,2},{4,5},{5,4},{6,7},{7,6},{8,9},{9,8},{10,11... | collective-permute-start | bytes 884744 | tf_op jit(solution)/shard_map/ppermute | solution.py:865
  60.4 20.9 %collective-permute-start.12 = (f32[48,1536]{1,0:T(8,128)S(1)}, f32[48,1536]{1,0:T(8,128)S(1)}, u32[]{:S(2)}, u32[]{:S(2)}) collective-permute-start(f32[48,1536]{1,0:T(8,128)S(1)} %get-tuple-element.61), channel_id=1, source_target_pairs={{0,3},{1,2},{2,1},{3,0},{4,7},{5,6},{6,5},{7,4},{8,11},{9,10},{10,... | collective-permute-start | bytes 884744 | tf_op jit(solution)/shard_map/ppermute | solution.py:865
  82.7 14.1 %collective-permute-start.13 = (f32[8,3968]{1,0:T(8,128)S(1)}, f32[8,3968]{1,0:T(8,128)S(1)}, u32[]{:S(2)}, u32[]{:S(2)}) collective-permute-start(f32[8,3968]{1,0:T(8,128)S(1)} %get-tuple-element.64), channel_id=1, source_target_pairs={{0,2},{1,3},{2,0},{3,1},{4,6},{5,7},{6,4},{7,5},{8,10},{9,11},{10,... | collective-permute-start | bytes 380936 | tf_op jit(solution)/shard_map/ppermute | solution.py:865
  88.5 8.6 %collective-permute-start.14 = (f32[8,3968]{1,0:T(8,128)S(1)}, f32[8,3968]{1,0:T(8,128)S(1)}, u32[]{:S(2)}, u32[]{:S(2)}) collective-permute-start(f32[8,3968]{1,0:T(8,128)S(1)} %get-tuple-element.65), channel_id=1, source_target_pairs={{0,1},{1,0},{2,3},{3,2},{4,5},{5,4},{6,7},{7,6},{8,9},{9,8},{10,11... | collective-permute-start | bytes 380936 | tf_op jit(solution)/shard_map/ppermute | solution.py:865
  88.5 9.8 %collective-permute-start.15 = (f32[8,3968]{1,0:T(8,128)S(1)}, f32[8,3968]{1,0:T(8,128)S(1)}, u32[]{:S(2)}, u32[]{:S(2)}) collective-permute-start(f32[8,3968]{1,0:T(8,128)S(1)} %get-tuple-element.66), channel_id=1, source_target_pairs={{0,3},{1,2},{2,1},{3,0},{4,7},{5,6},{6,5},{7,4},{8,11},{9,10},{10,... | collective-permute-start | bytes 380936 | tf_op jit(solution)/shard_map/ppermute | solution.py:865
  99.9 5.4 %collective-permute-start.16 = (f32[48,256]{1,0:T(8,128)S(1)}, f32[48,256]{1,0:T(8,128)S(1)}, u32[]{:S(2)}, u32[]{:S(2)}) collective-permute-start(f32[48,256]{1,0:T(8,128)S(1)} %get-tuple-element.69), channel_id=1, source_target_pairs={{0,24},{4,28},{8,16},{12,20},{16,8},{20,12},{24,0},{28,4},{1,25},{... | collective-permute-start | bytes 147464 | tf_op jit(solution)/shard_map/ppermute | solution.py:975
  102.1 4.8 %collective-permute-start.17 = (f32[48,256]{1,0:T(8,128)S(1)}, f32[48,256]{1,0:T(8,128)S(1)}, u32[]{:S(2)}, u32[]{:S(2)}) collective-permute-start(f32[48,256]{1,0:T(8,128)S(1)} %get-tuple-element.70), channel_id=1, source_target_pairs={{0,28},{4,8},{8,4},{12,16},{16,12},{20,24},{24,20},{28,0},{1,29},{... | collective-permute-start | bytes 147464 | tf_op jit(solution)/shard_map/ppermute | solution.py:975
  102.1 4.8 %collective-permute-start.18 = (f32[48,256]{1,0:T(8,128)S(1)}, f32[48,256]{1,0:T(8,128)S(1)}, u32[]{:S(2)}, u32[]{:S(2)}) collective-permute-start(f32[48,256]{1,0:T(8,128)S(1)} %get-tuple-element.71), channel_id=1, source_target_pairs={{0,8},{4,12},{8,0},{12,4},{16,24},{20,28},{24,16},{28,20},{1,9},{5... | collective-permute-start | bytes 147464 | tf_op jit(solution)/shard_map/ppermute | solution.py:975
  102.6 4.3 %collective-permute-start.19 = (f32[48,256]{1,0:T(8,128)S(1)}, f32[48,256]{1,0:T(8,128)S(1)}, u32[]{:S(2)}, u32[]{:S(2)}) collective-permute-start(f32[48,256]{1,0:T(8,128)S(1)} %get-tuple-element.72), channel_id=1, source_target_pairs={{0,4},{4,0},{8,12},{12,8},{16,20},{20,16},{24,28},{28,24},{1,5},{5... | collective-permute-start | bytes 147464 | tf_op jit(solution)/shard_map/ppermute | solution.py:975

commit v3 on v2

--- a/solution.py
+++ b/solution.py
@@ -187,12 +187,15 @@
 LANES = 128
 SLAB_TILES = 3
 STATE_TILES = 7
+RING_TILES = 6
+BASE_TILES = 11
 SEND_TILES = 12
 CHUNK_TILES = 6
 BODY_TILES = 5
 BACK_TILES = 31
 GROUP = 8
 PARTNERS = (0, 2, 1, 3)
+FIELDS_ORDER = (0, 1, 2, 3)
 STEP_VISC = step_size * viscosity
 
 
@@ -234,14 +237,16 @@
 def span_weights(planes):
     basis, slope, forward = span_numbers()
     local = MODES // planes
-    to_span, to_modes = [], []
+    to_span, to_span_last, to_modes = [], [], []
     for me in range(planes):
         came = np.concatenate([(me ^ step) * local + np.arange(local) for step in PARTNERS])
         high, low = in_two(np.concatenate([basis, slope])[:, came])
-        to_span.append(np.concatenate([high, high, low], axis=1))
+        early, last = slice(0, MODES - local), slice(MODES - local, MODES)
+        for table, columns in ((to_span, early), (to_span_last, last)):
+            table.append(np.concatenate([high[:, columns], high[:, columns], low[:, columns]], axis=1))
         high, low = in_two(forward[came])
         to_modes.append(np.concatenate([high, high, low], axis=1))
-    return np.stack(to_span), np.stack(to_modes)
+    return np.stack(to_span), np.stack(to_span_last), np.stack(to_modes)
 
 
 def eta_bands(first_lane, lanes, count):
@@ -266,30 +271,68 @@
     return plan
 
 
+def end_part(chunk, points):
+    part = points - 2 * NODES * 32
+    if chunk == 0:
+        return 2, 0, points - part, part, 3
+    if chunk == 3:
+        return 6, NODES * 32 - part, 0, part, -7
+    return None
+
+
 def send_segments(chunk, points):
     ring, slab = STATE_TILES * LANES, NODES * 32
     turned = (points - 2 * slab) * chunk
+    part = end_part(chunk, points)
     segments = []
-    for r in range(3):
-        start = (r * slab - turned) % ring
-        first = min(slab, ring - start)
-        segments.append((("state", 2 * chunk + r), 0, start, first))
-        if first < slab:
-            segments.append((("state", 2 * chunk + r), first, 0, slab - first))
-    gap = (3 * slab - turned) % ring
-    body = (points // LANES) * LANES
-    lane = points * chunk
-    for lane in range(points * chunk, points * (chunk + 1), 8):
-        at = lane - points * chunk
-        target = ring + at if at < body else gap + at - body
-        source = ("xi", lane // slab)
-        if segments[-1][0] == source and segments[-1][1] + segments[-1][3] == lane % slab and (
-            segments[-1][2] + segments[-1][3] == target
-        ):
-            segments[-1] = (source, segments[-1][1], segments[-1][2], segments[-1][3] + 8)
+
+    def add(source, src, dst, length):
+        split = RING_TILES * LANES
+        if dst < split < dst + length:
+            add(source, src, dst, split - dst)
+            add(source, src + split - dst, split, length - split + dst)
         else:
-            segments.append((source, lane % slab, target, 8))
+            segments.append((source, src, dst + (BASE_TILES - RING_TILES) * LANES * (dst >= split), length))
+
+    if part is None:
+        for r in range(3):
+            start = (r * slab - turned) % ring
+            first = min(slab, ring - start)
+            add(("state", 2 * chunk + r), 0, start, first)
+            if first < slab:
+                add(("state", 2 * chunk + r), first, 0, slab - first)
+        gap = (3 * slab - turned) % ring
+    else:
+        for i in range(NODES):
+            low, high = max(i * slab, points * chunk), min((i + 1) * slab, points * (chunk + 1))
+            if low < high:
+                add(("state", i), low - i * slab, low - points * chunk, high - low)
+        i, src, lane, length, ahead = part
+        start = (lane + 32 * ahead) % ring
+        add(("eta", i), src, start, length)
+        gap = start + length
+    body = points // LANES * LANES
+    for i in range(NODES):
+        low, high = max(i * slab, points * chunk), min((i + 1) * slab, points * (chunk + 1))
+        cut = points * chunk + body
+        if low < min(high, cut):
+            segments.append(
+                (("xi", i), low - i * slab, RING_TILES * LANES + low - points * chunk, min(high, cut) - low)
+            )
+        if max(low, cut) < high:
+            low = max(low, cut)
+            add(("xi", i), low - i * slab, gap + low - cut, high - low)
     return segments, gap
+
+
+def chunk_eta_bands(chunk, points):
+    bands = eta_bands((points - 2 * NODES * 32) * chunk, CHUNK_TILES * LANES, points)
+    part = end_part(chunk, points)
+    if part is not None:
+        _, _, lane, length, ahead = part
+        bands[:, lane : lane + length] = 0.0
+        bands[ahead + 8, lane : lane + length] = 1.0
+    return bands
 
 
 def return_segments(points):
@@ -389,44 +432,58 @@
                 xi[a, rows, pl.ds(t * LANES, LANES)] = value
 
 
-def make_buffer(plan, groups, state, xi, put):
+def used_offsets(tile):
+    nodes = range(4 * tile, min(4 * tile + 4, NODES))
+    return [d for d in range(-8, 9) if any(0 <= j + d < NODES for j in nodes)]
+
+
+def make_buffer(plan, groups, state, xi, bands, put):
     lanes = lane_ids(GROUP)
     for g in groups:
         rows = group_rows(g)
 
         def load(source, tile, rows=rows):
-            return tile_at(state if source[0] == "state" else xi, (source[1],), rows, tile)
+            name, i = source
+            if name != "eta":
+                return tile_at(state if name == "state" else xi, (i,), rows, tile)
+            turned = turned_tiles([tile_at(state, (i,), rows, t) for t in range(SLAB_TILES)], lanes)
+            return along_j(
+                turned, SLAB_TILES, tile, lambda d: tile_at(bands, (), pl.ds(d + 8, 1), tile), used_offsets(tile)
+            )
 
         turned = turner(load)
         for t, pieces in enumerate(plan):
-            put(rows, pl.ds(t * LANES, LANES), pieced(pieces, turned, lanes))
-
-
-def make_first(plans, state, xi, out):
+            value = pieced(pieces, turned, lanes) if pieces else jnp.zeros((GROUP, LANES), jnp.float32)
+            put(rows, t, value)
+
+
+def make_first(plans, state, xi, bands, out):
     target = lax.axis_index("plane") ^ PARTNERS[1]
 
-    def put(rows, at, value):
-        out[rows, at] = value
+    def put(rows, t, value):
+        out[rows, pl.ds(t * LANES, LANES)] = value
 
     for chunk, plan in enumerate(plans):
-        pl.when(target == chunk)(
-            functools.partial(make_buffer, plan, range(state.shape[1] // GROUP), state, xi, put)
-        )
-
-
-def rest_kernel(plans, state, xi, out0, out2, out3, staged):
+        groups = range(state.shape[1] // GROUP)
+        pl.when(target == chunk)(functools.partial(make_buffer, plan, groups, state, xi, bands, put))
+
+
+def rest_kernel(plans, state, xi, bands, out0, out2, out3, extra3, staged):
     me = lax.axis_index("plane")
     for chunk, plan in enumerate(plans):
 
-        def put(rows, at, value, chunk=chunk):
-            staged[chunk, rows, at] = value
-
-        make_buffer(plan, range(state.shape[1] // GROUP), state, xi, put)
-    for k, out in ((0, out0), (2, out2), (3, out3)):
-        out[...] = staged[me ^ PARTNERS[k]]
-
-
-def first_kernel(plans, adjoint, state, xi, out, taken, sems):
+        def put(rows, t, value, chunk=chunk):
+            staged[chunk, rows, pl.ds(t * LANES, LANES)] = value
+
+        make_buffer(plan, range(state.shape[1] // GROUP), state, xi, bands, put)
+    base, last = pl.ds(0, BASE_TILES * LANES), pl.ds(BASE_TILES * LANES, LANES)
+    out0[...] = staged[me ^ PARTNERS[0]]
+    out2[...] = staged[me ^ PARTNERS[2]]
+    out3[...] = staged[me ^ PARTNERS[3], :, base]
+    extra3[...] = staged[me ^ PARTNERS[3], :, last]
+
+
+def first_kernel(plans, adjoint, far_bands, state, xi, out, taken, sems, bands):
     comps, local = taken.shape[0], taken.shape[3]
 
     def copy(c):
@@ -434,6 +491,8 @@
 
     for c in range(comps):
         copy(c).start()
+    fetch = pltpu.make_async_copy(far_bands, bands, sems.at[comps])
+    fetch.start()
 
     for c in range(comps):
         copy(c).wait()
@@ -444,7 +503,8 @@
                 parts += [jnp.zeros_like(parts[0])] * (4 - len(parts))
                 state[i, rows, pl.ds(t * LANES, LANES)] = jnp.concatenate(parts, axis=1)
         make_xi(range(c * local // GROUP, (c + 1) * local // GROUP), state, xi)
-    make_first(plans, state, xi, out)
+    fetch.wait()
+    make_first(plans, state, xi, bands, out)
 
 
 def metric_rows(metric):
@@ -537,13 +597,10 @@
     g_ii = xi_x * xi_x + xi_y * xi_y
     g_ij = xi_x * eta_x + xi_y * eta_y
     g_jj = eta_x * eta_x + eta_y * eta_y
-    used = [[d for d in range(-8, 9) if any(0 <= j + d < NODES for j in range(4 * t, min(4 * t + 4, NODES)))]
-            for t in range(SLAB_TILES)]
-
     def eta_of(tiles):
         turned = turned_tiles(tiles, lanes)
         return [
-            along_j(turned, SLAB_TILES, t, lambda d, t=t: tile_at(bands, (), pl.ds(d + 8, 1), t), used[t])
+            along_j(turned, SLAB_TILES, t, lambda d, t=t: tile_at(bands, (), pl.ds(d + 8, 1), t), used_offsets(t))
             for t in range(SLAB_TILES)
         ]
 
@@ -580,20 +637,22 @@
     return high, (value - high.astype(jnp.float32)).astype(jnp.bfloat16)
 
 
-def fields_kernel(gaps, source, bands, *refs):
+def fields_kernel(gaps, split, source, *refs):
+    extra, bands = (refs[0], refs[1]) if split else (None, refs[0])
     fields = refs[-1]
     me = lax.axis_index("plane")
     rows_total = source.shape[0]
     local = fields.shape[2]
     lanes = lane_ids(GROUP)
     gap = sum(jnp.where(me == b, g, 0) for b, g in enumerate(gaps))
-    gap_tile, gap_lane = gap // LANES, lax.rem(gap, LANES)
+    gap_late, gap_shift = gap >= RING_TILES * LANES, lax.rem(LANES - lax.rem(gap, LANES), LANES)
 
     for g in range(rows_total // GROUP):
         rows = group_rows(g)
         c = g * GROUP // local
         target = pl.ds(g * GROUP % local, GROUP)
-        tiles = [tile_at(source, (), rows, t) for t in range(STATE_TILES)]
+        tiles = [tile_at(source, (), rows, t) for t in range(RING_TILES)]
+        tiles.append(extra[rows, :] if split else tile_at(source, (), rows, BASE_TILES))
         turned = turned_tiles(tiles, lanes)
         for t in range(CHUNK_TILES):
             at = pl.ds(t * LANES, LANES)
@@ -602,63 +661,66 @@
                 turned, STATE_TILES, t, lambda d, at=at: bands[me, pl.ds(d + 8, 1), at], range(-8, 9)
             )
         for t in range(BODY_TILES):
-            fields[1, c, target, pl.ds(t * LANES, LANES)] = tile_at(source, (), rows, STATE_TILES + t)
-        tail = source[rows, pl.ds(pl.multiple_of(gap_tile * LANES, LANES), LANES)]
-        fields[1, c, target, pl.ds(BODY_TILES * LANES, LANES)] = pltpu.roll(
-            tail, lax.rem(LANES - gap_lane, LANES), 1
-        )
-
-
-def advect_kernel(fields0, fields1, fields2, fields3, flow, to_span, to_modes, *outs):
+            fields[1, c, target, pl.ds(t * LANES, LANES)] = tile_at(source, (), rows, RING_TILES + t)
+        tail = jnp.where(gap_late, tiles[RING_TILES], tiles[RING_TILES - 1])
+        fields[1, c, target, pl.ds(BODY_TILES * LANES, LANES)] = pltpu.roll(tail, gap_shift, 1)
+
+
+def span_dot(a, value):
+    high, low = halves(value)
+    stacked = jnp.concatenate([high, low, high], axis=0)
+    return jnp.dot(a, stacked, preferred_element_type=jnp.float32)
+
+
+LANE_PARTS = [pl.ds(first, 2 * LANES) for first in range(0, CHUNK_TILES * LANES, 2 * LANES)]
+
+
+def products(sources, flow, both, part):
+    def field(kind, c):
+        return jnp.concatenate([fields[kind, c, :, part] for fields in sources], axis=0)
+
+    comps, basis = sources[0].shape[1], both[:MODES]
+    values, sums = [], []
+    for c in range(comps):
+        out = span_dot(both, field(0, c))
+        values.append(out[:MODES])
+        along_x = flow[0, :, part] * span_dot(basis, field(1, c))
+        along_y = flow[1, :, part] * span_dot(basis, field(2, c))
+        sums.append(along_x + along_y + flow[2, :, part] * out[MODES:])
+    for c in range(comps):
+        taken = values[0] * flow[3 + c, :, part]
+        taken += values[1] * flow[6 + c, :, part]
+        taken += values[2] * flow[9 + c, :, part]
+        yield c, sums[c] - taken
+
+
+def early_kernel(fields0, fields1, fields2, flow, to_span, early):
+    both = to_span[lax.axis_index("plane")]
+    for part in LANE_PARTS:
+        for c, product in products((fields0, fields1, fields2), flow, both, part):
+            early[c, :, part] = product
+
+
+def advect_kernel(fields3, early, flow, to_span, to_modes, *outs):
     me = lax.axis_index("plane")
-    comps = fields0.shape[1]
-    both = to_span[me]
-    basis = both[:MODES]
-    back = to_modes[me]
-    width = 2 * LANES
-    chunks = CHUNK_TILES * LANES // width
+    both, back = to_span[me], to_modes[me]
     lanes = lane_ids(GROUP)
-
-    def dot(a, value):
-        high, low = halves(value)
-        stacked = jnp.concatenate([high, low, high], axis=0)
-        return jnp.dot(a, stacked, preferred_element_type=jnp.float32)
-
-    def results(part):
-        def field(kind, c):
-            return jnp.concatenate(
-                [fields[kind, c, :, part] for fields in (fields0, fields1, fields2, fields3)], axis=0
-            )
-
-        values, sums = [], []
-        for c in range(comps):
-            out = dot(both, field(0, c))
-            values.append(out[:MODES])
-            along_x = flow[0, :, part] * dot(basis, field(1, c))
-            along_y = flow[1, :, part] * dot(basis, field(2, c))
-            sums.append(along_x + along_y + flow[2, :, part] * out[MODES:])
-        for c in range(comps):
-            taken = values[0] * flow[3 + c, :, part]
-            taken += values[1] * flow[6 + c, :, part]
-            taken += values[2] * flow[9 + c, :, part]
-            yield c, dot(back, sums[c] - taken)
-
-    def split(c, result):
-        for k, out in enumerate(outs):
-            for half in range(MODES // len(outs) // GROUP):
-                first = k * (MODES // len(outs)) + half * GROUP
-                yield k, out, c * (MODES // len(outs) // GROUP) + half, result[first : first + GROUP]
-
-    for first in range(0, (chunks - 1) * width, width):
-        for c, result in results(pl.ds(first, width)):
-            for _, out, g, piece in split(c, result):
-                out[:, pl.ds(BODY_TILES * g * LANES + first, width)] = piece
+    local = MODES // len(outs)
     tails = [None] * len(outs)
-    for c, result in results(pl.ds((chunks - 1) * width, width)):
-        for k, out, g, piece in split(c, result):
-            out[:, pl.ds((BODY_TILES * (g + 1) - 1) * LANES, LANES)] = piece[:, :LANES]
-            tail = turn(piece[:, LANES:], 8 * g)
-            tails[k] = tail if g == 0 else jnp.where(lanes >= 8 * g, tail, tails[k])
+    for n, part in enumerate(LANE_PARTS):
+        for c, product in products((fields3,), flow, both, part):
+            result = span_dot(back, product + early[c, :, part])
+            for k, out in enumerate(outs):
+                for half in range(local // GROUP):
+                    g = c * (local // GROUP) + half
+                    piece = result[k * local + half * GROUP : k * local + (half + 1) * GROUP]
+                    first = (BODY_TILES * g + 2 * n) * LANES
+                    if n < len(LANE_PARTS) - 1:
+                        out[:, pl.ds(first, 2 * LANES)] = piece
+                        continue
+                    out[:, pl.ds(first, LANES)] = piece[:, :LANES]
+                    tail = turn(piece[:, LANES:], 8 * g)
+                    tails[k] = tail if g == 0 else jnp.where(lanes >= 8 * g, tail, tails[k])
     for out, tail in zip(outs, tails):
         out[:, pl.ds((BACK_TILES - 1) * LANES, LANES)] = tail
 
@@ -795,7 +857,7 @@
                     put(g, i, t, total * scale[i if i in (0, last) else 1, t])
 
 
-def next_kernel(plans, table, updated, own, r0, r1, r2, r3, state, xi, out, sums):
+def next_kernel(plans, table, updated, own, r0, r1, r2, r3, bands, state, xi, out, sums):
     def put(g, i, t, value):
         state[i, group_rows(g), pl.ds(t * LANES, LANES)] = value
 
@@ -803,43 +865,27 @@
         state[i, :, pl.ds(LANES, LANES)] = updated[i, :, pl.ds(LANES, LANES)]
     join_edges(table, updated, own, (r0, r1, r2, r3), sums, put)
     make_xi(range(updated.shape[1] // GROUP), state, xi)
-    make_first(plans, state, xi, out)
-
-
-def inner_kernel(updated, out, given, sems):
+    make_first(plans, state, xi, bands, out)
+
+
+def last_kernel(table, updated, own, r0, r1, r2, r3, out, state, sums, given, sems):
     comps, local, elements = given.shape[0], given.shape[3], given.shape[4]
-    inner = pl.ds(1, NODES - 2)
+
+    def put(g, i, t, value):
+        state[i, group_rows(g), pl.ds(t * LANES, LANES)] = value
+
+    join_edges(table, updated, own, (r0, r1, r2, r3), sums, put)
     copies = []
-    for i in range(1, NODES - 1):
+    for i in range(NODES):
         for c in range(comps):
             rows = pl.ds(c * local, local)
-            for j in range(1, NODES - 1):
-                tile = tile_at(updated, (i,), rows, j // 4)
-                given[c, i, j] = turn(tile, -32 * (j % 4))[:, :elements]
-        copies.append(pltpu.make_async_copy(given.at[:, i, inner], out.at[:, i, inner], sems.at[i]))
+            for t in range(SLAB_TILES):
+                joined = t != 1 or i in (0, NODES - 1)
+                tile = tile_at(state if joined else updated, (i,), rows, t)
+                for q in range(min(4, NODES - 4 * t)):
+                    given[c, i, 4 * t + q] = turn(tile, -32 * q)[:, :elements]
+        copies.append(pltpu.make_async_copy(given.at[:, i], out.at[:, i], sems.at[i]))
         copies[-1].start()
-    for copy in copies:
-        copy.wait()
-
-
-def last_kernel(table, updated, own, r0, r1, r2, r3, _, out, given, sums, sems):
-    local, elements = given.shape[3], given.shape[4]
-    last = NODES - 1
-
-    def put(g, i, t, value):
-        c, rows = g * GROUP // local, pl.ds(g * GROUP % local, GROUP)
-        for j in range(4 * t, min(4 * t + 4, NODES)):
-            if i in (0, last) or j in (0, last):
-                given[c, i, j, rows, :] = turn(value, -32 * (j % 4))[:, :elements]
-
-    join_edges(table, updated, own, (r0, r1, r2, r3), sums, put)
-    inner = pl.ds(1, NODES - 2)
-    places = [(slice(None), 0), (slice(None), last), (slice(None), inner, 0), (slice(None), inner, last)]
-    copies = [
-        pltpu.make_async_copy(given.at[place], out.at[place], sems.at[n]) for n, place in enumerate(places)
-    ]
-    for copy in copies:
-        copy.start()
     for copy in copies:
         copy.wait()
 
@@ -860,11 +906,11 @@
 
 
 def swapped(buffers):
-    planes = range(len(buffers))
-    return [buffers[0]] + [
-        lax.ppermute(buffer, "plane", [(i, i ^ step) for i in planes])
-        for buffer, step in zip(buffers[1:], PARTNERS[1:])
-    ]
+    return [buffers[0]] + [swap(buffer, step) for buffer, step in zip(buffers[1:], PARTNERS[1:])]
+
+
+def swap(buffer, step, wanted=range(4)):
+    return lax.ppermute(buffer, "plane", sorted((i ^ step, i) for i in wanted))
 
 
 def packed_shards(adjoint, metric, base_flow, edge_list, flips):
@@ -879,40 +925,40 @@
     plans = [tile_plan(segments, SEND_TILES) for segments, _ in layouts]
     gaps = [gap for _, gap in layouts]
     back_plans = return_segments(points)
-    to_span, to_modes = span_weights(planes)
+    to_span, to_span_last, to_modes = span_weights(planes)
     slab_bands = eta_bands(0, SLAB_TILES * LANES, nodes * elements)
-    chunk_bands = np.stack(
-        [eta_bands((points - 2 * nodes * elements) * b, CHUNK_TILES * LANES, points) for b in range(planes)]
-    )
+    middle = [chunk for chunk, plan in enumerate(plans) if plan[-1]]
+    chunk_bands = np.stack([chunk_eta_bands(b, points) for b in range(planes)])
 
     in_hbm, vmem = (pl.BlockSpec(memory_space=space) for space in (pltpu.HBM, pltpu.VMEM))
-    buffer = f32(rows_total, SEND_TILES * LANES)
+    buffer, base, extra = (f32(rows_total, tiles * LANES) for tiles in (SEND_TILES, BASE_TILES, 1))
     row_copies = [
         pltpu.VMEM((comps, nodes, nodes, local, elements), jnp.float32),
         pltpu.SemaphoreType.DMA((nodes,)),
     ]
     edge_scratch = pltpu.VMEM((nodes, rows_total, LANES), jnp.float32)
 
-    def with_rest(state, xi, first):
-        own, *others = kernel_call(
+    def forward(state, xi, first):
+        own, second, third, last_tile = kernel_call(
             functools.partial(rest_kernel, plans),
-            [buffer] * (planes - 1),
+            [buffer, buffer, base, extra],
             [pltpu.VMEM((planes, *buffer.shape), jnp.float32)],
             10**6,
             2 * 10**6,
-        )(state, xi)
-        return [own, first, *others]
+        )(state, xi, slab_bands)
+        came = swapped([own, first, second, third])
+        return [(part,) for part in came[:-1]] + [(came[-1], swap(last_tile, PARTNERS[-1], middle))]
 
     in_rows = pltpu.with_memory_space_constraint(adjoint.transpose(0, 2, 3, 1, 4), pltpu.HBM)
-    state, xi, first = kernel_call(
+    state, *prepared = kernel_call(
         functools.partial(first_kernel, plans),
         [f32(*state_shape), f32(*state_shape), buffer],
-        row_copies,
+        row_copies + [pltpu.VMEM(slab_bands.shape, jnp.float32)],
         4 * 10**6,
         4 * 10**6,
-        in_specs=[in_hbm],
-    )(in_rows)
-    outgoing = with_rest(state, xi, first)
+        in_specs=[in_hbm, in_hbm],
+    )(in_rows, pltpu.with_memory_space_constraint(jnp.asarray(slab_bands), pltpu.HBM))
+    incoming = forward(state, *prepared)
     whole, two_fields = (12, MODES, CHUNK_TILES * LANES), (2, MODES, CHUNK_TILES * LANES)
     lay = base_flow.transpose(1, 0, 2)
     flows = kernel_call(
@@ -937,26 +983,29 @@
     )(edge_list.transpose(1, 0, 2), flips.transpose(1, 0, 2))
 
     for step_index in range(STEPS):
-        fields = []
-        for came in swapped(outgoing):
-            before = fields[1:][-1:]
-            fields.append(
-                kernel_call(
-                    functools.partial(fields_kernel, gaps),
-                    f32(3, comps, local, CHUNK_TILES * LANES),
-                    [],
-                    2 * 10**6,
-                    10**6,
-                    in_specs=[vmem, vmem] + [pl.BlockSpec(memory_space=pl.ANY)] * len(before),
-                )(came, chunk_bands, *before)
-            )
+        fields = [None] * planes
+        before = []
+        for k in FIELDS_ORDER:
+            parts = incoming[k]
+            fields[k] = kernel_call(
+                functools.partial(fields_kernel, gaps, len(parts) > 1),
+                f32(3, comps, local, CHUNK_TILES * LANES),
+                [],
+                2 * 10**6,
+                10**6,
+                in_specs=[vmem] * (len(parts) + 1) + [pl.BlockSpec(memory_space=pl.ANY)] * len(before),
+            )(*parts, chunk_bands, *before)
+            before = [fields[k]] if k > 0 else []
+        early = kernel_call(
+            early_kernel, f32(comps, MODES, CHUNK_TILES * LANES), [], 50 * 10**6, 5 * 10**6
+        )(*fields[:-1], flows[step_index], to_span)
         returning = kernel_call(
             advect_kernel,
             [f32(GROUP, BACK_TILES * LANES)] * planes,
             [],
-            80 * 10**6,
+            30 * 10**6,
             5 * 10**6,
-        )(*fields, flows[step_index], to_span, to_modes)
+        )(fields[-1], early, flows[step_index], to_span_last, to_modes)
         local_sum = kernel_call(
             diffuse_kernel,
             f32(*state_shape),
@@ -978,33 +1027,23 @@
             for matching, buffer in enumerate(leaving)
         ]
         if step_index + 1 < STEPS:
-            state, xi, first = kernel_call(
+            state, *prepared = kernel_call(
                 functools.partial(next_kernel, plans),
                 [f32(*state_shape), f32(*state_shape), buffer],
                 [edge_scratch],
                 6 * 10**6,
                 4 * 10**6,
-            )(table, updated, own, *traces)
-            outgoing = with_rest(state, xi, first)
+            )(table, updated, own, *traces, slab_bands)
+            incoming = forward(state, *prepared)
         else:
-            inner = kernel_call(
-                inner_kernel,
-                f32(comps, nodes, nodes, local, elements),
-                row_copies,
-                10**6,
-                2 * 10**6,
-                out_specs=in_hbm,
-            )(updated)
             result = kernel_call(
                 last_kernel,
                 f32(comps, nodes, nodes, local, elements),
-                [row_copies[0], edge_scratch, row_copies[1]],
+                [pltpu.VMEM(state_shape, jnp.float32), edge_scratch, *row_copies],
                 2 * 10**6,
                 3 * 10**6,
-                in_specs=[vmem] * 7 + [in_hbm],
                 out_specs=in_hbm,
-                input_output_aliases={7: 0},
-            )(table, updated, own, *traces, inner)
+            )(table, updated, own, *traces)
     return result.transpose(0, 3, 1, 2, 4)
 
 

time: 110 us -> 108 us (0.982)
  waiting for transfers between devices: 39.9 us -> 37.2 us
    ppermute x12 -> x14, waiting for transfers between devices: 35.6 us -> 31.4 us  [swap(): lax.ppermute(buffer, 'plane', sorted(((i ^ step, i) for i in wanted)))]
    ppermute x8, waiting for transfers between devices: 4.32 us -> 5.73 us  [packed_shards(): lax.ppermute(buffer, 'dom', [(i, trace_partner(i, matching, partitions))...]
    pallas_call x12 -> x13, Pallas kernels: 7.51 us -> 8.32 us  [the longest x8 2.41 us: packed_shards(): kernel_call(functools.partial(fields_kernel, gaps, len(parts) > 1), f32(3...]
    ppermute x12 -> x14, starting transfers between devices: 27.4 us -> 27 us  [swap(): lax.ppermute(buffer, 'plane', sorted(((i ^ step, i) for i in wanted)))]
  transfers between devices with their start and end apart: 20 -> 22, of which waited for: 12 -> 13; matrix products, arithmetic and copies ran while one was open for 0% -> 0% of each run, Pallas kernels for 19% -> 21%
where the time goes in v3:
time: 108 us
  waiting for transfers between devices  37.2 us (34%)
  starting transfers between devices  35.4 us (33%)
  Pallas kernels  34.2 us (32%)
    ppermute x14, waiting for transfers between devices, swap(): lax.ppermute(buffer, 'plane', sorted(((i ^ step, i) for i in wanted)))  31.4 us
    ppermute x14, starting transfers between devices, swap(): lax.ppermute(buffer, 'plane', sorted(((i ^ step, i) for i in wanted)))  27 us
    pallas_call x1, Pallas kernels, packed_shards(): kernel_call(functools.partial(flow_kernel, points), [f32(*whole)] * STEPS...  11.3 us
    ppermute x8, starting transfers between devices, packed_shards(): lax.ppermute(buffer, 'dom', [(i, trace_partner(i, matching, partitions))...  8.37 us
    ppermute x8, waiting for transfers between devices, packed_shards(): lax.ppermute(buffer, 'dom', [(i, trace_partner(i, matching, partitions))...  5.73 us
    pallas_call x2, Pallas kernels, packed_shards(): kernel_call(diffuse_kernel, f32(*state_shape), [pltpu.VMEM((nodes, GROUP,...  5.64 us
    pallas_call x2, Pallas kernels, packed_shards(): kernel_call(functools.partial(update_kernel, back_plans), [f32(*state_sha...  3.25 us
    pallas_call x8, Pallas kernels, packed_shards(): kernel_call(functools.partial(fields_kernel, gaps, len(parts) > 1), f32(3...  2.41 us
  transfers between devices with their start and end apart: 22, of which 13 were waited for; matrix products, arithmetic and copies ran while one was open for 0% of the time, Pallas kernels for 21%

profile of v3, /device:TPU:0, one launch (start us, length us, event | category | flops | bytes accessed | tf_op | source)
XLA Modules:
  0.0 108.1 jit_solution(12552581520766778575)
XLA Ops:
  0.0 2.1 %shard_map.101 = (f32[9,48,384]{2,1,0:T(8,128)S(1)}, f32[9,48,384]{2,1,0:T(8,128)S(1)}, f32[48,1536]{1,0:T(8,128)S(1)}) custom-call(f32[3,9,9,16,32]{4,3,2,1,0:T(8,128)} %bitcast.8, f32[24,384]{1,0:T(8,128)} %constant.10.clone.far_bands.bands), custom_call_target="tpu_custom_call" | custom-call | flops 4000000 | bytes 4000000 | tf_op jit(solution)/shard_map/pallas_call | solution.py:953
  2.1 4.2 %collective-permute-start.3 = (f32[48,1536]{1,0:T(8,128)S(1)}, f32[48,1536]{1,0:T(8,128)S(1)}, u32[]{:S(2)}, u32[]{:S(2)}) collective-permute-start(f32[48,1536]{1,0:T(8,128)S(1)} %get-tuple-element.46), channel_id=1, source_target_pairs={{0,2},{1,3},{2,0},{3,1},{4,6},{5,7},{6,4},{7,5},{8,10},{9,11},{10,... | collective-permute-start | bytes 884744 | tf_op jit(solution)/shard_map/ppermute | solution.py:913
  7.1 1.2 %shard_map.102 = (f32[48,1536]{1,0:T(8,128)S(1)}, f32[48,1536]{1,0:T(8,128)S(1)}, f32[48,1408]{1,0:T(8,128)S(1)}, f32[48,128]{1,0:T(8,128)S(1)}) custom-call(f32[9,48,384]{2,1,0:T(8,128)S(1)} %get-tuple-element.41.state, f32[9,48,384]{2,1,0:T(8,128)S(1)} %get-tuple-element.42.xi, f32[24,384]{1,0:T(8,128)S(1)} %copy-done.2), custom_call_target="tpu_custom_call" | custom-call | flops 1000000 | bytes 2000000 | tf_op jit(solution)/shard_map/pallas_call | solution.py:942
  8.3 1.6 %collective-permute-start.2 = (f32[48,1536]{1,0:T(8,128)S(1)}, f32[48,1536]{1,0:T(8,128)S(1)}, u32[]{:S(2)}, u32[]{:S(2)}) collective-permute-start(f32[48,1536]{1,0:T(8,128)S(1)} %get-tuple-element.45), channel_id=1, source_target_pairs={{0,1},{1,0},{2,3},{3,2},{4,5},{5,4},{6,7},{7,6},{8,9},{9,8},{10,11... | collective-permute-start | bytes 884744 | tf_op jit(solution)/shard_map/ppermute | solution.py:913
  10.9 11.3 %shard_map.107 = (f32[12,64,768]{2,1,0:T(8,128)S(1)}, f32[12,64,768]{2,1,0:T(8,128)S(1)}) custom-call(f32[12,2,41472]{2,1,0:T(2,128)S(1)} %bitcast.5, f32[4,32]{1,0:T(4,128)S(1)} %copy-done.7), custom_call_target="tpu_custom_call" | custom-call | flops 4000000 | bytes 9000000 | tf_op jit(solution)/shard_map/pallas_call | solution.py:964
  22.5 5.1 %collective-permute-done.2.source = f32[48,1536]{1,0:T(8,128)S(1)} collective-permute-done((f32[48,1536]{1,0:T(8,128)S(1)}, f32[48,1536]{1,0:T(8,128)S(1)}, u32[]{:S(2)}, u32[]{:S(2)}) %collective-permute-start.2) | collective-permute-done | bytes 294944 | tf_op jit(solution)/shard_map/ppermute | solution.py:913
  29.0 1.1 %shard_map.109 = (f32[8,3968]{1,0:T(8,128)S(1)}, f32[8,3968]{1,0:T(8,128)S(1)}, f32[8,3968]{1,0:T(8,128)S(1)}, f32[8,3968]{1,0:T(8,128)S(1)}) custom-call(f32[3,3,16,768]{3,2,1,0:T(8,128)S(1)} %shard_map.105.fields3, f32[3,64,768]{2,1,0:T(8,128)S(1)} %shard_map.108.early, f32[12,64,768]{2,1,0:T(8,128)S(1)} %get-tuple-element.48.flow, ...), custom_call_target="tpu_custom_call" | custom-call | flops 30000000 | bytes 5000000 | tf_op jit(solution)/shard_map/pallas_call | solution.py:1002
  30.1 5.8 %collective-permute-start.4 = (f32[8,3968]{1,0:T(8,128)S(1)}, f32[8,3968]{1,0:T(8,128)S(1)}, u32[]{:S(2)}, u32[]{:S(2)}) collective-permute-start(f32[8,3968]{1,0:T(8,128)S(1)} %get-tuple-element.50), channel_id=1, source_target_pairs={{0,2},{1,3},{2,0},{3,1},{4,6},{5,7},{6,4},{7,5},{8,10},{9,11},{10,... | collective-permute-start | bytes 380936 | tf_op jit(solution)/shard_map/ppermute | solution.py:913
  35.9 1.5 %collective-permute-start.6 = (f32[8,3968]{1,0:T(8,128)S(1)}, f32[8,3968]{1,0:T(8,128)S(1)}, u32[]{:S(2)}, u32[]{:S(2)}) collective-permute-start(f32[8,3968]{1,0:T(8,128)S(1)} %get-tuple-element.52), channel_id=1, source_target_pairs={{0,3},{1,2},{2,1},{3,0},{4,7},{5,6},{6,5},{7,4},{8,11},{9,10},{10,... | collective-permute-start | bytes 380936 | tf_op jit(solution)/shard_map/ppermute | solution.py:913
  37.7 2.8 %shard_map.110.local_sum = f32[9,48,384]{2,1,0:T(8,128)S(1)} custom-call(f32[9,48,384]{2,1,0:T(8,128)S(1)} %get-tuple-element.41.state, f32[4,32]{1,0:T(4,128)S(1)} %copy-done.7, f32[24,384]{1,0:T(8,128)S(1)} %copy-done.3), custom_call_target="tpu_custom_call" | custom-call | flops 12000000 | bytes 2000000 | tf_op jit(solution)/shard_map/pallas_call | solution.py:1009
  40.6 4.7 %collective-permute-done.4.in1 = f32[8,3968]{1,0:T(8,128)S(1)} collective-permute-done((f32[8,3968]{1,0:T(8,128)S(1)}, f32[8,3968]{1,0:T(8,128)S(1)}, u32[]{:S(2)}, u32[]{:S(2)}) %collective-permute-start.4) | collective-permute-done | bytes 127008 | tf_op jit(solution)/shard_map/ppermute | solution.py:913
  46.2 1.6 %shard_map.111 = (f32[9,48,384]{2,1,0:T(8,128)S(1)}, f32[9,48,128]{2,1,0:T(8,128)S(1)}, f32[48,256]{1,0:T(8,128)S(1)}, f32[48,256]{1,0:T(8,128)S(1)}, f32[48,256]{1,0:T(8,128)S(1)}, /*index=5*/f32[48,256]{1,0:T(8,128)S(1)}) custom-call(f32[8,3968]{1,0:T(8,128)S(1)} %get-tuple-element.49.in0, f32[8,3968]{1,0:T(8,128)S(1)} %collective-permute-done.4.in1, ...), custom_call_target="tpu_custom_call" | custom-call | flops 2000000 | bytes 3000000 | tf_op jit(solution)/shard_map/pallas_call | solution.py:1016
  47.9 2.5 %collective-permute-start.7 = (f32[48,256]{1,0:T(8,128)S(1)}, f32[48,256]{1,0:T(8,128)S(1)}, u32[]{:S(2)}, u32[]{:S(2)}) collective-permute-start(f32[48,256]{1,0:T(8,128)S(1)} %get-tuple-element.55), channel_id=1, source_target_pairs={{0,24},{4,28},{8,16},{12,20},{16,8},{20,12},{24,0},{28,4},{1,25},{... | collective-permute-start | bytes 147464 | tf_op jit(solution)/shard_map/ppermute | solution.py:1024
  50.7 1.5 %collective-permute-start.9 = (f32[48,256]{1,0:T(8,128)S(1)}, f32[48,256]{1,0:T(8,128)S(1)}, u32[]{:S(2)}, u32[]{:S(2)}) collective-permute-start(f32[48,256]{1,0:T(8,128)S(1)} %get-tuple-element.57), channel_id=1, source_target_pairs={{0,8},{4,12},{8,0},{12,4},{16,24},{20,28},{24,16},{28,20},{1,9},{5... | collective-permute-start | bytes 147464 | tf_op jit(solution)/shard_map/ppermute | solution.py:1024
  53.0 1.9 %collective-permute-done.8.r1 = f32[48,256]{1,0:T(8,128)S(1)} collective-permute-done((f32[48,256]{1,0:T(8,128)S(1)}, f32[48,256]{1,0:T(8,128)S(1)}, u32[]{:S(2)}, u32[]{:S(2)}) %collective-permute-start.8) | collective-permute-done | bytes 49184 | tf_op jit(solution)/shard_map/ppermute | solution.py:1024
  55.4 1.2 %shard_map.112 = (f32[9,48,384]{2,1,0:T(8,128)S(1)}, f32[9,48,384]{2,1,0:T(8,128)S(1)}, f32[48,1536]{1,0:T(8,128)S(1)}) custom-call(s32[24,128]{1,0:T(8,128)S(1)} %shard_map.100.table, f32[9,48,384]{2,1,0:T(8,128)S(1)} %get-tuple-element.53.updated, f32[9,48,128]{2,1,0:T(8,128)S(1)} %get-tuple-element.54.own, f32[48,256]{1,0:T(8,128)S(1)} %collective-permute-done.7.r0, ...), custom_call_target="tpu_custom_call" | custom-call | flops 6000000 | bytes 4000000 | tf_op jit(solution)/shard_map/pallas_call | solution.py:1030
  56.7 1.3 %collective-permute-start.14 = (f32[48,1536]{1,0:T(8,128)S(1)}, f32[48,1536]{1,0:T(8,128)S(1)}, u32[]{:S(2)}, u32[]{:S(2)}) collective-permute-start(f32[48,1536]{1,0:T(8,128)S(1)} %get-tuple-element.64), channel_id=1, source_target_pairs={{0,2},{1,3},{2,0},{3,1},{4,6},{5,7},{6,4},{7,5},{8,10},{9,11},{10,... | collective-permute-start | bytes 884744 | tf_op jit(solution)/shard_map/ppermute | solution.py:913
  57.9 1.2 %shard_map.113 = (f32[48,1536]{1,0:T(8,128)S(1)}, f32[48,1536]{1,0:T(8,128)S(1)}, f32[48,1408]{1,0:T(8,128)S(1)}, f32[48,128]{1,0:T(8,128)S(1)}) custom-call(f32[9,48,384]{2,1,0:T(8,128)S(1)} %get-tuple-element.59.state, f32[9,48,384]{2,1,0:T(8,128)S(1)} %get-tuple-element.60.xi, f32[24,384]{1,0:T(8,128)S(1)} %copy-done.3), custom_call_target="tpu_custom_call" | custom-call | flops 1000000 | bytes 2000000 | tf_op jit(solution)/shard_map/pallas_call | solution.py:942
  59.1 1.8 %collective-permute-start.13 = (f32[48,1536]{1,0:T(8,128)S(1)}, f32[48,1536]{1,0:T(8,128)S(1)}, u32[]{:S(2)}, u32[]{:S(2)}) collective-permute-start(f32[48,1536]{1,0:T(8,128)S(1)} %get-tuple-element.63), channel_id=1, source_target_pairs={{0,1},{1,0},{2,3},{3,2},{4,5},{5,4},{6,7},{7,6},{8,9},{9,8},{10,11... | collective-permute-start | bytes 884744 | tf_op jit(solution)/shard_map/ppermute | solution.py:913
  60.9 1.9 %collective-permute-start.11 = (f32[48,1408]{1,0:T(8,128)S(1)}, f32[48,1408]{1,0:T(8,128)S(1)}, u32[]{:S(2)}, u32[]{:S(2)}) collective-permute-start(f32[48,1408]{1,0:T(8,128)S(1)} %get-tuple-element.61), channel_id=1, source_target_pairs={{0,3},{1,2},{2,1},{3,0},{4,7},{5,6},{6,5},{7,4},{8,11},{9,10},{10,... | collective-permute-start | bytes 811016 | tf_op jit(solution)/shard_map/ppermute | solution.py:913
  63.9 10.4 %collective-permute-done.14.source = f32[48,1536]{1,0:T(8,128)S(1)} collective-permute-done((f32[48,1536]{1,0:T(8,128)S(1)}, f32[48,1536]{1,0:T(8,128)S(1)}, u32[]{:S(2)}, u32[]{:S(2)}) %collective-permute-start.14) | collective-permute-done | bytes 294944 | tf_op jit(solution)/shard_map/ppermute | solution.py:913
  75.7 4.7 %collective-permute-done.11.source = f32[48,1408]{1,0:T(8,128)S(1)} collective-permute-done((f32[48,1408]{1,0:T(8,128)S(1)}, f32[48,1408]{1,0:T(8,128)S(1)}, u32[]{:S(2)}, u32[]{:S(2)}) %collective-permute-start.11) | collective-permute-done | bytes 270368 | tf_op jit(solution)/shard_map/ppermute | solution.py:913
  81.8 5.7 %collective-permute-start.15 = (f32[8,3968]{1,0:T(8,128)S(1)}, f32[8,3968]{1,0:T(8,128)S(1)}, u32[]{:S(2)}, u32[]{:S(2)}) collective-permute-start(f32[8,3968]{1,0:T(8,128)S(1)} %get-tuple-element.68), channel_id=1, source_target_pairs={{0,2},{1,3},{2,0},{3,1},{4,6},{5,7},{6,4},{7,5},{8,10},{9,11},{10,... | collective-permute-start | bytes 380936 | tf_op jit(solution)/shard_map/ppermute | solution.py:913
  87.5 1.7 %collective-permute-start.17 = (f32[8,3968]{1,0:T(8,128)S(1)}, f32[8,3968]{1,0:T(8,128)S(1)}, u32[]{:S(2)}, u32[]{:S(2)}) collective-permute-start(f32[8,3968]{1,0:T(8,128)S(1)} %get-tuple-element.70), channel_id=1, source_target_pairs={{0,3},{1,2},{2,1},{3,0},{4,7},{5,6},{6,5},{7,4},{8,11},{9,10},{10,... | collective-permute-start | bytes 380936 | tf_op jit(solution)/shard_map/ppermute | solution.py:913
  89.2 2.8 %shard_map.120.local_sum = f32[9,48,384]{2,1,0:T(8,128)S(1)} custom-call(f32[9,48,384]{2,1,0:T(8,128)S(1)} %get-tuple-element.59.state, f32[4,32]{1,0:T(4,128)S(1)} %copy-done.7, f32[24,384]{1,0:T(8,128)S(1)} %copy-done.3), custom_call_target="tpu_custom_call" | custom-call | flops 12000000 | bytes 2000000 | tf_op jit(solution)/shard_map/pallas_call | solution.py:1009
  92.0 3.5 %collective-permute-done.15.in1 = f32[8,3968]{1,0:T(8,128)S(1)} collective-permute-done((f32[8,3968]{1,0:T(8,128)S(1)}, f32[8,3968]{1,0:T(8,128)S(1)}, u32[]{:S(2)}, u32[]{:S(2)}) %collective-permute-start.15) | collective-permute-done | bytes 127008 | tf_op jit(solution)/shard_map/ppermute | solution.py:913
  95.5 2.1 %collective-permute-done.16.in2 = f32[8,3968]{1,0:T(8,128)S(1)} collective-permute-done((f32[8,3968]{1,0:T(8,128)S(1)}, f32[8,3968]{1,0:T(8,128)S(1)}, u32[]{:S(2)}, u32[]{:S(2)}) %collective-permute-start.16) | collective-permute-done | bytes 127008 | tf_op jit(solution)/shard_map/ppermute | solution.py:913
  97.6 1.6 %shard_map.121 = (f32[9,48,384]{2,1,0:T(8,128)S(1)}, f32[9,48,128]{2,1,0:T(8,128)S(1)}, f32[48,256]{1,0:T(8,128)S(1)}, f32[48,256]{1,0:T(8,128)S(1)}, f32[48,256]{1,0:T(8,128)S(1)}, /*index=5*/f32[48,256]{1,0:T(8,128)S(1)}) custom-call(f32[8,3968]{1,0:T(8,128)S(1)} %get-tuple-element.67.in0, f32[8,3968]{1,0:T(8,128)S(1)} %collective-permute-done.15.in1, ...), custom_call_target="tpu_custom_call" | custom-call | flops 2000000 | bytes 3000000 | tf_op jit(solution)/shard_map/pallas_call | solution.py:1016
  99.2 1.5 %collective-permute-start.18 = (f32[48,256]{1,0:T(8,128)S(1)}, f32[48,256]{1,0:T(8,128)S(1)}, u32[]{:S(2)}, u32[]{:S(2)}) collective-permute-start(f32[48,256]{1,0:T(8,128)S(1)} %get-tuple-element.73), channel_id=1, source_target_pairs={{0,24},{4,28},{8,16},{12,20},{16,8},{20,12},{24,0},{28,4},{1,25},{... | collective-permute-start | bytes 147464 | tf_op jit(solution)/shard_map/ppermute | solution.py:1024
  101.7 1.4 %collective-permute-start.21 = (f32[48,256]{1,0:T(8,128)S(1)}, f32[48,256]{1,0:T(8,128)S(1)}, u32[]{:S(2)}, u32[]{:S(2)}) collective-permute-start(f32[48,256]{1,0:T(8,128)S(1)} %get-tuple-element.76), channel_id=1, source_target_pairs={{0,4},{4,0},{8,12},{12,8},{16,20},{20,16},{24,28},{28,24},{1,5},{5... | collective-permute-start | bytes 147464 | tf_op jit(solution)/shard_map/ppermute | solution.py:1024
  104.2 1.2 %collective-permute-done.19.r1 = f32[48,256]{1,0:T(8,128)S(1)} collective-permute-done((f32[48,256]{1,0:T(8,128)S(1)}, f32[48,256]{1,0:T(8,128)S(1)}, u32[]{:S(2)}, u32[]{:S(2)}) %collective-permute-start.19) | collective-permute-done | bytes 49184 | tf_op jit(solution)/shard_map/ppermute | solution.py:1024
  105.7 2.2 %shard_map.122 = f32[3,9,9,16,32]{4,3,2,1,0:T(8,128)} custom-call(s32[24,128]{1,0:T(8,128)S(1)} %shard_map.100.table, f32[9,48,384]{2,1,0:T(8,128)S(1)} %get-tuple-element.71.updated, f32[9,48,128]{2,1,0:T(8,128)S(1)} %get-tuple-element.72.own, f32[48,256]{1,0:T(8,128)S(1)} %collective-permute-done.18.r0, f32[48,256]{1,0:T(8,128)S(1)} %collective-permute-done.19.r1, ...), custom_call_target="tpu_custom_call" | custom-call | flops 2000000 | bytes 3000000 | tf_op jit(solution)/shard_map/pallas_call | solution.py:1039
  (55 shorter events, 12.4 us)
Async XLA Ops:
  0.0 10.6 %copy-start = (f32[4,24,768]{2,1,0:T(8,128)S(1)}, f32[4,24,768]{2,1,0:T(8,128)}, u32[]{:S(2)}) copy-start(f32[4,24,768]{2,1,0:T(8,128)} %constant.11.clone.refs_0_.refs_1_) | copy-start | bytes 884740
  0.0 10.9 %copy-start.1 = (f32[2,12,41472]{2,0,1:T(2,128)S(1)}, f32[2,12,41472]{2,0,1:T(2,128)}, u32[]{:S(2)}) copy-start(f32[2,12,41472]{2,0,1:T(2,128)} %param.12) | copy-start | bytes 11943940
  2.1 20.1 %collective-permute-start.3 = (f32[48,1536]{1,0:T(8,128)S(1)}, f32[48,1536]{1,0:T(8,128)S(1)}, u32[]{:S(2)}, u32[]{:S(2)}) collective-permute-start(f32[48,1536]{1,0:T(8,128)S(1)} %get-tuple-element.46), channel_id=1, source_target_pairs={{0,2},{1,3},{2,0},{3,1},{4,6},{5,7},{6,4},{7,5},{8,10},{9,11},{10,... | collective-permute-start | bytes 884744 | tf_op jit(solution)/shard_map/ppermute | solution.py:913
  6.3 0.8 copy-start.2
  7.1 3.8 %copy-start.7 = (f32[4,32]{1,0:T(4,128)S(1)}, f32[4,32]{1,0:T(4,128)}, u32[]{:S(2)}) copy-start(f32[4,32]{1,0:T(4,128)} %metric.5) | copy-start | bytes 1540
  8.3 19.3 %collective-permute-start.2 = (f32[48,1536]{1,0:T(8,128)S(1)}, f32[48,1536]{1,0:T(8,128)S(1)}, u32[]{:S(2)}, u32[]{:S(2)}) collective-permute-start(f32[48,1536]{1,0:T(8,128)S(1)} %get-tuple-element.45), channel_id=1, source_target_pairs={{0,1},{1,0},{2,3},{3,2},{4,5},{5,4},{6,7},{7,6},{8,9},{9,8},{10,11... | collective-permute-start | bytes 884744 | tf_op jit(solution)/shard_map/ppermute | solution.py:913
  9.8 18.8 %collective-permute-start = (f32[48,1408]{1,0:T(8,128)S(1)}, f32[48,1408]{1,0:T(8,128)S(1)}, u32[]{:S(2)}, u32[]{:S(2)}) collective-permute-start(f32[48,1408]{1,0:T(8,128)S(1)} %get-tuple-element.43), channel_id=1, source_target_pairs={{0,3},{1,2},{2,1},{3,0},{4,7},{5,6},{6,5},{7,4},{8,11},{9,10},{10,... | collective-permute-start | bytes 811016 | tf_op jit(solution)/shard_map/ppermute | solution.py:913
  9.9 18.8 %collective-permute-start.1 = (f32[48,128]{1,0:T(8,128)S(1)}, f32[48,128]{1,0:T(8,128)S(1)}, u32[]{:S(2)}, u32[]{:S(2)}) collective-permute-start(f32[48,128]{1,0:T(8,128)S(1)} %get-tuple-element.44), channel_id=1, source_target_pairs={{1,2},{2,1},{5,6},{6,5},{9,10},{10,9},{13,14},{14,13},{17,18},{18,... | collective-permute-start | bytes 73736 | tf_op jit(solution)/shard_map/ppermute | solution.py:913
  10.9 17.0 %copy-start.4 = (bf16[4,128,144]{2,1,0:T(8,128)(2,1)S(1)}, bf16[4,128,144]{2,1,0:T(8,128)(2,1)}, u32[]{:S(2)}) copy-start(bf16[4,128,144]{2,1,0:T(8,128)(2,1)} %constant.12.clone.to_span) | copy-start | bytes 442372
  27.9 1.1 %copy-start.5 = (bf16[4,128,48]{2,1,0:T(8,128)(2,1)S(1)}, bf16[4,128,48]{2,1,0:T(8,128)(2,1)}, u32[]{:S(2)}) copy-start(bf16[4,128,48]{2,1,0:T(8,128)(2,1)} %constant.13.clone.to_span) | copy-start | bytes 147460
  27.9 1.1 %copy-start.6 = (bf16[4,64,192]{2,1,0:T(8,128)(2,1)S(1)}, bf16[4,64,192]{2,1,0:T(8,128)(2,1)}, u32[]{:S(2)}) copy-start(bf16[4,64,192]{2,1,0:T(8,128)(2,1)} %constant.14.clone.to_modes) | copy-start | bytes 294916
  28.6 8.9 %copy-start.8 = (s32[1,5,24]{2,0,1:T(1,128)S(1)}, s32[1,5,24]{2,0,1:T(1,128)}, u32[]{:S(2)}) copy-start(s32[1,5,24]{2,0,1:T(1,128)} %param.13) | copy-start | bytes 1444
  28.6 8.8 %copy-start.9 = (s32[1,5,24]{2,0,1:T(1,128)S(1)}, s32[1,5,24]{2,0,1:T(1,128)}, u32[]{:S(2)}) copy-start(s32[1,5,24]{2,0,1:T(1,128)} %param.14) | copy-start | bytes 1444
  28.7 9.1 %copy-start.3 = (f32[24,384]{1,0:T(8,128)S(1)}, f32[24,384]{1,0:T(8,128)}, u32[]{:S(2)}) copy-start(f32[24,384]{1,0:T(8,128)} %constant.10.clone.far_bands.bands) | copy-start | bytes 110596
  30.1 15.2 %collective-permute-start.4 = (f32[8,3968]{1,0:T(8,128)S(1)}, f32[8,3968]{1,0:T(8,128)S(1)}, u32[]{:S(2)}, u32[]{:S(2)}) collective-permute-start(f32[8,3968]{1,0:T(8,128)S(1)} %get-tuple-element.50), channel_id=1, source_target_pairs={{0,2},{1,3},{2,0},{3,1},{4,6},{5,7},{6,4},{7,5},{8,10},{9,11},{10,... | collective-permute-start | bytes 380936 | tf_op jit(solution)/shard_map/ppermute | solution.py:913
  35.9 10.2 %collective-permute-start.5 = (f32[8,3968]{1,0:T(8,128)S(1)}, f32[8,3968]{1,0:T(8,128)S(1)}, u32[]{:S(2)}, u32[]{:S(2)}) collective-permute-start(f32[8,3968]{1,0:T(8,128)S(1)} %get-tuple-element.51), channel_id=1, source_target_pairs={{0,1},{1,0},{2,3},{3,2},{4,5},{5,4},{6,7},{7,6},{8,9},{9,8},{10,11... | collective-permute-start | bytes 380936 | tf_op jit(solution)/shard_map/ppermute | solution.py:913
  35.9 10.2 %collective-permute-start.6 = (f32[8,3968]{1,0:T(8,128)S(1)}, f32[8,3968]{1,0:T(8,128)S(1)}, u32[]{:S(2)}, u32[]{:S(2)}) collective-permute-start(f32[8,3968]{1,0:T(8,128)S(1)} %get-tuple-element.52), channel_id=1, source_target_pairs={{0,3},{1,2},{2,1},{3,0},{4,7},{5,6},{6,5},{7,4},{8,11},{9,10},{10,... | collective-permute-start | bytes 380936 | tf_op jit(solution)/shard_map/ppermute | solution.py:913
  47.8 4.4 %collective-permute-start.10 = (f32[48,256]{1,0:T(8,128)S(1)}, f32[48,256]{1,0:T(8,128)S(1)}, u32[]{:S(2)}, u32[]{:S(2)}) collective-permute-start(f32[48,256]{1,0:T(8,128)S(1)} %get-tuple-element.58), channel_id=1, source_target_pairs={{0,4},{4,0},{8,12},{12,8},{16,20},{20,16},{24,28},{28,24},{1,5},{5... | collective-permute-start | bytes 147464 | tf_op jit(solution)/shard_map/ppermute | solution.py:1024
  47.9 5.1 %collective-permute-start.7 = (f32[48,256]{1,0:T(8,128)S(1)}, f32[48,256]{1,0:T(8,128)S(1)}, u32[]{:S(2)}, u32[]{:S(2)}) collective-permute-start(f32[48,256]{1,0:T(8,128)S(1)} %get-tuple-element.55), channel_id=1, source_target_pairs={{0,24},{4,28},{8,16},{12,20},{16,8},{20,12},{24,0},{28,4},{1,25},{... | collective-permute-start | bytes 147464 | tf_op jit(solution)/shard_map/ppermute | solution.py:1024
  50.4 4.4 %collective-permute-start.8 = (f32[48,256]{1,0:T(8,128)S(1)}, f32[48,256]{1,0:T(8,128)S(1)}, u32[]{:S(2)}, u32[]{:S(2)}) collective-permute-start(f32[48,256]{1,0:T(8,128)S(1)} %get-tuple-element.56), channel_id=1, source_target_pairs={{0,28},{4,8},{8,4},{12,16},{16,12},{20,24},{24,20},{28,0},{1,29},{... | collective-permute-start | bytes 147464 | tf_op jit(solution)/shard_map/ppermute | solution.py:1024
  50.7 4.8 %collective-permute-start.9 = (f32[48,256]{1,0:T(8,128)S(1)}, f32[48,256]{1,0:T(8,128)S(1)}, u32[]{:S(2)}, u32[]{:S(2)}) collective-permute-start(f32[48,256]{1,0:T(8,128)S(1)} %get-tuple-element.57), channel_id=1, source_target_pairs={{0,8},{4,12},{8,0},{12,4},{16,24},{20,28},{24,16},{28,20},{1,9},{5... | collective-permute-start | bytes 147464 | tf_op jit(solution)/shard_map/ppermute | solution.py:1024
  56.7 17.7 %collective-permute-start.14 = (f32[48,1536]{1,0:T(8,128)S(1)}, f32[48,1536]{1,0:T(8,128)S(1)}, u32[]{:S(2)}, u32[]{:S(2)}) collective-permute-start(f32[48,1536]{1,0:T(8,128)S(1)} %get-tuple-element.64), channel_id=1, source_target_pairs={{0,2},{1,3},{2,0},{3,1},{4,6},{5,7},{6,4},{7,5},{8,10},{9,11},{10,... | collective-permute-start | bytes 884744 | tf_op jit(solution)/shard_map/ppermute | solution.py:913
  59.1 15.6 %collective-permute-start.13 = (f32[48,1536]{1,0:T(8,128)S(1)}, f32[48,1536]{1,0:T(8,128)S(1)}, u32[]{:S(2)}, u32[]{:S(2)}) collective-permute-start(f32[48,1536]{1,0:T(8,128)S(1)} %get-tuple-element.63), channel_id=1, source_target_pairs={{0,1},{1,0},{2,3},{3,2},{4,5},{5,4},{6,7},{7,6},{8,9},{9,8},{10,11... | collective-permute-start | bytes 884744 | tf_op jit(solution)/shard_map/ppermute | solution.py:913
  60.9 19.5 %collective-permute-start.11 = (f32[48,1408]{1,0:T(8,128)S(1)}, f32[48,1408]{1,0:T(8,128)S(1)}, u32[]{:S(2)}, u32[]{:S(2)}) collective-permute-start(f32[48,1408]{1,0:T(8,128)S(1)} %get-tuple-element.61), channel_id=1, source_target_pairs={{0,3},{1,2},{2,1},{3,0},{4,7},{5,6},{6,5},{7,4},{8,11},{9,10},{10,... | collective-permute-start | bytes 811016 | tf_op jit(solution)/shard_map/ppermute | solution.py:913
  62.8 12.9 %collective-permute-start.12 = (f32[48,128]{1,0:T(8,128)S(1)}, f32[48,128]{1,0:T(8,128)S(1)}, u32[]{:S(2)}, u32[]{:S(2)}) collective-permute-start(f32[48,128]{1,0:T(8,128)S(1)} %get-tuple-element.62), channel_id=1, source_target_pairs={{1,2},{2,1},{5,6},{6,5},{9,10},{10,9},{13,14},{14,13},{17,18},{18,... | collective-permute-start | bytes 73736 | tf_op jit(solution)/shard_map/ppermute | solution.py:913
  81.8 13.7 %collective-permute-start.15 = (f32[8,3968]{1,0:T(8,128)S(1)}, f32[8,3968]{1,0:T(8,128)S(1)}, u32[]{:S(2)}, u32[]{:S(2)}) collective-permute-start(f32[8,3968]{1,0:T(8,128)S(1)} %get-tuple-element.68), channel_id=1, source_target_pairs={{0,2},{1,3},{2,0},{3,1},{4,6},{5,7},{6,4},{7,5},{8,10},{9,11},{10,... | collective-permute-start | bytes 380936 | tf_op jit(solution)/shard_map/ppermute | solution.py:913
  87.5 10.1 %collective-permute-start.16 = (f32[8,3968]{1,0:T(8,128)S(1)}, f32[8,3968]{1,0:T(8,128)S(1)}, u32[]{:S(2)}, u32[]{:S(2)}) collective-permute-start(f32[8,3968]{1,0:T(8,128)S(1)} %get-tuple-element.69), channel_id=1, source_target_pairs={{0,1},{1,0},{2,3},{3,2},{4,5},{5,4},{6,7},{7,6},{8,9},{9,8},{10,11... | collective-permute-start | bytes 380936 | tf_op jit(solution)/shard_map/ppermute | solution.py:913
  87.5 10.1 %collective-permute-start.17 = (f32[8,3968]{1,0:T(8,128)S(1)}, f32[8,3968]{1,0:T(8,128)S(1)}, u32[]{:S(2)}, u32[]{:S(2)}) collective-permute-start(f32[8,3968]{1,0:T(8,128)S(1)} %get-tuple-element.70), channel_id=1, source_target_pairs={{0,3},{1,2},{2,1},{3,0},{4,7},{5,6},{6,5},{7,4},{8,11},{9,10},{10,... | collective-permute-start | bytes 380936 | tf_op jit(solution)/shard_map/ppermute | solution.py:913
  99.2 5.1 %collective-permute-start.18 = (f32[48,256]{1,0:T(8,128)S(1)}, f32[48,256]{1,0:T(8,128)S(1)}, u32[]{:S(2)}, u32[]{:S(2)}) collective-permute-start(f32[48,256]{1,0:T(8,128)S(1)} %get-tuple-element.73), channel_id=1, source_target_pairs={{0,24},{4,28},{8,16},{12,20},{16,8},{20,12},{24,0},{28,4},{1,25},{... | collective-permute-start | bytes 147464 | tf_op jit(solution)/shard_map/ppermute | solution.py:1024
  100.6 4.8 %collective-permute-start.19 = (f32[48,256]{1,0:T(8,128)S(1)}, f32[48,256]{1,0:T(8,128)S(1)}, u32[]{:S(2)}, u32[]{:S(2)}) collective-permute-start(f32[48,256]{1,0:T(8,128)S(1)} %get-tuple-element.74), channel_id=1, source_target_pairs={{0,28},{4,8},{8,4},{12,16},{16,12},{20,24},{24,20},{28,0},{1,29},{... | collective-permute-start | bytes 147464 | tf_op jit(solution)/shard_map/ppermute | solution.py:1024
  101.1 4.5 %collective-permute-start.20 = (f32[48,256]{1,0:T(8,128)S(1)}, f32[48,256]{1,0:T(8,128)S(1)}, u32[]{:S(2)}, u32[]{:S(2)}) collective-permute-start(f32[48,256]{1,0:T(8,128)S(1)} %get-tuple-element.75), channel_id=1, source_target_pairs={{0,8},{4,12},{8,0},{12,4},{16,24},{20,28},{24,16},{28,20},{1,9},{5... | collective-permute-start | bytes 147464 | tf_op jit(solution)/shard_map/ppermute | solution.py:1024
  101.7 3.9 %collective-permute-start.21 = (f32[48,256]{1,0:T(8,128)S(1)}, f32[48,256]{1,0:T(8,128)S(1)}, u32[]{:S(2)}, u32[]{:S(2)}) collective-permute-start(f32[48,256]{1,0:T(8,128)S(1)} %get-tuple-element.76), channel_id=1, source_target_pairs={{0,4},{4,0},{8,12},{12,8},{16,20},{20,16},{24,28},{28,24},{1,5},{5... | collective-permute-start | bytes 147464 | tf_op jit(solution)/shard_map/ppermute | solution.py:1024

commit v4 on v3

--- a/solution.py
+++ b/solution.py
@@ -465,10 +465,12 @@
 
     for chunk, plan in enumerate(plans):
         groups = range(state.shape[1] // GROUP)
-        pl.when(target == chunk)(functools.partial(make_buffer, plan, groups, state, xi, bands, put))
-
-
-def rest_kernel(plans, state, xi, bands, out0, out2, out3, extra3, staged):
+        pl.when(target == chunk)(
+            functools.partial(make_buffer, plan[:BASE_TILES], groups, state, xi, bands, put)
+        )
+
+
+def rest_kernel(plans, state, xi, bands, out0, out2, out3, extra1, extra2, extra3, staged):
     me = lax.axis_index("plane")
     for chunk, plan in enumerate(plans):
 
@@ -478,24 +480,29 @@
         make_buffer(plan, range(state.shape[1] // GROUP), state, xi, bands, put)
     base, last = pl.ds(0, BASE_TILES * LANES), pl.ds(BASE_TILES * LANES, LANES)
     out0[...] = staged[me ^ PARTNERS[0]]
-    out2[...] = staged[me ^ PARTNERS[2]]
+    out2[...] = staged[me ^ PARTNERS[2], :, base]
     out3[...] = staged[me ^ PARTNERS[3], :, base]
-    extra3[...] = staged[me ^ PARTNERS[3], :, last]
+    for k, extra in ((1, extra1), (2, extra2), (3, extra3)):
+        extra[...] = staged[me ^ PARTNERS[k], :, last]
 
 
 def first_kernel(plans, adjoint, far_bands, state, xi, out, taken, sems, bands):
     comps, local = taken.shape[0], taken.shape[3]
 
-    def copy(c):
-        return pltpu.make_async_copy(adjoint.at[c], taken.at[c], sems.at[c])
+    def copies(c):
+        for n in range(3):
+            part = pl.ds(3 * n, 3)
+            yield pltpu.make_async_copy(adjoint.at[c, part], taken.at[c, part], sems.at[3 * c + n])
 
     for c in range(comps):
-        copy(c).start()
-    fetch = pltpu.make_async_copy(far_bands, bands, sems.at[comps])
+        for copy in copies(c):
+            copy.start()
+    fetch = pltpu.make_async_copy(far_bands, bands, sems.at[3 * comps])
     fetch.start()
 
     for c in range(comps):
-        copy(c).wait()
+        for copy in copies(c):
+            copy.wait()
         rows = pl.ds(c * local, local)
         for i in range(NODES):
             for t in range(SLAB_TILES):
@@ -512,7 +519,7 @@
     return jnp.concatenate([wide, wide], axis=0)
 
 
-def flow_kernel(points, flow, metric, out0, out1, flat):
+def flow_kernel(points, step_index, flow, metric, out, flat):
     me = lax.axis_index("plane")
     lanes, subs = lane_ids(8), lax.broadcasted_iota(jnp.int32, (8, LANES), 0)
     shift = lax.rem(LANES - lax.rem(me * points, LANES), LANES)
@@ -526,30 +533,28 @@
     last = CHUNK_TILES - 1
 
     for f in range(2):
-        for s in range(STEPS):
-            flat[f, s] = flow[f, s].reshape(flat.shape[2:])
-
-    for s, out in enumerate((out0, out1)):
-        for half in range(2):
-            moved = (lanes + 64 * half + 8 * subs) & (LANES - 1)
-            kept = lanes < LANES - 64 * half - 8 * subs
-
-            def some_rows(h, _, s=s, half=half, out=out, moved=moved, kept=kept):
-                rows = pl.ds(pl.multiple_of(16 * h + 8 * half, 8), 8)
-
-                def field(f):
-                    spun = []
-                    for k in range(CHUNK_TILES):
-                        start = per_sixteen * h + 40 * half + k
-                        spun.append(pick(flat[f, s, pl.ds(start, 8, stride=5), :], moved))
-                    return [jnp.where(kept, spun[k], spun[k + 1]) for k in range(last)] + [spun[last]]
-
-                for t, (one, two) in enumerate(zip(field(0), field(1))):
-                    out[0, rows, pl.ds(t * LANES, LANES)] = one * first_first + two * first_second
-                    out[1, rows, pl.ds(t * LANES, LANES)] = one * second_first + two * second_second
-                return 0
-
-            lax.fori_loop(0, MODES // 16, some_rows, 0)
+        flat[f] = flow[f, step_index].reshape(flat.shape[1:])
+
+    for half in range(2):
+        moved = (lanes + 64 * half + 8 * subs) & (LANES - 1)
+        kept = lanes < LANES - 64 * half - 8 * subs
+
+        def some_rows(h, _, half=half, moved=moved, kept=kept):
+            rows = pl.ds(pl.multiple_of(16 * h + 8 * half, 8), 8)
+
+            def field(f):
+                spun = []
+                for k in range(CHUNK_TILES):
+                    start = per_sixteen * h + 40 * half + k
+                    spun.append(pick(flat[f, pl.ds(start, 8, stride=5), :], moved))
+                return [jnp.where(kept, spun[k], spun[k + 1]) for k in range(last)] + [spun[last]]
+
+            for t, (one, two) in enumerate(zip(field(0), field(1))):
+                out[0, rows, pl.ds(t * LANES, LANES)] = one * first_first + two * first_second
+                out[1, rows, pl.ds(t * LANES, LANES)] = one * second_first + two * second_second
+            return 0
+
+        lax.fori_loop(0, MODES // 16, some_rows, 0)
 
 
 def tables_kernel(edges, flags, table, square):
@@ -701,15 +706,20 @@
             early[c, :, part] = product
 
 
-def advect_kernel(fields3, early, flow, to_span, to_modes, *outs):
+def advect_kernel(fields3, early, flow, to_span, to_modes, *refs):
+    *outs, stacked = refs
     me = lax.axis_index("plane")
     both, back = to_span[me], to_modes[me]
     lanes = lane_ids(GROUP)
     local = MODES // len(outs)
+    for part in LANE_PARTS:
+        for c, product in products((fields3,), flow, both, part):
+            high, low = halves(product + early[c, :, part])
+            stacked[c, :, part] = jnp.concatenate([high, low, high], axis=0)
     tails = [None] * len(outs)
-    for n, part in enumerate(LANE_PARTS):
-        for c, product in products((fields3,), flow, both, part):
-            result = span_dot(back, product + early[c, :, part])
+    for c in range(stacked.shape[0]):
+        for n, part in enumerate(LANE_PARTS):
+            result = jnp.dot(back, stacked[c, :, part], preferred_element_type=jnp.float32)
             for k, out in enumerate(outs):
                 for half in range(local // GROUP):
                     g = c * (local // GROUP) + half
@@ -735,7 +745,7 @@
     return (((me + start) ^ step) - start) % size
 
 
-def update_kernel(plans, in0, in1, in2, in3, local_sum, table, updated, own, out0, out1, out2, out3, chunks, traces):
+def update_kernel(plans, in0, in1, in2, in3, local_sum, table, updated, traces, out0, out1, out2, out3, chunks):
     me = lax.axis_index("plane")
     rows_total = local_sum.shape[1]
     last = NODES - 1
@@ -753,7 +763,7 @@
     def wide(row):
         return jnp.broadcast_to(table[pl.ds(row, 1), :], (8, LANES))
 
-    turned_round, partner = wide(15) == 1, wide(16)
+    turned_round = wide(15) == 1
     slot_edges = [wide(o) for o in blocks]
     groups = range(rows_total // GROUP)
     for g in groups:
@@ -786,8 +796,15 @@
                     value = pick(traces[k, rows, :], slot_edge)
                     total = value if total is None else jnp.where(lanes >= 24 * (k - 5 * t), value, total)
                 out[rows, pl.ds(t * LANES, LANES)] = total
+
+
+def own_kernel(table, traces, own):
+    partner = jnp.broadcast_to(table[16:17, :], (GROUP, LANES))
+    present = jnp.broadcast_to(table[12:13, :], (GROUP, LANES)) > 0
+    for g in range(traces.shape[1] // GROUP):
+        rows = group_rows(g)
         for k in range(NODES):
-            own[k, rows, :] = pick(traces[k, rows, :], partner)
+            own[k, rows, :] = jnp.where(present, pick(traces[k, rows, :], partner), 0.0)
 
 
 def pick(value, index):
@@ -805,7 +822,6 @@
 
     share = wide(17).astype(jnp.float32)
     quarter = lanes // 32
-    own_has = wide(12) > 0
     has = [wide(10 + o) > 0 for o in blocks]
     slots = [wide(5 + o) for o in blocks]
 
@@ -839,7 +855,7 @@
     for g in groups:
         rows = group_rows(g)
         for k in range(NODES):
-            total = jnp.where(own_has, own[k, rows, :], 0.0)
+            total = own[k, rows, :]
             for slot, there, source in zip(slots, has, came):
                 value = pick(tile_at(source, (), rows, k // 5), slot + 24 * (k % 5))
                 total = jnp.where(there, value, total)
@@ -934,25 +950,26 @@
     buffer, base, extra = (f32(rows_total, tiles * LANES) for tiles in (SEND_TILES, BASE_TILES, 1))
     row_copies = [
         pltpu.VMEM((comps, nodes, nodes, local, elements), jnp.float32),
-        pltpu.SemaphoreType.DMA((nodes,)),
+        pltpu.SemaphoreType.DMA((nodes + 1,)),
     ]
     edge_scratch = pltpu.VMEM((nodes, rows_total, LANES), jnp.float32)
 
     def forward(state, xi, first):
-        own, second, third, last_tile = kernel_call(
+        own, second, third, *extras = kernel_call(
             functools.partial(rest_kernel, plans),
-            [buffer, buffer, base, extra],
+            [buffer, base, base, extra, extra, extra],
             [pltpu.VMEM((planes, *buffer.shape), jnp.float32)],
             10**6,
             2 * 10**6,
         )(state, xi, slab_bands)
         came = swapped([own, first, second, third])
-        return [(part,) for part in came[:-1]] + [(came[-1], swap(last_tile, PARTNERS[-1], middle))]
+        late = [swap(part, step, middle) for part, step in zip(extras, PARTNERS[1:])]
+        return [(own,), *zip(came[1:], late)]
 
     in_rows = pltpu.with_memory_space_constraint(adjoint.transpose(0, 2, 3, 1, 4), pltpu.HBM)
     state, *prepared = kernel_call(
         functools.partial(first_kernel, plans),
-        [f32(*state_shape), f32(*state_shape), buffer],
+        [f32(*state_shape), f32(*state_shape), base],
         row_copies + [pltpu.VMEM(slab_bands.shape, jnp.float32)],
         4 * 10**6,
         4 * 10**6,
@@ -961,19 +978,6 @@
     incoming = forward(state, *prepared)
     whole, two_fields = (12, MODES, CHUNK_TILES * LANES), (2, MODES, CHUNK_TILES * LANES)
     lay = base_flow.transpose(1, 0, 2)
-    flows = kernel_call(
-        functools.partial(flow_kernel, points),
-        [f32(*whole)] * STEPS,
-        [pltpu.VMEM((2, STEPS, lay.shape[2] // LANES, LANES), jnp.float32)],
-        4 * 10**6,
-        9 * 10**6,
-        grid=(6,),
-        in_specs=[
-            pl.BlockSpec((2, *lay.shape[1:]), lambda pair: (pair, 0, 0)),
-            pl.BlockSpec(metric.shape, lambda pair: (0, 0)),
-        ],
-        out_specs=[pl.BlockSpec(two_fields, lambda pair: (pair, 0, 0))] * STEPS,
-    )(lay, metric)
     table = kernel_call(
         tables_kernel,
         jax.ShapeDtypeStruct((24, LANES), jnp.int32),
@@ -983,6 +987,19 @@
     )(edge_list.transpose(1, 0, 2), flips.transpose(1, 0, 2))
 
     for step_index in range(STEPS):
+        flow = kernel_call(
+            functools.partial(flow_kernel, points, step_index),
+            f32(*whole),
+            [pltpu.VMEM((2, lay.shape[2] // LANES, LANES), jnp.float32)],
+            2 * 10**6,
+            7 * 10**6,
+            grid=(6,),
+            in_specs=[
+                pl.BlockSpec((2, *lay.shape[1:]), lambda pair: (pair, 0, 0)),
+                pl.BlockSpec(metric.shape, lambda pair: (0, 0)),
+            ],
+            out_specs=pl.BlockSpec(two_fields, lambda pair: (pair, 0, 0)),
+        )(lay, metric)
         fields = [None] * planes
         before = []
         for k in FIELDS_ORDER:
@@ -998,14 +1015,14 @@
             before = [fields[k]] if k > 0 else []
         early = kernel_call(
             early_kernel, f32(comps, MODES, CHUNK_TILES * LANES), [], 50 * 10**6, 5 * 10**6
-        )(*fields[:-1], flows[step_index], to_span)
+        )(*fields[:-1], flow, to_span)
         returning = kernel_call(
             advect_kernel,
             [f32(GROUP, BACK_TILES * LANES)] * planes,
-            [],
+            [pltpu.VMEM((comps, 3 * MODES, CHUNK_TILES * LANES), jnp.bfloat16)],
             30 * 10**6,
             5 * 10**6,
-        )(fields[-1], early, flows[step_index], to_span_last, to_modes)
+        )(fields[-1], early, flow, to_span_last, to_modes)
         local_sum = kernel_call(
             diffuse_kernel,
             f32(*state_shape),
@@ -1013,10 +1030,10 @@
             12 * 10**6,
             2 * 10**6,
         )(state, metric, slab_bands)
-        updated, own, *leaving = kernel_call(
+        updated, seen, *leaving = kernel_call(
             functools.partial(update_kernel, back_plans),
             [f32(*state_shape), f32(nodes, rows_total, LANES)] + [f32(rows_total, 2 * LANES)] * 4,
-            [pltpu.VMEM((planes, GROUP, BACK_TILES * LANES), jnp.float32), edge_scratch],
+            [pltpu.VMEM((planes, GROUP, BACK_TILES * LANES), jnp.float32)],
             2 * 10**6,
             3 * 10**6,
         )(*swapped(returning), local_sum, table)
@@ -1026,10 +1043,11 @@
             )
             for matching, buffer in enumerate(leaving)
         ]
+        own = kernel_call(own_kernel, f32(nodes, rows_total, LANES), [], 10**5, 10**6)(table, seen)
         if step_index + 1 < STEPS:
             state, *prepared = kernel_call(
                 functools.partial(next_kernel, plans),
-                [f32(*state_shape), f32(*state_shape), buffer],
+                [f32(*state_shape), f32(*state_shape), base],
                 [edge_scratch],
                 6 * 10**6,
                 4 * 10**6,

time: 108 us -> 113 us (1.046)
  starting transfers between devices: 35.4 us -> 44.8 us
  waiting for transfers between devices: 37.2 us -> 32.3 us
    ppermute x14 -> x18, starting transfers between devices: 27 us -> 36.7 us  [swap(): lax.ppermute(buffer, 'plane', sorted(((i ^ step, i) for i in wanted)))]
    ppermute x14 -> x18, waiting for transfers between devices: 31.4 us -> 26.1 us  [swap(): lax.ppermute(buffer, 'plane', sorted(((i ^ step, i) for i in wanted)))]
    pallas_call x5 -> x8, Pallas kernels: 15.8 us -> 16.2 us  [the longest x2 11.9 us: packed_shards(): kernel_call(functools.partial(flow_kernel, points, step_index), f32(*whol...]
  transfers between devices with their start and end apart: 22 -> 26, of which waited for: 13 -> 11; matrix products, arithmetic and copies ran while one was open for 0% -> 0% of each run, Pallas kernels for 21% -> 20%
where the time goes in v4:
time: 113 us
  starting transfers between devices  44.8 us (40%)
  Pallas kernels  34.2 us (30%)
  waiting for transfers between devices  32.3 us (29%)
    ppermute x18, starting transfers between devices, swap(): lax.ppermute(buffer, 'plane', sorted(((i ^ step, i) for i in wanted)))  36.7 us
    ppermute x18, waiting for transfers between devices, swap(): lax.ppermute(buffer, 'plane', sorted(((i ^ step, i) for i in wanted)))  26.1 us
    pallas_call x2, Pallas kernels, packed_shards(): kernel_call(functools.partial(flow_kernel, points, step_index), f32(*whol...  11.9 us
    ppermute x8, starting transfers between devices, packed_shards(): lax.ppermute(buffer, 'dom', [(i, trace_partner(i, matching, partitions))...  8.07 us
    ppermute x8, waiting for transfers between devices, packed_shards(): lax.ppermute(buffer, 'dom', [(i, trace_partner(i, matching, partitions))...  6.15 us
    pallas_call x2, Pallas kernels, packed_shards(): kernel_call(diffuse_kernel, f32(*state_shape), [pltpu.VMEM((nodes, GROUP,...  5.48 us
    pallas_call x2, Pallas kernels, packed_shards(): kernel_call(functools.partial(update_kernel, back_plans), [f32(*state_sha...  3.12 us
    pallas_call x2, Pallas kernels, forward(): kernel_call(functools.partial(rest_kernel, plans), [buffer, base, base, e...  2.33 us
  transfers between devices with their start and end apart: 26, of which 11 were waited for; matrix products, arithmetic and copies ran while one was open for 0% of the time, Pallas kernels for 20%

profile of v4, /device:TPU:0, one launch (start us, length us, event | category | flops | bytes accessed | tf_op | source)
XLA Modules:
  0.0 113.0 jit_solution(1254383000738767459)
XLA Ops:
  0.0 2.2 %shard_map.101 = (f32[9,48,384]{2,1,0:T(8,128)S(1)}, f32[9,48,384]{2,1,0:T(8,128)S(1)}, f32[48,1408]{1,0:T(8,128)S(1)}) custom-call(f32[3,9,9,16,32]{4,3,2,1,0:T(8,128)} %bitcast.9, f32[24,384]{1,0:T(8,128)} %constant.10.clone.far_bands.bands), custom_call_target="tpu_custom_call" | custom-call | flops 4000000 | bytes 4000000 | tf_op jit(solution)/shard_map/pallas_call | solution.py:970
  2.2 4.2 %collective-permute-start.4 = (f32[48,1408]{1,0:T(8,128)S(1)}, f32[48,1408]{1,0:T(8,128)S(1)}, u32[]{:S(2)}, u32[]{:S(2)}) collective-permute-start(f32[48,1408]{1,0:T(8,128)S(1)} %get-tuple-element.49), channel_id=1, source_target_pairs={{0,2},{1,3},{2,0},{3,1},{4,6},{5,7},{6,4},{7,5},{8,10},{9,11},{10,... | collective-permute-start | bytes 811016 | tf_op jit(solution)/shard_map/ppermute | solution.py:929
  8.4 1.6 %collective-permute-start.2 = (f32[48,1408]{1,0:T(8,128)S(1)}, f32[48,1408]{1,0:T(8,128)S(1)}, u32[]{:S(2)}, u32[]{:S(2)}) collective-permute-start(f32[48,1408]{1,0:T(8,128)S(1)} %get-tuple-element.47), channel_id=1, source_target_pairs={{0,1},{1,0},{2,3},{3,2},{4,5},{5,4},{6,7},{7,6},{8,9},{9,8},{10,11... | collective-permute-start | bytes 811016 | tf_op jit(solution)/shard_map/ppermute | solution.py:929
  10.0 3.8 %collective-permute-start.5 = (f32[48,128]{1,0:T(8,128)S(1)}, f32[48,128]{1,0:T(8,128)S(1)}, u32[]{:S(2)}, u32[]{:S(2)}) collective-permute-start(f32[48,128]{1,0:T(8,128)S(1)} %get-tuple-element.50), channel_id=1, source_target_pairs={{0,2},{3,1},{4,6},{7,5},{8,10},{11,9},{12,14},{15,13},{16,18},{19,... | collective-permute-start | bytes 73736 | tf_op jit(solution)/shard_map/ppermute | solution.py:929
  13.8 1.3 %collective-permute-start.3 = (f32[48,128]{1,0:T(8,128)S(1)}, f32[48,128]{1,0:T(8,128)S(1)}, u32[]{:S(2)}, u32[]{:S(2)}) collective-permute-start(f32[48,128]{1,0:T(8,128)S(1)} %get-tuple-element.48), channel_id=1, source_target_pairs={{0,1},{3,2},{4,5},{7,6},{8,9},{11,10},{12,13},{15,14},{16,17},{19,... | collective-permute-start | bytes 73736 | tf_op jit(solution)/shard_map/ppermute | solution.py:929
  15.1 9.5 %collective-permute-done.5.refs_0_ = f32[48,128]{1,0:T(8,128)S(1)} collective-permute-done((f32[48,128]{1,0:T(8,128)S(1)}, f32[48,128]{1,0:T(8,128)S(1)}, u32[]{:S(2)}, u32[]{:S(2)}) %collective-permute-start.5) | collective-permute-done | bytes 24608 | tf_op jit(solution)/shard_map/ppermute | solution.py:929
  25.6 5.9 %shard_map.107.flow = f32[12,64,768]{2,1,0:T(8,128)S(1)} custom-call(f32[12,2,41472]{2,1,0:T(2,128)S(1)} %bitcast.5, f32[4,32]{1,0:T(4,128)S(1)} %copy-done.7), custom_call_target="tpu_custom_call" | custom-call | flops 2000000 | bytes 7000000 | tf_op jit(solution)/shard_map/pallas_call | solution.py:990
  34.4 5.3 %collective-permute-start.6 = (f32[8,3968]{1,0:T(8,128)S(1)}, f32[8,3968]{1,0:T(8,128)S(1)}, u32[]{:S(2)}, u32[]{:S(2)}) collective-permute-start(f32[8,3968]{1,0:T(8,128)S(1)} %get-tuple-element.53), channel_id=1, source_target_pairs={{0,2},{1,3},{2,0},{3,1},{4,6},{5,7},{6,4},{7,5},{8,10},{9,11},{10,... | collective-permute-start | bytes 380936 | tf_op jit(solution)/shard_map/ppermute | solution.py:929
  39.8 2.3 %collective-permute-start.8 = (f32[8,3968]{1,0:T(8,128)S(1)}, f32[8,3968]{1,0:T(8,128)S(1)}, u32[]{:S(2)}, u32[]{:S(2)}) collective-permute-start(f32[8,3968]{1,0:T(8,128)S(1)} %get-tuple-element.55), channel_id=1, source_target_pairs={{0,3},{1,2},{2,1},{3,0},{4,7},{5,6},{6,5},{7,4},{8,11},{9,10},{10,... | collective-permute-start | bytes 380936 | tf_op jit(solution)/shard_map/ppermute | solution.py:929
  42.4 2.7 %shard_map.110.local_sum = f32[9,48,384]{2,1,0:T(8,128)S(1)} custom-call(f32[9,48,384]{2,1,0:T(8,128)S(1)} %get-tuple-element.43.state, f32[4,32]{1,0:T(4,128)S(1)} %copy-done.7, f32[24,384]{1,0:T(8,128)S(1)} %copy-done.3), custom_call_target="tpu_custom_call" | custom-call | flops 12000000 | bytes 2000000 | tf_op jit(solution)/shard_map/pallas_call | solution.py:1026
  45.1 2.5 %collective-permute-done.6.in1 = f32[8,3968]{1,0:T(8,128)S(1)} collective-permute-done((f32[8,3968]{1,0:T(8,128)S(1)}, f32[8,3968]{1,0:T(8,128)S(1)}, u32[]{:S(2)}, u32[]{:S(2)}) %collective-permute-start.6) | collective-permute-done | bytes 127008 | tf_op jit(solution)/shard_map/ppermute | solution.py:929
  47.6 1.5 %collective-permute-done.8.in3 = f32[8,3968]{1,0:T(8,128)S(1)} collective-permute-done((f32[8,3968]{1,0:T(8,128)S(1)}, f32[8,3968]{1,0:T(8,128)S(1)}, u32[]{:S(2)}, u32[]{:S(2)}) %collective-permute-start.8) | collective-permute-done | bytes 127008 | tf_op jit(solution)/shard_map/ppermute | solution.py:929
  49.1 1.6 %shard_map.111 = (f32[9,48,384]{2,1,0:T(8,128)S(1)}, f32[9,48,128]{2,1,0:T(8,128)S(1)}, f32[48,256]{1,0:T(8,128)S(1)}, f32[48,256]{1,0:T(8,128)S(1)}, f32[48,256]{1,0:T(8,128)S(1)}, /*index=5*/f32[48,256]{1,0:T(8,128)S(1)}) custom-call(f32[8,3968]{1,0:T(8,128)S(1)} %get-tuple-element.52.in0, f32[8,3968]{1,0:T(8,128)S(1)} %collective-permute-done.6.in1, ...), custom_call_target="tpu_custom_call" | custom-call | flops 2000000 | bytes 3000000 | tf_op jit(solution)/shard_map/pallas_call | solution.py:1033
  50.8 1.6 %collective-permute-start.11 = (f32[48,256]{1,0:T(8,128)S(1)}, f32[48,256]{1,0:T(8,128)S(1)}, u32[]{:S(2)}, u32[]{:S(2)}) collective-permute-start(f32[48,256]{1,0:T(8,128)S(1)} %get-tuple-element.60), channel_id=1, source_target_pairs={{0,8},{4,12},{8,0},{12,4},{16,24},{20,28},{24,16},{28,20},{1,9},{5... | collective-permute-start | bytes 147464 | tf_op jit(solution)/shard_map/ppermute | solution.py:1041
  52.3 1.2 %collective-permute-start.12 = (f32[48,256]{1,0:T(8,128)S(1)}, f32[48,256]{1,0:T(8,128)S(1)}, u32[]{:S(2)}, u32[]{:S(2)}) collective-permute-start(f32[48,256]{1,0:T(8,128)S(1)} %get-tuple-element.61), channel_id=1, source_target_pairs={{0,4},{4,0},{8,12},{12,8},{16,20},{20,16},{24,28},{28,24},{1,5},{5... | collective-permute-start | bytes 147464 | tf_op jit(solution)/shard_map/ppermute | solution.py:1041
  53.6 1.5 %collective-permute-start.9 = (f32[48,256]{1,0:T(8,128)S(1)}, f32[48,256]{1,0:T(8,128)S(1)}, u32[]{:S(2)}, u32[]{:S(2)}) collective-permute-start(f32[48,256]{1,0:T(8,128)S(1)} %get-tuple-element.58), channel_id=1, source_target_pairs={{0,24},{4,28},{8,16},{12,20},{16,8},{20,12},{24,0},{28,4},{1,25},{... | collective-permute-start | bytes 147464 | tf_op jit(solution)/shard_map/ppermute | solution.py:1041
  55.6 3.0 %collective-permute-done.9.r0 = f32[48,256]{1,0:T(8,128)S(1)} collective-permute-done((f32[48,256]{1,0:T(8,128)S(1)}, f32[48,256]{1,0:T(8,128)S(1)}, u32[]{:S(2)}, u32[]{:S(2)}) %collective-permute-start.9) | collective-permute-done | bytes 49184 | tf_op jit(solution)/shard_map/ppermute | solution.py:1041
  59.7 2.1 %collective-permute-start.17 = (f32[48,1408]{1,0:T(8,128)S(1)}, f32[48,1408]{1,0:T(8,128)S(1)}, u32[]{:S(2)}, u32[]{:S(2)}) collective-permute-start(f32[48,1408]{1,0:T(8,128)S(1)} %get-tuple-element.68), channel_id=1, source_target_pairs={{0,2},{1,3},{2,0},{3,1},{4,6},{5,7},{6,4},{7,5},{8,10},{9,11},{10,... | collective-permute-start | bytes 811016 | tf_op jit(solution)/shard_map/ppermute | solution.py:929
  63.2 2.3 %collective-permute-start.13 = (f32[48,1408]{1,0:T(8,128)S(1)}, f32[48,1408]{1,0:T(8,128)S(1)}, u32[]{:S(2)}, u32[]{:S(2)}) collective-permute-start(f32[48,1408]{1,0:T(8,128)S(1)} %get-tuple-element.64), channel_id=1, source_target_pairs={{0,3},{1,2},{2,1},{3,0},{4,7},{5,6},{6,5},{7,4},{8,11},{9,10},{10,... | collective-permute-start | bytes 811016 | tf_op jit(solution)/shard_map/ppermute | solution.py:929
  65.5 3.0 %collective-permute-start.18 = (f32[48,128]{1,0:T(8,128)S(1)}, f32[48,128]{1,0:T(8,128)S(1)}, u32[]{:S(2)}, u32[]{:S(2)}) collective-permute-start(f32[48,128]{1,0:T(8,128)S(1)} %get-tuple-element.69), channel_id=1, source_target_pairs={{0,2},{3,1},{4,6},{7,5},{8,10},{11,9},{12,14},{15,13},{16,18},{19,... | collective-permute-start | bytes 73736 | tf_op jit(solution)/shard_map/ppermute | solution.py:929
  68.5 1.3 %collective-permute-start.16 = (f32[48,128]{1,0:T(8,128)S(1)}, f32[48,128]{1,0:T(8,128)S(1)}, u32[]{:S(2)}, u32[]{:S(2)}) collective-permute-start(f32[48,128]{1,0:T(8,128)S(1)} %get-tuple-element.67), channel_id=1, source_target_pairs={{0,1},{3,2},{4,5},{7,6},{8,9},{11,10},{12,13},{15,14},{16,17},{19,... | collective-permute-start | bytes 73736 | tf_op jit(solution)/shard_map/ppermute | solution.py:929
  69.8 9.3 %collective-permute-done.18.refs_0_ = f32[48,128]{1,0:T(8,128)S(1)} collective-permute-done((f32[48,128]{1,0:T(8,128)S(1)}, f32[48,128]{1,0:T(8,128)S(1)}, u32[]{:S(2)}, u32[]{:S(2)}) %collective-permute-start.18) | collective-permute-done | bytes 24608 | tf_op jit(solution)/shard_map/ppermute | solution.py:929
  79.9 5.9 %shard_map.119.flow = f32[12,64,768]{2,1,0:T(8,128)S(1)} custom-call(f32[12,2,41472]{2,1,0:T(2,128)S(1)} %bitcast.6, f32[4,32]{1,0:T(4,128)S(1)} %copy-done.7), custom_call_target="tpu_custom_call" | custom-call | flops 2000000 | bytes 7000000 | tf_op jit(solution)/shard_map/pallas_call | solution.py:990
  88.6 6.2 %collective-permute-start.19 = (f32[8,3968]{1,0:T(8,128)S(1)}, f32[8,3968]{1,0:T(8,128)S(1)}, u32[]{:S(2)}, u32[]{:S(2)}) collective-permute-start(f32[8,3968]{1,0:T(8,128)S(1)} %get-tuple-element.72), channel_id=1, source_target_pairs={{0,2},{1,3},{2,0},{3,1},{4,6},{5,7},{6,4},{7,5},{8,10},{9,11},{10,... | collective-permute-start | bytes 380936 | tf_op jit(solution)/shard_map/ppermute | solution.py:929
  94.8 1.6 %collective-permute-start.21 = (f32[8,3968]{1,0:T(8,128)S(1)}, f32[8,3968]{1,0:T(8,128)S(1)}, u32[]{:S(2)}, u32[]{:S(2)}) collective-permute-start(f32[8,3968]{1,0:T(8,128)S(1)} %get-tuple-element.74), channel_id=1, source_target_pairs={{0,3},{1,2},{2,1},{3,0},{4,7},{5,6},{6,5},{7,4},{8,11},{9,10},{10,... | collective-permute-start | bytes 380936 | tf_op jit(solution)/shard_map/ppermute | solution.py:929
  96.4 2.7 %shard_map.122.local_sum = f32[9,48,384]{2,1,0:T(8,128)S(1)} custom-call(f32[9,48,384]{2,1,0:T(8,128)S(1)} %get-tuple-element.62.state, f32[4,32]{1,0:T(4,128)S(1)} %copy-done.7, f32[24,384]{1,0:T(8,128)S(1)} %copy-done.3), custom_call_target="tpu_custom_call" | custom-call | flops 12000000 | bytes 2000000 | tf_op jit(solution)/shard_map/pallas_call | solution.py:1026
  99.1 1.8 %collective-permute-done.19.in1 = f32[8,3968]{1,0:T(8,128)S(1)} collective-permute-done((f32[8,3968]{1,0:T(8,128)S(1)}, f32[8,3968]{1,0:T(8,128)S(1)}, u32[]{:S(2)}, u32[]{:S(2)}) %collective-permute-start.19) | collective-permute-done | bytes 127008 | tf_op jit(solution)/shard_map/ppermute | solution.py:929
  100.9 1.4 %collective-permute-done.21.in3 = f32[8,3968]{1,0:T(8,128)S(1)} collective-permute-done((f32[8,3968]{1,0:T(8,128)S(1)}, f32[8,3968]{1,0:T(8,128)S(1)}, u32[]{:S(2)}, u32[]{:S(2)}) %collective-permute-start.21) | collective-permute-done | bytes 127008 | tf_op jit(solution)/shard_map/ppermute | solution.py:929
  102.4 1.6 %shard_map.123 = (f32[9,48,384]{2,1,0:T(8,128)S(1)}, f32[9,48,128]{2,1,0:T(8,128)S(1)}, f32[48,256]{1,0:T(8,128)S(1)}, f32[48,256]{1,0:T(8,128)S(1)}, f32[48,256]{1,0:T(8,128)S(1)}, /*index=5*/f32[48,256]{1,0:T(8,128)S(1)}) custom-call(f32[8,3968]{1,0:T(8,128)S(1)} %get-tuple-element.71.in0, f32[8,3968]{1,0:T(8,128)S(1)} %collective-permute-done.19.in1, ...), custom_call_target="tpu_custom_call" | custom-call | flops 2000000 | bytes 3000000 | tf_op jit(solution)/shard_map/pallas_call | solution.py:1033
  103.9 1.6 %collective-permute-start.22 = (f32[48,256]{1,0:T(8,128)S(1)}, f32[48,256]{1,0:T(8,128)S(1)}, u32[]{:S(2)}, u32[]{:S(2)}) collective-permute-start(f32[48,256]{1,0:T(8,128)S(1)} %get-tuple-element.77), channel_id=1, source_target_pairs={{0,24},{4,28},{8,16},{12,20},{16,8},{20,12},{24,0},{28,4},{1,25},{... | collective-permute-start | bytes 147464 | tf_op jit(solution)/shard_map/ppermute | solution.py:1041
  109.0 1.4 %collective-permute-done.23.r1 = f32[48,256]{1,0:T(8,128)S(1)} collective-permute-done((f32[48,256]{1,0:T(8,128)S(1)}, f32[48,256]{1,0:T(8,128)S(1)}, u32[]{:S(2)}, u32[]{:S(2)}) %collective-permute-start.23) | collective-permute-done | bytes 49184 | tf_op jit(solution)/shard_map/ppermute | solution.py:1041
  110.6 2.2 %shard_map.125 = f32[3,9,9,16,32]{4,3,2,1,0:T(8,128)} custom-call(s32[24,128]{1,0:T(8,128)S(1)} %shard_map.100.table, f32[9,48,384]{2,1,0:T(8,128)S(1)} %get-tuple-element.75.updated, f32[9,48,128]{2,1,0:T(8,128)S(1)} %shard_map.124.own, f32[48,256]{1,0:T(8,128)S(1)} %collective-permute-done.22.r0, f32[48,256]{1,0:T(8,128)S(1)} %collective-permute-done.23.r1, ...), custom_call_target="tpu_custom_call" | custom-call | flops 2000000 | bytes 3000000 | tf_op jit(solution)/shard_map/pallas_call | solution.py:1057
  (66 shorter events, 16.2 us)
Async XLA Ops:
  0.0 25.3 %copy-start = (f32[4,24,768]{2,1,0:T(8,128)S(1)}, f32[4,24,768]{2,1,0:T(8,128)}, u32[]{:S(2)}) copy-start(f32[4,24,768]{2,1,0:T(8,128)} %constant.11.clone.refs_1_.refs_0_) | copy-start | bytes 884740
  0.0 25.6 %copy-start.1 = (f32[2,12,41472]{2,0,1:T(2,128)S(1)}, f32[2,12,41472]{2,0,1:T(2,128)}, u32[]{:S(2)}) copy-start(f32[2,12,41472]{2,0,1:T(2,128)} %param.12) | copy-start | bytes 11943940
  2.2 29.3 %collective-permute-start.4 = (f32[48,1408]{1,0:T(8,128)S(1)}, f32[48,1408]{1,0:T(8,128)S(1)}, u32[]{:S(2)}, u32[]{:S(2)}) collective-permute-start(f32[48,1408]{1,0:T(8,128)S(1)} %get-tuple-element.49), channel_id=1, source_target_pairs={{0,2},{1,3},{2,0},{3,1},{4,6},{5,7},{6,4},{7,5},{8,10},{9,11},{10,... | collective-permute-start | bytes 811016 | tf_op jit(solution)/shard_map/ppermute | solution.py:929
  7.2 18.4 %copy-start.7 = (f32[4,32]{1,0:T(4,128)S(1)}, f32[4,32]{1,0:T(4,128)}, u32[]{:S(2)}) copy-start(f32[4,32]{1,0:T(4,128)} %metric.7) | copy-start | bytes 1540
  8.4 23.5 %collective-permute-start.2 = (f32[48,1408]{1,0:T(8,128)S(1)}, f32[48,1408]{1,0:T(8,128)S(1)}, u32[]{:S(2)}, u32[]{:S(2)}) collective-permute-start(f32[48,1408]{1,0:T(8,128)S(1)} %get-tuple-element.47), channel_id=1, source_target_pairs={{0,1},{1,0},{2,3},{3,2},{4,5},{5,4},{6,7},{7,6},{8,9},{9,8},{10,11... | collective-permute-start | bytes 811016 | tf_op jit(solution)/shard_map/ppermute | solution.py:929
  9.9 23.3 %collective-permute-start = (f32[48,1408]{1,0:T(8,128)S(1)}, f32[48,1408]{1,0:T(8,128)S(1)}, u32[]{:S(2)}, u32[]{:S(2)}) collective-permute-start(f32[48,1408]{1,0:T(8,128)S(1)} %get-tuple-element.45), channel_id=1, source_target_pairs={{0,3},{1,2},{2,1},{3,0},{4,7},{5,6},{6,5},{7,4},{8,11},{9,10},{10,... | collective-permute-start | bytes 811016 | tf_op jit(solution)/shard_map/ppermute | solution.py:929
  10.0 14.6 %collective-permute-start.5 = (f32[48,128]{1,0:T(8,128)S(1)}, f32[48,128]{1,0:T(8,128)S(1)}, u32[]{:S(2)}, u32[]{:S(2)}) collective-permute-start(f32[48,128]{1,0:T(8,128)S(1)} %get-tuple-element.50), channel_id=1, source_target_pairs={{0,2},{3,1},{4,6},{7,5},{8,10},{11,9},{12,14},{15,13},{16,18},{19,... | collective-permute-start | bytes 73736 | tf_op jit(solution)/shard_map/ppermute | solution.py:929
  13.8 18.1 %collective-permute-start.3 = (f32[48,128]{1,0:T(8,128)S(1)}, f32[48,128]{1,0:T(8,128)S(1)}, u32[]{:S(2)}, u32[]{:S(2)}) collective-permute-start(f32[48,128]{1,0:T(8,128)S(1)} %get-tuple-element.48), channel_id=1, source_target_pairs={{0,1},{3,2},{4,5},{7,6},{8,9},{11,10},{12,13},{15,14},{16,17},{19,... | collective-permute-start | bytes 73736 | tf_op jit(solution)/shard_map/ppermute | solution.py:929
  24.6 8.6 %collective-permute-start.1 = (f32[48,128]{1,0:T(8,128)S(1)}, f32[48,128]{1,0:T(8,128)S(1)}, u32[]{:S(2)}, u32[]{:S(2)}) collective-permute-start(f32[48,128]{1,0:T(8,128)S(1)} %get-tuple-element.46), channel_id=1, source_target_pairs={{1,2},{2,1},{5,6},{6,5},{9,10},{10,9},{13,14},{14,13},{17,18},{18,... | collective-permute-start | bytes 73736 | tf_op jit(solution)/shard_map/ppermute | solution.py:929
  33.2 9.0 %copy-start.8 = (s32[1,5,24]{2,0,1:T(1,128)S(1)}, s32[1,5,24]{2,0,1:T(1,128)}, u32[]{:S(2)}) copy-start(s32[1,5,24]{2,0,1:T(1,128)} %param.13) | copy-start | bytes 1444
  33.2 8.9 %copy-start.9 = (s32[1,5,24]{2,0,1:T(1,128)S(1)}, s32[1,5,24]{2,0,1:T(1,128)}, u32[]{:S(2)}) copy-start(s32[1,5,24]{2,0,1:T(1,128)} %param.14) | copy-start | bytes 1444
  33.2 9.2 %copy-start.3 = (f32[24,384]{1,0:T(8,128)S(1)}, f32[24,384]{1,0:T(8,128)}, u32[]{:S(2)}) copy-start(f32[24,384]{1,0:T(8,128)} %constant.10.clone.far_bands.bands) | copy-start | bytes 110596
  34.4 13.2 %collective-permute-start.6 = (f32[8,3968]{1,0:T(8,128)S(1)}, f32[8,3968]{1,0:T(8,128)S(1)}, u32[]{:S(2)}, u32[]{:S(2)}) collective-permute-start(f32[8,3968]{1,0:T(8,128)S(1)} %get-tuple-element.53), channel_id=1, source_target_pairs={{0,2},{1,3},{2,0},{3,1},{4,6},{5,7},{6,4},{7,5},{8,10},{9,11},{10,... | collective-permute-start | bytes 380936 | tf_op jit(solution)/shard_map/ppermute | solution.py:929
  39.8 7.8 %collective-permute-start.7 = (f32[8,3968]{1,0:T(8,128)S(1)}, f32[8,3968]{1,0:T(8,128)S(1)}, u32[]{:S(2)}, u32[]{:S(2)}) collective-permute-start(f32[8,3968]{1,0:T(8,128)S(1)} %get-tuple-element.54), channel_id=1, source_target_pairs={{0,1},{1,0},{2,3},{3,2},{4,5},{5,4},{6,7},{7,6},{8,9},{9,8},{10,11... | collective-permute-start | bytes 380936 | tf_op jit(solution)/shard_map/ppermute | solution.py:929
  39.8 9.3 %collective-permute-start.8 = (f32[8,3968]{1,0:T(8,128)S(1)}, f32[8,3968]{1,0:T(8,128)S(1)}, u32[]{:S(2)}, u32[]{:S(2)}) collective-permute-start(f32[8,3968]{1,0:T(8,128)S(1)} %get-tuple-element.55), channel_id=1, source_target_pairs={{0,3},{1,2},{2,1},{3,0},{4,7},{5,6},{6,5},{7,4},{8,11},{9,10},{10,... | collective-permute-start | bytes 380936 | tf_op jit(solution)/shard_map/ppermute | solution.py:929
  50.7 4.9 %collective-permute-start.10 = (f32[48,256]{1,0:T(8,128)S(1)}, f32[48,256]{1,0:T(8,128)S(1)}, u32[]{:S(2)}, u32[]{:S(2)}) collective-permute-start(f32[48,256]{1,0:T(8,128)S(1)} %get-tuple-element.59), channel_id=1, source_target_pairs={{0,28},{4,8},{8,4},{12,16},{16,12},{20,24},{24,20},{28,0},{1,29},{... | collective-permute-start | bytes 147464 | tf_op jit(solution)/shard_map/ppermute | solution.py:1041
  50.8 4.8 %collective-permute-start.11 = (f32[48,256]{1,0:T(8,128)S(1)}, f32[48,256]{1,0:T(8,128)S(1)}, u32[]{:S(2)}, u32[]{:S(2)}) collective-permute-start(f32[48,256]{1,0:T(8,128)S(1)} %get-tuple-element.60), channel_id=1, source_target_pairs={{0,8},{4,12},{8,0},{12,4},{16,24},{20,28},{24,16},{28,20},{1,9},{5... | collective-permute-start | bytes 147464 | tf_op jit(solution)/shard_map/ppermute | solution.py:1041
  52.3 3.3 %collective-permute-start.12 = (f32[48,256]{1,0:T(8,128)S(1)}, f32[48,256]{1,0:T(8,128)S(1)}, u32[]{:S(2)}, u32[]{:S(2)}) collective-permute-start(f32[48,256]{1,0:T(8,128)S(1)} %get-tuple-element.61), channel_id=1, source_target_pairs={{0,4},{4,0},{8,12},{12,8},{16,20},{20,16},{24,28},{28,24},{1,5},{5... | collective-permute-start | bytes 147464 | tf_op jit(solution)/shard_map/ppermute | solution.py:1041
  53.6 5.0 %collective-permute-start.9 = (f32[48,256]{1,0:T(8,128)S(1)}, f32[48,256]{1,0:T(8,128)S(1)}, u32[]{:S(2)}, u32[]{:S(2)}) collective-permute-start(f32[48,256]{1,0:T(8,128)S(1)} %get-tuple-element.58), channel_id=1, source_target_pairs={{0,24},{4,28},{8,16},{12,20},{16,8},{20,12},{24,0},{28,4},{1,25},{... | collective-permute-start | bytes 147464 | tf_op jit(solution)/shard_map/ppermute | solution.py:1041
  59.7 26.4 %collective-permute-start.17 = (f32[48,1408]{1,0:T(8,128)S(1)}, f32[48,1408]{1,0:T(8,128)S(1)}, u32[]{:S(2)}, u32[]{:S(2)}) collective-permute-start(f32[48,1408]{1,0:T(8,128)S(1)} %get-tuple-element.68), channel_id=1, source_target_pairs={{0,2},{1,3},{2,0},{3,1},{4,6},{5,7},{6,4},{7,5},{8,10},{9,11},{10,... | collective-permute-start | bytes 811016 | tf_op jit(solution)/shard_map/ppermute | solution.py:929
  63.0 23.5 %collective-permute-start.15 = (f32[48,1408]{1,0:T(8,128)S(1)}, f32[48,1408]{1,0:T(8,128)S(1)}, u32[]{:S(2)}, u32[]{:S(2)}) collective-permute-start(f32[48,1408]{1,0:T(8,128)S(1)} %get-tuple-element.66), channel_id=1, source_target_pairs={{0,1},{1,0},{2,3},{3,2},{4,5},{5,4},{6,7},{7,6},{8,9},{9,8},{10,11... | collective-permute-start | bytes 811016 | tf_op jit(solution)/shard_map/ppermute | solution.py:929
  63.2 24.3 %collective-permute-start.13 = (f32[48,1408]{1,0:T(8,128)S(1)}, f32[48,1408]{1,0:T(8,128)S(1)}, u32[]{:S(2)}, u32[]{:S(2)}) collective-permute-start(f32[48,1408]{1,0:T(8,128)S(1)} %get-tuple-element.64), channel_id=1, source_target_pairs={{0,3},{1,2},{2,1},{3,0},{4,7},{5,6},{6,5},{7,4},{8,11},{9,10},{10,... | collective-permute-start | bytes 811016 | tf_op jit(solution)/shard_map/ppermute | solution.py:929
  65.5 13.6 %collective-permute-start.18 = (f32[48,128]{1,0:T(8,128)S(1)}, f32[48,128]{1,0:T(8,128)S(1)}, u32[]{:S(2)}, u32[]{:S(2)}) collective-permute-start(f32[48,128]{1,0:T(8,128)S(1)} %get-tuple-element.69), channel_id=1, source_target_pairs={{0,2},{3,1},{4,6},{7,5},{8,10},{11,9},{12,14},{15,13},{16,18},{19,... | collective-permute-start | bytes 73736 | tf_op jit(solution)/shard_map/ppermute | solution.py:929
  68.5 18.0 %collective-permute-start.16 = (f32[48,128]{1,0:T(8,128)S(1)}, f32[48,128]{1,0:T(8,128)S(1)}, u32[]{:S(2)}, u32[]{:S(2)}) collective-permute-start(f32[48,128]{1,0:T(8,128)S(1)} %get-tuple-element.67), channel_id=1, source_target_pairs={{0,1},{3,2},{4,5},{7,6},{8,9},{11,10},{12,13},{15,14},{16,17},{19,... | collective-permute-start | bytes 73736 | tf_op jit(solution)/shard_map/ppermute | solution.py:929
  79.1 8.3 %collective-permute-start.14 = (f32[48,128]{1,0:T(8,128)S(1)}, f32[48,128]{1,0:T(8,128)S(1)}, u32[]{:S(2)}, u32[]{:S(2)}) collective-permute-start(f32[48,128]{1,0:T(8,128)S(1)} %get-tuple-element.65), channel_id=1, source_target_pairs={{1,2},{2,1},{5,6},{6,5},{9,10},{10,9},{13,14},{14,13},{17,18},{18,... | collective-permute-start | bytes 73736 | tf_op jit(solution)/shard_map/ppermute | solution.py:929
  88.6 12.3 %collective-permute-start.19 = (f32[8,3968]{1,0:T(8,128)S(1)}, f32[8,3968]{1,0:T(8,128)S(1)}, u32[]{:S(2)}, u32[]{:S(2)}) collective-permute-start(f32[8,3968]{1,0:T(8,128)S(1)} %get-tuple-element.72), channel_id=1, source_target_pairs={{0,2},{1,3},{2,0},{3,1},{4,6},{5,7},{6,4},{7,5},{8,10},{9,11},{10,... | collective-permute-start | bytes 380936 | tf_op jit(solution)/shard_map/ppermute | solution.py:929
  94.8 6.2 %collective-permute-start.20 = (f32[8,3968]{1,0:T(8,128)S(1)}, f32[8,3968]{1,0:T(8,128)S(1)}, u32[]{:S(2)}, u32[]{:S(2)}) collective-permute-start(f32[8,3968]{1,0:T(8,128)S(1)} %get-tuple-element.73), channel_id=1, source_target_pairs={{0,1},{1,0},{2,3},{3,2},{4,5},{5,4},{6,7},{7,6},{8,9},{9,8},{10,11... | collective-permute-start | bytes 380936 | tf_op jit(solution)/shard_map/ppermute | solution.py:929
  94.8 7.6 %collective-permute-start.21 = (f32[8,3968]{1,0:T(8,128)S(1)}, f32[8,3968]{1,0:T(8,128)S(1)}, u32[]{:S(2)}, u32[]{:S(2)}) collective-permute-start(f32[8,3968]{1,0:T(8,128)S(1)} %get-tuple-element.74), channel_id=1, source_target_pairs={{0,3},{1,2},{2,1},{3,0},{4,7},{5,6},{6,5},{7,4},{8,11},{9,10},{10,... | collective-permute-start | bytes 380936 | tf_op jit(solution)/shard_map/ppermute | solution.py:929
  103.9 5.1 %collective-permute-start.22 = (f32[48,256]{1,0:T(8,128)S(1)}, f32[48,256]{1,0:T(8,128)S(1)}, u32[]{:S(2)}, u32[]{:S(2)}) collective-permute-start(f32[48,256]{1,0:T(8,128)S(1)} %get-tuple-element.77), channel_id=1, source_target_pairs={{0,24},{4,28},{8,16},{12,20},{16,8},{20,12},{24,0},{28,4},{1,25},{... | collective-permute-start | bytes 147464 | tf_op jit(solution)/shard_map/ppermute | solution.py:1041
  105.5 4.9 %collective-permute-start.23 = (f32[48,256]{1,0:T(8,128)S(1)}, f32[48,256]{1,0:T(8,128)S(1)}, u32[]{:S(2)}, u32[]{:S(2)}) collective-permute-start(f32[48,256]{1,0:T(8,128)S(1)} %get-tuple-element.78), channel_id=1, source_target_pairs={{0,28},{4,8},{8,4},{12,16},{16,12},{20,24},{24,20},{28,0},{1,29},{... | collective-permute-start | bytes 147464 | tf_op jit(solution)/shard_map/ppermute | solution.py:1041
  105.5 5.1 %collective-permute-start.24 = (f32[48,256]{1,0:T(8,128)S(1)}, f32[48,256]{1,0:T(8,128)S(1)}, u32[]{:S(2)}, u32[]{:S(2)}) collective-permute-start(f32[48,256]{1,0:T(8,128)S(1)} %get-tuple-element.79), channel_id=1, source_target_pairs={{0,8},{4,12},{8,0},{12,4},{16,24},{20,28},{24,16},{28,20},{1,9},{5... | collective-permute-start | bytes 147464 | tf_op jit(solution)/shard_map/ppermute | solution.py:1041
  106.6 4.0 %collective-permute-start.25 = (f32[48,256]{1,0:T(8,128)S(1)}, f32[48,256]{1,0:T(8,128)S(1)}, u32[]{:S(2)}, u32[]{:S(2)}) collective-permute-start(f32[48,256]{1,0:T(8,128)S(1)} %get-tuple-element.80), channel_id=1, source_target_pairs={{0,4},{4,0},{8,12},{12,8},{16,20},{20,16},{24,28},{28,24},{1,5},{5... | collective-permute-start | bytes 147464 | tf_op jit(solution)/shard_map/ppermute | solution.py:1041
  (4 other events, 3.7 us)

commit v5 on v3

--- a/solution.py
+++ b/solution.py
@@ -701,15 +701,20 @@
             early[c, :, part] = product
 
 
-def advect_kernel(fields3, early, flow, to_span, to_modes, *outs):
+def advect_kernel(fields3, early, flow, to_span, to_modes, *refs):
+    *outs, stacked = refs
     me = lax.axis_index("plane")
     both, back = to_span[me], to_modes[me]
     lanes = lane_ids(GROUP)
     local = MODES // len(outs)
+    for part in LANE_PARTS:
+        for c, product in products((fields3,), flow, both, part):
+            high, low = halves(product + early[c, :, part])
+            stacked[c, :, part] = jnp.concatenate([high, low, high], axis=0)
     tails = [None] * len(outs)
-    for n, part in enumerate(LANE_PARTS):
-        for c, product in products((fields3,), flow, both, part):
-            result = span_dot(back, product + early[c, :, part])
+    for c in range(stacked.shape[0]):
+        for n, part in enumerate(LANE_PARTS):
+            result = jnp.dot(back, stacked[c, :, part], preferred_element_type=jnp.float32)
             for k, out in enumerate(outs):
                 for half in range(local // GROUP):
                     g = c * (local // GROUP) + half
@@ -735,7 +740,7 @@
     return (((me + start) ^ step) - start) % size
 
 
-def update_kernel(plans, in0, in1, in2, in3, local_sum, table, updated, own, out0, out1, out2, out3, chunks, traces):
+def update_kernel(plans, in0, in1, in2, in3, local_sum, table, updated, traces, out0, out1, out2, out3, chunks):
     me = lax.axis_index("plane")
     rows_total = local_sum.shape[1]
     last = NODES - 1
@@ -753,7 +758,7 @@
     def wide(row):
         return jnp.broadcast_to(table[pl.ds(row, 1), :], (8, LANES))
 
-    turned_round, partner = wide(15) == 1, wide(16)
+    turned_round = wide(15) == 1
     slot_edges = [wide(o) for o in blocks]
     groups = range(rows_total // GROUP)
     for g in groups:
@@ -786,8 +791,15 @@
                     value = pick(traces[k, rows, :], slot_edge)
                     total = value if total is None else jnp.where(lanes >= 24 * (k - 5 * t), value, total)
                 out[rows, pl.ds(t * LANES, LANES)] = total
+
+
+def own_kernel(table, traces, own):
+    partner = jnp.broadcast_to(table[16:17, :], (GROUP, LANES))
+    present = jnp.broadcast_to(table[12:13, :], (GROUP, LANES)) > 0
+    for g in range(traces.shape[1] // GROUP):
+        rows = group_rows(g)
         for k in range(NODES):
-            own[k, rows, :] = pick(traces[k, rows, :], partner)
+            own[k, rows, :] = jnp.where(present, pick(traces[k, rows, :], partner), 0.0)
 
 
 def pick(value, index):
@@ -805,7 +817,6 @@
 
     share = wide(17).astype(jnp.float32)
     quarter = lanes // 32
-    own_has = wide(12) > 0
     has = [wide(10 + o) > 0 for o in blocks]
     slots = [wide(5 + o) for o in blocks]
 
@@ -839,7 +850,7 @@
     for g in groups:
         rows = group_rows(g)
         for k in range(NODES):
-            total = jnp.where(own_has, own[k, rows, :], 0.0)
+            total = own[k, rows, :]
             for slot, there, source in zip(slots, has, came):
                 value = pick(tile_at(source, (), rows, k // 5), slot + 24 * (k % 5))
                 total = jnp.where(there, value, total)
@@ -1002,7 +1013,7 @@
         returning = kernel_call(
             advect_kernel,
             [f32(GROUP, BACK_TILES * LANES)] * planes,
-            [],
+            [pltpu.VMEM((comps, 3 * MODES, CHUNK_TILES * LANES), jnp.bfloat16)],
             30 * 10**6,
             5 * 10**6,
         )(fields[-1], early, flows[step_index], to_span_last, to_modes)
@@ -1013,10 +1024,10 @@
             12 * 10**6,
             2 * 10**6,
         )(state, metric, slab_bands)
-        updated, own, *leaving = kernel_call(
+        updated, seen, *leaving = kernel_call(
             functools.partial(update_kernel, back_plans),
             [f32(*state_shape), f32(nodes, rows_total, LANES)] + [f32(rows_total, 2 * LANES)] * 4,
-            [pltpu.VMEM((planes, GROUP, BACK_TILES * LANES), jnp.float32), edge_scratch],
+            [pltpu.VMEM((planes, GROUP, BACK_TILES * LANES), jnp.float32)],
             2 * 10**6,
             3 * 10**6,
         )(*swapped(returning), local_sum, table)
@@ -1026,6 +1037,7 @@
             )
             for matching, buffer in enumerate(leaving)
         ]
+        own = kernel_call(own_kernel, f32(nodes, rows_total, LANES), [], 10**5, 10**6)(table, seen)
         if step_index + 1 < STEPS:
             state, *prepared = kernel_call(
                 functools.partial(next_kernel, plans),

time: 108 us -> 108 us (level)
    pallas_call x2 -> x4, Pallas kernels: 2.16 us -> 2.16 us  [the longest x2 1.92 us: packed_shards(): kernel_call(advect_kernel, [f32(GROUP, BACK_TILES * LANES)] * planes, [pl...]
where the time goes in v5:
time: 108 us
  waiting for transfers between devices  36.9 us (34%)
  starting transfers between devices  35.4 us (33%)
  Pallas kernels  34.1 us (32%)
    ppermute x14, waiting for transfers between devices, swap(): lax.ppermute(buffer, 'plane', sorted(((i ^ step, i) for i in wanted)))  31.4 us
    ppermute x14, starting transfers between devices, swap(): lax.ppermute(buffer, 'plane', sorted(((i ^ step, i) for i in wanted)))  27 us
    pallas_call x1, Pallas kernels, packed_shards(): kernel_call(functools.partial(flow_kernel, points), [f32(*whole)] * STEPS...  11.3 us
    ppermute x8, starting transfers between devices, packed_shards(): lax.ppermute(buffer, 'dom', [(i, trace_partner(i, matching, partitions))...  8.38 us
    pallas_call x2, Pallas kernels, packed_shards(): kernel_call(diffuse_kernel, f32(*state_shape), [pltpu.VMEM((nodes, GROUP,...  5.64 us
    ppermute x8, waiting for transfers between devices, packed_shards(): lax.ppermute(buffer, 'dom', [(i, trace_partner(i, matching, partitions))...  5.46 us
    pallas_call x2, Pallas kernels, packed_shards(): kernel_call(functools.partial(update_kernel, back_plans), [f32(*state_sha...  3.12 us
    pallas_call x8, Pallas kernels, packed_shards(): kernel_call(functools.partial(fields_kernel, gaps, len(parts) > 1), f32(3...  2.42 us
  transfers between devices with their start and end apart: 22, of which 13 were waited for; matrix products, arithmetic and copies ran while one was open for 0% of the time, Pallas kernels for 21%

profile of v5, /device:TPU:0, one launch (start us, length us, event | category | flops | bytes accessed | tf_op | source)
XLA Modules:
  0.0 107.7 jit_solution(3775722160492554811)
XLA Ops:
  0.0 2.1 %shard_map.101 = (f32[9,48,384]{2,1,0:T(8,128)S(1)}, f32[9,48,384]{2,1,0:T(8,128)S(1)}, f32[48,1536]{1,0:T(8,128)S(1)}) custom-call(f32[3,9,9,16,32]{4,3,2,1,0:T(8,128)} %bitcast.8, f32[24,384]{1,0:T(8,128)} %constant.10.clone.far_bands.bands), custom_call_target="tpu_custom_call" | custom-call | flops 4000000 | bytes 4000000 | tf_op jit(solution)/shard_map/pallas_call | solution.py:964
  2.1 4.2 %collective-permute-start.3 = (f32[48,1536]{1,0:T(8,128)S(1)}, f32[48,1536]{1,0:T(8,128)S(1)}, u32[]{:S(2)}, u32[]{:S(2)}) collective-permute-start(f32[48,1536]{1,0:T(8,128)S(1)} %get-tuple-element.46), channel_id=1, source_target_pairs={{0,2},{1,3},{2,0},{3,1},{4,6},{5,7},{6,4},{7,5},{8,10},{9,11},{10,... | collective-permute-start | bytes 884744 | tf_op jit(solution)/shard_map/ppermute | solution.py:924
  7.1 1.2 %shard_map.102 = (f32[48,1536]{1,0:T(8,128)S(1)}, f32[48,1536]{1,0:T(8,128)S(1)}, f32[48,1408]{1,0:T(8,128)S(1)}, f32[48,128]{1,0:T(8,128)S(1)}) custom-call(f32[9,48,384]{2,1,0:T(8,128)S(1)} %get-tuple-element.41.state, f32[9,48,384]{2,1,0:T(8,128)S(1)} %get-tuple-element.42.xi, f32[24,384]{1,0:T(8,128)S(1)} %copy-done.2), custom_call_target="tpu_custom_call" | custom-call | flops 1000000 | bytes 2000000 | tf_op jit(solution)/shard_map/pallas_call | solution.py:953
  8.3 1.6 %collective-permute-start.2 = (f32[48,1536]{1,0:T(8,128)S(1)}, f32[48,1536]{1,0:T(8,128)S(1)}, u32[]{:S(2)}, u32[]{:S(2)}) collective-permute-start(f32[48,1536]{1,0:T(8,128)S(1)} %get-tuple-element.45), channel_id=1, source_target_pairs={{0,1},{1,0},{2,3},{3,2},{4,5},{5,4},{6,7},{7,6},{8,9},{9,8},{10,11... | collective-permute-start | bytes 884744 | tf_op jit(solution)/shard_map/ppermute | solution.py:924
  10.9 11.3 %shard_map.107 = (f32[12,64,768]{2,1,0:T(8,128)S(1)}, f32[12,64,768]{2,1,0:T(8,128)S(1)}) custom-call(f32[12,2,41472]{2,1,0:T(2,128)S(1)} %bitcast.5, f32[4,32]{1,0:T(4,128)S(1)} %copy-done.7), custom_call_target="tpu_custom_call" | custom-call | flops 4000000 | bytes 9000000 | tf_op jit(solution)/shard_map/pallas_call | solution.py:975
  22.5 5.1 %collective-permute-done.2.source = f32[48,1536]{1,0:T(8,128)S(1)} collective-permute-done((f32[48,1536]{1,0:T(8,128)S(1)}, f32[48,1536]{1,0:T(8,128)S(1)}, u32[]{:S(2)}, u32[]{:S(2)}) %collective-permute-start.2) | collective-permute-done | bytes 294944 | tf_op jit(solution)/shard_map/ppermute | solution.py:924
  30.0 5.8 %collective-permute-start.4 = (f32[8,3968]{1,0:T(8,128)S(1)}, f32[8,3968]{1,0:T(8,128)S(1)}, u32[]{:S(2)}, u32[]{:S(2)}) collective-permute-start(f32[8,3968]{1,0:T(8,128)S(1)} %get-tuple-element.50), channel_id=1, source_target_pairs={{0,2},{1,3},{2,0},{3,1},{4,6},{5,7},{6,4},{7,5},{8,10},{9,11},{10,... | collective-permute-start | bytes 380936 | tf_op jit(solution)/shard_map/ppermute | solution.py:924
  35.8 1.5 %collective-permute-start.6 = (f32[8,3968]{1,0:T(8,128)S(1)}, f32[8,3968]{1,0:T(8,128)S(1)}, u32[]{:S(2)}, u32[]{:S(2)}) collective-permute-start(f32[8,3968]{1,0:T(8,128)S(1)} %get-tuple-element.52), channel_id=1, source_target_pairs={{0,3},{1,2},{2,1},{3,0},{4,7},{5,6},{6,5},{7,4},{8,11},{9,10},{10,... | collective-permute-start | bytes 380936 | tf_op jit(solution)/shard_map/ppermute | solution.py:924
  37.6 2.8 %shard_map.110.local_sum = f32[9,48,384]{2,1,0:T(8,128)S(1)} custom-call(f32[9,48,384]{2,1,0:T(8,128)S(1)} %get-tuple-element.41.state, f32[4,32]{1,0:T(4,128)S(1)} %copy-done.7, f32[24,384]{1,0:T(8,128)S(1)} %copy-done.3), custom_call_target="tpu_custom_call" | custom-call | flops 12000000 | bytes 2000000 | tf_op jit(solution)/shard_map/pallas_call | solution.py:1020
  40.4 4.7 %collective-permute-done.4.in1 = f32[8,3968]{1,0:T(8,128)S(1)} collective-permute-done((f32[8,3968]{1,0:T(8,128)S(1)}, f32[8,3968]{1,0:T(8,128)S(1)}, u32[]{:S(2)}, u32[]{:S(2)}) %collective-permute-start.4) | collective-permute-done | bytes 127008 | tf_op jit(solution)/shard_map/ppermute | solution.py:924
  46.1 1.6 %shard_map.111 = (f32[9,48,384]{2,1,0:T(8,128)S(1)}, f32[9,48,128]{2,1,0:T(8,128)S(1)}, f32[48,256]{1,0:T(8,128)S(1)}, f32[48,256]{1,0:T(8,128)S(1)}, f32[48,256]{1,0:T(8,128)S(1)}, /*index=5*/f32[48,256]{1,0:T(8,128)S(1)}) custom-call(f32[8,3968]{1,0:T(8,128)S(1)} %get-tuple-element.49.in0, f32[8,3968]{1,0:T(8,128)S(1)} %collective-permute-done.4.in1, ...), custom_call_target="tpu_custom_call" | custom-call | flops 2000000 | bytes 3000000 | tf_op jit(solution)/shard_map/pallas_call | solution.py:1027
  47.7 2.5 %collective-permute-start.7 = (f32[48,256]{1,0:T(8,128)S(1)}, f32[48,256]{1,0:T(8,128)S(1)}, u32[]{:S(2)}, u32[]{:S(2)}) collective-permute-start(f32[48,256]{1,0:T(8,128)S(1)} %get-tuple-element.55), channel_id=1, source_target_pairs={{0,24},{4,28},{8,16},{12,20},{16,8},{20,12},{24,0},{28,4},{1,25},{... | collective-permute-start | bytes 147464 | tf_op jit(solution)/shard_map/ppermute | solution.py:1035
  50.5 1.5 %collective-permute-start.9 = (f32[48,256]{1,0:T(8,128)S(1)}, f32[48,256]{1,0:T(8,128)S(1)}, u32[]{:S(2)}, u32[]{:S(2)}) collective-permute-start(f32[48,256]{1,0:T(8,128)S(1)} %get-tuple-element.57), channel_id=1, source_target_pairs={{0,8},{4,12},{8,0},{12,4},{16,24},{20,28},{24,16},{28,20},{1,9},{5... | collective-permute-start | bytes 147464 | tf_op jit(solution)/shard_map/ppermute | solution.py:1035
  52.8 1.9 %collective-permute-done.8.r1 = f32[48,256]{1,0:T(8,128)S(1)} collective-permute-done((f32[48,256]{1,0:T(8,128)S(1)}, f32[48,256]{1,0:T(8,128)S(1)}, u32[]{:S(2)}, u32[]{:S(2)}) %collective-permute-start.8) | collective-permute-done | bytes 49184 | tf_op jit(solution)/shard_map/ppermute | solution.py:1035
  55.3 1.2 %shard_map.113 = (f32[9,48,384]{2,1,0:T(8,128)S(1)}, f32[9,48,384]{2,1,0:T(8,128)S(1)}, f32[48,1536]{1,0:T(8,128)S(1)}) custom-call(s32[24,128]{1,0:T(8,128)S(1)} %shard_map.100.table, f32[9,48,384]{2,1,0:T(8,128)S(1)} %get-tuple-element.53.updated, f32[9,48,128]{2,1,0:T(8,128)S(1)} %shard_map.112.own, f32[48,256]{1,0:T(8,128)S(1)} %collective-permute-done.7.r0, ...), custom_call_target="tpu_custom_call" | custom-call | flops 6000000 | bytes 4000000 | tf_op jit(solution)/shard_map/pallas_call | solution.py:1042
  56.5 1.3 %collective-permute-start.14 = (f32[48,1536]{1,0:T(8,128)S(1)}, f32[48,1536]{1,0:T(8,128)S(1)}, u32[]{:S(2)}, u32[]{:S(2)}) collective-permute-start(f32[48,1536]{1,0:T(8,128)S(1)} %get-tuple-element.64), channel_id=1, source_target_pairs={{0,2},{1,3},{2,0},{3,1},{4,6},{5,7},{6,4},{7,5},{8,10},{9,11},{10,... | collective-permute-start | bytes 884744 | tf_op jit(solution)/shard_map/ppermute | solution.py:924
  57.7 1.2 %shard_map.114 = (f32[48,1536]{1,0:T(8,128)S(1)}, f32[48,1536]{1,0:T(8,128)S(1)}, f32[48,1408]{1,0:T(8,128)S(1)}, f32[48,128]{1,0:T(8,128)S(1)}) custom-call(f32[9,48,384]{2,1,0:T(8,128)S(1)} %get-tuple-element.59.state, f32[9,48,384]{2,1,0:T(8,128)S(1)} %get-tuple-element.60.xi, f32[24,384]{1,0:T(8,128)S(1)} %copy-done.3), custom_call_target="tpu_custom_call" | custom-call | flops 1000000 | bytes 2000000 | tf_op jit(solution)/shard_map/pallas_call | solution.py:953
  58.9 1.8 %collective-permute-start.13 = (f32[48,1536]{1,0:T(8,128)S(1)}, f32[48,1536]{1,0:T(8,128)S(1)}, u32[]{:S(2)}, u32[]{:S(2)}) collective-permute-start(f32[48,1536]{1,0:T(8,128)S(1)} %get-tuple-element.63), channel_id=1, source_target_pairs={{0,1},{1,0},{2,3},{3,2},{4,5},{5,4},{6,7},{7,6},{8,9},{9,8},{10,11... | collective-permute-start | bytes 884744 | tf_op jit(solution)/shard_map/ppermute | solution.py:924
  60.7 1.9 %collective-permute-start.11 = (f32[48,1408]{1,0:T(8,128)S(1)}, f32[48,1408]{1,0:T(8,128)S(1)}, u32[]{:S(2)}, u32[]{:S(2)}) collective-permute-start(f32[48,1408]{1,0:T(8,128)S(1)} %get-tuple-element.61), channel_id=1, source_target_pairs={{0,3},{1,2},{2,1},{3,0},{4,7},{5,6},{6,5},{7,4},{8,11},{9,10},{10,... | collective-permute-start | bytes 811016 | tf_op jit(solution)/shard_map/ppermute | solution.py:924
  63.7 10.4 %collective-permute-done.14.source = f32[48,1536]{1,0:T(8,128)S(1)} collective-permute-done((f32[48,1536]{1,0:T(8,128)S(1)}, f32[48,1536]{1,0:T(8,128)S(1)}, u32[]{:S(2)}, u32[]{:S(2)}) %collective-permute-start.14) | collective-permute-done | bytes 294944 | tf_op jit(solution)/shard_map/ppermute | solution.py:924
  75.5 4.7 %collective-permute-done.11.source = f32[48,1408]{1,0:T(8,128)S(1)} collective-permute-done((f32[48,1408]{1,0:T(8,128)S(1)}, f32[48,1408]{1,0:T(8,128)S(1)}, u32[]{:S(2)}, u32[]{:S(2)}) %collective-permute-start.11) | collective-permute-done | bytes 270368 | tf_op jit(solution)/shard_map/ppermute | solution.py:924
  80.5 1.0 shard_map.120
  81.5 5.7 %collective-permute-start.15 = (f32[8,3968]{1,0:T(8,128)S(1)}, f32[8,3968]{1,0:T(8,128)S(1)}, u32[]{:S(2)}, u32[]{:S(2)}) collective-permute-start(f32[8,3968]{1,0:T(8,128)S(1)} %get-tuple-element.68), channel_id=1, source_target_pairs={{0,2},{1,3},{2,0},{3,1},{4,6},{5,7},{6,4},{7,5},{8,10},{9,11},{10,... | collective-permute-start | bytes 380936 | tf_op jit(solution)/shard_map/ppermute | solution.py:924
  87.2 1.7 %collective-permute-start.17 = (f32[8,3968]{1,0:T(8,128)S(1)}, f32[8,3968]{1,0:T(8,128)S(1)}, u32[]{:S(2)}, u32[]{:S(2)}) collective-permute-start(f32[8,3968]{1,0:T(8,128)S(1)} %get-tuple-element.70), channel_id=1, source_target_pairs={{0,3},{1,2},{2,1},{3,0},{4,7},{5,6},{6,5},{7,4},{8,11},{9,10},{10,... | collective-permute-start | bytes 380936 | tf_op jit(solution)/shard_map/ppermute | solution.py:924
  88.8 2.8 %shard_map.121.local_sum = f32[9,48,384]{2,1,0:T(8,128)S(1)} custom-call(f32[9,48,384]{2,1,0:T(8,128)S(1)} %get-tuple-element.59.state, f32[4,32]{1,0:T(4,128)S(1)} %copy-done.7, f32[24,384]{1,0:T(8,128)S(1)} %copy-done.3), custom_call_target="tpu_custom_call" | custom-call | flops 12000000 | bytes 2000000 | tf_op jit(solution)/shard_map/pallas_call | solution.py:1020
  91.7 3.5 %collective-permute-done.15.in1 = f32[8,3968]{1,0:T(8,128)S(1)} collective-permute-done((f32[8,3968]{1,0:T(8,128)S(1)}, f32[8,3968]{1,0:T(8,128)S(1)}, u32[]{:S(2)}, u32[]{:S(2)}) %collective-permute-start.15) | collective-permute-done | bytes 127008 | tf_op jit(solution)/shard_map/ppermute | solution.py:924
  95.2 2.1 %collective-permute-done.16.in2 = f32[8,3968]{1,0:T(8,128)S(1)} collective-permute-done((f32[8,3968]{1,0:T(8,128)S(1)}, f32[8,3968]{1,0:T(8,128)S(1)}, u32[]{:S(2)}, u32[]{:S(2)}) %collective-permute-start.16) | collective-permute-done | bytes 127008 | tf_op jit(solution)/shard_map/ppermute | solution.py:924
  97.2 1.6 %shard_map.122 = (f32[9,48,384]{2,1,0:T(8,128)S(1)}, f32[9,48,128]{2,1,0:T(8,128)S(1)}, f32[48,256]{1,0:T(8,128)S(1)}, f32[48,256]{1,0:T(8,128)S(1)}, f32[48,256]{1,0:T(8,128)S(1)}, /*index=5*/f32[48,256]{1,0:T(8,128)S(1)}) custom-call(f32[8,3968]{1,0:T(8,128)S(1)} %get-tuple-element.67.in0, f32[8,3968]{1,0:T(8,128)S(1)} %collective-permute-done.15.in1, ...), custom_call_target="tpu_custom_call" | custom-call | flops 2000000 | bytes 3000000 | tf_op jit(solution)/shard_map/pallas_call | solution.py:1027
  98.8 1.5 %collective-permute-start.18 = (f32[48,256]{1,0:T(8,128)S(1)}, f32[48,256]{1,0:T(8,128)S(1)}, u32[]{:S(2)}, u32[]{:S(2)}) collective-permute-start(f32[48,256]{1,0:T(8,128)S(1)} %get-tuple-element.73), channel_id=1, source_target_pairs={{0,24},{4,28},{8,16},{12,20},{16,8},{20,12},{24,0},{28,4},{1,25},{... | collective-permute-start | bytes 147464 | tf_op jit(solution)/shard_map/ppermute | solution.py:1035
  101.4 1.4 %collective-permute-start.21 = (f32[48,256]{1,0:T(8,128)S(1)}, f32[48,256]{1,0:T(8,128)S(1)}, u32[]{:S(2)}, u32[]{:S(2)}) collective-permute-start(f32[48,256]{1,0:T(8,128)S(1)} %get-tuple-element.76), channel_id=1, source_target_pairs={{0,4},{4,0},{8,12},{12,8},{16,20},{20,16},{24,28},{28,24},{1,5},{5... | collective-permute-start | bytes 147464 | tf_op jit(solution)/shard_map/ppermute | solution.py:1035
  103.9 1.2 %collective-permute-done.19.r1 = f32[48,256]{1,0:T(8,128)S(1)} collective-permute-done((f32[48,256]{1,0:T(8,128)S(1)}, f32[48,256]{1,0:T(8,128)S(1)}, u32[]{:S(2)}, u32[]{:S(2)}) %collective-permute-start.19) | collective-permute-done | bytes 49184 | tf_op jit(solution)/shard_map/ppermute | solution.py:1035
  105.3 2.2 %shard_map.124 = f32[3,9,9,16,32]{4,3,2,1,0:T(8,128)} custom-call(s32[24,128]{1,0:T(8,128)S(1)} %shard_map.100.table, f32[9,48,384]{2,1,0:T(8,128)S(1)} %get-tuple-element.71.updated, f32[9,48,128]{2,1,0:T(8,128)S(1)} %shard_map.123.own, f32[48,256]{1,0:T(8,128)S(1)} %collective-permute-done.18.r0, f32[48,256]{1,0:T(8,128)S(1)} %collective-permute-done.19.r1, ...), custom_call_target="tpu_custom_call" | custom-call | flops 2000000 | bytes 3000000 | tf_op jit(solution)/shard_map/pallas_call | solution.py:1051
  (57 shorter events, 12.3 us)
Async XLA Ops:
  0.0 10.6 %copy-start = (f32[4,24,768]{2,1,0:T(8,128)S(1)}, f32[4,24,768]{2,1,0:T(8,128)}, u32[]{:S(2)}) copy-start(f32[4,24,768]{2,1,0:T(8,128)} %constant.11.clone.refs_0_.refs_1_) | copy-start | bytes 884740
  0.0 10.9 %copy-start.1 = (f32[2,12,41472]{2,0,1:T(2,128)S(1)}, f32[2,12,41472]{2,0,1:T(2,128)}, u32[]{:S(2)}) copy-start(f32[2,12,41472]{2,0,1:T(2,128)} %param.12) | copy-start | bytes 11943940
  2.1 20.1 %collective-permute-start.3 = (f32[48,1536]{1,0:T(8,128)S(1)}, f32[48,1536]{1,0:T(8,128)S(1)}, u32[]{:S(2)}, u32[]{:S(2)}) collective-permute-start(f32[48,1536]{1,0:T(8,128)S(1)} %get-tuple-element.46), channel_id=1, source_target_pairs={{0,2},{1,3},{2,0},{3,1},{4,6},{5,7},{6,4},{7,5},{8,10},{9,11},{10,... | collective-permute-start | bytes 884744 | tf_op jit(solution)/shard_map/ppermute | solution.py:924
  6.3 0.8 copy-start.2
  7.1 3.8 %copy-start.7 = (f32[4,32]{1,0:T(4,128)S(1)}, f32[4,32]{1,0:T(4,128)}, u32[]{:S(2)}) copy-start(f32[4,32]{1,0:T(4,128)} %metric.5) | copy-start | bytes 1540
  8.3 19.3 %collective-permute-start.2 = (f32[48,1536]{1,0:T(8,128)S(1)}, f32[48,1536]{1,0:T(8,128)S(1)}, u32[]{:S(2)}, u32[]{:S(2)}) collective-permute-start(f32[48,1536]{1,0:T(8,128)S(1)} %get-tuple-element.45), channel_id=1, source_target_pairs={{0,1},{1,0},{2,3},{3,2},{4,5},{5,4},{6,7},{7,6},{8,9},{9,8},{10,11... | collective-permute-start | bytes 884744 | tf_op jit(solution)/shard_map/ppermute | solution.py:924
  9.8 18.8 %collective-permute-start = (f32[48,1408]{1,0:T(8,128)S(1)}, f32[48,1408]{1,0:T(8,128)S(1)}, u32[]{:S(2)}, u32[]{:S(2)}) collective-permute-start(f32[48,1408]{1,0:T(8,128)S(1)} %get-tuple-element.43), channel_id=1, source_target_pairs={{0,3},{1,2},{2,1},{3,0},{4,7},{5,6},{6,5},{7,4},{8,11},{9,10},{10,... | collective-permute-start | bytes 811016 | tf_op jit(solution)/shard_map/ppermute | solution.py:924
  9.9 18.8 %collective-permute-start.1 = (f32[48,128]{1,0:T(8,128)S(1)}, f32[48,128]{1,0:T(8,128)S(1)}, u32[]{:S(2)}, u32[]{:S(2)}) collective-permute-start(f32[48,128]{1,0:T(8,128)S(1)} %get-tuple-element.44), channel_id=1, source_target_pairs={{1,2},{2,1},{5,6},{6,5},{9,10},{10,9},{13,14},{14,13},{17,18},{18,... | collective-permute-start | bytes 73736 | tf_op jit(solution)/shard_map/ppermute | solution.py:924
  10.9 17.0 %copy-start.4 = (bf16[4,128,144]{2,1,0:T(8,128)(2,1)S(1)}, bf16[4,128,144]{2,1,0:T(8,128)(2,1)}, u32[]{:S(2)}) copy-start(bf16[4,128,144]{2,1,0:T(8,128)(2,1)} %constant.12.clone.to_span) | copy-start | bytes 442372
  27.9 1.1 %copy-start.5 = (bf16[4,128,48]{2,1,0:T(8,128)(2,1)S(1)}, bf16[4,128,48]{2,1,0:T(8,128)(2,1)}, u32[]{:S(2)}) copy-start(bf16[4,128,48]{2,1,0:T(8,128)(2,1)} %constant.13.clone.to_span) | copy-start | bytes 147460
  27.9 1.1 %copy-start.6 = (bf16[4,64,192]{2,1,0:T(8,128)(2,1)S(1)}, bf16[4,64,192]{2,1,0:T(8,128)(2,1)}, u32[]{:S(2)}) copy-start(bf16[4,64,192]{2,1,0:T(8,128)(2,1)} %constant.14.clone.to_modes) | copy-start | bytes 294916
  28.6 8.7 %copy-start.8 = (s32[1,5,24]{2,0,1:T(1,128)S(1)}, s32[1,5,24]{2,0,1:T(1,128)}, u32[]{:S(2)}) copy-start(s32[1,5,24]{2,0,1:T(1,128)} %param.13) | copy-start | bytes 1444
  28.6 8.7 %copy-start.9 = (s32[1,5,24]{2,0,1:T(1,128)S(1)}, s32[1,5,24]{2,0,1:T(1,128)}, u32[]{:S(2)}) copy-start(s32[1,5,24]{2,0,1:T(1,128)} %param.14) | copy-start | bytes 1444
  28.7 8.9 %copy-start.3 = (f32[24,384]{1,0:T(8,128)S(1)}, f32[24,384]{1,0:T(8,128)}, u32[]{:S(2)}) copy-start(f32[24,384]{1,0:T(8,128)} %constant.10.clone.far_bands.bands) | copy-start | bytes 110596
  30.0 15.2 %collective-permute-start.4 = (f32[8,3968]{1,0:T(8,128)S(1)}, f32[8,3968]{1,0:T(8,128)S(1)}, u32[]{:S(2)}, u32[]{:S(2)}) collective-permute-start(f32[8,3968]{1,0:T(8,128)S(1)} %get-tuple-element.50), channel_id=1, source_target_pairs={{0,2},{1,3},{2,0},{3,1},{4,6},{5,7},{6,4},{7,5},{8,10},{9,11},{10,... | collective-permute-start | bytes 380936 | tf_op jit(solution)/shard_map/ppermute | solution.py:924
  35.8 10.2 %collective-permute-start.5 = (f32[8,3968]{1,0:T(8,128)S(1)}, f32[8,3968]{1,0:T(8,128)S(1)}, u32[]{:S(2)}, u32[]{:S(2)}) collective-permute-start(f32[8,3968]{1,0:T(8,128)S(1)} %get-tuple-element.51), channel_id=1, source_target_pairs={{0,1},{1,0},{2,3},{3,2},{4,5},{5,4},{6,7},{7,6},{8,9},{9,8},{10,11... | collective-permute-start | bytes 380936 | tf_op jit(solution)/shard_map/ppermute | solution.py:924
  35.8 10.2 %collective-permute-start.6 = (f32[8,3968]{1,0:T(8,128)S(1)}, f32[8,3968]{1,0:T(8,128)S(1)}, u32[]{:S(2)}, u32[]{:S(2)}) collective-permute-start(f32[8,3968]{1,0:T(8,128)S(1)} %get-tuple-element.52), channel_id=1, source_target_pairs={{0,3},{1,2},{2,1},{3,0},{4,7},{5,6},{6,5},{7,4},{8,11},{9,10},{10,... | collective-permute-start | bytes 380936 | tf_op jit(solution)/shard_map/ppermute | solution.py:924
  47.6 4.5 %collective-permute-start.10 = (f32[48,256]{1,0:T(8,128)S(1)}, f32[48,256]{1,0:T(8,128)S(1)}, u32[]{:S(2)}, u32[]{:S(2)}) collective-permute-start(f32[48,256]{1,0:T(8,128)S(1)} %get-tuple-element.58), channel_id=1, source_target_pairs={{0,4},{4,0},{8,12},{12,8},{16,20},{20,16},{24,28},{28,24},{1,5},{5... | collective-permute-start | bytes 147464 | tf_op jit(solution)/shard_map/ppermute | solution.py:1035
  47.7 5.1 %collective-permute-start.7 = (f32[48,256]{1,0:T(8,128)S(1)}, f32[48,256]{1,0:T(8,128)S(1)}, u32[]{:S(2)}, u32[]{:S(2)}) collective-permute-start(f32[48,256]{1,0:T(8,128)S(1)} %get-tuple-element.55), channel_id=1, source_target_pairs={{0,24},{4,28},{8,16},{12,20},{16,8},{20,12},{24,0},{28,4},{1,25},{... | collective-permute-start | bytes 147464 | tf_op jit(solution)/shard_map/ppermute | solution.py:1035
  50.2 4.4 %collective-permute-start.8 = (f32[48,256]{1,0:T(8,128)S(1)}, f32[48,256]{1,0:T(8,128)S(1)}, u32[]{:S(2)}, u32[]{:S(2)}) collective-permute-start(f32[48,256]{1,0:T(8,128)S(1)} %get-tuple-element.56), channel_id=1, source_target_pairs={{0,28},{4,8},{8,4},{12,16},{16,12},{20,24},{24,20},{28,0},{1,29},{... | collective-permute-start | bytes 147464 | tf_op jit(solution)/shard_map/ppermute | solution.py:1035
  50.5 4.8 %collective-permute-start.9 = (f32[48,256]{1,0:T(8,128)S(1)}, f32[48,256]{1,0:T(8,128)S(1)}, u32[]{:S(2)}, u32[]{:S(2)}) collective-permute-start(f32[48,256]{1,0:T(8,128)S(1)} %get-tuple-element.57), channel_id=1, source_target_pairs={{0,8},{4,12},{8,0},{12,4},{16,24},{20,28},{24,16},{28,20},{1,9},{5... | collective-permute-start | bytes 147464 | tf_op jit(solution)/shard_map/ppermute | solution.py:1035
  56.5 17.7 %collective-permute-start.14 = (f32[48,1536]{1,0:T(8,128)S(1)}, f32[48,1536]{1,0:T(8,128)S(1)}, u32[]{:S(2)}, u32[]{:S(2)}) collective-permute-start(f32[48,1536]{1,0:T(8,128)S(1)} %get-tuple-element.64), channel_id=1, source_target_pairs={{0,2},{1,3},{2,0},{3,1},{4,6},{5,7},{6,4},{7,5},{8,10},{9,11},{10,... | collective-permute-start | bytes 884744 | tf_op jit(solution)/shard_map/ppermute | solution.py:924
  58.9 15.6 %collective-permute-start.13 = (f32[48,1536]{1,0:T(8,128)S(1)}, f32[48,1536]{1,0:T(8,128)S(1)}, u32[]{:S(2)}, u32[]{:S(2)}) collective-permute-start(f32[48,1536]{1,0:T(8,128)S(1)} %get-tuple-element.63), channel_id=1, source_target_pairs={{0,1},{1,0},{2,3},{3,2},{4,5},{5,4},{6,7},{7,6},{8,9},{9,8},{10,11... | collective-permute-start | bytes 884744 | tf_op jit(solution)/shard_map/ppermute | solution.py:924
  60.7 19.5 %collective-permute-start.11 = (f32[48,1408]{1,0:T(8,128)S(1)}, f32[48,1408]{1,0:T(8,128)S(1)}, u32[]{:S(2)}, u32[]{:S(2)}) collective-permute-start(f32[48,1408]{1,0:T(8,128)S(1)} %get-tuple-element.61), channel_id=1, source_target_pairs={{0,3},{1,2},{2,1},{3,0},{4,7},{5,6},{6,5},{7,4},{8,11},{9,10},{10,... | collective-permute-start | bytes 811016 | tf_op jit(solution)/shard_map/ppermute | solution.py:924
  62.6 12.9 %collective-permute-start.12 = (f32[48,128]{1,0:T(8,128)S(1)}, f32[48,128]{1,0:T(8,128)S(1)}, u32[]{:S(2)}, u32[]{:S(2)}) collective-permute-start(f32[48,128]{1,0:T(8,128)S(1)} %get-tuple-element.62), channel_id=1, source_target_pairs={{1,2},{2,1},{5,6},{6,5},{9,10},{10,9},{13,14},{14,13},{17,18},{18,... | collective-permute-start | bytes 73736 | tf_op jit(solution)/shard_map/ppermute | solution.py:924
  81.5 13.7 %collective-permute-start.15 = (f32[8,3968]{1,0:T(8,128)S(1)}, f32[8,3968]{1,0:T(8,128)S(1)}, u32[]{:S(2)}, u32[]{:S(2)}) collective-permute-start(f32[8,3968]{1,0:T(8,128)S(1)} %get-tuple-element.68), channel_id=1, source_target_pairs={{0,2},{1,3},{2,0},{3,1},{4,6},{5,7},{6,4},{7,5},{8,10},{9,11},{10,... | collective-permute-start | bytes 380936 | tf_op jit(solution)/shard_map/ppermute | solution.py:924
  87.2 10.1 %collective-permute-start.16 = (f32[8,3968]{1,0:T(8,128)S(1)}, f32[8,3968]{1,0:T(8,128)S(1)}, u32[]{:S(2)}, u32[]{:S(2)}) collective-permute-start(f32[8,3968]{1,0:T(8,128)S(1)} %get-tuple-element.69), channel_id=1, source_target_pairs={{0,1},{1,0},{2,3},{3,2},{4,5},{5,4},{6,7},{7,6},{8,9},{9,8},{10,11... | collective-permute-start | bytes 380936 | tf_op jit(solution)/shard_map/ppermute | solution.py:924
  87.2 10.1 %collective-permute-start.17 = (f32[8,3968]{1,0:T(8,128)S(1)}, f32[8,3968]{1,0:T(8,128)S(1)}, u32[]{:S(2)}, u32[]{:S(2)}) collective-permute-start(f32[8,3968]{1,0:T(8,128)S(1)} %get-tuple-element.70), channel_id=1, source_target_pairs={{0,3},{1,2},{2,1},{3,0},{4,7},{5,6},{6,5},{7,4},{8,11},{9,10},{10,... | collective-permute-start | bytes 380936 | tf_op jit(solution)/shard_map/ppermute | solution.py:924
  98.8 5.1 %collective-permute-start.18 = (f32[48,256]{1,0:T(8,128)S(1)}, f32[48,256]{1,0:T(8,128)S(1)}, u32[]{:S(2)}, u32[]{:S(2)}) collective-permute-start(f32[48,256]{1,0:T(8,128)S(1)} %get-tuple-element.73), channel_id=1, source_target_pairs={{0,24},{4,28},{8,16},{12,20},{16,8},{20,12},{24,0},{28,4},{1,25},{... | collective-permute-start | bytes 147464 | tf_op jit(solution)/shard_map/ppermute | solution.py:1035
  100.3 4.8 %collective-permute-start.19 = (f32[48,256]{1,0:T(8,128)S(1)}, f32[48,256]{1,0:T(8,128)S(1)}, u32[]{:S(2)}, u32[]{:S(2)}) collective-permute-start(f32[48,256]{1,0:T(8,128)S(1)} %get-tuple-element.74), channel_id=1, source_target_pairs={{0,28},{4,8},{8,4},{12,16},{16,12},{20,24},{24,20},{28,0},{1,29},{... | collective-permute-start | bytes 147464 | tf_op jit(solution)/shard_map/ppermute | solution.py:1035
  100.8 4.5 %collective-permute-start.20 = (f32[48,256]{1,0:T(8,128)S(1)}, f32[48,256]{1,0:T(8,128)S(1)}, u32[]{:S(2)}, u32[]{:S(2)}) collective-permute-start(f32[48,256]{1,0:T(8,128)S(1)} %get-tuple-element.75), channel_id=1, source_target_pairs={{0,8},{4,12},{8,0},{12,4},{16,24},{20,28},{24,16},{28,20},{1,9},{5... | collective-permute-start | bytes 147464 | tf_op jit(solution)/shard_map/ppermute | solution.py:1035
  101.4 3.9 %collective-permute-start.21 = (f32[48,256]{1,0:T(8,128)S(1)}, f32[48,256]{1,0:T(8,128)S(1)}, u32[]{:S(2)}, u32[]{:S(2)}) collective-permute-start(f32[48,256]{1,0:T(8,128)S(1)} %get-tuple-element.76), channel_id=1, source_target_pairs={{0,4},{4,0},{8,12},{12,8},{16,20},{20,16},{24,28},{28,24},{1,5},{5... | collective-permute-start | bytes 147464 | tf_op jit(solution)/shard_map/ppermute | solution.py:1035

commit v6 on v5

--- a/solution.py
+++ b/solution.py
@@ -195,6 +195,7 @@
 BACK_TILES = 31
 GROUP = 8
 PARTNERS = (0, 2, 1, 3)
+BACK_PARTNERS = (0, 2, 3, 1)
 FIELDS_ORDER = (0, 1, 2, 3)
 STEP_VISC = step_size * viscosity
 
@@ -239,12 +240,15 @@
     local = MODES // planes
     to_span, to_span_last, to_modes = [], [], []
     for me in range(planes):
-        came = np.concatenate([(me ^ step) * local + np.arange(local) for step in PARTNERS])
+        came, goes = (
+            np.concatenate([(me ^ step) * local + np.arange(local) for step in steps])
+            for steps in (PARTNERS, BACK_PARTNERS)
+        )
         high, low = in_two(np.concatenate([basis, slope])[:, came])
         early, last = slice(0, MODES - local), slice(MODES - local, MODES)
         for table, columns in ((to_span, early), (to_span_last, last)):
             table.append(np.concatenate([high[:, columns], high[:, columns], low[:, columns]], axis=1))
-        high, low = in_two(forward[came])
+        high, low = in_two(forward[goes])
         to_modes.append(np.concatenate([high, high, low], axis=1))
     return np.stack(to_span), np.stack(to_span_last), np.stack(to_modes)
 
@@ -745,7 +749,7 @@
     rows_total = local_sum.shape[1]
     last = NODES - 1
     lanes = lane_ids(8)
-    for step, source in zip(PARTNERS, (in0, in1, in2, in3)):
+    for step, source in zip(BACK_PARTNERS, (in0, in1, in2, in3)):
         chunks[me ^ step] = source[...]
 
     trace_plans = [
@@ -916,8 +920,8 @@
     )
 
 
-def swapped(buffers):
-    return [buffers[0]] + [swap(buffer, step) for buffer, step in zip(buffers[1:], PARTNERS[1:])]
+def swapped(buffers, steps):
+    return [buffers[0]] + [swap(buffer, step) for buffer, step in zip(buffers[1:], steps[1:])]
 
 
 def swap(buffer, step, wanted=range(4)):
@@ -957,7 +961,7 @@
             10**6,
             2 * 10**6,
         )(state, xi, slab_bands)
-        came = swapped([own, first, second, third])
+        came = swapped([own, first, second, third], PARTNERS)
         return [(part,) for part in came[:-1]] + [(came[-1], swap(last_tile, PARTNERS[-1], middle))]
 
     in_rows = pltpu.with_memory_space_constraint(adjoint.transpose(0, 2, 3, 1, 4), pltpu.HBM)
@@ -1030,7 +1034,7 @@
             [pltpu.VMEM((planes, GROUP, BACK_TILES * LANES), jnp.float32)],
             2 * 10**6,
             3 * 10**6,
-        )(*swapped(returning), local_sum, table)
+        )(*swapped(returning, BACK_PARTNERS), local_sum, table)
         traces = [
             lax.ppermute(
                 buffer, "dom", [(i, trace_partner(i, matching, partitions)) for i in range(partitions)]

time: 108 us -> 108 us (level)
  waiting for transfers between devices: 36.9 us -> 38.2 us
  starting transfers between devices: 35.4 us -> 34.3 us
    ppermute x14, waiting for transfers between devices: 31.4 us -> 32.6 us  [swap(): lax.ppermute(buffer, 'plane', sorted(((i ^ step, i) for i in wanted)))]
  transfers between devices with their start and end apart: 22 -> 22, of which waited for: 13 -> 12; matrix products, arithmetic and copies ran while one was open for 0% -> 0% of each run, Pallas kernels for 21% -> 21%
where the time goes in v6:
time: 108 us
  waiting for transfers between devices  38.2 us (35%)
  starting transfers between devices  34.3 us (32%)
  Pallas kernels  34.1 us (32%)
    ppermute x14, waiting for transfers between devices, swap(): lax.ppermute(buffer, 'plane', sorted(((i ^ step, i) for i in wanted)))  32.6 us
    ppermute x14, starting transfers between devices, swap(): lax.ppermute(buffer, 'plane', sorted(((i ^ step, i) for i in wanted)))  26.1 us
    pallas_call x1, Pallas kernels, packed_shards(): kernel_call(functools.partial(flow_kernel, points), [f32(*whole)] * STEPS...  11.3 us
    ppermute x8, starting transfers between devices, packed_shards(): lax.ppermute(buffer, 'dom', [(i, trace_partner(i, matching, partitions))...  8.21 us
    pallas_call x2, Pallas kernels, packed_shards(): kernel_call(diffuse_kernel, f32(*state_shape), [pltpu.VMEM((nodes, GROUP,...  5.64 us
    ppermute x8, waiting for transfers between devices, packed_shards(): lax.ppermute(buffer, 'dom', [(i, trace_partner(i, matching, partitions))...  5.6 us
    pallas_call x2, Pallas kernels, packed_shards(): kernel_call(functools.partial(update_kernel, back_plans), [f32(*state_sha...  3.12 us
    pallas_call x8, Pallas kernels, packed_shards(): kernel_call(functools.partial(fields_kernel, gaps, len(parts) > 1), f32(3...  2.42 us
  transfers between devices with their start and end apart: 22, of which 12 were waited for; matrix products, arithmetic and copies ran while one was open for 0% of the time, Pallas kernels for 21%

profile of v6, /device:TPU:0, one launch (start us, length us, event | category | flops | bytes accessed | tf_op | source)
XLA Modules:
  0.0 107.9 jit_solution(2644903613760966038)
XLA Ops:
  0.0 2.1 %shard_map.101 = (f32[9,48,384]{2,1,0:T(8,128)S(1)}, f32[9,48,384]{2,1,0:T(8,128)S(1)}, f32[48,1536]{1,0:T(8,128)S(1)}) custom-call(f32[3,9,9,16,32]{4,3,2,1,0:T(8,128)} %bitcast.8, f32[24,384]{1,0:T(8,128)} %constant.10.clone.far_bands.bands), custom_call_target="tpu_custom_call" | custom-call | flops 4000000 | bytes 4000000 | tf_op jit(solution)/shard_map/pallas_call | solution.py:968
  2.1 4.2 %collective-permute-start.3 = (f32[48,1536]{1,0:T(8,128)S(1)}, f32[48,1536]{1,0:T(8,128)S(1)}, u32[]{:S(2)}, u32[]{:S(2)}) collective-permute-start(f32[48,1536]{1,0:T(8,128)S(1)} %get-tuple-element.46), channel_id=1, source_target_pairs={{0,2},{1,3},{2,0},{3,1},{4,6},{5,7},{6,4},{7,5},{8,10},{9,11},{10,... | collective-permute-start | bytes 884744 | tf_op jit(solution)/shard_map/ppermute | solution.py:928
  7.1 1.2 %shard_map.102 = (f32[48,1536]{1,0:T(8,128)S(1)}, f32[48,1536]{1,0:T(8,128)S(1)}, f32[48,1408]{1,0:T(8,128)S(1)}, f32[48,128]{1,0:T(8,128)S(1)}) custom-call(f32[9,48,384]{2,1,0:T(8,128)S(1)} %get-tuple-element.41.state, f32[9,48,384]{2,1,0:T(8,128)S(1)} %get-tuple-element.42.xi, f32[24,384]{1,0:T(8,128)S(1)} %copy-done.2), custom_call_target="tpu_custom_call" | custom-call | flops 1000000 | bytes 2000000 | tf_op jit(solution)/shard_map/pallas_call | solution.py:957
  8.3 1.6 %collective-permute-start.2 = (f32[48,1536]{1,0:T(8,128)S(1)}, f32[48,1536]{1,0:T(8,128)S(1)}, u32[]{:S(2)}, u32[]{:S(2)}) collective-permute-start(f32[48,1536]{1,0:T(8,128)S(1)} %get-tuple-element.45), channel_id=1, source_target_pairs={{0,1},{1,0},{2,3},{3,2},{4,5},{5,4},{6,7},{7,6},{8,9},{9,8},{10,11... | collective-permute-start | bytes 884744 | tf_op jit(solution)/shard_map/ppermute | solution.py:928
  10.9 11.3 %shard_map.107 = (f32[12,64,768]{2,1,0:T(8,128)S(1)}, f32[12,64,768]{2,1,0:T(8,128)S(1)}) custom-call(f32[12,2,41472]{2,1,0:T(2,128)S(1)} %bitcast.5, f32[4,32]{1,0:T(4,128)S(1)} %copy-done.7), custom_call_target="tpu_custom_call" | custom-call | flops 4000000 | bytes 9000000 | tf_op jit(solution)/shard_map/pallas_call | solution.py:979
  22.5 5.1 %collective-permute-done.2.source = f32[48,1536]{1,0:T(8,128)S(1)} collective-permute-done((f32[48,1536]{1,0:T(8,128)S(1)}, f32[48,1536]{1,0:T(8,128)S(1)}, u32[]{:S(2)}, u32[]{:S(2)}) %collective-permute-start.2) | collective-permute-done | bytes 294944 | tf_op jit(solution)/shard_map/ppermute | solution.py:928
  30.0 5.8 %collective-permute-start.4 = (f32[8,3968]{1,0:T(8,128)S(1)}, f32[8,3968]{1,0:T(8,128)S(1)}, u32[]{:S(2)}, u32[]{:S(2)}) collective-permute-start(f32[8,3968]{1,0:T(8,128)S(1)} %get-tuple-element.50), channel_id=1, source_target_pairs={{0,2},{1,3},{2,0},{3,1},{4,6},{5,7},{6,4},{7,5},{8,10},{9,11},{10,... | collective-permute-start | bytes 380936 | tf_op jit(solution)/shard_map/ppermute | solution.py:928
  36.7 2.8 %shard_map.110.local_sum = f32[9,48,384]{2,1,0:T(8,128)S(1)} custom-call(f32[9,48,384]{2,1,0:T(8,128)S(1)} %get-tuple-element.41.state, f32[4,32]{1,0:T(4,128)S(1)} %copy-done.7, f32[24,384]{1,0:T(8,128)S(1)} %copy-done.3), custom_call_target="tpu_custom_call" | custom-call | flops 12000000 | bytes 2000000 | tf_op jit(solution)/shard_map/pallas_call | solution.py:1024
  39.5 5.6 %collective-permute-done.4.in1 = f32[8,3968]{1,0:T(8,128)S(1)} collective-permute-done((f32[8,3968]{1,0:T(8,128)S(1)}, f32[8,3968]{1,0:T(8,128)S(1)}, u32[]{:S(2)}, u32[]{:S(2)}) %collective-permute-start.4) | collective-permute-done | bytes 127008 | tf_op jit(solution)/shard_map/ppermute | solution.py:928
  45.2 1.1 collective-permute-done.6.in3
  46.2 1.6 %shard_map.111 = (f32[9,48,384]{2,1,0:T(8,128)S(1)}, f32[9,48,128]{2,1,0:T(8,128)S(1)}, f32[48,256]{1,0:T(8,128)S(1)}, f32[48,256]{1,0:T(8,128)S(1)}, f32[48,256]{1,0:T(8,128)S(1)}, /*index=5*/f32[48,256]{1,0:T(8,128)S(1)}) custom-call(f32[8,3968]{1,0:T(8,128)S(1)} %get-tuple-element.49.in0, f32[8,3968]{1,0:T(8,128)S(1)} %collective-permute-done.4.in1, ...), custom_call_target="tpu_custom_call" | custom-call | flops 2000000 | bytes 3000000 | tf_op jit(solution)/shard_map/pallas_call | solution.py:1031
  47.9 2.5 %collective-permute-start.7 = (f32[48,256]{1,0:T(8,128)S(1)}, f32[48,256]{1,0:T(8,128)S(1)}, u32[]{:S(2)}, u32[]{:S(2)}) collective-permute-start(f32[48,256]{1,0:T(8,128)S(1)} %get-tuple-element.55), channel_id=1, source_target_pairs={{0,24},{4,28},{8,16},{12,20},{16,8},{20,12},{24,0},{28,4},{1,25},{... | collective-permute-start | bytes 147464 | tf_op jit(solution)/shard_map/ppermute | solution.py:1039
  50.6 1.5 %collective-permute-start.9 = (f32[48,256]{1,0:T(8,128)S(1)}, f32[48,256]{1,0:T(8,128)S(1)}, u32[]{:S(2)}, u32[]{:S(2)}) collective-permute-start(f32[48,256]{1,0:T(8,128)S(1)} %get-tuple-element.57), channel_id=1, source_target_pairs={{0,8},{4,12},{8,0},{12,4},{16,24},{20,28},{24,16},{28,20},{1,9},{5... | collective-permute-start | bytes 147464 | tf_op jit(solution)/shard_map/ppermute | solution.py:1039
  52.9 1.9 %collective-permute-done.8.r1 = f32[48,256]{1,0:T(8,128)S(1)} collective-permute-done((f32[48,256]{1,0:T(8,128)S(1)}, f32[48,256]{1,0:T(8,128)S(1)}, u32[]{:S(2)}, u32[]{:S(2)}) %collective-permute-start.8) | collective-permute-done | bytes 49184 | tf_op jit(solution)/shard_map/ppermute | solution.py:1039
  55.4 1.2 %shard_map.113 = (f32[9,48,384]{2,1,0:T(8,128)S(1)}, f32[9,48,384]{2,1,0:T(8,128)S(1)}, f32[48,1536]{1,0:T(8,128)S(1)}) custom-call(s32[24,128]{1,0:T(8,128)S(1)} %shard_map.100.table, f32[9,48,384]{2,1,0:T(8,128)S(1)} %get-tuple-element.53.updated, f32[9,48,128]{2,1,0:T(8,128)S(1)} %shard_map.112.own, f32[48,256]{1,0:T(8,128)S(1)} %collective-permute-done.7.r0, ...), custom_call_target="tpu_custom_call" | custom-call | flops 6000000 | bytes 4000000 | tf_op jit(solution)/shard_map/pallas_call | solution.py:1046
  56.6 1.1 %collective-permute-start.14 = (f32[48,1536]{1,0:T(8,128)S(1)}, f32[48,1536]{1,0:T(8,128)S(1)}, u32[]{:S(2)}, u32[]{:S(2)}) collective-permute-start(f32[48,1536]{1,0:T(8,128)S(1)} %get-tuple-element.64), channel_id=1, source_target_pairs={{0,2},{1,3},{2,0},{3,1},{4,6},{5,7},{6,4},{7,5},{8,10},{9,11},{10,... | collective-permute-start | bytes 884744 | tf_op jit(solution)/shard_map/ppermute | solution.py:928
  57.7 1.2 %shard_map.114 = (f32[48,1536]{1,0:T(8,128)S(1)}, f32[48,1536]{1,0:T(8,128)S(1)}, f32[48,1408]{1,0:T(8,128)S(1)}, f32[48,128]{1,0:T(8,128)S(1)}) custom-call(f32[9,48,384]{2,1,0:T(8,128)S(1)} %get-tuple-element.59.state, f32[9,48,384]{2,1,0:T(8,128)S(1)} %get-tuple-element.60.xi, f32[24,384]{1,0:T(8,128)S(1)} %copy-done.3), custom_call_target="tpu_custom_call" | custom-call | flops 1000000 | bytes 2000000 | tf_op jit(solution)/shard_map/pallas_call | solution.py:957
  58.9 1.2 %collective-permute-start.13 = (f32[48,1536]{1,0:T(8,128)S(1)}, f32[48,1536]{1,0:T(8,128)S(1)}, u32[]{:S(2)}, u32[]{:S(2)}) collective-permute-start(f32[48,1536]{1,0:T(8,128)S(1)} %get-tuple-element.63), channel_id=1, source_target_pairs={{0,1},{1,0},{2,3},{3,2},{4,5},{5,4},{6,7},{7,6},{8,9},{9,8},{10,11... | collective-permute-start | bytes 884744 | tf_op jit(solution)/shard_map/ppermute | solution.py:928
  60.1 2.4 %collective-permute-start.11 = (f32[48,1408]{1,0:T(8,128)S(1)}, f32[48,1408]{1,0:T(8,128)S(1)}, u32[]{:S(2)}, u32[]{:S(2)}) collective-permute-start(f32[48,1408]{1,0:T(8,128)S(1)} %get-tuple-element.61), channel_id=1, source_target_pairs={{0,3},{1,2},{2,1},{3,0},{4,7},{5,6},{6,5},{7,4},{8,11},{9,10},{10,... | collective-permute-start | bytes 811016 | tf_op jit(solution)/shard_map/ppermute | solution.py:928
  63.7 10.7 %collective-permute-done.14.source = f32[48,1536]{1,0:T(8,128)S(1)} collective-permute-done((f32[48,1536]{1,0:T(8,128)S(1)}, f32[48,1536]{1,0:T(8,128)S(1)}, u32[]{:S(2)}, u32[]{:S(2)}) %collective-permute-start.14) | collective-permute-done | bytes 294944 | tf_op jit(solution)/shard_map/ppermute | solution.py:928
  75.8 4.4 %collective-permute-done.11.source = f32[48,1408]{1,0:T(8,128)S(1)} collective-permute-done((f32[48,1408]{1,0:T(8,128)S(1)}, f32[48,1408]{1,0:T(8,128)S(1)}, u32[]{:S(2)}, u32[]{:S(2)}) %collective-permute-start.11) | collective-permute-done | bytes 270368 | tf_op jit(solution)/shard_map/ppermute | solution.py:928
  81.5 5.7 %collective-permute-start.15 = (f32[8,3968]{1,0:T(8,128)S(1)}, f32[8,3968]{1,0:T(8,128)S(1)}, u32[]{:S(2)}, u32[]{:S(2)}) collective-permute-start(f32[8,3968]{1,0:T(8,128)S(1)} %get-tuple-element.68), channel_id=1, source_target_pairs={{0,2},{1,3},{2,0},{3,1},{4,6},{5,7},{6,4},{7,5},{8,10},{9,11},{10,... | collective-permute-start | bytes 380936 | tf_op jit(solution)/shard_map/ppermute | solution.py:928
  87.1 1.8 %collective-permute-start.16 = (f32[8,3968]{1,0:T(8,128)S(1)}, f32[8,3968]{1,0:T(8,128)S(1)}, u32[]{:S(2)}, u32[]{:S(2)}) collective-permute-start(f32[8,3968]{1,0:T(8,128)S(1)} %get-tuple-element.69), channel_id=1, source_target_pairs={{0,3},{1,2},{2,1},{3,0},{4,7},{5,6},{6,5},{7,4},{8,11},{9,10},{10,... | collective-permute-start | bytes 380936 | tf_op jit(solution)/shard_map/ppermute | solution.py:928
  89.0 2.8 %shard_map.121.local_sum = f32[9,48,384]{2,1,0:T(8,128)S(1)} custom-call(f32[9,48,384]{2,1,0:T(8,128)S(1)} %get-tuple-element.59.state, f32[4,32]{1,0:T(4,128)S(1)} %copy-done.7, f32[24,384]{1,0:T(8,128)S(1)} %copy-done.3), custom_call_target="tpu_custom_call" | custom-call | flops 12000000 | bytes 2000000 | tf_op jit(solution)/shard_map/pallas_call | solution.py:1024
  91.8 4.9 %collective-permute-done.15.in1 = f32[8,3968]{1,0:T(8,128)S(1)} collective-permute-done((f32[8,3968]{1,0:T(8,128)S(1)}, f32[8,3968]{1,0:T(8,128)S(1)}, u32[]{:S(2)}, u32[]{:S(2)}) %collective-permute-start.15) | collective-permute-done | bytes 127008 | tf_op jit(solution)/shard_map/ppermute | solution.py:928
  97.5 1.6 %shard_map.122 = (f32[9,48,384]{2,1,0:T(8,128)S(1)}, f32[9,48,128]{2,1,0:T(8,128)S(1)}, f32[48,256]{1,0:T(8,128)S(1)}, f32[48,256]{1,0:T(8,128)S(1)}, f32[48,256]{1,0:T(8,128)S(1)}, /*index=5*/f32[48,256]{1,0:T(8,128)S(1)}) custom-call(f32[8,3968]{1,0:T(8,128)S(1)} %get-tuple-element.67.in0, f32[8,3968]{1,0:T(8,128)S(1)} %collective-permute-done.15.in1, ...), custom_call_target="tpu_custom_call" | custom-call | flops 2000000 | bytes 3000000 | tf_op jit(solution)/shard_map/pallas_call | solution.py:1031
  99.1 1.5 %collective-permute-start.18 = (f32[48,256]{1,0:T(8,128)S(1)}, f32[48,256]{1,0:T(8,128)S(1)}, u32[]{:S(2)}, u32[]{:S(2)}) collective-permute-start(f32[48,256]{1,0:T(8,128)S(1)} %get-tuple-element.73), channel_id=1, source_target_pairs={{0,24},{4,28},{8,16},{12,20},{16,8},{20,12},{24,0},{28,4},{1,25},{... | collective-permute-start | bytes 147464 | tf_op jit(solution)/shard_map/ppermute | solution.py:1039
  100.6 1.0 collective-permute-start.20
  101.6 1.3 %collective-permute-start.21 = (f32[48,256]{1,0:T(8,128)S(1)}, f32[48,256]{1,0:T(8,128)S(1)}, u32[]{:S(2)}, u32[]{:S(2)}) collective-permute-start(f32[48,256]{1,0:T(8,128)S(1)} %get-tuple-element.76), channel_id=1, source_target_pairs={{0,4},{4,0},{8,12},{12,8},{16,20},{20,16},{24,28},{28,24},{1,5},{5... | collective-permute-start | bytes 147464 | tf_op jit(solution)/shard_map/ppermute | solution.py:1039
  103.0 1.1 %collective-permute-done.18.r0 = f32[48,256]{1,0:T(8,128)S(1)} collective-permute-done((f32[48,256]{1,0:T(8,128)S(1)}, f32[48,256]{1,0:T(8,128)S(1)}, u32[]{:S(2)}, u32[]{:S(2)}) %collective-permute-start.18) | collective-permute-done | bytes 49184 | tf_op jit(solution)/shard_map/ppermute | solution.py:1039
  104.1 1.4 %collective-permute-done.19.r1 = f32[48,256]{1,0:T(8,128)S(1)} collective-permute-done((f32[48,256]{1,0:T(8,128)S(1)}, f32[48,256]{1,0:T(8,128)S(1)}, u32[]{:S(2)}, u32[]{:S(2)}) %collective-permute-start.19) | collective-permute-done | bytes 49184 | tf_op jit(solution)/shard_map/ppermute | solution.py:1039
  105.5 2.2 %shard_map.124 = f32[3,9,9,16,32]{4,3,2,1,0:T(8,128)} custom-call(s32[24,128]{1,0:T(8,128)S(1)} %shard_map.100.table, f32[9,48,384]{2,1,0:T(8,128)S(1)} %get-tuple-element.71.updated, f32[9,48,128]{2,1,0:T(8,128)S(1)} %shard_map.123.own, f32[48,256]{1,0:T(8,128)S(1)} %collective-permute-done.18.r0, f32[48,256]{1,0:T(8,128)S(1)} %collective-permute-done.19.r1, ...), custom_call_target="tpu_custom_call" | custom-call | flops 2000000 | bytes 3000000 | tf_op jit(solution)/shard_map/pallas_call | solution.py:1055
  (57 shorter events, 11.6 us)
Async XLA Ops:
  0.0 10.6 %copy-start = (f32[4,24,768]{2,1,0:T(8,128)S(1)}, f32[4,24,768]{2,1,0:T(8,128)}, u32[]{:S(2)}) copy-start(f32[4,24,768]{2,1,0:T(8,128)} %constant.11.clone.refs_0_.refs_1_) | copy-start | bytes 884740
  0.0 10.9 %copy-start.1 = (f32[2,12,41472]{2,0,1:T(2,128)S(1)}, f32[2,12,41472]{2,0,1:T(2,128)}, u32[]{:S(2)}) copy-start(f32[2,12,41472]{2,0,1:T(2,128)} %param.12) | copy-start | bytes 11943940
  2.1 20.1 %collective-permute-start.3 = (f32[48,1536]{1,0:T(8,128)S(1)}, f32[48,1536]{1,0:T(8,128)S(1)}, u32[]{:S(2)}, u32[]{:S(2)}) collective-permute-start(f32[48,1536]{1,0:T(8,128)S(1)} %get-tuple-element.46), channel_id=1, source_target_pairs={{0,2},{1,3},{2,0},{3,1},{4,6},{5,7},{6,4},{7,5},{8,10},{9,11},{10,... | collective-permute-start | bytes 884744 | tf_op jit(solution)/shard_map/ppermute | solution.py:928
  6.3 0.8 copy-start.2
  7.1 3.8 %copy-start.7 = (f32[4,32]{1,0:T(4,128)S(1)}, f32[4,32]{1,0:T(4,128)}, u32[]{:S(2)}) copy-start(f32[4,32]{1,0:T(4,128)} %metric.5) | copy-start | bytes 1540
  8.3 19.3 %collective-permute-start.2 = (f32[48,1536]{1,0:T(8,128)S(1)}, f32[48,1536]{1,0:T(8,128)S(1)}, u32[]{:S(2)}, u32[]{:S(2)}) collective-permute-start(f32[48,1536]{1,0:T(8,128)S(1)} %get-tuple-element.45), channel_id=1, source_target_pairs={{0,1},{1,0},{2,3},{3,2},{4,5},{5,4},{6,7},{7,6},{8,9},{9,8},{10,11... | collective-permute-start | bytes 884744 | tf_op jit(solution)/shard_map/ppermute | solution.py:928
  9.8 18.8 %collective-permute-start = (f32[48,1408]{1,0:T(8,128)S(1)}, f32[48,1408]{1,0:T(8,128)S(1)}, u32[]{:S(2)}, u32[]{:S(2)}) collective-permute-start(f32[48,1408]{1,0:T(8,128)S(1)} %get-tuple-element.43), channel_id=1, source_target_pairs={{0,3},{1,2},{2,1},{3,0},{4,7},{5,6},{6,5},{7,4},{8,11},{9,10},{10,... | collective-permute-start | bytes 811016 | tf_op jit(solution)/shard_map/ppermute | solution.py:928
  9.9 18.8 %collective-permute-start.1 = (f32[48,128]{1,0:T(8,128)S(1)}, f32[48,128]{1,0:T(8,128)S(1)}, u32[]{:S(2)}, u32[]{:S(2)}) collective-permute-start(f32[48,128]{1,0:T(8,128)S(1)} %get-tuple-element.44), channel_id=1, source_target_pairs={{1,2},{2,1},{5,6},{6,5},{9,10},{10,9},{13,14},{14,13},{17,18},{18,... | collective-permute-start | bytes 73736 | tf_op jit(solution)/shard_map/ppermute | solution.py:928
  10.9 17.0 %copy-start.4 = (bf16[4,128,144]{2,1,0:T(8,128)(2,1)S(1)}, bf16[4,128,144]{2,1,0:T(8,128)(2,1)}, u32[]{:S(2)}) copy-start(bf16[4,128,144]{2,1,0:T(8,128)(2,1)} %constant.12.clone.to_span) | copy-start | bytes 442372
  27.9 1.1 %copy-start.5 = (bf16[4,128,48]{2,1,0:T(8,128)(2,1)S(1)}, bf16[4,128,48]{2,1,0:T(8,128)(2,1)}, u32[]{:S(2)}) copy-start(bf16[4,128,48]{2,1,0:T(8,128)(2,1)} %constant.13.clone.to_span) | copy-start | bytes 147460
  27.9 1.1 %copy-start.6 = (bf16[4,64,192]{2,1,0:T(8,128)(2,1)S(1)}, bf16[4,64,192]{2,1,0:T(8,128)(2,1)}, u32[]{:S(2)}) copy-start(bf16[4,64,192]{2,1,0:T(8,128)(2,1)} %constant.14.clone.to_modes) | copy-start | bytes 294916
  28.6 7.8 %copy-start.8 = (s32[1,5,24]{2,0,1:T(1,128)S(1)}, s32[1,5,24]{2,0,1:T(1,128)}, u32[]{:S(2)}) copy-start(s32[1,5,24]{2,0,1:T(1,128)} %param.13) | copy-start | bytes 1444
  28.6 7.8 %copy-start.9 = (s32[1,5,24]{2,0,1:T(1,128)S(1)}, s32[1,5,24]{2,0,1:T(1,128)}, u32[]{:S(2)}) copy-start(s32[1,5,24]{2,0,1:T(1,128)} %param.14) | copy-start | bytes 1444
  28.7 8.0 %copy-start.3 = (f32[24,384]{1,0:T(8,128)S(1)}, f32[24,384]{1,0:T(8,128)}, u32[]{:S(2)}) copy-start(f32[24,384]{1,0:T(8,128)} %constant.10.clone.far_bands.bands) | copy-start | bytes 110596
  30.0 15.2 %collective-permute-start.4 = (f32[8,3968]{1,0:T(8,128)S(1)}, f32[8,3968]{1,0:T(8,128)S(1)}, u32[]{:S(2)}, u32[]{:S(2)}) collective-permute-start(f32[8,3968]{1,0:T(8,128)S(1)} %get-tuple-element.50), channel_id=1, source_target_pairs={{0,2},{1,3},{2,0},{3,1},{4,6},{5,7},{6,4},{7,5},{8,10},{9,11},{10,... | collective-permute-start | bytes 380936 | tf_op jit(solution)/shard_map/ppermute | solution.py:928
  35.8 9.3 %collective-permute-start.5 = (f32[8,3968]{1,0:T(8,128)S(1)}, f32[8,3968]{1,0:T(8,128)S(1)}, u32[]{:S(2)}, u32[]{:S(2)}) collective-permute-start(f32[8,3968]{1,0:T(8,128)S(1)} %get-tuple-element.51), channel_id=1, source_target_pairs={{0,3},{1,2},{2,1},{3,0},{4,7},{5,6},{6,5},{7,4},{8,11},{9,10},{10,... | collective-permute-start | bytes 380936 | tf_op jit(solution)/shard_map/ppermute | solution.py:928
  36.3 10.0 %collective-permute-start.6 = (f32[8,3968]{1,0:T(8,128)S(1)}, f32[8,3968]{1,0:T(8,128)S(1)}, u32[]{:S(2)}, u32[]{:S(2)}) collective-permute-start(f32[8,3968]{1,0:T(8,128)S(1)} %get-tuple-element.52), channel_id=1, source_target_pairs={{0,1},{1,0},{2,3},{3,2},{4,5},{5,4},{6,7},{7,6},{8,9},{9,8},{10,11... | collective-permute-start | bytes 380936 | tf_op jit(solution)/shard_map/ppermute | solution.py:928
  47.8 4.5 %collective-permute-start.10 = (f32[48,256]{1,0:T(8,128)S(1)}, f32[48,256]{1,0:T(8,128)S(1)}, u32[]{:S(2)}, u32[]{:S(2)}) collective-permute-start(f32[48,256]{1,0:T(8,128)S(1)} %get-tuple-element.58), channel_id=1, source_target_pairs={{0,4},{4,0},{8,12},{12,8},{16,20},{20,16},{24,28},{28,24},{1,5},{5... | collective-permute-start | bytes 147464 | tf_op jit(solution)/shard_map/ppermute | solution.py:1039
  47.9 5.1 %collective-permute-start.7 = (f32[48,256]{1,0:T(8,128)S(1)}, f32[48,256]{1,0:T(8,128)S(1)}, u32[]{:S(2)}, u32[]{:S(2)}) collective-permute-start(f32[48,256]{1,0:T(8,128)S(1)} %get-tuple-element.55), channel_id=1, source_target_pairs={{0,24},{4,28},{8,16},{12,20},{16,8},{20,12},{24,0},{28,4},{1,25},{... | collective-permute-start | bytes 147464 | tf_op jit(solution)/shard_map/ppermute | solution.py:1039
  50.4 4.4 %collective-permute-start.8 = (f32[48,256]{1,0:T(8,128)S(1)}, f32[48,256]{1,0:T(8,128)S(1)}, u32[]{:S(2)}, u32[]{:S(2)}) collective-permute-start(f32[48,256]{1,0:T(8,128)S(1)} %get-tuple-element.56), channel_id=1, source_target_pairs={{0,28},{4,8},{8,4},{12,16},{16,12},{20,24},{24,20},{28,0},{1,29},{... | collective-permute-start | bytes 147464 | tf_op jit(solution)/shard_map/ppermute | solution.py:1039
  50.6 4.8 %collective-permute-start.9 = (f32[48,256]{1,0:T(8,128)S(1)}, f32[48,256]{1,0:T(8,128)S(1)}, u32[]{:S(2)}, u32[]{:S(2)}) collective-permute-start(f32[48,256]{1,0:T(8,128)S(1)} %get-tuple-element.57), channel_id=1, source_target_pairs={{0,8},{4,12},{8,0},{12,4},{16,24},{20,28},{24,16},{28,20},{1,9},{5... | collective-permute-start | bytes 147464 | tf_op jit(solution)/shard_map/ppermute | solution.py:1039
  56.6 17.8 %collective-permute-start.14 = (f32[48,1536]{1,0:T(8,128)S(1)}, f32[48,1536]{1,0:T(8,128)S(1)}, u32[]{:S(2)}, u32[]{:S(2)}) collective-permute-start(f32[48,1536]{1,0:T(8,128)S(1)} %get-tuple-element.64), channel_id=1, source_target_pairs={{0,2},{1,3},{2,0},{3,1},{4,6},{5,7},{6,4},{7,5},{8,10},{9,11},{10,... | collective-permute-start | bytes 884744 | tf_op jit(solution)/shard_map/ppermute | solution.py:928
  58.9 15.9 %collective-permute-start.13 = (f32[48,1536]{1,0:T(8,128)S(1)}, f32[48,1536]{1,0:T(8,128)S(1)}, u32[]{:S(2)}, u32[]{:S(2)}) collective-permute-start(f32[48,1536]{1,0:T(8,128)S(1)} %get-tuple-element.63), channel_id=1, source_target_pairs={{0,1},{1,0},{2,3},{3,2},{4,5},{5,4},{6,7},{7,6},{8,9},{9,8},{10,11... | collective-permute-start | bytes 884744 | tf_op jit(solution)/shard_map/ppermute | solution.py:928
  60.1 20.1 %collective-permute-start.11 = (f32[48,1408]{1,0:T(8,128)S(1)}, f32[48,1408]{1,0:T(8,128)S(1)}, u32[]{:S(2)}, u32[]{:S(2)}) collective-permute-start(f32[48,1408]{1,0:T(8,128)S(1)} %get-tuple-element.61), channel_id=1, source_target_pairs={{0,3},{1,2},{2,1},{3,0},{4,7},{5,6},{6,5},{7,4},{8,11},{9,10},{10,... | collective-permute-start | bytes 811016 | tf_op jit(solution)/shard_map/ppermute | solution.py:928
  62.6 13.2 %collective-permute-start.12 = (f32[48,128]{1,0:T(8,128)S(1)}, f32[48,128]{1,0:T(8,128)S(1)}, u32[]{:S(2)}, u32[]{:S(2)}) collective-permute-start(f32[48,128]{1,0:T(8,128)S(1)} %get-tuple-element.62), channel_id=1, source_target_pairs={{1,2},{2,1},{5,6},{6,5},{9,10},{10,9},{13,14},{14,13},{17,18},{18,... | collective-permute-start | bytes 73736 | tf_op jit(solution)/shard_map/ppermute | solution.py:928
  81.5 15.2 %collective-permute-start.15 = (f32[8,3968]{1,0:T(8,128)S(1)}, f32[8,3968]{1,0:T(8,128)S(1)}, u32[]{:S(2)}, u32[]{:S(2)}) collective-permute-start(f32[8,3968]{1,0:T(8,128)S(1)} %get-tuple-element.68), channel_id=1, source_target_pairs={{0,2},{1,3},{2,0},{3,1},{4,6},{5,7},{6,4},{7,5},{8,10},{9,11},{10,... | collective-permute-start | bytes 380936 | tf_op jit(solution)/shard_map/ppermute | solution.py:928
  87.1 9.6 %collective-permute-start.16 = (f32[8,3968]{1,0:T(8,128)S(1)}, f32[8,3968]{1,0:T(8,128)S(1)}, u32[]{:S(2)}, u32[]{:S(2)}) collective-permute-start(f32[8,3968]{1,0:T(8,128)S(1)} %get-tuple-element.69), channel_id=1, source_target_pairs={{0,3},{1,2},{2,1},{3,0},{4,7},{5,6},{6,5},{7,4},{8,11},{9,10},{10,... | collective-permute-start | bytes 380936 | tf_op jit(solution)/shard_map/ppermute | solution.py:928
  89.0 8.5 %collective-permute-start.17 = (f32[8,3968]{1,0:T(8,128)S(1)}, f32[8,3968]{1,0:T(8,128)S(1)}, u32[]{:S(2)}, u32[]{:S(2)}) collective-permute-start(f32[8,3968]{1,0:T(8,128)S(1)} %get-tuple-element.70), channel_id=1, source_target_pairs={{0,1},{1,0},{2,3},{3,2},{4,5},{5,4},{6,7},{7,6},{8,9},{9,8},{10,11... | collective-permute-start | bytes 380936 | tf_op jit(solution)/shard_map/ppermute | solution.py:928
  99.1 5.1 %collective-permute-start.18 = (f32[48,256]{1,0:T(8,128)S(1)}, f32[48,256]{1,0:T(8,128)S(1)}, u32[]{:S(2)}, u32[]{:S(2)}) collective-permute-start(f32[48,256]{1,0:T(8,128)S(1)} %get-tuple-element.73), channel_id=1, source_target_pairs={{0,24},{4,28},{8,16},{12,20},{16,8},{20,12},{24,0},{28,4},{1,25},{... | collective-permute-start | bytes 147464 | tf_op jit(solution)/shard_map/ppermute | solution.py:1039
  100.6 4.9 %collective-permute-start.19 = (f32[48,256]{1,0:T(8,128)S(1)}, f32[48,256]{1,0:T(8,128)S(1)}, u32[]{:S(2)}, u32[]{:S(2)}) collective-permute-start(f32[48,256]{1,0:T(8,128)S(1)} %get-tuple-element.74), channel_id=1, source_target_pairs={{0,28},{4,8},{8,4},{12,16},{16,12},{20,24},{24,20},{28,0},{1,29},{... | collective-permute-start | bytes 147464 | tf_op jit(solution)/shard_map/ppermute | solution.py:1039
  100.6 4.9 %collective-permute-start.20 = (f32[48,256]{1,0:T(8,128)S(1)}, f32[48,256]{1,0:T(8,128)S(1)}, u32[]{:S(2)}, u32[]{:S(2)}) collective-permute-start(f32[48,256]{1,0:T(8,128)S(1)} %get-tuple-element.75), channel_id=1, source_target_pairs={{0,8},{4,12},{8,0},{12,4},{16,24},{20,28},{24,16},{28,20},{1,9},{5... | collective-permute-start | bytes 147464 | tf_op jit(solution)/shard_map/ppermute | solution.py:1039
  101.6 3.9 %collective-permute-start.21 = (f32[48,256]{1,0:T(8,128)S(1)}, f32[48,256]{1,0:T(8,128)S(1)}, u32[]{:S(2)}, u32[]{:S(2)}) collective-permute-start(f32[48,256]{1,0:T(8,128)S(1)} %get-tuple-element.76), channel_id=1, source_target_pairs={{0,4},{4,0},{8,12},{12,8},{16,20},{20,16},{24,28},{28,24},{1,5},{5... | collective-permute-start | bytes 147464 | tf_op jit(solution)/shard_map/ppermute | solution.py:1039

commit v7 on v6

--- a/solution.py
+++ b/solution.py
@@ -736,11 +736,11 @@
 
 def trace_blocks(me):
     odd, late = lax.rem(me, 2), lax.rem(me, 4) // 2
-    return 4 * late, 1 + 2 * odd, 4 - 4 * late, 3 - 2 * odd
+    return 1 + 2 * odd, 4 * late, 4 - 4 * late, 3 - 2 * odd
 
 
 def trace_partner(me, matching, size):
-    step, start = ((2, 2), (1, 1), (2, 0), (1, 0))[matching]
+    step, start = ((1, 1), (2, 2), (2, 0), (1, 0))[matching]
     return (((me + start) ^ step) - start) % size
 
 

time: 108 us -> 107 us (level)
  starting transfers between devices: 34.3 us -> 33 us
    ppermute x14, starting transfers between devices: 26.1 us -> 24.8 us  [swap(): lax.ppermute(buffer, 'plane', sorted(((i ^ step, i) for i in wanted)))]
  transfers between devices with their start and end apart: 22 -> 22, of which waited for: 12 -> 10; matrix products, arithmetic and copies ran while one was open for 0% -> 0% of each run, Pallas kernels for 21% -> 21%
where the time goes in v7:
time: 107 us
  waiting for transfers between devices  38.5 us (36%)
  Pallas kernels  34.1 us (32%)
  starting transfers between devices  33 us (31%)
    ppermute x14, waiting for transfers between devices, swap(): lax.ppermute(buffer, 'plane', sorted(((i ^ step, i) for i in wanted)))  32.9 us
    ppermute x14, starting transfers between devices, swap(): lax.ppermute(buffer, 'plane', sorted(((i ^ step, i) for i in wanted)))  24.8 us
    pallas_call x1, Pallas kernels, packed_shards(): kernel_call(functools.partial(flow_kernel, points), [f32(*whole)] * STEPS...  11.3 us
    ppermute x8, starting transfers between devices, packed_shards(): lax.ppermute(buffer, 'dom', [(i, trace_partner(i, matching, partitions))...  8.18 us
    pallas_call x2, Pallas kernels, packed_shards(): kernel_call(diffuse_kernel, f32(*state_shape), [pltpu.VMEM((nodes, GROUP,...  5.64 us
    ppermute x8, waiting for transfers between devices, packed_shards(): lax.ppermute(buffer, 'dom', [(i, trace_partner(i, matching, partitions))...  5.63 us
    pallas_call x2, Pallas kernels, packed_shards(): kernel_call(functools.partial(update_kernel, back_plans), [f32(*state_sha...  3.12 us
    pallas_call x8, Pallas kernels, packed_shards(): kernel_call(functools.partial(fields_kernel, gaps, len(parts) > 1), f32(3...  2.42 us
  transfers between devices with their start and end apart: 22, of which 10 were waited for; matrix products, arithmetic and copies ran while one was open for 0% of the time, Pallas kernels for 21%

profile of v7, /device:TPU:0, one launch (start us, length us, event | category | flops | bytes accessed | tf_op | source)
XLA Modules:
  0.0 106.9 jit_solution(8487332359904851867)
XLA Ops:
  0.0 2.1 %shard_map.101 = (f32[9,48,384]{2,1,0:T(8,128)S(1)}, f32[9,48,384]{2,1,0:T(8,128)S(1)}, f32[48,1536]{1,0:T(8,128)S(1)}) custom-call(f32[3,9,9,16,32]{4,3,2,1,0:T(8,128)} %bitcast.8, f32[24,384]{1,0:T(8,128)} %constant.10.clone.far_bands.bands), custom_call_target="tpu_custom_call" | custom-call | flops 4000000 | bytes 4000000 | tf_op jit(solution)/shard_map/pallas_call | solution.py:968
  2.1 4.2 %collective-permute-start.3 = (f32[48,1536]{1,0:T(8,128)S(1)}, f32[48,1536]{1,0:T(8,128)S(1)}, u32[]{:S(2)}, u32[]{:S(2)}) collective-permute-start(f32[48,1536]{1,0:T(8,128)S(1)} %get-tuple-element.46), channel_id=1, source_target_pairs={{0,2},{1,3},{2,0},{3,1},{4,6},{5,7},{6,4},{7,5},{8,10},{9,11},{10,... | collective-permute-start | bytes 884744 | tf_op jit(solution)/shard_map/ppermute | solution.py:928
  7.1 1.2 %shard_map.102 = (f32[48,1536]{1,0:T(8,128)S(1)}, f32[48,1536]{1,0:T(8,128)S(1)}, f32[48,1408]{1,0:T(8,128)S(1)}, f32[48,128]{1,0:T(8,128)S(1)}) custom-call(f32[9,48,384]{2,1,0:T(8,128)S(1)} %get-tuple-element.41.state, f32[9,48,384]{2,1,0:T(8,128)S(1)} %get-tuple-element.42.xi, f32[24,384]{1,0:T(8,128)S(1)} %copy-done.2), custom_call_target="tpu_custom_call" | custom-call | flops 1000000 | bytes 2000000 | tf_op jit(solution)/shard_map/pallas_call | solution.py:957
  8.3 1.6 %collective-permute-start.2 = (f32[48,1536]{1,0:T(8,128)S(1)}, f32[48,1536]{1,0:T(8,128)S(1)}, u32[]{:S(2)}, u32[]{:S(2)}) collective-permute-start(f32[48,1536]{1,0:T(8,128)S(1)} %get-tuple-element.45), channel_id=1, source_target_pairs={{0,1},{1,0},{2,3},{3,2},{4,5},{5,4},{6,7},{7,6},{8,9},{9,8},{10,11... | collective-permute-start | bytes 884744 | tf_op jit(solution)/shard_map/ppermute | solution.py:928
  10.9 11.3 %shard_map.107 = (f32[12,64,768]{2,1,0:T(8,128)S(1)}, f32[12,64,768]{2,1,0:T(8,128)S(1)}) custom-call(f32[12,2,41472]{2,1,0:T(2,128)S(1)} %bitcast.5, f32[4,32]{1,0:T(4,128)S(1)} %copy-done.7), custom_call_target="tpu_custom_call" | custom-call | flops 4000000 | bytes 9000000 | tf_op jit(solution)/shard_map/pallas_call | solution.py:979
  22.5 5.1 %collective-permute-done.2.source = f32[48,1536]{1,0:T(8,128)S(1)} collective-permute-done((f32[48,1536]{1,0:T(8,128)S(1)}, f32[48,1536]{1,0:T(8,128)S(1)}, u32[]{:S(2)}, u32[]{:S(2)}) %collective-permute-start.2) | collective-permute-done | bytes 294944 | tf_op jit(solution)/shard_map/ppermute | solution.py:928
  29.0 1.0 shard_map.109
  30.0 5.8 %collective-permute-start.4 = (f32[8,3968]{1,0:T(8,128)S(1)}, f32[8,3968]{1,0:T(8,128)S(1)}, u32[]{:S(2)}, u32[]{:S(2)}) collective-permute-start(f32[8,3968]{1,0:T(8,128)S(1)} %get-tuple-element.50), channel_id=1, source_target_pairs={{0,2},{1,3},{2,0},{3,1},{4,6},{5,7},{6,4},{7,5},{8,10},{9,11},{10,... | collective-permute-start | bytes 380936 | tf_op jit(solution)/shard_map/ppermute | solution.py:928
  36.7 2.8 %shard_map.110.local_sum = f32[9,48,384]{2,1,0:T(8,128)S(1)} custom-call(f32[9,48,384]{2,1,0:T(8,128)S(1)} %get-tuple-element.41.state, f32[4,32]{1,0:T(4,128)S(1)} %copy-done.7, f32[24,384]{1,0:T(8,128)S(1)} %copy-done.3), custom_call_target="tpu_custom_call" | custom-call | flops 12000000 | bytes 2000000 | tf_op jit(solution)/shard_map/pallas_call | solution.py:1024
  39.5 5.6 %collective-permute-done.4.in1 = f32[8,3968]{1,0:T(8,128)S(1)} collective-permute-done((f32[8,3968]{1,0:T(8,128)S(1)}, f32[8,3968]{1,0:T(8,128)S(1)}, u32[]{:S(2)}, u32[]{:S(2)}) %collective-permute-start.4) | collective-permute-done | bytes 127008 | tf_op jit(solution)/shard_map/ppermute | solution.py:928
  45.2 1.1 %collective-permute-done.6.in3 = f32[8,3968]{1,0:T(8,128)S(1)} collective-permute-done((f32[8,3968]{1,0:T(8,128)S(1)}, f32[8,3968]{1,0:T(8,128)S(1)}, u32[]{:S(2)}, u32[]{:S(2)}) %collective-permute-start.6) | collective-permute-done | bytes 127008 | tf_op jit(solution)/shard_map/ppermute | solution.py:928
  46.2 1.6 %shard_map.111 = (f32[9,48,384]{2,1,0:T(8,128)S(1)}, f32[9,48,128]{2,1,0:T(8,128)S(1)}, f32[48,256]{1,0:T(8,128)S(1)}, f32[48,256]{1,0:T(8,128)S(1)}, f32[48,256]{1,0:T(8,128)S(1)}, /*index=5*/f32[48,256]{1,0:T(8,128)S(1)}) custom-call(f32[8,3968]{1,0:T(8,128)S(1)} %get-tuple-element.49.in0, f32[8,3968]{1,0:T(8,128)S(1)} %collective-permute-done.4.in1, ...), custom_call_target="tpu_custom_call" | custom-call | flops 2000000 | bytes 3000000 | tf_op jit(solution)/shard_map/pallas_call | solution.py:1031
  47.9 2.5 %collective-permute-start.7 = (f32[48,256]{1,0:T(8,128)S(1)}, f32[48,256]{1,0:T(8,128)S(1)}, u32[]{:S(2)}, u32[]{:S(2)}) collective-permute-start(f32[48,256]{1,0:T(8,128)S(1)} %get-tuple-element.55), channel_id=1, source_target_pairs={{0,28},{4,8},{8,4},{12,16},{16,12},{20,24},{24,20},{28,0},{1,29},{... | collective-permute-start | bytes 147464 | tf_op jit(solution)/shard_map/ppermute | solution.py:1039
  51.0 1.4 %collective-permute-start.9 = (f32[48,256]{1,0:T(8,128)S(1)}, f32[48,256]{1,0:T(8,128)S(1)}, u32[]{:S(2)}, u32[]{:S(2)}) collective-permute-start(f32[48,256]{1,0:T(8,128)S(1)} %get-tuple-element.57), channel_id=1, source_target_pairs={{0,8},{4,12},{8,0},{12,4},{16,24},{20,28},{24,16},{28,20},{1,9},{5... | collective-permute-start | bytes 147464 | tf_op jit(solution)/shard_map/ppermute | solution.py:1039
  52.5 2.9 %collective-permute-done.8.r1 = f32[48,256]{1,0:T(8,128)S(1)} collective-permute-done((f32[48,256]{1,0:T(8,128)S(1)}, f32[48,256]{1,0:T(8,128)S(1)}, u32[]{:S(2)}, u32[]{:S(2)}) %collective-permute-start.8) | collective-permute-done | bytes 49184 | tf_op jit(solution)/shard_map/ppermute | solution.py:1039
  55.4 1.2 %shard_map.113 = (f32[9,48,384]{2,1,0:T(8,128)S(1)}, f32[9,48,384]{2,1,0:T(8,128)S(1)}, f32[48,1536]{1,0:T(8,128)S(1)}) custom-call(s32[24,128]{1,0:T(8,128)S(1)} %shard_map.100.table, f32[9,48,384]{2,1,0:T(8,128)S(1)} %get-tuple-element.53.updated, f32[9,48,128]{2,1,0:T(8,128)S(1)} %shard_map.112.own, f32[48,256]{1,0:T(8,128)S(1)} %collective-permute-done.7.r0, ...), custom_call_target="tpu_custom_call" | custom-call | flops 6000000 | bytes 4000000 | tf_op jit(solution)/shard_map/pallas_call | solution.py:1046
  56.6 1.1 %collective-permute-start.14 = (f32[48,1536]{1,0:T(8,128)S(1)}, f32[48,1536]{1,0:T(8,128)S(1)}, u32[]{:S(2)}, u32[]{:S(2)}) collective-permute-start(f32[48,1536]{1,0:T(8,128)S(1)} %get-tuple-element.64), channel_id=1, source_target_pairs={{0,2},{1,3},{2,0},{3,1},{4,6},{5,7},{6,4},{7,5},{8,10},{9,11},{10,... | collective-permute-start | bytes 884744 | tf_op jit(solution)/shard_map/ppermute | solution.py:928
  57.7 1.2 %shard_map.114 = (f32[48,1536]{1,0:T(8,128)S(1)}, f32[48,1536]{1,0:T(8,128)S(1)}, f32[48,1408]{1,0:T(8,128)S(1)}, f32[48,128]{1,0:T(8,128)S(1)}) custom-call(f32[9,48,384]{2,1,0:T(8,128)S(1)} %get-tuple-element.59.state, f32[9,48,384]{2,1,0:T(8,128)S(1)} %get-tuple-element.60.xi, f32[24,384]{1,0:T(8,128)S(1)} %copy-done.3), custom_call_target="tpu_custom_call" | custom-call | flops 1000000 | bytes 2000000 | tf_op jit(solution)/shard_map/pallas_call | solution.py:957
  58.9 1.2 %collective-permute-start.13 = (f32[48,1536]{1,0:T(8,128)S(1)}, f32[48,1536]{1,0:T(8,128)S(1)}, u32[]{:S(2)}, u32[]{:S(2)}) collective-permute-start(f32[48,1536]{1,0:T(8,128)S(1)} %get-tuple-element.63), channel_id=1, source_target_pairs={{0,1},{1,0},{2,3},{3,2},{4,5},{5,4},{6,7},{7,6},{8,9},{9,8},{10,11... | collective-permute-start | bytes 884744 | tf_op jit(solution)/shard_map/ppermute | solution.py:928
  60.1 2.4 %collective-permute-start.11 = (f32[48,1408]{1,0:T(8,128)S(1)}, f32[48,1408]{1,0:T(8,128)S(1)}, u32[]{:S(2)}, u32[]{:S(2)}) collective-permute-start(f32[48,1408]{1,0:T(8,128)S(1)} %get-tuple-element.61), channel_id=1, source_target_pairs={{0,3},{1,2},{2,1},{3,0},{4,7},{5,6},{6,5},{7,4},{8,11},{9,10},{10,... | collective-permute-start | bytes 811016 | tf_op jit(solution)/shard_map/ppermute | solution.py:928
  63.7 15.5 %collective-permute-done.14.source = f32[48,1536]{1,0:T(8,128)S(1)} collective-permute-done((f32[48,1536]{1,0:T(8,128)S(1)}, f32[48,1536]{1,0:T(8,128)S(1)}, u32[]{:S(2)}, u32[]{:S(2)}) %collective-permute-start.14) | collective-permute-done | bytes 294944 | tf_op jit(solution)/shard_map/ppermute | solution.py:928
  80.8 1.0 shard_map.120
  81.8 4.3 %collective-permute-start.15 = (f32[8,3968]{1,0:T(8,128)S(1)}, f32[8,3968]{1,0:T(8,128)S(1)}, u32[]{:S(2)}, u32[]{:S(2)}) collective-permute-start(f32[8,3968]{1,0:T(8,128)S(1)} %get-tuple-element.68), channel_id=1, source_target_pairs={{0,2},{1,3},{2,0},{3,1},{4,6},{5,7},{6,4},{7,5},{8,10},{9,11},{10,... | collective-permute-start | bytes 380936 | tf_op jit(solution)/shard_map/ppermute | solution.py:928
  86.1 1.9 %collective-permute-start.16 = (f32[8,3968]{1,0:T(8,128)S(1)}, f32[8,3968]{1,0:T(8,128)S(1)}, u32[]{:S(2)}, u32[]{:S(2)}) collective-permute-start(f32[8,3968]{1,0:T(8,128)S(1)} %get-tuple-element.69), channel_id=1, source_target_pairs={{0,3},{1,2},{2,1},{3,0},{4,7},{5,6},{6,5},{7,4},{8,11},{9,10},{10,... | collective-permute-start | bytes 380936 | tf_op jit(solution)/shard_map/ppermute | solution.py:928
  88.0 2.8 %shard_map.121.local_sum = f32[9,48,384]{2,1,0:T(8,128)S(1)} custom-call(f32[9,48,384]{2,1,0:T(8,128)S(1)} %get-tuple-element.59.state, f32[4,32]{1,0:T(4,128)S(1)} %copy-done.7, f32[24,384]{1,0:T(8,128)S(1)} %copy-done.3), custom_call_target="tpu_custom_call" | custom-call | flops 12000000 | bytes 2000000 | tf_op jit(solution)/shard_map/pallas_call | solution.py:1024
  90.8 4.6 %collective-permute-done.15.in1 = f32[8,3968]{1,0:T(8,128)S(1)} collective-permute-done((f32[8,3968]{1,0:T(8,128)S(1)}, f32[8,3968]{1,0:T(8,128)S(1)}, u32[]{:S(2)}, u32[]{:S(2)}) %collective-permute-start.15) | collective-permute-done | bytes 127008 | tf_op jit(solution)/shard_map/ppermute | solution.py:928
  95.4 1.1 %collective-permute-done.17.in3 = f32[8,3968]{1,0:T(8,128)S(1)} collective-permute-done((f32[8,3968]{1,0:T(8,128)S(1)}, f32[8,3968]{1,0:T(8,128)S(1)}, u32[]{:S(2)}, u32[]{:S(2)}) %collective-permute-start.17) | collective-permute-done | bytes 127008 | tf_op jit(solution)/shard_map/ppermute | solution.py:928
  96.5 1.6 %shard_map.122 = (f32[9,48,384]{2,1,0:T(8,128)S(1)}, f32[9,48,128]{2,1,0:T(8,128)S(1)}, f32[48,256]{1,0:T(8,128)S(1)}, f32[48,256]{1,0:T(8,128)S(1)}, f32[48,256]{1,0:T(8,128)S(1)}, /*index=5*/f32[48,256]{1,0:T(8,128)S(1)}) custom-call(f32[8,3968]{1,0:T(8,128)S(1)} %get-tuple-element.67.in0, f32[8,3968]{1,0:T(8,128)S(1)} %collective-permute-done.15.in1, ...), custom_call_target="tpu_custom_call" | custom-call | flops 2000000 | bytes 3000000 | tf_op jit(solution)/shard_map/pallas_call | solution.py:1031
  98.2 2.0 %collective-permute-start.19 = (f32[48,256]{1,0:T(8,128)S(1)}, f32[48,256]{1,0:T(8,128)S(1)}, u32[]{:S(2)}, u32[]{:S(2)}) collective-permute-start(f32[48,256]{1,0:T(8,128)S(1)} %get-tuple-element.74), channel_id=1, source_target_pairs={{0,24},{4,28},{8,16},{12,20},{16,8},{20,12},{24,0},{28,4},{1,25},{... | collective-permute-start | bytes 147464 | tf_op jit(solution)/shard_map/ppermute | solution.py:1039
  100.6 1.0 collective-permute-start.21
  103.4 1.2 %collective-permute-done.20.r2 = f32[48,256]{1,0:T(8,128)S(1)} collective-permute-done((f32[48,256]{1,0:T(8,128)S(1)}, f32[48,256]{1,0:T(8,128)S(1)}, u32[]{:S(2)}, u32[]{:S(2)}) %collective-permute-start.20) | collective-permute-done | bytes 49184 | tf_op jit(solution)/shard_map/ppermute | solution.py:1039
  104.5 2.2 %shard_map.124 = f32[3,9,9,16,32]{4,3,2,1,0:T(8,128)} custom-call(s32[24,128]{1,0:T(8,128)S(1)} %shard_map.100.table, f32[9,48,384]{2,1,0:T(8,128)S(1)} %get-tuple-element.71.updated, f32[9,48,128]{2,1,0:T(8,128)S(1)} %shard_map.123.own, f32[48,256]{1,0:T(8,128)S(1)} %collective-permute-done.18.r0, f32[48,256]{1,0:T(8,128)S(1)} %collective-permute-done.19.r1, ...), custom_call_target="tpu_custom_call" | custom-call | flops 2000000 | bytes 3000000 | tf_op jit(solution)/shard_map/pallas_call | solution.py:1055
  (57 shorter events, 10.1 us)
Async XLA Ops:
  0.0 10.6 %copy-start = (f32[4,24,768]{2,1,0:T(8,128)S(1)}, f32[4,24,768]{2,1,0:T(8,128)}, u32[]{:S(2)}) copy-start(f32[4,24,768]{2,1,0:T(8,128)} %constant.11.clone.refs_0_.refs_1_) | copy-start | bytes 884740
  0.0 10.9 %copy-start.1 = (f32[2,12,41472]{2,0,1:T(2,128)S(1)}, f32[2,12,41472]{2,0,1:T(2,128)}, u32[]{:S(2)}) copy-start(f32[2,12,41472]{2,0,1:T(2,128)} %param.12) | copy-start | bytes 11943940
  2.1 20.1 %collective-permute-start.3 = (f32[48,1536]{1,0:T(8,128)S(1)}, f32[48,1536]{1,0:T(8,128)S(1)}, u32[]{:S(2)}, u32[]{:S(2)}) collective-permute-start(f32[48,1536]{1,0:T(8,128)S(1)} %get-tuple-element.46), channel_id=1, source_target_pairs={{0,2},{1,3},{2,0},{3,1},{4,6},{5,7},{6,4},{7,5},{8,10},{9,11},{10,... | collective-permute-start | bytes 884744 | tf_op jit(solution)/shard_map/ppermute | solution.py:928
  6.3 0.8 copy-start.2
  7.1 3.8 %copy-start.7 = (f32[4,32]{1,0:T(4,128)S(1)}, f32[4,32]{1,0:T(4,128)}, u32[]{:S(2)}) copy-start(f32[4,32]{1,0:T(4,128)} %metric.5) | copy-start | bytes 1540
  8.3 19.3 %collective-permute-start.2 = (f32[48,1536]{1,0:T(8,128)S(1)}, f32[48,1536]{1,0:T(8,128)S(1)}, u32[]{:S(2)}, u32[]{:S(2)}) collective-permute-start(f32[48,1536]{1,0:T(8,128)S(1)} %get-tuple-element.45), channel_id=1, source_target_pairs={{0,1},{1,0},{2,3},{3,2},{4,5},{5,4},{6,7},{7,6},{8,9},{9,8},{10,11... | collective-permute-start | bytes 884744 | tf_op jit(solution)/shard_map/ppermute | solution.py:928
  9.8 18.8 %collective-permute-start = (f32[48,1408]{1,0:T(8,128)S(1)}, f32[48,1408]{1,0:T(8,128)S(1)}, u32[]{:S(2)}, u32[]{:S(2)}) collective-permute-start(f32[48,1408]{1,0:T(8,128)S(1)} %get-tuple-element.43), channel_id=1, source_target_pairs={{0,3},{1,2},{2,1},{3,0},{4,7},{5,6},{6,5},{7,4},{8,11},{9,10},{10,... | collective-permute-start | bytes 811016 | tf_op jit(solution)/shard_map/ppermute | solution.py:928
  9.9 18.8 %collective-permute-start.1 = (f32[48,128]{1,0:T(8,128)S(1)}, f32[48,128]{1,0:T(8,128)S(1)}, u32[]{:S(2)}, u32[]{:S(2)}) collective-permute-start(f32[48,128]{1,0:T(8,128)S(1)} %get-tuple-element.44), channel_id=1, source_target_pairs={{1,2},{2,1},{5,6},{6,5},{9,10},{10,9},{13,14},{14,13},{17,18},{18,... | collective-permute-start | bytes 73736 | tf_op jit(solution)/shard_map/ppermute | solution.py:928
  10.9 17.0 %copy-start.4 = (bf16[4,128,144]{2,1,0:T(8,128)(2,1)S(1)}, bf16[4,128,144]{2,1,0:T(8,128)(2,1)}, u32[]{:S(2)}) copy-start(bf16[4,128,144]{2,1,0:T(8,128)(2,1)} %constant.12.clone.to_span) | copy-start | bytes 442372
  27.9 1.1 %copy-start.5 = (bf16[4,128,48]{2,1,0:T(8,128)(2,1)S(1)}, bf16[4,128,48]{2,1,0:T(8,128)(2,1)}, u32[]{:S(2)}) copy-start(bf16[4,128,48]{2,1,0:T(8,128)(2,1)} %constant.13.clone.to_span) | copy-start | bytes 147460
  27.9 1.1 %copy-start.6 = (bf16[4,64,192]{2,1,0:T(8,128)(2,1)S(1)}, bf16[4,64,192]{2,1,0:T(8,128)(2,1)}, u32[]{:S(2)}) copy-start(bf16[4,64,192]{2,1,0:T(8,128)(2,1)} %constant.14.clone.to_modes) | copy-start | bytes 294916
  28.6 7.8 %copy-start.8 = (s32[1,5,24]{2,0,1:T(1,128)S(1)}, s32[1,5,24]{2,0,1:T(1,128)}, u32[]{:S(2)}) copy-start(s32[1,5,24]{2,0,1:T(1,128)} %param.13) | copy-start | bytes 1444
  28.6 7.8 %copy-start.9 = (s32[1,5,24]{2,0,1:T(1,128)S(1)}, s32[1,5,24]{2,0,1:T(1,128)}, u32[]{:S(2)}) copy-start(s32[1,5,24]{2,0,1:T(1,128)} %param.14) | copy-start | bytes 1444
  28.7 8.0 %copy-start.3 = (f32[24,384]{1,0:T(8,128)S(1)}, f32[24,384]{1,0:T(8,128)}, u32[]{:S(2)}) copy-start(f32[24,384]{1,0:T(8,128)} %constant.10.clone.far_bands.bands) | copy-start | bytes 110596
  30.0 15.2 %collective-permute-start.4 = (f32[8,3968]{1,0:T(8,128)S(1)}, f32[8,3968]{1,0:T(8,128)S(1)}, u32[]{:S(2)}, u32[]{:S(2)}) collective-permute-start(f32[8,3968]{1,0:T(8,128)S(1)} %get-tuple-element.50), channel_id=1, source_target_pairs={{0,2},{1,3},{2,0},{3,1},{4,6},{5,7},{6,4},{7,5},{8,10},{9,11},{10,... | collective-permute-start | bytes 380936 | tf_op jit(solution)/shard_map/ppermute | solution.py:928
  35.8 9.3 %collective-permute-start.5 = (f32[8,3968]{1,0:T(8,128)S(1)}, f32[8,3968]{1,0:T(8,128)S(1)}, u32[]{:S(2)}, u32[]{:S(2)}) collective-permute-start(f32[8,3968]{1,0:T(8,128)S(1)} %get-tuple-element.51), channel_id=1, source_target_pairs={{0,3},{1,2},{2,1},{3,0},{4,7},{5,6},{6,5},{7,4},{8,11},{9,10},{10,... | collective-permute-start | bytes 380936 | tf_op jit(solution)/shard_map/ppermute | solution.py:928
  36.3 10.0 %collective-permute-start.6 = (f32[8,3968]{1,0:T(8,128)S(1)}, f32[8,3968]{1,0:T(8,128)S(1)}, u32[]{:S(2)}, u32[]{:S(2)}) collective-permute-start(f32[8,3968]{1,0:T(8,128)S(1)} %get-tuple-element.52), channel_id=1, source_target_pairs={{0,1},{1,0},{2,3},{3,2},{4,5},{5,4},{6,7},{7,6},{8,9},{9,8},{10,11... | collective-permute-start | bytes 380936 | tf_op jit(solution)/shard_map/ppermute | solution.py:928
  47.8 4.7 %collective-permute-start.10 = (f32[48,256]{1,0:T(8,128)S(1)}, f32[48,256]{1,0:T(8,128)S(1)}, u32[]{:S(2)}, u32[]{:S(2)}) collective-permute-start(f32[48,256]{1,0:T(8,128)S(1)} %get-tuple-element.58), channel_id=1, source_target_pairs={{0,4},{4,0},{8,12},{12,8},{16,20},{20,16},{24,28},{28,24},{1,5},{5... | collective-permute-start | bytes 147464 | tf_op jit(solution)/shard_map/ppermute | solution.py:1039
  47.9 4.7 %collective-permute-start.7 = (f32[48,256]{1,0:T(8,128)S(1)}, f32[48,256]{1,0:T(8,128)S(1)}, u32[]{:S(2)}, u32[]{:S(2)}) collective-permute-start(f32[48,256]{1,0:T(8,128)S(1)} %get-tuple-element.55), channel_id=1, source_target_pairs={{0,28},{4,8},{8,4},{12,16},{16,12},{20,24},{24,20},{28,0},{1,29},{... | collective-permute-start | bytes 147464 | tf_op jit(solution)/shard_map/ppermute | solution.py:1039
  50.4 5.0 %collective-permute-start.8 = (f32[48,256]{1,0:T(8,128)S(1)}, f32[48,256]{1,0:T(8,128)S(1)}, u32[]{:S(2)}, u32[]{:S(2)}) collective-permute-start(f32[48,256]{1,0:T(8,128)S(1)} %get-tuple-element.56), channel_id=1, source_target_pairs={{0,24},{4,28},{8,16},{12,20},{16,8},{20,12},{24,0},{28,4},{1,25},{... | collective-permute-start | bytes 147464 | tf_op jit(solution)/shard_map/ppermute | solution.py:1039
  51.0 4.5 %collective-permute-start.9 = (f32[48,256]{1,0:T(8,128)S(1)}, f32[48,256]{1,0:T(8,128)S(1)}, u32[]{:S(2)}, u32[]{:S(2)}) collective-permute-start(f32[48,256]{1,0:T(8,128)S(1)} %get-tuple-element.57), channel_id=1, source_target_pairs={{0,8},{4,12},{8,0},{12,4},{16,24},{20,28},{24,16},{28,20},{1,9},{5... | collective-permute-start | bytes 147464 | tf_op jit(solution)/shard_map/ppermute | solution.py:1039
  56.6 22.6 %collective-permute-start.14 = (f32[48,1536]{1,0:T(8,128)S(1)}, f32[48,1536]{1,0:T(8,128)S(1)}, u32[]{:S(2)}, u32[]{:S(2)}) collective-permute-start(f32[48,1536]{1,0:T(8,128)S(1)} %get-tuple-element.64), channel_id=1, source_target_pairs={{0,2},{1,3},{2,0},{3,1},{4,6},{5,7},{6,4},{7,5},{8,10},{9,11},{10,... | collective-permute-start | bytes 884744 | tf_op jit(solution)/shard_map/ppermute | solution.py:928
  58.9 20.6 %collective-permute-start.13 = (f32[48,1536]{1,0:T(8,128)S(1)}, f32[48,1536]{1,0:T(8,128)S(1)}, u32[]{:S(2)}, u32[]{:S(2)}) collective-permute-start(f32[48,1536]{1,0:T(8,128)S(1)} %get-tuple-element.63), channel_id=1, source_target_pairs={{0,1},{1,0},{2,3},{3,2},{4,5},{5,4},{6,7},{7,6},{8,9},{9,8},{10,11... | collective-permute-start | bytes 884744 | tf_op jit(solution)/shard_map/ppermute | solution.py:928
  60.1 20.4 %collective-permute-start.11 = (f32[48,1408]{1,0:T(8,128)S(1)}, f32[48,1408]{1,0:T(8,128)S(1)}, u32[]{:S(2)}, u32[]{:S(2)}) collective-permute-start(f32[48,1408]{1,0:T(8,128)S(1)} %get-tuple-element.61), channel_id=1, source_target_pairs={{0,3},{1,2},{2,1},{3,0},{4,7},{5,6},{6,5},{7,4},{8,11},{9,10},{10,... | collective-permute-start | bytes 811016 | tf_op jit(solution)/shard_map/ppermute | solution.py:928
  62.6 17.9 %collective-permute-start.12 = (f32[48,128]{1,0:T(8,128)S(1)}, f32[48,128]{1,0:T(8,128)S(1)}, u32[]{:S(2)}, u32[]{:S(2)}) collective-permute-start(f32[48,128]{1,0:T(8,128)S(1)} %get-tuple-element.62), channel_id=1, source_target_pairs={{1,2},{2,1},{5,6},{6,5},{9,10},{10,9},{13,14},{14,13},{17,18},{18,... | collective-permute-start | bytes 73736 | tf_op jit(solution)/shard_map/ppermute | solution.py:928
  81.8 13.6 %collective-permute-start.15 = (f32[8,3968]{1,0:T(8,128)S(1)}, f32[8,3968]{1,0:T(8,128)S(1)}, u32[]{:S(2)}, u32[]{:S(2)}) collective-permute-start(f32[8,3968]{1,0:T(8,128)S(1)} %get-tuple-element.68), channel_id=1, source_target_pairs={{0,2},{1,3},{2,0},{3,1},{4,6},{5,7},{6,4},{7,5},{8,10},{9,11},{10,... | collective-permute-start | bytes 380936 | tf_op jit(solution)/shard_map/ppermute | solution.py:928
  86.1 9.3 %collective-permute-start.16 = (f32[8,3968]{1,0:T(8,128)S(1)}, f32[8,3968]{1,0:T(8,128)S(1)}, u32[]{:S(2)}, u32[]{:S(2)}) collective-permute-start(f32[8,3968]{1,0:T(8,128)S(1)} %get-tuple-element.69), channel_id=1, source_target_pairs={{0,3},{1,2},{2,1},{3,0},{4,7},{5,6},{6,5},{7,4},{8,11},{9,10},{10,... | collective-permute-start | bytes 380936 | tf_op jit(solution)/shard_map/ppermute | solution.py:928
  88.0 8.5 %collective-permute-start.17 = (f32[8,3968]{1,0:T(8,128)S(1)}, f32[8,3968]{1,0:T(8,128)S(1)}, u32[]{:S(2)}, u32[]{:S(2)}) collective-permute-start(f32[8,3968]{1,0:T(8,128)S(1)} %get-tuple-element.70), channel_id=1, source_target_pairs={{0,1},{1,0},{2,3},{3,2},{4,5},{5,4},{6,7},{7,6},{8,9},{9,8},{10,11... | collective-permute-start | bytes 380936 | tf_op jit(solution)/shard_map/ppermute | solution.py:928
  98.0 4.6 %collective-permute-start.18 = (f32[48,256]{1,0:T(8,128)S(1)}, f32[48,256]{1,0:T(8,128)S(1)}, u32[]{:S(2)}, u32[]{:S(2)}) collective-permute-start(f32[48,256]{1,0:T(8,128)S(1)} %get-tuple-element.73), channel_id=1, source_target_pairs={{0,28},{4,8},{8,4},{12,16},{16,12},{20,24},{24,20},{28,0},{1,29},{... | collective-permute-start | bytes 147464 | tf_op jit(solution)/shard_map/ppermute | solution.py:1039
  98.2 5.2 %collective-permute-start.19 = (f32[48,256]{1,0:T(8,128)S(1)}, f32[48,256]{1,0:T(8,128)S(1)}, u32[]{:S(2)}, u32[]{:S(2)}) collective-permute-start(f32[48,256]{1,0:T(8,128)S(1)} %get-tuple-element.74), channel_id=1, source_target_pairs={{0,24},{4,28},{8,16},{12,20},{16,8},{20,12},{24,0},{28,4},{1,25},{... | collective-permute-start | bytes 147464 | tf_op jit(solution)/shard_map/ppermute | solution.py:1039
  100.1 4.4 %collective-permute-start.20 = (f32[48,256]{1,0:T(8,128)S(1)}, f32[48,256]{1,0:T(8,128)S(1)}, u32[]{:S(2)}, u32[]{:S(2)}) collective-permute-start(f32[48,256]{1,0:T(8,128)S(1)} %get-tuple-element.75), channel_id=1, source_target_pairs={{0,8},{4,12},{8,0},{12,4},{16,24},{20,28},{24,16},{28,20},{1,9},{5... | collective-permute-start | bytes 147464 | tf_op jit(solution)/shard_map/ppermute | solution.py:1039
  100.6 3.9 %collective-permute-start.21 = (f32[48,256]{1,0:T(8,128)S(1)}, f32[48,256]{1,0:T(8,128)S(1)}, u32[]{:S(2)}, u32[]{:S(2)}) collective-permute-start(f32[48,256]{1,0:T(8,128)S(1)} %get-tuple-element.76), channel_id=1, source_target_pairs={{0,4},{4,0},{8,12},{12,8},{16,20},{20,16},{24,28},{28,24},{1,5},{5... | collective-permute-start | bytes 147464 | tf_op jit(solution)/shard_map/ppermute | solution.py:1039
